TPU v7x, 32 devices: a whole 2x2x4 slice. The times are simulated.
32 devices in a mesh: seq: 8 (over y, x, core), lvl: 4 (over z).
Axes of the slice: x: 2, y: 2, z: 4, core: 2. Of those that a mesh axis runs over, the one named last changes fastest.
Arguments:
- queries: bfloat16 [16384, 1024], P(('seq', 'lvl')), may hold values from -24 to 24
- keys: bfloat16 [16384, 1024], P(('seq', 'lvl')), may hold values from -24 to 24
- values: bfloat16 [16384, 1024], P(('seq', 'lvl')), may hold values from -6 to 6
- grad_out: bfloat16 [16384, 1024], P(('seq', 'lvl')), may hold values from -6 to 6
- mid_offset: int32 [8], replicated, may hold values from 0 to 3
- far_offset: int32 [8], replicated, may hold values from 0 to 31
Outputs:
- grad_queries: bfloat16 [16384, 1024], P(('seq', 'lvl'))
- grad_keys: bfloat16 [16384, 1024], P(('seq', 'lvl'))
- grad_values: bfloat16 [16384, 1024], P(('seq', 'lvl'))
All inputs are finite; a program needn't handle non-finite values.
Results may differ from a plain program's by a relative error of at most 0.0087.
Values may be sent and summed in bfloat16 or wider, within the bound.
No kernel may reach another device: no remote copies, remote signals or barrier semaphores. Data moves between devices by JAX's collectives and lax.ppermute only.
A program may use at most 128 MiB of HBM per device.

v0:
```python
import jax
import jax.numpy as jnp
from jax import lax
from jax.sharding import PartitionSpec as P


def onehot_table(offset, stride, dtype):
    return (jnp.arange(stride)[:, None] == offset[None, :]).astype(dtype)


def select_rows(source, offset, stride):
    groups = source.shape[0] // stride
    shaped = source.reshape(groups, stride, source.shape[1], source.shape[2])
    onehot = onehot_table(offset, stride, source.dtype)
    return jnp.einsum("nrhd,rh->nhd", shaped, onehot, preferred_element_type=jnp.float32).astype(
        source.dtype
    )


def select_stats(stat_rows, offset, stride):
    groups = stat_rows.shape[0] // stride
    onehot = onehot_table(offset, stride, jnp.float32)
    return jnp.sum(stat_rows.reshape(groups, stride, stat_rows.shape[1]) * onehot[None], axis=1)


def spread_rows(pieces, offset, stride):
    onehot = onehot_table(offset, stride, jnp.float32)
    whole_rows = pieces[:, None] * onehot[None, :, :, None]
    return whole_rows.reshape(pieces.shape[0] * stride, pieces.shape[1], pieces.shape[2])


def spread_stats(stat_rows, offset, stride):
    chosen = jnp.arange(stride)[:, None] == offset[None, :]
    whole_rows = jnp.where(chosen[None], stat_rows[:, None, :], -jnp.inf)
    return whole_rows.reshape(stat_rows.shape[0] * stride, stat_rows.shape[1])


def head_scores(query_part, key_part, score_scale):
    return (
        jnp.einsum("qhd,khd->hqk", query_part, key_part, preferred_element_type=jnp.float32)
        * score_scale
    )


def masked_logs(scores, allowed):
    peak_score = jnp.max(jnp.where(allowed[None], scores, -jnp.inf), axis=2)
    exp_total = jnp.sum(
        jnp.where(allowed[None], jnp.exp(scores - peak_score[:, :, None]), 0.0), axis=2
    )
    return (peak_score + jnp.log(exp_total)).T


def soft_weights(scores, allowed, log_part):
    return jnp.where(allowed[None], jnp.exp(scores - log_part.T[:, :, None]), 0.0)


def score_grads(weight_part, grad_part, value_part, delta_part, score_scale):
    grad_weights = jnp.einsum(
        "qhd,khd->hqk", grad_part, value_part, preferred_element_type=jnp.float32
    )
    return (weight_part * (grad_weights - delta_part.T[:, :, None]) * score_scale).astype(
        jnp.bfloat16
    )


def local(queries, keys, values, grad_out, mid_offset, far_offset):
    row_count = queries.shape[0]
    head_count = mid_offset.shape[0]
    head_width = queries.shape[1] // head_count
    flat_width = head_count * head_width
    score_scale = head_width ** (-0.5)
    query_rows = queries.reshape(row_count, head_count, head_width)
    key_rows = keys.reshape(row_count, head_count, head_width)
    value_rows = values.reshape(row_count, head_count, head_width)
    grad_rows = grad_out.reshape(row_count, head_count, head_width)
    level_count = lax.axis_size("lvl")
    sequence_count = lax.axis_size("seq")
    level_index = lax.axis_index("lvl")
    flat_index = lax.axis_index("seq") * level_count + level_index
    position = jnp.arange(row_count)
    near_allowed = position[None, :] <= position[:, None]
    near_scores = head_scores(query_rows, key_rows, score_scale)
    log_total = masked_logs(near_scores, near_allowed)
    levels = []
    for level_name in ("mid", "far"):
        if level_name == "mid":
            stride, offset, group_index = (level_count, mid_offset, level_index)
        else:
            stride, offset, group_index = (sequence_count * level_count, far_offset, flat_index)
        picked_count = row_count // stride
        picked = [
            select_rows(source, offset, stride)
            for source in (query_rows, key_rows, value_rows, grad_rows)
        ]
        packed = (
            picked[1].reshape(picked_count, flat_width),
            picked[2].reshape(picked_count, flat_width),
        )
        if level_name == "mid":
            gathered = (
                lax.all_gather(packed[0], "lvl", axis=0, tiled=True),
                lax.all_gather(packed[1], "lvl", axis=0, tiled=True),
            )
        else:
            gathered = (
                lax.all_gather(packed[0], ("seq", "lvl"), axis=0, tiled=True),
                lax.all_gather(packed[1], ("seq", "lvl"), axis=0, tiled=True),
            )
        key_all = gathered[0].reshape(row_count, head_count, head_width)
        value_all = gathered[1].reshape(row_count, head_count, head_width)
        own_index = group_index * picked_count + jnp.arange(picked_count)
        allowed = position[None, :] <= own_index[:, None]
        scores = head_scores(picked[0], key_all, score_scale)
        level_logs = masked_logs(scores, allowed)
        log_total = jnp.logaddexp(log_total, spread_stats(level_logs, offset, stride))
        levels.append(
            (
                level_name,
                stride,
                offset,
                picked_count,
                own_index,
                picked,
                key_all,
                value_all,
                allowed,
                scores,
            )
        )
    near_weights = soft_weights(near_scores, near_allowed, log_total)
    near_cast = near_weights.astype(jnp.bfloat16)
    merged = jnp.einsum("hqk,khd->qhd", near_cast, value_rows, preferred_element_type=jnp.float32)
    level_extra = []
    for level_data in levels:
        (
            level_name,
            stride,
            offset,
            picked_count,
            own_index,
            picked,
            key_all,
            value_all,
            allowed,
            scores,
        ) = level_data
        log_part = select_stats(log_total, offset, stride)
        level_weights = soft_weights(scores, allowed, log_part)
        weights_cast = level_weights.astype(jnp.bfloat16)
        level_output = jnp.einsum(
            "hqk,khd->qhd", weights_cast, value_all, preferred_element_type=jnp.float32
        )
        merged = merged + spread_rows(level_output, offset, stride)
        level_extra.append((log_part, level_weights, weights_cast))
    delta_rows = jnp.sum(grad_rows.astype(jnp.float32) * merged, axis=2)
    near_grads = score_grads(near_weights, grad_rows, value_rows, delta_rows, score_scale)
    grad_query = jnp.einsum(
        "hqk,khd->qhd", near_grads, key_rows, preferred_element_type=jnp.float32
    )
    grad_key = jnp.einsum(
        "hqk,qhd->khd", near_grads, query_rows, preferred_element_type=jnp.float32
    )
    grad_value = jnp.einsum(
        "hqk,qhd->khd", near_cast, grad_rows, preferred_element_type=jnp.float32
    )
    for level_data, extra_data in zip(levels, level_extra):
        (
            level_name,
            stride,
            offset,
            picked_count,
            own_index,
            picked,
            key_all,
            value_all,
            allowed,
            scores,
        ) = level_data
        log_part, level_weights, weights_cast = extra_data
        delta_part = select_stats(delta_rows, offset, stride)
        grad_scores = score_grads(level_weights, picked[3], value_all, delta_part, score_scale)
        query_part = jnp.einsum(
            "hqk,khd->qhd", grad_scores, key_all, preferred_element_type=jnp.float32
        )
        grad_query = grad_query + spread_rows(query_part, offset, stride)
        packed_rows = (
            picked[0].reshape(picked_count, flat_width),
            picked[3].reshape(picked_count, flat_width),
        )
        packed_stats = (log_part, delta_part)
        if level_name == "mid":
            query_flat, grad_flat = (
                lax.all_gather(packed_rows[0], "lvl", axis=0, tiled=True),
                lax.all_gather(packed_rows[1], "lvl", axis=0, tiled=True),
            )
            log_all, delta_all = (
                lax.all_gather(packed_stats[0], "lvl", axis=0, tiled=True),
                lax.all_gather(packed_stats[1], "lvl", axis=0, tiled=True),
            )
        else:
            query_flat, grad_flat = (
                lax.all_gather(packed_rows[0], ("seq", "lvl"), axis=0, tiled=True),
                lax.all_gather(packed_rows[1], ("seq", "lvl"), axis=0, tiled=True),
            )
            log_all, delta_all = (
                lax.all_gather(packed_stats[0], ("seq", "lvl"), axis=0, tiled=True),
                lax.all_gather(packed_stats[1], ("seq", "lvl"), axis=0, tiled=True),
            )
        query_all = query_flat.reshape(row_count, head_count, head_width)
        grad_all = grad_flat.reshape(row_count, head_count, head_width)
        back_allowed = own_index[None, :] <= position[:, None]
        back_scores = head_scores(query_all, picked[1], score_scale)
        back_weights = soft_weights(back_scores, back_allowed, log_all)
        back_grads = score_grads(back_weights, grad_all, picked[2], delta_all, score_scale)
        key_part = jnp.einsum(
            "hqk,qhd->khd", back_grads, query_all, preferred_element_type=jnp.float32
        )
        value_part = jnp.einsum(
            "hqk,qhd->khd",
            back_weights.astype(jnp.bfloat16),
            grad_all,
            preferred_element_type=jnp.float32,
        )
        grad_key = grad_key + spread_rows(key_part, offset, stride)
        grad_value = grad_value + spread_rows(value_part, offset, stride)
    return (
        grad_query.reshape(row_count, flat_width).astype(jnp.bfloat16),
        grad_key.reshape(row_count, flat_width).astype(jnp.bfloat16),
        grad_value.reshape(row_count, flat_width).astype(jnp.bfloat16),
    )


def solution(mesh):
    in_specs = (
        P(("seq", "lvl"), None),
        P(("seq", "lvl"), None),
        P(("seq", "lvl"), None),
        P(("seq", "lvl"), None),
        P(),
        P(),
    )
    out_specs = (P(("seq", "lvl"), None), P(("seq", "lvl"), None), P(("seq", "lvl"), None))
    return jax.shard_map(local, mesh=mesh, in_specs=in_specs, out_specs=out_specs, check_vma=False)
```

profile of v0, /device:TPU:0, one launch (start us, length us, event | category | flops | bytes accessed | tf_op | source)
XLA Modules:
  0.0 458.4 jit_solution(4415075588341511142)
XLA Ops:
  7.2 1.6 copy.306
  10.8 3.0 multiply_reduce_fusion
  13.8 1.8 copy.253
  17.0 1.5 fusion.33
  19.3 1.0 fusion.31
  21.0 1.8 copy.271
  22.9 1.1 fusion.35
  25.3 1.0 fusion.29
  27.0 1.8 copy.246
  31.3 1.6 copy.302
  33.0 1.3 copy.175
  34.3 2.3 copy.304
  41.6 1.5 select_reduce_fusion.1
  43.2 3.2 copy-done
  46.4 1.7 select_reduce_fusion
  48.7 1.8 select_reduce_fusion.3
  50.6 1.4 copy-done.7
  52.9 50.9 %all-gather.13.cloned.1.call-done = bf16[512,1024]{1,0:T(8,128)(2,1)} async-done(((bf16[16,1024]{1,0:T(8,128)(2,1)}), bf16[512,1024]{1,0:T(8,128)(2,1)}) %all-gather.13.cloned.1.call-update) | async-done | bytes 1048592 | tf_op jit(solution)/shard_map/all_gather | solution.py:106
  103.8 1.5 copy.172
  107.6 51.9 %all-gather.17.cloned.1.call-done = bf16[512,1024]{1,0:T(8,128)(2,1)} async-done(((bf16[16,1024]{1,0:T(8,128)(2,1)}), bf16[512,1024]{1,0:T(8,128)(2,1)}) %all-gather.17.cloned.1.call-update) | async-done | bytes 1048592 | tf_op jit(solution)/shard_map/all_gather | solution.py:107
  159.6 1.5 copy.185
  161.5 1.4 mul.220
  163.0 2.9 copy.191
  165.9 1.1 multiply_reduce_fusion.7
  167.7 22.5 %all-gather.15.cloned.1.call-done = bf16[512,1024]{0,1:T(8,128)(2,1)} async-done(((bf16[128,1024]{0,1:T(8,128)(2,1)}), bf16[512,1024]{0,1:T(8,128)(2,1)}) %all-gather.15.cloned.1.call-update) | async-done | bytes 1048592 | tf_op jit(solution)/shard_map/all_gather | solution.py:102
  190.2 3.3 convolution_bitcast_fusion.1
  193.4 2.1 copy.182
  195.5 2.5 mul.213
  198.0 3.0 copy.184
  201.0 8.1 %fusion.9 = f32[512,8]{0,1:T(8,128)} fusion(f32[512,8,128]{0,2,1:T(8,128)} %copy.191, f32[512,8,128]{0,2,1:T(8,128)} %copy.184, bf16[512,8,128]{0,2,1:T(8,128)(2,1)} %bitcast.300, bf16[512,8,128]{0,2,1:T(8,128)(2,1)} %bitcast.303, f32[512,8]{0,1:T(8,128)} %copy.190, f32[512,8]{0,1:T(8,128)} %copy.183, f32[8,512,512]{1,2,0:T(8,128)} %copy-done, ...), kind=kOutput, calls=%fused_computation.17 | convolution fusion | flops 548925440 | bytes 15007744 | tf_op jit(solution)/shard_map/hqk,khd->qhd/dot_general | solution.py:132
  209.0 1.6 copy.197
  210.6 1.6 multiply_reduce_fusion.4
  212.2 1.4 copy.226
  214.3 1.9 fusion.26
  217.1 1.5 mul.237
  218.6 2.0 copy.207
  222.3 4.4 fusion.13
  226.7 2.0 copy.199
  228.8 2.5 mul.231
  231.3 3.0 copy.200
  234.3 7.3 %multiply_convert_fusion = bf16[8,512,512]{1,2,0:T(8,128)(2,1)S(1)} fusion(f32[8,512,512]{1,2,0:T(8,128)} %copy-done, f32[8,512]{1,0:T(8,128)S(1)} %bitcast.333, f32[8,512]{1,0:T(8,128)S(1)} %bitcast.331, pred[512,512]{0,1:T(8,128)(4,1)S(1)} %copy-done.18, bf16[512,8,128]{0,2,1:T(8,128)(2,1)} %bitcast.304, bf16[512,8,128]{0,2,1:T(8,128)(2,1)} %bitcast.301), kind=kOutput, calls=%fused_computation | convolution fusion | flops 551550976 | bytes 14974976 | tf_op jit(solution)/shard_map/qhd,khd->hqk/dot_general | solution.py:58
  241.7 2.3 fusion.6
  244.0 2.3 copy.237
  246.3 66.9 %all-gather = f32[32,16,8]{1,2,0:T(8,128)S(1)} all-gather(f32[1,16,8]{1,2,0:T(8,128)S(1)} %bitcast.334), channel_id=1, replica_groups=mesh['seq'=8,'lvl'=4] {'seq','lvl'}, dimensions={0}, use_global_device_ids=true | all-gather | bytes 16896 | tf_op jit(solution)/shard_map/all_gather | solution.py:206
  313.4 65.2 %all-gather.1 = f32[32,16,8]{1,2,0:T(8,128)S(1)} all-gather(f32[1,16,8]{1,2,0:T(8,128)S(1)} %bitcast.335), channel_id=1, replica_groups=mesh['seq'=8,'lvl'=4] {'seq','lvl'}, dimensions={0}, use_global_device_ids=true | all-gather | bytes 16896 | tf_op jit(solution)/shard_map/all_gather | solution.py:207
  379.3 1.5 copy.218
  380.8 1.5 copy.223
  382.6 1.3 fusion.27
  384.0 1.4 mul.249
  385.4 3.0 copy.230
  388.4 14.5 %all_gather.41 = f32[512,8]{1,0:T(8,128)S(1)} all-gather(f32[128,8]{1,0:T(8,128)S(1)} %multiply_reduce_fusion.7), channel_id=1, replica_groups=mesh['seq'=8,'lvl'=4] {'lvl'}, dimensions={0}, use_global_device_ids=true | all-gather | bytes 20480 | tf_op jit(solution)/shard_map/all_gather | solution.py:197
  403.0 13.8 %all_gather.43 = f32[512,8]{1,0:T(8,128)S(1)} all-gather(f32[128,8]{1,0:T(8,128)S(1)} %copy-done.22), channel_id=1, replica_groups=mesh['seq'=8,'lvl'=4] {'lvl'}, dimensions={0}, use_global_device_ids=true | all-gather | bytes 20480 | tf_op jit(solution)/shard_map/all_gather | solution.py:198
  417.2 2.4 exponential_select_fusion.1
  419.7 2.5 convolution_bitcast_fusion
  422.2 3.4 fusion.14
  425.7 1.3 copy.216
  427.0 1.5 mul.243
  428.4 3.1 copy.217
  431.5 5.3 %fusion.4 = bf16[512,8,128]{0,2,1:T(8,128)(2,1)} fusion(f32[512,8,128]{0,2,1:T(8,128)S(1)} %copy-done.5, f32[512,8,128]{0,2,1:T(8,128)} %copy.217, bf16[8,512,512]{1,2,0:T(8,128)(2,1)} %copy-done.1, bf16[512,8,128]{0,2,1:T(8,128)(2,1)S(1)} %bitcast.272, f32[512,8]{0,1:T(8,128)S(1)} %copy-done.29, f32[512,8]{0,1:T(8,128)S(1)} %copy-done.31), kind=kOutput, calls=%fused_computation.10 | convolution fusion | flops 539492352 | bytes 10518528 | tf_op jit(solution)/shard_map/hqk,qhd->khd/dot_general | solution.py:160
  436.8 2.3 copy.238
  439.3 1.9 copy.236
  441.6 1.8 copy.233
  443.4 6.8 %fusion.2 = bf16[512,8,128]{0,2,1:T(8,128)(2,1)S(1)} fusion(f32[512,8,128]{0,2,1:T(8,128)} %copy.236, f32[512,8,128]{0,2,1:T(8,128)} %copy.233, bf16[512,8,128]{0,2,1:T(8,128)(2,1)S(1)} %bitcast.302, f32[512,8]{0,1:T(8,128)S(1)} %copy-done.29, f32[512,8]{0,1:T(8,128)S(1)} %copy-done.31, f32[8,512,512]{1,2,0:T(8,128)} %copy-done, f32[8,512]{1,0:T(8,128)S(1)} %bitcast.332, ...), kind=kOutput, calls=%fused_computation.7 | convolution fusion | flops 547880960 | bytes 14991360 | tf_op jit(solution)/shard_map/hqk,qhd->khd/dot_general | solution.py:163
  450.2 1.3 copy.239
  (186 shorter events, 24.8 us)
Async XLA Ops:
  7.2 1.7 copy-start.12
  7.2 41.5 %all-gather.11.cloned.1.call-start = ((), (), s32[]{:S(2)}) async-start(), calls=%async_computation | async-start | bytes 1310720 | tf_op jit(solution)/shard_map/all_gather | solution.py:101
  7.2 2.0 copy-start.8
  8.9 2.0 copy-start.2
  8.9 0.7 copy-start.48
  8.9 1.6 copy-start.10
  10.8 4.9 %copy-start.49 = (s32[8]{0:T(128)S(1)}, s32[8]{0:T(128)}, u32[]{:S(2)}) copy-start(s32[8]{0:T(128)} %param.11) | copy-start | bytes 100
  15.7 88.1 %all-gather.13.cloned.1.call-start = ((), (), s32[]{:S(2)}) async-start(), calls=%async_computation.1 | async-start | bytes 1081344 | tf_op jit(solution)/shard_map/all_gather | solution.py:106
  16.4 0.6 copy-start.34
  19.2 140.3 %all-gather.17.cloned.1.call-start = ((), (), s32[]{:S(2)}) async-start(), calls=%async_computation.3 | async-start | bytes 1081344 | tf_op jit(solution)/shard_map/all_gather | solution.py:107
  20.9 169.3 %all-gather.15.cloned.1.call-start = ((), (), s32[]{:S(2)}) async-start(), calls=%async_computation.2 | async-start | bytes 1310720 | tf_op jit(solution)/shard_map/all_gather | solution.py:102
  22.8 356.5 %all-gather.23.cloned.1.call-start = ((), (), s32[]{:S(2)}) async-start(), calls=%async_computation.6 | async-start | bytes 1081344 | tf_op jit(solution)/shard_map/all_gather | solution.py:202
  22.9 7.9 %copy-start.9 = (bf16[512,1024]{1,0:T(8,128)(2,1)S(1)}, bf16[512,1024]{1,0:T(8,128)(2,1)}, u32[]{:S(2)}) copy-start(bf16[512,1024]{1,0:T(8,128)(2,1)} %param.6) | copy-start | bytes 3145732
  23.9 0.6 copy-start.23
  24.6 5.4 %copy-start.24 = (bf16[8,1,16,128]{3,1,2,0:T(2,128)(2,1)S(1)}, bf16[8,1,16,128]{3,1,2,0:T(2,128)(2,1)}, u32[]{:S(2)}) copy-start(bf16[8,1,16,128]{3,1,2,0:T(2,128)(2,1)} %copy-done.23) | copy-start | bytes 98308
  25.3 355.6 %all-gather.25.cloned.1.call-start = ((), (), s32[]{:S(2)}) async-start(), calls=%async_computation.7 | async-start | bytes 1081344 | tf_op jit(solution)/shard_map/all_gather | solution.py:203
  26.3 4.5 copy-start.25
  27.0 390.3 %all-gather.19.cloned.1.call-start = ((), (), s32[]{:S(2)}) async-start(), calls=%async_computation.4 | async-start | bytes 1310720 | tf_op jit(solution)/shard_map/all_gather | solution.py:193
  28.9 390.8 %all-gather.21.cloned.1.call-start = ((), (), s32[]{:S(2)}) async-start(), calls=%async_computation.5 | async-start | bytes 1310720 | tf_op jit(solution)/shard_map/all_gather | solution.py:194
  30.8 12.4 %copy-start.17 = (pred[512,512]{0,1:T(8,128)(4,1)}, pred[512,512]{0,1:T(8,128)(4,1)S(1)}, u32[]{:S(2)}) copy-start(pred[512,512]{0,1:T(8,128)(4,1)S(1)} %iota_compare_fusion) | copy-start | bytes 786436
  31.3 1.6 copy-start.11
  32.9 8.6 %copy-start.3 = (bf16[512,1024]{0,1:T(8,128)(2,1)}, bf16[512,1024]{0,1:T(8,128)(2,1)S(1)}, u32[]{:S(2)}) copy-start(bf16[512,1024]{0,1:T(8,128)(2,1)S(1)} %copy.302) | copy-start | bytes 3145732
  34.3 2.3 copy-start.26
  34.3 5.7 %copy-start.45 = (pred[32,8]{1,0:T(8,128)(4,1)S(1)}, pred[32,8]{1,0:T(8,128)(4,1)}, u32[]{:S(2)}) copy-start(pred[32,8]{1,0:T(8,128)(4,1)} %get-tuple-element.22) | copy-start | bytes 772
  34.3 6.6 %copy-start.39 = (f32[4,8]{1,0:T(4,128)S(1)}, f32[4,8]{1,0:T(4,128)}, u32[]{:S(2)}) copy-start(f32[4,8]{1,0:T(4,128)} %get-tuple-element.19) | copy-start | bytes 388
  37.3 68.3 %copy-start.27 = (pred[16,512]{1,0:T(8,128)(4,1)}, pred[16,512]{1,0:T(8,128)(4,1)S(1)}, u32[]{:S(2)}) copy-start(pred[16,512]{1,0:T(8,128)(4,1)S(1)} %iota_compare_fusion.4) | copy-start | bytes 24580
  43.1 3.3 copy-start
  46.4 2.3 copy-start.16
  48.7 4.0 copy-start.47
  50.5 1.4 copy-start.7
  51.9 53.4 %copy-start.33 = (bf16[8,1,16,128]{3,0,2,1:T(8,128)(2,1)S(1)}, bf16[8,1,16,128]{3,0,2,1:T(8,128)(2,1)}, u32[]{:S(2)}) copy-start(bf16[8,1,16,128]{3,0,2,1:T(8,128)(2,1)} %copy.364) | copy-start | bytes 98308
  106.0 55.0 %copy-start.28 = (pred[16,512]{1,0:T(8,128)(4,1)S(1)}, pred[16,512]{1,0:T(8,128)(4,1)}, u32[]{:S(2)}) copy-start(pred[16,512]{1,0:T(8,128)(4,1)} %copy-done.27) | copy-start | bytes 24580
  106.1 0.6 copy-start.35
  106.8 0.8 copy-start.15
  107.6 53.4 %copy-start.38 = (f32[8,16]{1,0:T(8,128)}, f32[8,16]{1,0:T(8,128)S(1)}, u32[]{:S(2)}) copy-start(f32[8,16]{1,0:T(8,128)S(1)} %copy.187) | copy-start | bytes 1540
  218.6 2.0 copy-start.14
  218.6 2.0 copy-start.40
  218.6 3.7 copy-start.46
  231.3 3.0 copy-start.18
  231.3 3.0 copy-start.36
  231.3 3.0 copy-start.42
  234.3 7.4 %copy-start.4 = (bf16[512,1024]{0,1:T(8,128)(2,1)S(1)}, bf16[512,1024]{0,1:T(8,128)(2,1)}, u32[]{:S(2)}) copy-start(bf16[512,1024]{0,1:T(8,128)(2,1)} %copy-done.3) | copy-start | bytes 3145732
  234.3 7.4 %copy-start.6 = (f32[512,8,128]{0,2,1:T(8,128)S(1)}, f32[512,8,128]{0,2,1:T(8,128)}, u32[]{:S(2)}) copy-start(f32[512,8,128]{0,2,1:T(8,128)} %copy.200) | copy-start | bytes 6291460
  234.3 7.4 %copy-start.29 = (f32[512,8]{0,1:T(8,128)S(1)}, f32[512,8]{0,1:T(8,128)}, u32[]{:S(2)}) copy-start(f32[512,8]{0,1:T(8,128)} %copy.190) | copy-start | bytes 49156
  234.3 7.4 %copy-start.30 = (f32[512,8]{0,1:T(8,128)S(1)}, f32[512,8]{0,1:T(8,128)}, u32[]{:S(2)}) copy-start(f32[512,8]{0,1:T(8,128)} %copy.183) | copy-start | bytes 49156
  241.7 2.4 copy-start.1
  244.0 2.3 copy-start.43
  244.0 69.3 %copy-start.44 = (f32[16,8]{0,1:T(8,128)S(1)}, f32[16,8]{0,1:T(8,128)}, u32[]{:S(2)}) copy-start(f32[16,8]{0,1:T(8,128)} %copy.226) | copy-start | bytes 1540
  379.3 3.1 copy-start.32
  379.3 3.1 copy-start.41
  385.4 17.6 %copy-start.22 = (f32[128,8]{1,0:T(8,128)S(1)}, f32[128,8]{1,0:T(8,128)}, u32[]{:S(2)}) copy-start(f32[128,8]{1,0:T(8,128)} %multiply_reduce_fusion.5) | copy-start | bytes 12292
  419.7 2.6 copy-start.13
  428.4 3.1 copy-start.5
  428.4 3.1 copy-start.31
  439.3 1.9 copy-start.20
  441.6 1.9 copy-start.19
  441.6 1.9 copy-start.21
  441.6 1.9 copy-start.37
Sparse Core Ops, SparseCore 0:
  15.8 32.8 all-gather.10
  51.7 52.0 all-gather.12
  106.8 52.7 all-gather.16
  161.0 29.1 all-gather.14
  193.0 52.0 all-gather.22
  248.0 52.7 all-gather.24
  302.3 29.2 all-gather.18
  333.2 30.0 all-gather.20
where the time goes:
time: 460 us; the launch traced here: 458 us
  blocking collectives  160 us (35%)
  waiting for transfers between devices  126 us (27%)
  local copies, waits for them, and re-layouts  86 us (19%)
  matrix products  58.4 us (13%)
  between operations  14.9 us (3%)
  other arithmetic  12.1 us (3%)
    all_gather x1, blocking collectives, local(): lax.all_gather(packed_stats[0], ('seq', 'lvl'), axis=0, tiled=True)  66.9 us
    all_gather x1, blocking collectives, local(): lax.all_gather(packed_stats[1], ('seq', 'lvl'), axis=0, tiled=True)  65.2 us
    all_gather x1, waiting for transfers between devices, local(): lax.all_gather(packed[1], ('seq', 'lvl'), axis=0, tiled=True)  51.9 us
    all_gather x1, waiting for transfers between devices, local(): lax.all_gather(packed[0], ('seq', 'lvl'), axis=0, tiled=True)  50.9 us
    mul x18, local copies, waits for them, and re-layouts, spread_rows(): whole_rows = pieces[:, None] * onehot[None, :, :, None]  33.2 us
    all_gather x1, waiting for transfers between devices, local(): lax.all_gather(packed[1], 'lvl', axis=0, tiled=True)  22.5 us
    unnamed x114, local copies, waits for them, and re-layouts  20 us
    all_gather x1, blocking collectives, local(): lax.all_gather(packed_stats[0], 'lvl', axis=0, tiled=True)  14.5 us
  transfers between devices with their start and end apart: 8, of which 4 were waited for; matrix products, arithmetic and copies ran while one was open for 24% of the time, Pallas kernels for 0%

commit v1 on v0

v1 whole, which is shorter than its diff:
```python
import functools

import jax
import jax.numpy as jnp
from jax import lax
from jax.experimental import pallas as pl
from jax.experimental.pallas import tpu as pltpu
from jax.sharding import PartitionSpec as P

F32 = jnp.float32
BF16 = jnp.bfloat16
LANES = 128
LOW = -1e30
VMEM_LIMIT = 48 * 1024 * 1024


def mm(a, b):
    return lax.dot_general(a, b, (((1,), (0,)), ((), ())), preferred_element_type=F32)


def mm_t(a, b):
    return lax.dot_general(a, b, (((1,), (1,)), ((), ())), preferred_element_type=F32)


def t_mm(a, b):
    return lax.dot_general(a, b, (((0,), (0,)), ((), ())), preferred_element_type=F32)


def exact(a, b):
    return lax.dot_general(
        a, b, (((1,), (0,)), ((), ())), preferred_element_type=F32, precision=lax.Precision.HIGHEST
    )


def iota(shape, axis):
    return lax.broadcasted_iota(jnp.int32, shape, axis)


def params():
    return pltpu.CompilerParams(
        vmem_limit_bytes=VMEM_LIMIT, dimension_semantics=("arbitrary",)
    )


def smem():
    return pl.BlockSpec(memory_space=pltpu.SMEM)


def columns(rows, width):
    return pl.BlockSpec((rows, width), lambda h: (0, h))


def fixed(shape):
    return pl.BlockSpec(shape, lambda h: (0,) * len(shape))


def pick_lane(ref, head):
    block = ref[...]
    return jnp.sum(jnp.where(iota(block.shape, 1) == head, block, 0.0), axis=1, keepdims=True)


def put_lane(ref, rows, head, value):
    block = ref[rows, :]
    ref[rows, :] = jnp.where(iota(block.shape, 1) == head, value, block)


def select_kernel(place, mid_off, far_off, q, k, v, g, kv, qg, far, *pays):
    head = pl.program_id(0)
    level = place[1]
    rows = q.shape[0]
    whole = jnp.concatenate([k[...], v[...], q[...], g[...]], axis=1)

    def picked(count, offset):
        stride = rows // count
        table = iota((count, rows), 1) == iota((count, rows), 0) * stride + offset
        return mm(table.astype(BF16), whole).astype(BF16)

    mid = picked(kv.shape[0], mid_off[head])
    half = kv.shape[1]
    kv[...] = mid[:, :half]
    qg[...] = mid[:, half:]
    for step, pay in enumerate(pays, 1):
        upward = (level ^ step) > level

        @pl.when(upward)
        def _():
            pay[...] = mid[:, :half]

        @pl.when(jnp.logical_not(upward))
        def _():
            pay[...] = mid[:, half:]

    far[...] = picked(far.shape[0], far_off[head])


def near_stats_kernel(scale, parts, q, k, v, g, logs, dots):
    head = pl.program_id(0)

    @pl.when(head == 0)
    def _():
        logs[...] = jnp.zeros_like(logs)
        dots[...] = jnp.zeros_like(dots)

    size = q.shape[0] // parts
    for part in range(parts):
        rows = slice(part * size, (part + 1) * size)
        width = (part + 1) * size
        scores = mm_t(q[rows, :], k[:width, :]) * scale
        grads = mm_t(g[rows, :], v[:width, :])
        seen = iota((size, width), 1) <= iota((size, width), 0) + part * size
        log_part, dot_part = row_stats(jnp.where(seen, scores, LOW), grads)
        put_lane(logs, rows, head, log_part)
        put_lane(dots, rows, head, dot_part)


def row_stats(scores, grads):
    peak = jnp.max(scores, axis=1, keepdims=True)
    weights = jnp.exp(scores - peak)
    total = jnp.sum(weights, axis=1, keepdims=True)
    return peak + jnp.log(total), jnp.sum(weights * grads, axis=1, keepdims=True) / total


def choose(first, when_first, otherwise):
    return (first & when_first) | (jnp.logical_not(first) & otherwise)


def mid_mask(count, total, level, back):
    row, col = iota((count, total), 0), iota((count, total), 1)
    slot, rest = col // count, col % count
    other = slot ^ level
    if back:
        return choose(slot == 0, rest >= row, other > level)
    return choose(slot == 0, rest <= row, other < level)


def far_mask(count, total, block, level, ring, back):
    row, col = iota((count, total), 0), iota((count, total), 1)
    ring_slot, in_block = col // block, col % block
    slot, rest = in_block // count, in_block % count
    ring_other, other = ring_slot ^ ring, slot ^ level
    if back:
        own = choose(slot == 0, rest >= row, other > level)
        return choose(ring_slot == 0, own, ring_other > ring)
    own = choose(slot == 0, rest <= row, other < level)
    return choose(ring_slot == 0, own, ring_other < ring)


def stack(refs, first):
    blocks = [ref[:, first : first + LANES] for ref in refs]
    return blocks[0] if len(blocks) == 1 else jnp.concatenate(blocks, axis=0)


def repeat_table(rows, count):
    return (iota((rows, count), 0) // (rows // count) == iota((rows, count), 1)).astype(F32)


def gather_table(rows, count):
    return (iota((count, rows), 1) // (rows // count) == iota((count, rows), 0)).astype(F32)


def level_stats_kernel(scale, mids, fars, block, *refs):
    place, mid_lane, far_lane, kv, qg, far_own, near_logs, near_dots = refs[:8]
    mid_in = refs[8 : 8 + mids]
    far_in = refs[8 + mids : 8 + mids + fars]
    (log_all, dot_all, mid_log, mid_dot, far_log, far_dot, mid_row, far_row) = refs[8 + mids + fars :][:8]
    mlog, mdot, flog, fdot = refs[16 + mids + fars :]
    head = pl.program_id(0)
    ring, level = place[0], place[1]
    mid_count, far_count = kv.shape[0], far_own.shape[0]

    @pl.when(head == 0)
    def _():
        for ref in (mlog, mdot, flog, fdot):
            ref[...] = jnp.zeros_like(ref)

    keys = stack((kv,) + mid_in, 0)
    vals = stack((kv,) + mid_in, LANES)
    scores = mm_t(qg[:, :LANES], keys) * scale
    grads = mm_t(qg[:, LANES:], vals)
    seen = mid_mask(mid_count, keys.shape[0], level, False)
    log_part, dot_part = row_stats(jnp.where(seen, scores, LOW), grads)
    every = slice(None)
    put_lane(mlog, every, head, log_part)
    put_lane(mdot, every, head, dot_part)

    keys = stack(far_in, 0)
    vals = stack(far_in, LANES)
    scores = mm_t(far_own[:, 2 * LANES : 3 * LANES], keys) * scale
    grads = mm_t(far_own[:, 3 * LANES :], vals)
    seen = far_mask(far_count, keys.shape[0], block, level, ring, False)
    log_part, dot_part = row_stats(jnp.where(seen, scores, LOW), grads)
    put_lane(flog, every, head, log_part)
    put_lane(fdot, every, head, dot_part)

    @pl.when(head == pl.num_programs(0) - 1)
    def _():
        rows = near_logs.shape[0]
        row = iota((rows, LANES), 0)
        mid_here = row % (rows // mid_count) == mid_lane[...]
        far_here = row % (rows // far_count) == far_lane[...]
        mid_table, far_table = repeat_table(rows, mid_count), repeat_table(rows, far_count)
        near = near_logs[...]
        mid = jnp.where(mid_here, exact(mid_table, mlog[...]), LOW)
        far = jnp.where(far_here, exact(far_table, flog[...]), LOW)
        peak = jnp.maximum(near, jnp.maximum(mid, far))
        near, mid, far = jnp.exp(near - peak), jnp.exp(mid - peak), jnp.exp(far - peak)
        total = near + mid + far
        logs = peak + jnp.log(total)
        dots = (
            near * near_dots[...]
            + mid * exact(mid_table, mdot[...])
            + far * exact(far_table, fdot[...])
        ) / total
        log_all[...] = logs
        dot_all[...] = dots
        heads = mid_row.shape[0] // 2
        for here, count, outs, flat in (
            (mid_here, mid_count, (mid_log, mid_dot), mid_row),
            (far_here, far_count, (far_log, far_dot), far_row),
        ):
            table = gather_table(rows, count)
            for place_row, (source, out) in enumerate(zip((logs, dots), outs)):
                chosen = exact(table, jnp.where(here, source, 0.0))
                out[...] = chosen
                flat[place_row * heads : (place_row + 1) * heads, :] = chosen.T[:heads, :]


def near_grads_kernel(scale, parts, q, k, v, g, logs, dots, dq, dk, dv):
    head = pl.program_id(0)
    size = q.shape[0] // parts
    log_all, dot_all = pick_lane(logs, head), pick_lane(dots, head)
    for part in reversed(range(parts)):
        rows = slice(part * size, (part + 1) * size)
        width = (part + 1) * size
        scores = mm_t(q[rows, :], k[:width, :]) * scale
        grads = mm_t(g[rows, :], v[:width, :])
        seen = iota((size, width), 1) <= iota((size, width), 0) + part * size
        soft = jnp.exp(jnp.where(seen, scores - log_all[rows, :], LOW))
        slopes = (soft * (grads - dot_all[rows, :]) * scale).astype(BF16)
        dq[rows, :] = mm(slopes, k[:width, :])
        key_part = t_mm(slopes, q[rows, :])
        value_part = t_mm(soft.astype(BF16), g[rows, :])
        if part == parts - 1:
            dk[...] = key_part
            dv[...] = value_part
        else:
            dk[:width, :] += key_part
            dv[:width, :] += value_part


def spread(rows, offset, piece):
    count = piece.shape[0]
    table = (iota((rows, count), 0) == iota((rows, count), 1) * (rows // count) + offset).astype(BF16)
    high = piece.astype(BF16)
    low = (piece - high.astype(F32)).astype(BF16)
    return mm(table, high) + mm(table, low)


def query_grads_kernel(scale, mids, fars, block, *refs):
    place, mid_off, far_off, kv, qg, far_own, near = refs[:7]
    mid_log, mid_dot, far_log, far_dot = refs[7:11]
    mid_in = refs[11 : 11 + mids]
    far_in = refs[11 + mids : 11 + mids + fars]
    out = refs[-1]
    head = pl.program_id(0)
    ring, level = place[0], place[1]
    rows = out.shape[0]

    keys = stack((kv,) + mid_in, 0)
    vals = stack((kv,) + mid_in, LANES)
    scores = mm_t(qg[:, :LANES], keys) * scale
    grads = mm_t(qg[:, LANES:], vals)
    seen = mid_mask(kv.shape[0], keys.shape[0], level, False)
    soft = jnp.exp(jnp.where(seen, scores - pick_lane(mid_log, head), LOW))
    slopes = (soft * (grads - pick_lane(mid_dot, head)) * scale).astype(BF16)
    total = near[...] + spread(rows, mid_off[head], mm(slopes, keys))

    keys = stack(far_in, 0)
    vals = stack(far_in, LANES)
    scores = mm_t(far_own[:, 2 * LANES : 3 * LANES], keys) * scale
    grads = mm_t(far_own[:, 3 * LANES :], vals)
    seen = far_mask(far_own.shape[0], keys.shape[0], block, level, ring, False)
    soft = jnp.exp(jnp.where(seen, scores - pick_lane(far_log, head), LOW))
    slopes = (soft * (grads - pick_lane(far_dot, head)) * scale).astype(BF16)
    out[...] = (total + spread(rows, far_off[head], mm(slopes, keys))).astype(BF16)


def key_grads_kernel(scale, mids, fars, block, *refs):
    place, mid_off, far_off, kv, qg, far_own, near_dk, near_dv, mid_rows, far_rows = refs[:10]
    mid_in = refs[10 : 10 + mids]
    far_in = refs[10 + mids : 10 + mids + fars]
    out_k, out_v = refs[-2:]
    head = pl.program_id(0)
    ring, level = place[0], place[1]
    rows = out_k.shape[0]
    heads = mid_rows.shape[0] // 2

    def one(keys, vals, queries, cots, seen, stats):
        logs = stats[pl.ds(head, 1), :]
        dots = stats[pl.ds(head + heads, 1), :]
        scores = mm_t(keys, queries) * scale
        grads = mm_t(vals, cots)
        soft = jnp.exp(jnp.where(seen, scores - logs, LOW))
        slopes = (soft * (grads - dots) * scale).astype(BF16)
        return mm(slopes, queries), mm(soft.astype(BF16), cots)

    queries, cots = stack((qg,) + mid_in, 0), stack((qg,) + mid_in, LANES)
    seen = mid_mask(kv.shape[0], queries.shape[0], level, True)
    mid_k, mid_v = one(kv[:, :LANES], kv[:, LANES:], queries, cots, seen, mid_rows)
    queries, cots = stack(far_in, 0), stack(far_in, LANES)
    seen = far_mask(far_own.shape[0], queries.shape[0], block, level, ring, True)
    far_k, far_v = one(
        far_own[:, :LANES], far_own[:, LANES : 2 * LANES], queries, cots, seen, far_rows
    )
    out_k[...] = (
        near_dk[...] + spread(rows, mid_off[head], mid_k) + spread(rows, far_off[head], far_k)
    ).astype(BF16)
    out_v[...] = (
        near_dv[...] + spread(rows, mid_off[head], mid_v) + spread(rows, far_off[head], far_v)
    ).astype(BF16)


def ring_payload_kernel(place, kv_in, qg_in, *pays):
    ring = place[0]
    for step, pay in enumerate(pays, 1):
        upward = (ring ^ step) > ring

        @pl.when(upward)
        def _():
            pay[...] = kv_in[...]

        @pl.when(jnp.logical_not(upward))
        def _():
            pay[...] = qg_in[...]


def swap(array, axis, size, step):
    return lax.ppermute(array, axis, [(i, i ^ step) for i in range(size)])


def call(kernel, heads, ins, outs, scratch, cost):
    specs, arrays = zip(*ins)
    out_specs, out_shapes = zip(*outs)
    return pl.pallas_call(
        kernel,
        grid=(heads,),
        in_specs=list(specs),
        out_specs=list(out_specs),
        out_shape=list(out_shapes),
        scratch_shapes=scratch,
        compiler_params=params(),
        cost_estimate=pl.CostEstimate(flops=cost[0], bytes_accessed=cost[1], transcendentals=cost[2]),
    )(*arrays)


def local(queries, keys, values, grad_out, mid_offset, far_offset):
    rows, flat = queries.shape
    heads = mid_offset.shape[0]
    width = flat // heads
    scale = width ** (-0.5)
    levels, rings = lax.axis_size("lvl"), lax.axis_size("seq")
    mid_count, far_count = rows // levels, rows // (levels * rings)
    block = far_count * levels
    place = jnp.stack([lax.axis_index("seq"), lax.axis_index("lvl")]).astype(jnp.int32)
    mid_lane = jnp.tile(mid_offset, LANES // heads)[None, :]
    far_lane = jnp.tile(far_offset, LANES // heads)[None, :]
    shape = jax.ShapeDtypeStruct
    parts = 2
    tile = columns(rows, width)
    sources = [(tile, queries), (tile, keys), (tile, values), (tile, grad_out)]
    scalars = [(smem(), place), (smem(), mid_offset), (smem(), far_offset)]
    unit = rows * rows * width * 2 * heads

    kv, qg, far, *pays = call(
        select_kernel,
        heads,
        scalars + sources,
        [(columns(mid_count, 2 * width), shape((mid_count, 2 * flat), BF16))] * 2
        + [(columns(far_count, 4 * width), shape((far_count, 4 * flat), BF16))]
        + [(columns(mid_count, 2 * width), shape((mid_count, 2 * flat), BF16))] * (levels - 1),
        [],
        (unit, rows * flat * 8, 0),
    )
    far_level = [far] + [swap(far, "lvl", levels, step) for step in range(1, levels)]
    mid_in = [swap(pays[step - 1], "lvl", levels, step) for step in range(1, levels)]

    split = [piece.reshape(far_count, heads, 2, 2 * width) for piece in far_level]
    split = jnp.concatenate(split, axis=0)
    column_kv = split[:, :, 0].reshape(block, 2 * flat)
    column_qg = split[:, :, 1].reshape(block, 2 * flat)
    whole_column = columns(block, 2 * width)
    ring_pays = call(
        ring_payload_kernel,
        heads,
        scalars[:1] + [(whole_column, column_kv), (whole_column, column_qg)],
        [(whole_column, shape((block, 2 * flat), BF16))] * (rings - 1),
        [],
        (0, block * flat * 4 * (rings + 1), 0),
    )
    far_ring = [swap(ring_pays[step - 1], "seq", rings, step) for step in range(1, rings)]

    stat = shape((rows, LANES), F32)
    stat_spec = fixed((rows, LANES))
    near_logs, near_dots = call(
        functools.partial(near_stats_kernel, scale, parts),
        heads,
        sources,
        [(stat_spec, stat)] * 2,
        [],
        (2 * unit, rows * flat * 8, rows * rows * heads),
    )

    def far_list(own):
        pieces = [own] + far_ring
        if block % 16:
            pieces = [jnp.concatenate(pieces, axis=0)]
        return [(columns(piece.shape[0], 2 * width), piece) for piece in pieces]

    far_kv, far_qg = far_list(column_kv), far_list(column_qg)
    mid_spec = columns(mid_count, 2 * width)
    mid_list = [(mid_spec, piece) for piece in mid_in]
    own = [(mid_spec, kv), (mid_spec, qg), (columns(far_count, 4 * width), far)]
    mid_stat, far_stat = shape((mid_count, LANES), F32), shape((far_count, LANES), F32)
    counts = (len(mid_list), len(far_kv), block)
    log_all, dot_all, mid_log, mid_dot, far_log, far_dot, mid_row, far_row = call(
        functools.partial(level_stats_kernel, scale, *counts),
        heads,
        [scalars[0], (fixed((1, LANES)), mid_lane), (fixed((1, LANES)), far_lane)]
        + own
        + [(stat_spec, near_logs), (stat_spec, near_dots)]
        + mid_list
        + far_kv,
        [
            (stat_spec, stat),
            (stat_spec, stat),
            (fixed(mid_stat.shape), mid_stat),
            (fixed(mid_stat.shape), mid_stat),
            (fixed(far_stat.shape), far_stat),
            (fixed(far_stat.shape), far_stat),
            (fixed((2 * heads, mid_count)), shape((2 * heads, mid_count), F32)),
            (fixed((2 * heads, far_count)), shape((2 * heads, far_count), F32)),
        ],
        [pltpu.VMEM((mid_count, LANES), F32)] * 2 + [pltpu.VMEM((far_count, LANES), F32)] * 2,
        (unit, rows * flat * 16, rows * mid_count * heads),
    )

    both = jnp.concatenate([mid_row, far_row], axis=1)
    stat_in = [both] + [swap(both, "lvl", levels, step) for step in range(1, levels)]
    mid_rows = jnp.concatenate([piece[:, :mid_count] for piece in stat_in], axis=1)
    far_block = jnp.concatenate([piece[:, mid_count:] for piece in stat_in], axis=1)
    far_rows = jnp.concatenate(
        [far_block] + [swap(far_block, "seq", rings, step) for step in range(1, rings)], axis=1
    )

    grad_tile = shape((rows, flat), F32)
    near_dq, near_dk, near_dv = call(
        functools.partial(near_grads_kernel, scale, parts),
        heads,
        sources + [(stat_spec, log_all), (stat_spec, dot_all)],
        [(tile, grad_tile)] * 3,
        [],
        (5 * unit, rows * flat * 20, rows * rows * heads),
    )
    out = shape((rows, flat), BF16)
    (grad_query,) = call(
        functools.partial(query_grads_kernel, scale, *counts),
        heads,
        scalars
        + own
        + [(tile, near_dq)]
        + [(fixed(mid_stat.shape), mid_log), (fixed(mid_stat.shape), mid_dot)]
        + [(fixed(far_stat.shape), far_log), (fixed(far_stat.shape), far_dot)]
        + mid_list
        + far_kv,
        [(tile, out)],
        [],
        (unit, rows * flat * 16, rows * mid_count * heads),
    )
    row_spec = fixed((2 * heads, rows))
    grad_key, grad_value = call(
        functools.partial(key_grads_kernel, scale, *counts),
        heads,
        scalars
        + own
        + [(tile, near_dk), (tile, near_dv), (row_spec, mid_rows), (row_spec, far_rows)]
        + mid_list
        + far_qg,
        [(tile, out)] * 2,
        [],
        (2 * unit, rows * flat * 16, rows * mid_count * heads),
    )
    return grad_query, grad_key, grad_value


def solution(mesh):
    row_spec = P(("seq", "lvl"), None)
    return jax.shard_map(
        local,
        mesh=mesh,
        in_specs=(row_spec, row_spec, row_spec, row_spec, P(), P()),
        out_specs=(row_spec, row_spec, row_spec),
        check_vma=False,
    )
```

time: 460 us -> 153 us (0.33)
  blocking collectives: 160 us -> 0 us
  waiting for transfers between devices: 126 us -> 31.3 us
  local copies, waits for them, and re-layouts: 86 us -> 27.3 us
  matrix products: 58.4 us -> 0 us
  Pallas kernels: 0 us -> 55.3 us
  starting transfers between devices: 0.51 us -> 36.4 us
  between operations: 14.9 us -> 0.99 us
  other arithmetic: 12.1 us -> 0.77 us
    all_gather x4 -> x0, blocking collectives: 160 us -> none  [the longest x1 66.9 us: local(): lax.all_gather(packed_stats[0], ('seq', 'lvl'), axis=0, tiled=True)]
    all_gather x8 -> x0, waiting for transfers between devices: 126 us -> none  [the longest x1 51.9 us: local(): lax.all_gather(packed[1], ('seq', 'lvl'), axis=0, tiled=True)]
    dot_general x22 -> x0, matrix products: 58.4 us -> none  [the longest x1 8.07 us: local(): jnp.einsum('hqk,khd->qhd', near_cast, value_rows, preferred_element_type=...]
    pallas_call x0 -> x7, Pallas kernels: none -> 55.3 us  [call(): pl.pallas_call(kernel, grid=(heads,), in_specs=list(specs), out_specs=lis...]
    ppermute x0 -> x23, starting transfers between devices: none -> 36.4 us  [swap(): return lax.ppermute(array, axis, [(i, i ^ step) for i in range(size)])]
    mul x20 -> x0, local copies, waits for them, and re-layouts: 33.2 us -> none  [the longest x18 33.2 us: spread_rows(): whole_rows = pieces[:, None] * onehot[None, :, :, None]]
    ppermute x0 -> x23, waiting for transfers between devices: none -> 31.3 us  [swap(): return lax.ppermute(array, axis, [(i, i ^ step) for i in range(size)])]
    transpose x14 -> x0, local copies, waits for them, and re-layouts: 9.13 us -> none  [the longest x2 2.89 us: local(): jnp.einsum('hqk,khd->qhd', grad_scores, key_all, preferred_element_type=j...]
  transfers between devices with their start and end apart: 8 -> 23, of which waited for: 4 -> 7; matrix products, arithmetic and copies ran while one was open for 24% -> 3% of each run, Pallas kernels for 0% -> 18%
where the time goes in v1:
time: 153 us; the launch traced here: 152 us
  Pallas kernels  55.3 us (36%)
  starting transfers between devices  36.4 us (24%)
  waiting for transfers between devices  31.3 us (20%)
  local copies, waits for them, and re-layouts  27.3 us (18%)
    pallas_call x7, Pallas kernels, call(): pl.pallas_call(kernel, grid=(heads,), in_specs=list(specs), out_specs=lis...  55.3 us
    ppermute x23, starting transfers between devices, swap(): return lax.ppermute(array, axis, [(i, i ^ step) for i in range(size)])  36.4 us
    ppermute x23, waiting for transfers between devices, swap(): return lax.ppermute(array, axis, [(i, i ^ step) for i in range(size)])  31.3 us
    unnamed x84, local copies, waits for them, and re-layouts  21.7 us
  transfers between devices with their start and end apart: 23, of which 7 were waited for; matrix products, arithmetic and copies ran while one was open for 3% of the time, Pallas kernels for 18%

profile of v1, /device:TPU:0, one launch (start us, length us, event | category | flops | bytes accessed | tf_op | source)
XLA Modules:
  0.0 152.1 jit_solution(5772216965411276430)
XLA Ops:
  0.7 1.2 copy-done
  1.9 1.2 copy-done.3
  3.2 1.2 copy-done.6
  4.4 0.7 copy-done.23
  5.0 0.7 copy-done.25
  5.7 6.7 %shard_map.85 = (bf16[128,2048]{1,0:T(8,128)(2,1)S(1)}, bf16[128,2048]{1,0:T(8,128)(2,1)S(1)}, bf16[16,4096]{1,0:T(8,128)(2,1)S(1)}, bf16[128,2048]{1,0:T(8,128)...) custom-call(s32[2]{0:T(128)S(1)} %pad_add_fusion.place.refs_0_, s32[8]{0:T(128)S(1)} %copy-done.23, ...), custom_call_target="tpu_custom_call" | custom-call | flops 536870912 | bytes 4194304 | tf_op jit(solution)/shard_map/pallas_call | solution.py:344
  12.4 0.8 copy-done.31
  13.2 0.8 copy-done.32
  14.0 0.8 copy-done.33
  14.7 3.0 %collective-permute-start.3 = (bf16[16,4096]{1,0:T(8,128)(2,1)S(1)}, bf16[16,4096]{1,0:T(8,128)(2,1)S(1)}, u32[]{:S(2)}, u32[]{:S(2)}) collective-permute-start(bf16[16,4096]{1,0:T(8,128)(2,1)S(1)} %get-tuple-element.33.refs_5_), channel_id=1, source_target_pairs={{0,1},{1,0},{2,3},{3,2},{4,5},{5,4},{6,7},{7,6},{8,9},{9,8},{10,11... | collective-permute-start | bytes 393224 | tf_op jit(solution)/shard_map/ppermute | solution.py:338
  17.8 2.6 %collective-permute-start.4 = (bf16[16,4096]{1,0:T(8,128)(2,1)S(1)}, bf16[16,4096]{1,0:T(8,128)(2,1)S(1)}, u32[]{:S(2)}, u32[]{:S(2)}) collective-permute-start(bf16[16,4096]{1,0:T(8,128)(2,1)S(1)} %get-tuple-element.33.refs_5_), channel_id=1, source_target_pairs={{0,2},{1,3},{2,0},{3,1},{4,6},{5,7},{6,4},{7,5},{8,10},{9,11},{10,... | collective-permute-start | bytes 393224 | tf_op jit(solution)/shard_map/ppermute | solution.py:338
  20.4 0.1 reshape.20
  20.5 2.3 %collective-permute-done.3 = bf16[16,4096]{1,0:T(8,128)(2,1)S(1)} collective-permute-done((bf16[16,4096]{1,0:T(8,128)(2,1)S(1)}, bf16[16,4096]{1,0:T(8,128)(2,1)S(1)}, u32[]{:S(2)}, u32[]{:S(2)}) %collective-permute-start.3) | collective-permute-done | bytes 131104 | tf_op jit(solution)/shard_map/ppermute | solution.py:338
  22.8 0.1 reshape.21
  22.9 7.8 %collective-permute-done.4 = bf16[16,4096]{1,0:T(8,128)(2,1)S(1)} collective-permute-done((bf16[16,4096]{1,0:T(8,128)(2,1)S(1)}, bf16[16,4096]{1,0:T(8,128)(2,1)S(1)}, u32[]{:S(2)}, u32[]{:S(2)}) %collective-permute-start.4) | collective-permute-done | bytes 131104 | tf_op jit(solution)/shard_map/ppermute | solution.py:338
  30.7 0.1 reshape.22
  30.8 0.1 reshape.23
  31.1 3.7 %shard_map.87 = (bf16[64,2048]{1,0:T(8,128)(2,1)S(1)}, bf16[64,2048]{1,0:T(8,128)(2,1)S(1)}, bf16[64,2048]{1,0:T(8,128)(2,1)S(1)}, bf16[64,2048]{1,0:T(8,128)(2,...) custom-call(s32[2]{0:T(128)S(1)} %pad_add_fusion.place.refs_0_, ...), custom_call_target="tpu_custom_call" | custom-call | bytes 2359296 | tf_op jit(solution)/shard_map/pallas_call | solution.py:344
  34.8 1.5 collective-permute-start.7
  36.3 0.4 collective-permute-start.8
  36.6 1.9 %collective-permute-start = (bf16[128,2048]{1,0:T(8,128)(2,1)}, bf16[128,2048]{1,0:T(8,128)(2,1)S(1)}, u32[]{:S(2)}, u32[]{:S(2)}) collective-permute-start(bf16[128,2048]{1,0:T(8,128)(2,1)} %copy-done.33), channel_id=1, source_target_pairs={{0,1},{1,0},{2,3},{3,2},{4,5},{5,4},{6,7},{7,6},{8,9},{9,8},{10,11... | collective-permute-start | bytes 1572872 | tf_op jit(solution)/shard_map/ppermute | solution.py:338
  38.5 1.5 collective-permute-start.9
  40.0 3.9 %collective-permute-done.7.refs_13_.refs_16_.refs_15_ = bf16[64,2048]{1,0:T(8,128)(2,1)S(1)} collective-permute-done((bf16[64,2048]{1,0:T(8,128)(2,1)S(1)}, bf16[64,2048]{1,0:T(8,128)(2,1)S(1)}, u32[]{:S(2)}, u32[]{:S(2)}) %collective-permute-start.7) | collective-permute-done | bytes 262176 | tf_op jit(solution)/shard_map/ppermute | solution.py:338
  43.9 2.9 %collective-permute-start.1 = (bf16[128,2048]{1,0:T(8,128)(2,1)}, bf16[128,2048]{1,0:T(8,128)(2,1)S(1)}, u32[]{:S(2)}, u32[]{:S(2)}) collective-permute-start(bf16[128,2048]{1,0:T(8,128)(2,1)} %copy-done.32), channel_id=1, source_target_pairs={{0,2},{1,3},{2,0},{3,1},{4,6},{5,7},{6,4},{7,5},{8,10},{9,11},{10,... | collective-permute-start | bytes 1572872 | tf_op jit(solution)/shard_map/ppermute | solution.py:338
  46.7 2.0 %collective-permute-done.8.refs_14_.refs_17_.refs_16_ = bf16[64,2048]{1,0:T(8,128)(2,1)S(1)} collective-permute-done((bf16[64,2048]{1,0:T(8,128)(2,1)S(1)}, bf16[64,2048]{1,0:T(8,128)(2,1)S(1)}, u32[]{:S(2)}, u32[]{:S(2)}) %collective-permute-start.8) | collective-permute-done | bytes 262176 | tf_op jit(solution)/shard_map/ppermute | solution.py:338
  48.7 0.7 copy-done.10
  49.5 2.3 %collective-permute-start.2 = (bf16[128,2048]{1,0:T(8,128)(2,1)}, bf16[128,2048]{1,0:T(8,128)(2,1)S(1)}, u32[]{:S(2)}, u32[]{:S(2)}) collective-permute-start(bf16[128,2048]{1,0:T(8,128)(2,1)} %copy-done.31), channel_id=1, source_target_pairs={{0,3},{1,2},{2,1},{3,0},{4,7},{5,6},{6,5},{7,4},{8,11},{9,10},{10,... | collective-permute-start | bytes 1572872 | tf_op jit(solution)/shard_map/ppermute | solution.py:338
  51.8 0.7 copy-done.13
  52.5 2.4 %collective-permute-start.11 = (bf16[64,2048]{1,0:T(8,128)(2,1)}, bf16[64,2048]{1,0:T(8,128)(2,1)}, u32[]{:S(2)}, u32[]{:S(2)}) collective-permute-start(bf16[64,2048]{1,0:T(8,128)(2,1)} %get-tuple-element.44), channel_id=1, source_target_pairs={{0,24},{4,28},{8,16},{12,20},{16,8},{20,12},{24,0},{28,4},{1,25},{... | collective-permute-start | bytes 786440 | tf_op jit(solution)/shard_map/ppermute | solution.py:338
  54.9 0.7 copy-done.16
  55.7 0.6 tile.4
  56.3 1.3 broadcast_in_dim_tile.6.refs_1_
  57.6 0.6 tile.5
  58.2 1.4 broadcast_in_dim_tile.7.refs_2_
  59.5 1.2 copy-done.1
  60.8 1.2 copy-done.4
  62.0 1.2 copy-done.7
  63.2 1.2 copy-done.8
  64.5 5.8 %shard_map.86 = (f32[512,128]{1,0:T(8,128)S(1)}, f32[512,128]{1,0:T(8,128)S(1)}) custom-call(bf16[512,1024]{1,0:T(8,128)(2,1)S(1)} %copy-done.1, bf16[512,1024]{1,0:T(8,128)(2,1)S(1)} %copy-done.4, bf16[512,1024]{1,0:T(8,128)(2,1)S(1)} %copy-done.7, bf16[512,1024]{1,0:T(8,128)(2,1)S(1)} %copy-done.8), custom_call_target="tpu_custom_call" | custom-call | flops 1073741824 | bytes 4194304 | tf_op jit(solution)/shard_map/pallas_call | solution.py:344
  70.3 12.0 %collective-permute-done.1.refs_9_.refs_12_.refs_11_ = bf16[128,2048]{1,0:T(8,128)(2,1)S(1)} collective-permute-done((bf16[128,2048]{1,0:T(8,128)(2,1)}, bf16[128,2048]{1,0:T(8,128)(2,1)S(1)}, u32[]{:S(2)}, u32[]{:S(2)}) %collective-permute-start.1) | collective-permute-done | bytes 524320 | tf_op jit(solution)/shard_map/ppermute | solution.py:338
  82.4 8.1 %shard_map.88 = (f32[512,128]{1,0:T(8,128)S(1)}, f32[512,128]{1,0:T(8,128)S(1)}, f32[128,128]{1,0:T(8,128)S(1)}, f32[128,128]{1,0:T(8,128)S(1)}, f32[16,128]{1,0...) custom-call(s32[2]{0:T(128)S(1)} %pad_add_fusion.place.refs_0_, ...), custom_call_target="tpu_custom_call" | custom-call | flops 536870912 | bytes 8388608 | tf_op jit(solution)/shard_map/pallas_call | solution.py:344
  90.5 2.4 %collective-permute-start.15 = (f32[16,144]{1,0:T(8,128)S(1)}, f32[16,144]{1,0:T(8,128)S(1)}, u32[]{:S(2)}, u32[]{:S(2)}) collective-permute-start(f32[16,144]{1,0:T(8,128)S(1)} %constant_dynamic-update-slice_fusion), channel_id=1, source_target_pairs={{0,3},{1,2},{2,1},{3,0},{4,7},{5,6},{6,5},{7,4},{8,11},{9,10},{10,... | collective-permute-start | bytes 27656 | tf_op jit(solution)/shard_map/ppermute | solution.py:338
  92.9 9.5 %collective-permute-start.14 = (f32[16,144]{1,0:T(8,128)S(1)}, f32[16,144]{1,0:T(8,128)S(1)}, u32[]{:S(2)}, u32[]{:S(2)}) collective-permute-start(f32[16,144]{1,0:T(8,128)S(1)} %constant_dynamic-update-slice_fusion), channel_id=1, source_target_pairs={{0,2},{1,3},{2,0},{3,1},{4,6},{5,7},{6,4},{7,5},{8,10},{9,11},{10,... | collective-permute-start | bytes 27656 | tf_op jit(solution)/shard_map/ppermute | solution.py:338
  102.5 9.7 %shard_map.89 = (f32[512,1024]{1,0:T(8,128)}, f32[512,1024]{1,0:T(8,128)}, f32[512,1024]{1,0:T(8,128)}) custom-call(bf16[512,1024]{1,0:T(8,128)(2,1)S(1)} %copy-done.2, bf16[512,1024]{1,0:T(8,128)(2,1)S(1)} %copy-done.5, bf16[512,1024]{1,0:T(8,128)(2,1)S(1)} %copy-done.7, bf16[512,1024]{1,0:T(8,128)(2,1)S(1)} %copy-done.9, ...), custom_call_target="tpu_custom_call" | custom-call | flops 2684354560 | bytes 10485760 | tf_op jit(solution)/shard_map/pallas_call | solution.py:344
  112.2 0.5 copy-done.34
  112.8 0.1 pad_maximum_fusion.1
  112.9 0.5 copy-done.36
  113.4 1.5 collective-permute-start.17
  114.9 11.2 %shard_map.90 = bf16[512,1024]{1,0:T(8,128)(2,1)} custom-call(s32[2]{0:T(128)S(1)} %pad_add_fusion.place.refs_0_, s32[8]{0:T(128)S(1)} %copy-done.24, s32[8]{0:T(128)S(1)} %copy-done.27, bf16[128,2048]{1,0:T(8,128)(2,1)S(1)} %get-tuple-element.31.refs_3_, bf16[128,2048]{1,0:T(8,128)(2,1)S(1)} %get-tuple-element.32.refs_4_, ...), custom_call_target="tpu_custom_call" | custom-call | flops 536870912 | bytes 8388608 | tf_op jit(solution)/shard_map/pallas_call | solution.py:344
  126.1 1.5 collective-permute-start.19
  127.6 0.5 collective-permute-start.20
  128.1 2.5 %collective-permute-start.21 = (f32[16,64]{1,0:T(8,128)S(1)}, f32[16,64]{1,0:T(8,128)S(1)}, u32[]{:S(2)}, u32[]{:S(2)}) collective-permute-start(f32[16,64]{1,0:T(8,128)S(1)} %pad_maximum_fusion.1), channel_id=1, source_target_pairs={{0,24},{4,28},{8,16},{12,20},{16,8},{20,12},{24,0},{28,4},{1,25},{... | collective-permute-start | bytes 12296 | tf_op jit(solution)/shard_map/ppermute | solution.py:338
  130.6 0.6 pad_maximum_fusion.refs_8_
  131.3 1.4 collective-permute-done.21
  132.7 1.9 %collective-permute-done.22 = f32[16,64]{1,0:T(8,128)S(1)} collective-permute-done((f32[16,64]{1,0:T(8,128)S(1)}, f32[16,64]{1,0:T(8,128)S(1)}, u32[]{:S(2)}, u32[]{:S(2)}) %collective-permute-start.22) | collective-permute-done | bytes 4128 | tf_op jit(solution)/shard_map/ppermute | solution.py:338
  134.6 1.5 concatenate.20.refs_9_
  136.1 0.9 copy-done.12
  137.0 0.9 copy-done.15
  138.0 0.9 copy-done.18
  138.9 0.9 copy-done.20
  139.9 0.8 copy-done.21
  140.6 0.8 copy-done.22
  141.4 0.7 copy-done.28
  142.0 10.1 %shard_map.91 = (bf16[512,1024]{1,0:T(8,128)(2,1)}, bf16[512,1024]{1,0:T(8,128)(2,1)}) custom-call(s32[2]{0:T(128)S(1)} %pad_add_fusion.place.refs_0_, s32[8]{0:T(128)S(1)} %copy-done.24, s32[8]{0:T(128)S(1)} %copy-done.28, bf16[128,2048]{1,0:T(8,128)(2,1)S(1)} %get-tuple-element.31.refs_3_, bf16[128,2048]{1,0:T(8,128)(2,1)S(1)} %get-tuple-element.32.refs_4_, ...), custom_call_target="tpu_custom_call" | custom-call | flops 1073741824 | bytes 8388608 | tf_op jit(solution)/shard_map/pallas_call | solution.py:344
  (94 shorter events, 0.5 us)
Async XLA Ops:
  0.7 1.2 copy-start
  1.9 1.2 copy-start.3
  3.2 1.2 copy-start.6
  4.4 0.7 copy-start.23
  5.0 0.7 copy-start.25
  12.4 0.8 copy-start.31
  13.2 0.8 copy-start.32
  14.0 0.8 copy-start.33
  14.7 8.1 %collective-permute-start.3 = (bf16[16,4096]{1,0:T(8,128)(2,1)S(1)}, bf16[16,4096]{1,0:T(8,128)(2,1)S(1)}, u32[]{:S(2)}, u32[]{:S(2)}) collective-permute-start(bf16[16,4096]{1,0:T(8,128)(2,1)S(1)} %get-tuple-element.33.refs_5_), channel_id=1, source_target_pairs={{0,1},{1,0},{2,3},{3,2},{4,5},{5,4},{6,7},{7,6},{8,9},{9,8},{10,11... | collective-permute-start | bytes 393224 | tf_op jit(solution)/shard_map/ppermute | solution.py:338
  17.8 12.9 %collective-permute-start.4 = (bf16[16,4096]{1,0:T(8,128)(2,1)S(1)}, bf16[16,4096]{1,0:T(8,128)(2,1)S(1)}, u32[]{:S(2)}, u32[]{:S(2)}) collective-permute-start(bf16[16,4096]{1,0:T(8,128)(2,1)S(1)} %get-tuple-element.33.refs_5_), channel_id=1, source_target_pairs={{0,2},{1,3},{2,0},{3,1},{4,6},{5,7},{6,4},{7,5},{8,10},{9,11},{10,... | collective-permute-start | bytes 393224 | tf_op jit(solution)/shard_map/ppermute | solution.py:338
  20.4 10.4 %collective-permute-start.5 = (bf16[16,4096]{1,0:T(8,128)(2,1)S(1)}, bf16[16,4096]{1,0:T(8,128)(2,1)S(1)}, u32[]{:S(2)}, u32[]{:S(2)}) collective-permute-start(bf16[16,4096]{1,0:T(8,128)(2,1)S(1)} %get-tuple-element.33.refs_5_), channel_id=1, source_target_pairs={{0,3},{1,2},{2,1},{3,0},{4,7},{5,6},{6,5},{7,4},{8,11},{9,10},{10,... | collective-permute-start | bytes 393224 | tf_op jit(solution)/shard_map/ppermute | solution.py:338
  20.5 35.2 %copy-start.24 = (s32[8]{0:T(128)S(1)}, s32[8]{0:T(128)}, u32[]{:S(2)}) copy-start(s32[8]{0:T(128)} %refs_1_.3) | copy-start | bytes 100
  20.5 37.1 %copy-start.26 = (s32[8]{0:T(128)S(1)}, s32[8]{0:T(128)}, u32[]{:S(2)}) copy-start(s32[8]{0:T(128)} %refs_2_.3) | copy-start | bytes 100
  31.1 23.9 %copy-start.19 = (bf16[8,8,8,256]{3,1,2,0:T(8,128)(2,1)}, bf16[8,8,8,256]{3,1,2,0:T(8,128)(2,1)S(1)}, u32[]{:S(2)}) copy-start(bf16[8,8,8,256]{3,1,2,0:T(8,128)(2,1)S(1)} %copy.18) | copy-start | bytes 786436
  34.8 5.2 %collective-permute-start.6 = (bf16[64,2048]{1,0:T(8,128)(2,1)S(1)}, bf16[64,2048]{1,0:T(8,128)(2,1)S(1)}, u32[]{:S(2)}, u32[]{:S(2)}) collective-permute-start(bf16[64,2048]{1,0:T(8,128)(2,1)S(1)} %get-tuple-element.39), channel_id=1, source_target_pairs={{0,4},{4,0},{8,12},{12,8},{16,20},{20,16},{24,28},{28,24},{1,5},{5... | collective-permute-start | bytes 786440 | tf_op jit(solution)/shard_map/ppermute | solution.py:338
  34.8 9.1 %collective-permute-start.7 = (bf16[64,2048]{1,0:T(8,128)(2,1)S(1)}, bf16[64,2048]{1,0:T(8,128)(2,1)S(1)}, u32[]{:S(2)}, u32[]{:S(2)}) collective-permute-start(bf16[64,2048]{1,0:T(8,128)(2,1)S(1)} %get-tuple-element.40), channel_id=1, source_target_pairs={{0,8},{4,12},{8,0},{12,4},{16,24},{20,28},{24,16},{28,20},{1,9},{5... | collective-permute-start | bytes 786440 | tf_op jit(solution)/shard_map/ppermute | solution.py:338
  36.3 12.5 %collective-permute-start.8 = (bf16[64,2048]{1,0:T(8,128)(2,1)S(1)}, bf16[64,2048]{1,0:T(8,128)(2,1)S(1)}, u32[]{:S(2)}, u32[]{:S(2)}) collective-permute-start(bf16[64,2048]{1,0:T(8,128)(2,1)S(1)} %get-tuple-element.41), channel_id=1, source_target_pairs={{0,12},{4,8},{8,4},{12,0},{16,28},{20,24},{24,20},{28,16},{1,13},{... | collective-permute-start | bytes 786440 | tf_op jit(solution)/shard_map/ppermute | solution.py:338
  36.6 33.7 %collective-permute-start = (bf16[128,2048]{1,0:T(8,128)(2,1)}, bf16[128,2048]{1,0:T(8,128)(2,1)S(1)}, u32[]{:S(2)}, u32[]{:S(2)}) collective-permute-start(bf16[128,2048]{1,0:T(8,128)(2,1)} %copy-done.33), channel_id=1, source_target_pairs={{0,1},{1,0},{2,3},{3,2},{4,5},{5,4},{6,7},{7,6},{8,9},{9,8},{10,11... | collective-permute-start | bytes 1572872 | tf_op jit(solution)/shard_map/ppermute | solution.py:338
  38.5 13.3 %collective-permute-start.9 = (bf16[64,2048]{1,0:T(8,128)(2,1)S(1)}, bf16[64,2048]{1,0:T(8,128)(2,1)S(1)}, u32[]{:S(2)}, u32[]{:S(2)}) collective-permute-start(bf16[64,2048]{1,0:T(8,128)(2,1)S(1)} %get-tuple-element.42), channel_id=1, source_target_pairs={{0,16},{4,20},{8,24},{12,28},{16,0},{20,4},{24,8},{28,12},{1,17},{... | collective-permute-start | bytes 786440 | tf_op jit(solution)/shard_map/ppermute | solution.py:338
  40.0 14.9 %collective-permute-start.10 = (bf16[64,2048]{1,0:T(8,128)(2,1)S(1)}, bf16[64,2048]{1,0:T(8,128)(2,1)S(1)}, u32[]{:S(2)}, u32[]{:S(2)}) collective-permute-start(bf16[64,2048]{1,0:T(8,128)(2,1)S(1)} %get-tuple-element.43), channel_id=1, source_target_pairs={{0,20},{4,16},{8,28},{12,24},{16,4},{20,0},{24,12},{28,8},{1,21},{... | collective-permute-start | bytes 786440 | tf_op jit(solution)/shard_map/ppermute | solution.py:338
  43.9 38.4 %collective-permute-start.1 = (bf16[128,2048]{1,0:T(8,128)(2,1)}, bf16[128,2048]{1,0:T(8,128)(2,1)S(1)}, u32[]{:S(2)}, u32[]{:S(2)}) collective-permute-start(bf16[128,2048]{1,0:T(8,128)(2,1)} %copy-done.32), channel_id=1, source_target_pairs={{0,2},{1,3},{2,0},{3,1},{4,6},{5,7},{6,4},{7,5},{8,10},{9,11},{10,... | collective-permute-start | bytes 1572872 | tf_op jit(solution)/shard_map/ppermute | solution.py:338
  48.7 0.7 copy-start.10
  49.5 32.8 %collective-permute-start.2 = (bf16[128,2048]{1,0:T(8,128)(2,1)}, bf16[128,2048]{1,0:T(8,128)(2,1)S(1)}, u32[]{:S(2)}, u32[]{:S(2)}) collective-permute-start(bf16[128,2048]{1,0:T(8,128)(2,1)} %copy-done.31), channel_id=1, source_target_pairs={{0,3},{1,2},{2,1},{3,0},{4,7},{5,6},{6,5},{7,4},{8,11},{9,10},{10,... | collective-permute-start | bytes 1572872 | tf_op jit(solution)/shard_map/ppermute | solution.py:338
  51.8 0.7 copy-start.13
  52.5 17.8 %collective-permute-start.11 = (bf16[64,2048]{1,0:T(8,128)(2,1)}, bf16[64,2048]{1,0:T(8,128)(2,1)}, u32[]{:S(2)}, u32[]{:S(2)}) collective-permute-start(bf16[64,2048]{1,0:T(8,128)(2,1)} %get-tuple-element.44), channel_id=1, source_target_pairs={{0,24},{4,28},{8,16},{12,20},{16,8},{20,12},{24,0},{28,4},{1,25},{... | collective-permute-start | bytes 786440 | tf_op jit(solution)/shard_map/ppermute | solution.py:338
  54.9 0.7 copy-start.16
  55.7 14.6 %collective-permute-start.12 = (bf16[64,2048]{1,0:T(8,128)(2,1)}, bf16[64,2048]{1,0:T(8,128)(2,1)}, u32[]{:S(2)}, u32[]{:S(2)}) collective-permute-start(bf16[64,2048]{1,0:T(8,128)(2,1)} %get-tuple-element.45), channel_id=1, source_target_pairs={{0,28},{4,24},{8,20},{12,16},{16,12},{20,8},{24,4},{28,0},{1,29},{... | collective-permute-start | bytes 786440 | tf_op jit(solution)/shard_map/ppermute | solution.py:338
  59.5 1.2 copy-start.1
  60.8 1.2 copy-start.4
  62.0 1.2 copy-start.7
  63.2 1.2 copy-start.8
  64.4 17.9 %copy-start.11 = (bf16[64,2048]{1,0:T(8,128)(2,1)S(1)}, bf16[64,2048]{1,0:T(8,128)(2,1)}, u32[]{:S(2)}) copy-start(bf16[64,2048]{1,0:T(8,128)(2,1)} %copy-done.10) | copy-start | bytes 786436
  64.5 17.9 %copy-start.14 = (bf16[64,2048]{1,0:T(8,128)(2,1)S(1)}, bf16[64,2048]{1,0:T(8,128)(2,1)}, u32[]{:S(2)}) copy-start(bf16[64,2048]{1,0:T(8,128)(2,1)} %copy-done.13) | copy-start | bytes 786436
  64.5 17.9 %copy-start.17 = (bf16[64,2048]{1,0:T(8,128)(2,1)S(1)}, bf16[64,2048]{1,0:T(8,128)(2,1)}, u32[]{:S(2)}) copy-start(bf16[64,2048]{1,0:T(8,128)(2,1)} %copy-done.16) | copy-start | bytes 786436
  64.5 17.9 %copy-start.29 = (s32[1,128]{1,0:T(1,128)S(1)}, s32[1,128]{1,0:T(1,128)}, u32[]{:S(2)}) copy-start(s32[1,128]{1,0:T(1,128)} %broadcast_in_dim_tile.6.refs_1_) | copy-start | bytes 1540
  64.5 17.9 %copy-start.30 = (s32[1,128]{1,0:T(1,128)S(1)}, s32[1,128]{1,0:T(1,128)}, u32[]{:S(2)}) copy-start(s32[1,128]{1,0:T(1,128)} %broadcast_in_dim_tile.7.refs_2_) | copy-start | bytes 1540
  82.3 20.1 %copy-start.2 = (bf16[512,1024]{1,0:T(8,128)(2,1)S(1)}, bf16[512,1024]{1,0:T(8,128)(2,1)}, u32[]{:S(2)}) copy-start(bf16[512,1024]{1,0:T(8,128)(2,1)} %q.5) | copy-start | bytes 3145732
  82.4 20.1 %copy-start.5 = (bf16[512,1024]{1,0:T(8,128)(2,1)S(1)}, bf16[512,1024]{1,0:T(8,128)(2,1)}, u32[]{:S(2)}) copy-start(bf16[512,1024]{1,0:T(8,128)(2,1)} %k.5) | copy-start | bytes 3145732
  82.4 20.1 %copy-start.9 = (bf16[512,1024]{1,0:T(8,128)(2,1)S(1)}, bf16[512,1024]{1,0:T(8,128)(2,1)}, u32[]{:S(2)}) copy-start(bf16[512,1024]{1,0:T(8,128)(2,1)} %g.5) | copy-start | bytes 3145732
  90.5 21.7 %collective-permute-start.15 = (f32[16,144]{1,0:T(8,128)S(1)}, f32[16,144]{1,0:T(8,128)S(1)}, u32[]{:S(2)}, u32[]{:S(2)}) collective-permute-start(f32[16,144]{1,0:T(8,128)S(1)} %constant_dynamic-update-slice_fusion), channel_id=1, source_target_pairs={{0,3},{1,2},{2,1},{3,0},{4,7},{5,6},{6,5},{7,4},{8,11},{9,10},{10,... | collective-permute-start | bytes 27656 | tf_op jit(solution)/shard_map/ppermute | solution.py:338
  92.9 19.3 %collective-permute-start.14 = (f32[16,144]{1,0:T(8,128)S(1)}, f32[16,144]{1,0:T(8,128)S(1)}, u32[]{:S(2)}, u32[]{:S(2)}) collective-permute-start(f32[16,144]{1,0:T(8,128)S(1)} %constant_dynamic-update-slice_fusion), channel_id=1, source_target_pairs={{0,2},{1,3},{2,0},{3,1},{4,6},{5,7},{6,4},{7,5},{8,10},{9,11},{10,... | collective-permute-start | bytes 27656 | tf_op jit(solution)/shard_map/ppermute | solution.py:338
  102.4 9.8 %collective-permute-start.13 = (f32[16,144]{1,0:T(8,128)S(1)}, f32[16,144]{1,0:T(8,128)S(1)}, u32[]{:S(2)}, u32[]{:S(2)}) collective-permute-start(f32[16,144]{1,0:T(8,128)S(1)} %constant_dynamic-update-slice_fusion), channel_id=1, source_target_pairs={{0,1},{1,0},{2,3},{3,2},{4,5},{5,4},{6,7},{7,6},{8,9},{9,8},{10,11... | collective-permute-start | bytes 27656 | tf_op jit(solution)/shard_map/ppermute | solution.py:338
  102.4 12.4 %copy-start.27 = (s32[8]{0:T(128)S(1)}, s32[8]{0:T(128)}, u32[]{:S(2)}) copy-start(s32[8]{0:T(128)} %refs_2_.3) | copy-start | bytes 100
  112.2 0.6 copy-start.34
  112.2 0.7 copy-start.35
  112.8 0.6 copy-start.36
  112.9 15.2 %collective-permute-start.16 = (f32[16,64]{1,0:T(8,128)S(1)}, f32[16,64]{1,0:T(8,128)S(1)}, u32[]{:S(2)}, u32[]{:S(2)}) collective-permute-start(f32[16,64]{1,0:T(8,128)S(1)} %pad_maximum_fusion.1), channel_id=1, source_target_pairs={{0,4},{4,0},{8,12},{12,8},{16,20},{20,16},{24,28},{28,24},{1,5},{5... | collective-permute-start | bytes 12296 | tf_op jit(solution)/shard_map/ppermute | solution.py:338
  113.4 17.2 %collective-permute-start.17 = (f32[16,64]{1,0:T(8,128)S(1)}, f32[16,64]{1,0:T(8,128)S(1)}, u32[]{:S(2)}, u32[]{:S(2)}) collective-permute-start(f32[16,64]{1,0:T(8,128)S(1)} %pad_maximum_fusion.1), channel_id=1, source_target_pairs={{0,8},{4,12},{8,0},{12,4},{16,24},{20,28},{24,16},{28,20},{1,9},{5... | collective-permute-start | bytes 12296 | tf_op jit(solution)/shard_map/ppermute | solution.py:338
  126.1 5.2 %collective-permute-start.18 = (f32[16,64]{1,0:T(8,128)S(1)}, f32[16,64]{1,0:T(8,128)S(1)}, u32[]{:S(2)}, u32[]{:S(2)}) collective-permute-start(f32[16,64]{1,0:T(8,128)S(1)} %pad_maximum_fusion.1), channel_id=1, source_target_pairs={{0,12},{4,8},{8,4},{12,0},{16,28},{20,24},{24,20},{28,16},{1,13},{... | collective-permute-start | bytes 12296 | tf_op jit(solution)/shard_map/ppermute | solution.py:338
  126.1 5.2 %collective-permute-start.19 = (f32[16,64]{1,0:T(8,128)S(1)}, f32[16,64]{1,0:T(8,128)S(1)}, u32[]{:S(2)}, u32[]{:S(2)}) collective-permute-start(f32[16,64]{1,0:T(8,128)S(1)} %pad_maximum_fusion.1), channel_id=1, source_target_pairs={{0,16},{4,20},{8,24},{12,28},{16,0},{20,4},{24,8},{28,12},{1,17},{... | collective-permute-start | bytes 12296 | tf_op jit(solution)/shard_map/ppermute | solution.py:338
  127.6 3.7 %collective-permute-start.20 = (f32[16,64]{1,0:T(8,128)S(1)}, f32[16,64]{1,0:T(8,128)S(1)}, u32[]{:S(2)}, u32[]{:S(2)}) collective-permute-start(f32[16,64]{1,0:T(8,128)S(1)} %pad_maximum_fusion.1), channel_id=1, source_target_pairs={{0,20},{4,16},{8,28},{12,24},{16,4},{20,0},{24,12},{28,8},{1,21},{... | collective-permute-start | bytes 12296 | tf_op jit(solution)/shard_map/ppermute | solution.py:338
  128.1 4.6 %copy-start.37 = (f32[16,64]{1,0:T(8,128)}, f32[16,64]{1,0:T(8,128)S(1)}, u32[]{:S(2)}) copy-start(f32[16,64]{1,0:T(8,128)S(1)} %collective-permute-done.16) | copy-start | bytes 12292
  128.1 4.6 %collective-permute-start.21 = (f32[16,64]{1,0:T(8,128)S(1)}, f32[16,64]{1,0:T(8,128)S(1)}, u32[]{:S(2)}, u32[]{:S(2)}) collective-permute-start(f32[16,64]{1,0:T(8,128)S(1)} %pad_maximum_fusion.1), channel_id=1, source_target_pairs={{0,24},{4,28},{8,16},{12,20},{16,8},{20,12},{24,0},{28,4},{1,25},{... | collective-permute-start | bytes 12296 | tf_op jit(solution)/shard_map/ppermute | solution.py:338
  130.6 2.1 %copy-start.38 = (f32[16,64]{1,0:T(8,128)}, f32[16,64]{1,0:T(8,128)S(1)}, u32[]{:S(2)}) copy-start(f32[16,64]{1,0:T(8,128)S(1)} %collective-permute-done.17) | copy-start | bytes 12292
  130.6 4.0 %collective-permute-start.22 = (f32[16,64]{1,0:T(8,128)S(1)}, f32[16,64]{1,0:T(8,128)S(1)}, u32[]{:S(2)}, u32[]{:S(2)}) collective-permute-start(f32[16,64]{1,0:T(8,128)S(1)} %pad_maximum_fusion.1), channel_id=1, source_target_pairs={{0,28},{4,24},{8,20},{12,16},{16,12},{20,8},{24,4},{28,0},{1,29},{... | collective-permute-start | bytes 12296 | tf_op jit(solution)/shard_map/ppermute | solution.py:338
  136.1 0.9 copy-start.12
  137.0 0.9 copy-start.15
  138.0 0.9 copy-start.18
  138.9 0.9 copy-start.20
  139.9 0.8 copy-start.21
  140.6 0.8 copy-start.22
  141.4 0.7 copy-start.28

commit v2 on v1

v2 whole, which is shorter than its diff:
```python
import functools

import jax
import jax.numpy as jnp
from jax import lax
from jax.experimental import pallas as pl
from jax.experimental.pallas import tpu as pltpu
from jax.sharding import PartitionSpec as P

F32 = jnp.float32
BF16 = jnp.bfloat16
LANES = 128
LOW = -1e30
VMEM_LIMIT = 60 * 1024 * 1024
GROUP = 2


def mm(a, b):
    return lax.dot_general(a, b, (((1,), (0,)), ((), ())), preferred_element_type=F32)


def mm_t(a, b):
    return lax.dot_general(a, b, (((1,), (1,)), ((), ())), preferred_element_type=F32)


def t_mm(a, b):
    return lax.dot_general(a, b, (((0,), (0,)), ((), ())), preferred_element_type=F32)


def exact(a, b):
    return lax.dot_general(
        a, b, (((1,), (0,)), ((), ())), preferred_element_type=F32, precision=lax.Precision.HIGHEST
    )


def iota(shape, axis):
    return lax.broadcasted_iota(jnp.int32, shape, axis)


def params():
    return pltpu.CompilerParams(
        vmem_limit_bytes=VMEM_LIMIT, dimension_semantics=("arbitrary",)
    )


def smem():
    return pl.BlockSpec(memory_space=pltpu.SMEM)


def columns(rows, width):
    return pl.BlockSpec((rows, width), lambda h: (0, h))


def fixed(shape):
    return pl.BlockSpec(shape, lambda h: (0,) * len(shape))


def pick_lane(ref, head):
    block = ref[...]
    return jnp.sum(jnp.where(iota(block.shape, 1) == head, block, 0.0), axis=1, keepdims=True)


def put_lane(ref, rows, head, value):
    block = ref[rows, :]
    ref[rows, :] = jnp.where(iota(block.shape, 1) == head, value, block)


def select_kernel(place, mid_off, far_off, q, k, v, g, kv, qg, far, *pays):
    level = place[1]
    rows = q.shape[0]
    for at in range(GROUP):
        head = pl.program_id(0) * GROUP + at
        cut = slice(at * LANES, (at + 1) * LANES)
        wide = slice(2 * at * LANES, 2 * (at + 1) * LANES)
        whole = jnp.concatenate([k[:, cut], v[:, cut], q[:, cut], g[:, cut]], axis=1)

        def picked(count, offset):
            stride = rows // count
            table = iota((count, rows), 1) == iota((count, rows), 0) * stride + offset
            return mm(table.astype(BF16), whole).astype(BF16)

        mid = picked(kv.shape[0], mid_off[head])
        half = 2 * LANES
        kv[:, wide] = mid[:, :half]
        qg[:, wide] = mid[:, half:]
        picks = picked(far.shape[1], far_off[head])
        far[0, :, wide] = picks[:, :half]
        far[1, :, wide] = picks[:, half:]
    for step, pay in enumerate(pays, 1):
        upward = (level ^ step) > level

        @pl.when(upward)
        def _():
            pay[...] = kv[...]

        @pl.when(jnp.logical_not(upward))
        def _():
            pay[...] = qg[...]


def near_kernel(scale, parts, q, k, v, g, logs, dots, soft_out, slope_out):
    @pl.when(pl.program_id(0) == 0)
    def _():
        logs[...] = jnp.zeros_like(logs)
        dots[...] = jnp.zeros_like(dots)

    size = q.shape[0] // parts
    for at in range(GROUP):
        head = pl.program_id(0) * GROUP + at
        cut = slice(at * LANES, (at + 1) * LANES)
        for part in range(parts):
            rows = slice(part * size, (part + 1) * size)
            width = (part + 1) * size
            scores = mm_t(q[rows, cut], k[:width, cut]) * scale
            grads = mm_t(g[rows, cut], v[:width, cut])
            seen = iota((size, width), 1) <= iota((size, width), 0) + part * size
            scores = jnp.where(seen, scores, LOW)
            peak = jnp.max(scores, axis=1, keepdims=True)
            weights = jnp.exp(scores - peak)
            total = jnp.sum(weights, axis=1, keepdims=True)
            soft = weights / total
            dot_part = jnp.sum(soft * grads, axis=1, keepdims=True)
            soft_out[at, rows, :width] = soft.astype(BF16)
            slope_out[at, rows, :width] = (soft * (grads - dot_part)).astype(BF16)
            put_lane(logs, rows, head, peak + jnp.log(total))
            put_lane(dots, rows, head, dot_part)


def row_stats(scores, grads):
    peak = jnp.max(scores, axis=1, keepdims=True)
    weights = jnp.exp(scores - peak)
    total = jnp.sum(weights, axis=1, keepdims=True)
    return peak + jnp.log(total), jnp.sum(weights * grads, axis=1, keepdims=True) / total


def mid_places(count, total, level):
    col = iota((count, total), 1)
    other = ((col >> (count.bit_length() - 1)) ^ level) * count + (col & (count - 1))
    return other, level * count + iota((count, total), 0)


def far_places(count, total, flat):
    return iota((count, total), 1), flat * count + iota((count, total), 0)


def bias(seen):
    return jnp.where(seen, 0.0, LOW)


def stack(refs, cut):
    return jnp.concatenate([ref[:, cut] for ref in refs], axis=0)


def repeat_table(rows, count):
    return (iota((rows, count), 0) // (rows // count) == iota((rows, count), 1)).astype(F32)


def gather_table(rows, count):
    return (iota((count, rows), 1) // (rows // count) == iota((count, rows), 0)).astype(F32)


def lane_offsets(offsets, heads):
    lane = iota((1, LANES), 1)
    values = jnp.zeros((1, LANES), jnp.int32)
    for head in range(heads):
        values = jnp.where(lane == head, offsets[head], values)
    return values


def level_stats_kernel(scale, heads, levels, mids, *refs):
    place, mid_off, far_off, kv, qg, far_own, near_logs, near_dots, far_in = refs[:9]
    mid_in = refs[9 : 9 + mids]
    (factors, shifts, mid_log, mid_dot, far_log, far_dot, mid_row, far_pack) = refs[9 + mids :][:8]
    mlog, mdot, flog, fdot = refs[17 + mids :]
    ring, level = place[0], place[1]
    mid_count, far_count = kv.shape[0], far_own.shape[1]
    total = mid_count * levels

    @pl.when(pl.program_id(0) == 0)
    def _():
        for ref in (mlog, mdot, flog, fdot):
            ref[...] = jnp.zeros_like(ref)

    keys_at, query_at = mid_places(mid_count, total, level)
    mid_bias = bias(keys_at <= query_at)
    keys_at, query_at = far_places(far_count, total, ring * levels + level)
    far_bias = bias(keys_at <= query_at)
    far_all = far_in[...].reshape(total, GROUP * 2 * LANES)
    every = slice(None)
    for at in range(GROUP):
        head = pl.program_id(0) * GROUP + at
        low = slice(2 * at * LANES, (2 * at + 1) * LANES)
        high = slice((2 * at + 1) * LANES, (2 * at + 2) * LANES)
        scores = mm_t(qg[:, low], stack((kv,) + mid_in, low)) * scale + mid_bias
        grads = mm_t(qg[:, high], stack((kv,) + mid_in, high))
        log_part, dot_part = row_stats(scores, grads)
        put_lane(mlog, every, head, log_part)
        put_lane(mdot, every, head, dot_part)
        scores = mm_t(far_own[1, :, low], far_all[:, low]) * scale + far_bias
        grads = mm_t(far_own[1, :, high], far_all[:, high])
        log_part, dot_part = row_stats(scores, grads)
        put_lane(flog, every, head, log_part)
        put_lane(fdot, every, head, dot_part)

    @pl.when(pl.program_id(0) == pl.num_programs(0) - 1)
    def _():
        rows = near_logs.shape[0]
        row = iota((rows, LANES), 0)
        mid_here = (row & (rows // mid_count - 1)) == lane_offsets(mid_off, heads)
        far_here = (row & (rows // far_count - 1)) == lane_offsets(far_off, heads)
        mid_table, far_table = repeat_table(rows, mid_count), repeat_table(rows, far_count)
        near = near_logs[...]
        mid = jnp.where(mid_here, exact(mid_table, mlog[...]), LOW)
        far = jnp.where(far_here, exact(far_table, flog[...]), LOW)
        peak = jnp.maximum(near, jnp.maximum(mid, far))
        near_part = jnp.exp(near - peak)
        mid, far = jnp.exp(mid - peak), jnp.exp(far - peak)
        whole = near_part + mid + far
        logs = peak + jnp.log(whole)
        dots = (
            near_part * near_dots[...]
            + mid * exact(mid_table, mdot[...])
            + far * exact(far_table, fdot[...])
        ) / whole
        factors[...] = jnp.exp(near - logs)
        shifts[...] = dots - near_dots[...]
        table = gather_table(rows, mid_count)
        mid_log[...] = exact(table, jnp.where(mid_here, logs, 0.0))
        mid_dot[...] = exact(table, jnp.where(mid_here, dots, 0.0))
        mid_row[:heads, :] = mid_log[...].T[:heads, :]
        mid_row[heads:, :] = mid_dot[...].T[:heads, :]
        table = gather_table(rows, far_count)
        far_log[...] = exact(table, jnp.where(far_here, logs, 0.0))
        far_dot[...] = exact(table, jnp.where(far_here, dots, 0.0))
        pack = jnp.concatenate([far_log[:, :heads], far_dot[:, :heads]], axis=1)
        far_pack[...] = jnp.broadcast_to(pack[None], far_pack.shape)


def spread(rows, offset, piece):
    count = piece.shape[0]
    table = (iota((rows, count), 0) == iota((rows, count), 1) * (rows // count) + offset).astype(BF16)
    high = piece.astype(BF16)
    low = (piece - high.astype(F32)).astype(BF16)
    return mm(table, high) + mm(table, low)


def grads_kernel(scale, heads, levels, parts, mids, *refs):
    place, mid_off, far_off, q, k, v, g, soft_in, slope_in, kv, qg, far_own, far_kv, far_qg = refs[:14]
    factors, shifts, mid_log, mid_dot, far_log, far_dot, mid_row, far_pack = refs[14:22]
    mid_in = refs[22 : 22 + mids]
    mid_rows = (mid_row,) + refs[22 + mids : 22 + 2 * mids]
    out_q, out_k, out_v, far_rows = refs[22 + 2 * mids :]
    ring, level = place[0], place[1]
    rows = q.shape[0]
    mid_count, far_count = kv.shape[0], far_own.shape[1]
    total = mid_count * levels
    size = rows // parts

    @pl.when(pl.program_id(0) == 0)
    def _():
        far_rows[...] = far_pack[...].reshape(total, 2 * heads).T

    other, own = mid_places(mid_count, total, level)
    mid_bias, mid_back = bias(other <= own), bias(other >= own)
    other, own = far_places(far_count, total, ring * levels + level)
    far_bias, far_back = bias(other <= own), bias(other >= own)
    far_k = far_kv[...].reshape(total, GROUP * 2 * LANES)
    far_q = far_qg[...].reshape(total, GROUP * 2 * LANES)

    def row_side(queries, cots, keys, vals, hide, logs, dots):
        scores = mm_t(queries, keys) * scale + hide
        soft = jnp.exp(scores - logs)
        slopes = soft * (mm_t(cots, vals) - dots)
        return soft.astype(BF16), slopes.astype(BF16)

    for at in range(GROUP):
        head = pl.program_id(0) * GROUP + at
        cut = slice(at * LANES, (at + 1) * LANES)
        low = slice(2 * at * LANES, (2 * at + 1) * LANES)
        high = slice((2 * at + 1) * LANES, (2 * at + 2) * LANES)
        mid_at, far_at = mid_off[head], far_off[head]

        keys = stack((kv,) + mid_in, low)
        vals = stack((kv,) + mid_in, high)
        _, slopes = row_side(
            qg[:, low], qg[:, high], keys, vals, mid_bias, pick_lane(mid_log, head), pick_lane(mid_dot, head)
        )
        mid_dq = mm(slopes, keys)
        queries = stack((qg,) + mid_in, low)
        cots = stack((qg,) + mid_in, high)
        logs = jnp.concatenate([ref[pl.ds(head, 1), :] for ref in mid_rows], axis=1)
        dots = jnp.concatenate([ref[pl.ds(head + heads, 1), :] for ref in mid_rows], axis=1)
        soft, slopes = row_side(kv[:, low], kv[:, high], queries, cots, mid_back, logs, dots)
        mid_dk, mid_dv = mm(slopes, queries), mm(soft, cots)

        _, slopes = row_side(
            far_own[1, :, low],
            far_own[1, :, high],
            far_k[:, low],
            far_k[:, high],
            far_bias,
            pick_lane(far_log, head),
            pick_lane(far_dot, head),
        )
        far_dq = mm(slopes, far_k[:, low])
        soft, slopes = row_side(
            far_own[0, :, low],
            far_own[0, :, high],
            far_q[:, low],
            far_q[:, high],
            far_back,
            far_rows[pl.ds(head, 1), :],
            far_rows[pl.ds(head + heads, 1), :],
        )
        far_dk, far_dv = mm(slopes, far_q[:, low]), mm(soft, far_q[:, high])

        whole = spread(rows, mid_at, jnp.concatenate([mid_dq, mid_dk, mid_dv], axis=1))
        whole += spread(rows, far_at, jnp.concatenate([far_dq, far_dk, far_dv], axis=1))
        dq, dk, dv = (whole[:, i * LANES : (i + 1) * LANES] for i in range(3))

        factor, shift = pick_lane(factors, head), pick_lane(shifts, head)
        for part in range(parts):
            part_rows = slice(part * size, (part + 1) * size)
            width = (part + 1) * size
            soft = soft_in[at, part_rows, :width].astype(F32)
            slopes = slope_in[at, part_rows, :width].astype(F32)
            slopes = (factor[part_rows] * (slopes - soft * shift[part_rows])).astype(BF16)
            soft = (factor[part_rows] * soft).astype(BF16)
            near_dq = mm(slopes, k[:width, cut])
            out_q[part_rows, cut] = ((dq[part_rows] + near_dq) * scale).astype(BF16)
            key_part = t_mm(slopes, q[part_rows, cut])
            value_part = t_mm(soft, g[part_rows, cut])
            if width < rows:
                rest = jnp.zeros((rows - width, LANES), F32)
                key_part = jnp.concatenate([key_part, rest], axis=0)
                value_part = jnp.concatenate([value_part, rest], axis=0)
            dk, dv = dk + key_part, dv + value_part
        out_k[:, cut] = (dk * scale).astype(BF16)
        out_v[:, cut] = dv.astype(BF16)


def swap(array, axis, size, step):
    return lax.ppermute(array, axis, [(i, i ^ step) for i in range(size)])


def call(kernel, steps, ins, outs, scratch, cost):
    specs, arrays = zip(*ins)
    out_specs, out_shapes = zip(*outs)
    return pl.pallas_call(
        kernel,
        grid=(steps,),
        in_specs=list(specs),
        out_specs=list(out_specs),
        out_shape=list(out_shapes),
        scratch_shapes=scratch,
        compiler_params=params(),
        cost_estimate=pl.CostEstimate(flops=cost[0], bytes_accessed=cost[1], transcendentals=cost[2]),
    )(*arrays)


def local(queries, keys, values, grad_out, mid_offset, far_offset):
    rows, flat = queries.shape
    heads = mid_offset.shape[0]
    width = flat // heads
    scale = width ** (-0.5)
    levels, rings = lax.axis_size("lvl"), lax.axis_size("seq")
    mid_count, far_count = rows // levels, rows // (levels * rings)
    block = far_count * levels
    level = lax.axis_index("lvl")
    place = jnp.stack([lax.axis_index("seq"), level]).astype(jnp.int32)
    shape = jax.ShapeDtypeStruct
    parts = 2
    steps = heads // GROUP
    tile = columns(rows, GROUP * width)
    mid_spec = columns(mid_count, GROUP * 2 * width)
    far_spec = pl.BlockSpec((2, far_count, GROUP * 2 * width), lambda h: (0, 0, h))
    sources = [(tile, queries), (tile, keys), (tile, values), (tile, grad_out)]
    scalars = [(smem(), place), (smem(), mid_offset), (smem(), far_offset)]
    unit = rows * rows * width * 2 * heads
    mid_shape = shape((mid_count, 2 * flat), BF16)

    kv, qg, far, *pays = call(
        select_kernel,
        steps,
        scalars + sources,
        [(mid_spec, mid_shape)] * 2
        + [(far_spec, shape((2, far_count, 2 * flat), BF16))]
        + [(mid_spec, mid_shape)] * (levels - 1),
        [],
        (unit, rows * flat * 16, 0),
    )
    pieces = [far] + [swap(far, "lvl", levels, step) for step in range(1, levels)]
    mid_in = [swap(pays[step - 1], "lvl", levels, step) for step in range(1, levels)]

    def at_level(where):
        chosen = pieces[0]
        for step in range(1, levels):
            chosen = jnp.where((where ^ level) == step, pieces[step], chosen)
        return chosen

    column = jnp.concatenate([at_level(where) for where in range(levels)], axis=1)
    far_all = lax.all_gather(column, "seq", axis=0)

    stat, stat_spec = shape((rows, LANES), F32), fixed((rows, LANES))
    square = shape((heads, rows, rows), BF16)
    square_spec = pl.BlockSpec((GROUP, rows, rows), lambda h: (h, 0, 0))
    near_logs, near_dots, near_soft, near_slopes = call(
        functools.partial(near_kernel, scale, parts),
        steps,
        sources,
        [(stat_spec, stat)] * 2 + [(square_spec, square)] * 2,
        [],
        (2 * unit, rows * flat * 8 + rows * rows * heads * 4, rows * rows * heads),
    )

    def gathered(which):
        spec = pl.BlockSpec((rings, 1, block, GROUP * 2 * width), lambda h: (0, which, 0, h))
        return (spec, far_all)

    mid_list = [(mid_spec, piece) for piece in mid_in]
    own = [(mid_spec, kv), (mid_spec, qg), (far_spec, far)]
    mid_stat, far_stat = shape((mid_count, LANES), F32), shape((far_count, LANES), F32)
    row_shape = shape((2 * heads, mid_count), F32)
    pack_shape = shape((levels * rings, far_count, 2 * heads), F32)
    stat_outs = [stat] * 2 + [mid_stat] * 2 + [far_stat] * 2 + [row_shape, pack_shape]
    stats = call(
        functools.partial(level_stats_kernel, scale, heads, levels, levels - 1),
        steps,
        scalars
        + own
        + [(stat_spec, near_logs), (stat_spec, near_dots)]
        + [gathered(0)]
        + mid_list,
        [(fixed(out.shape), out) for out in stat_outs],
        [pltpu.VMEM((mid_count, LANES), F32)] * 2 + [pltpu.VMEM((far_count, LANES), F32)] * 2,
        (unit, rows * flat * 16, rows * mid_count * heads),
    )
    mid_row, far_pack = stats[-2:]
    row_in = [swap(mid_row, "lvl", levels, step) for step in range(1, levels)]
    far_pack = lax.all_to_all(far_pack, ("seq", "lvl"), 0, 0, tiled=True)

    out = shape((rows, flat), BF16)
    stat_ins = [(fixed(array.shape), array) for array in list(stats[:-1]) + [far_pack] + row_in]
    return call(
        functools.partial(grads_kernel, scale, heads, levels, parts, levels - 1),
        steps,
        scalars
        + sources
        + [(square_spec, near_soft), (square_spec, near_slopes)]
        + own
        + [gathered(0), gathered(1)]
        + stat_ins[:8]
        + mid_list
        + stat_ins[8:],
        [(tile, out)] * 3,
        [pltpu.VMEM((2 * heads, rows), F32)],
        (6 * unit, rows * flat * 24 + rows * rows * heads * 4, rows * mid_count * heads),
    )


def solution(mesh):
    row_spec = P(("seq", "lvl"), None)
    return jax.shard_map(
        local,
        mesh=mesh,
        in_specs=(row_spec, row_spec, row_spec, row_spec, P(), P()),
        out_specs=(row_spec, row_spec, row_spec),
        check_vma=False,
    )
```

time: 153 us -> 128 us (0.84)
  local copies, waits for them, and re-layouts: 27.3 us -> 4.57 us
  Pallas kernels: 55.3 us -> 37.6 us
  between operations: 0.99 us -> 14.1 us
  waiting for transfers between devices: 31.3 us -> 41.5 us
  starting transfers between devices: 36.4 us -> 27.1 us
  other arithmetic: 0.77 us -> 3.1 us
    ppermute x23 -> x9, starting transfers between devices: 36.4 us -> 14.6 us  [swap(): return lax.ppermute(array, axis, [(i, i ^ step) for i in range(size)])]
    pallas_call x7 -> x4, Pallas kernels: 55.3 us -> 37.6 us  [call(): pl.pallas_call(kernel, grid=(steps,), in_specs=list(specs), out_specs=lis...]
    unnamed x84 -> x14, local copies, waits for them, and re-layouts: 21.7 us -> 4.06 us
    all_to_all x0 -> x1, starting transfers between devices: none -> 12.4 us  [local(): far_pack = lax.all_to_all(far_pack, ('seq', 'lvl'), 0, 0, tiled=True)]
    ppermute x23 -> x9, waiting for transfers between devices: 31.3 us -> 38.6 us  [swap(): return lax.ppermute(array, axis, [(i, i ^ step) for i in range(size)])]
    another operation x4 -> x0, local copies, waits for them, and re-layouts: 3.86 us -> none  [the longest x2 1.95 us: local(): far_lane = jnp.tile(far_offset, LANES // heads)[None, :]]
    all_to_all x0 -> x1, waiting for transfers between devices: none -> 2.84 us  [local(): far_pack = lax.all_to_all(far_pack, ('seq', 'lvl'), 0, 0, tiled=True)]
  transfers between devices with their start and end apart: 23 -> 11, of which waited for: 7 -> 5; matrix products, arithmetic and copies ran while one was open for 3% -> 2% of each run, Pallas kernels for 18% -> 6%
where the time goes in v2:
time: 128 us
  waiting for transfers between devices  41.5 us (32%)
  Pallas kernels  37.6 us (29%)
  starting transfers between devices  27.1 us (21%)
  between operations  14.1 us (11%)
  local copies, waits for them, and re-layouts  4.57 us (4%)
  other arithmetic  3.1 us (2%)
    ppermute x9, waiting for transfers between devices, swap(): return lax.ppermute(array, axis, [(i, i ^ step) for i in range(size)])  38.6 us
    pallas_call x4, Pallas kernels, call(): pl.pallas_call(kernel, grid=(steps,), in_specs=list(specs), out_specs=lis...  37.6 us
    ppermute x9, starting transfers between devices, swap(): return lax.ppermute(array, axis, [(i, i ^ step) for i in range(size)])  14.6 us
    all_to_all x1, starting transfers between devices, local(): far_pack = lax.all_to_all(far_pack, ('seq', 'lvl'), 0, 0, tiled=True)  12.4 us
    unnamed x14, local copies, waits for them, and re-layouts  4.06 us
    all_to_all x1, waiting for transfers between devices, local(): far_pack = lax.all_to_all(far_pack, ('seq', 'lvl'), 0, 0, tiled=True)  2.84 us
  transfers between devices with their start and end apart: 11, of which 5 were waited for; matrix products, arithmetic and copies ran while one was open for 2% of the time, Pallas kernels for 6%

profile of v2, /device:TPU:0, one launch (start us, length us, event | category | flops | bytes accessed | tf_op | source)
XLA Modules:
  0.0 128.0 jit_solution(114115716727581071)
XLA Ops:
  7.2 0.0 all-gather.3.cloned.1.call-start
  7.2 0.6 pad_add_fusion.place.refs_0_
  7.8 5.1 %shard_map.86 = (bf16[128,2048]{1,0:T(8,128)(2,1)}, bf16[128,2048]{1,0:T(8,128)(2,1)}, bf16[2,16,2048]{2,1,0:T(8,128)(2,1)}, bf16[128,2048]{1,0:T(8,128)(2,1)}, ...) custom-call(s32[2]{0:T(128)} %pad_add_fusion.place.refs_0_, s32[8]{0:T(128)} %refs_1_.3, s32[8]{0:T(128)} %refs_2_.3, ...), custom_call_target="tpu_custom_call" | custom-call | flops 536870912 | bytes 8388608 | tf_op jit(solution)/shard_map/pallas_call | solution.py:349
  12.9 3.1 %collective-permute-start.2 = (bf16[2,16,2048]{2,1,0:T(8,128)(2,1)}, bf16[2,16,2048]{2,1,0:T(8,128)(2,1)S(1)}, u32[]{:S(2)}, u32[]{:S(2)}) collective-permute-start(bf16[2,16,2048]{2,1,0:T(8,128)(2,1)} %get-tuple-element.25.refs_5_.refs_11_), channel_id=1, source_target_pairs={{0,1},{1,0},{2,3},{3,2},{4,5},{5,4},{6,7},{7,6},{8,9},{9,8},{10,11... | collective-permute-start | bytes 393224 | tf_op jit(solution)/shard_map/ppermute | solution.py:343
  16.0 2.6 %collective-permute-start.1 = (bf16[2,16,2048]{2,1,0:T(8,128)(2,1)}, bf16[2,16,2048]{2,1,0:T(8,128)(2,1)S(1)}, u32[]{:S(2)}, u32[]{:S(2)}) collective-permute-start(bf16[2,16,2048]{2,1,0:T(8,128)(2,1)} %get-tuple-element.25.refs_5_.refs_11_), channel_id=1, source_target_pairs={{0,2},{1,3},{2,0},{3,1},{4,6},{5,7},{6,4},{7,5},{8,10},{9,11},{10,... | collective-permute-start | bytes 393224 | tf_op jit(solution)/shard_map/ppermute | solution.py:343
  18.6 0.0 collective-permute-start
  18.6 2.6 %collective-permute-done.2 = bf16[2,16,2048]{2,1,0:T(8,128)(2,1)S(1)} collective-permute-done((bf16[2,16,2048]{2,1,0:T(8,128)(2,1)}, bf16[2,16,2048]{2,1,0:T(8,128)(2,1)S(1)}, u32[]{:S(2)}, u32[]{:S(2)}) %collective-permute-start.2) | collective-permute-done | bytes 131104 | tf_op jit(solution)/shard_map/ppermute | solution.py:343
  21.2 7.9 %collective-permute-done.1 = bf16[2,16,2048]{2,1,0:T(8,128)(2,1)S(1)} collective-permute-done((bf16[2,16,2048]{2,1,0:T(8,128)(2,1)}, bf16[2,16,2048]{2,1,0:T(8,128)(2,1)S(1)}, u32[]{:S(2)}, u32[]{:S(2)}) %collective-permute-start.1) | collective-permute-done | bytes 131104 | tf_op jit(solution)/shard_map/ppermute | solution.py:343
  29.2 0.0 collective-permute-done
  29.2 1.0 select_select_fusion.3
  30.1 0.9 pad_maximum_fusion
  31.0 0.0 all-gather.3.cloned.1.call-update
  31.0 2.0 %collective-permute-start.3 = (bf16[128,2048]{1,0:T(8,128)(2,1)}, bf16[128,2048]{1,0:T(8,128)(2,1)S(1)}, u32[]{:S(2)}, u32[]{:S(2)}) collective-permute-start(bf16[128,2048]{1,0:T(8,128)(2,1)} %get-tuple-element.28), channel_id=1, source_target_pairs={{0,1},{1,0},{2,3},{3,2},{4,5},{5,4},{6,7},{7,6},{8,9},{9,8},{10,11... | collective-permute-start | bytes 1572872 | tf_op jit(solution)/shard_map/ppermute | solution.py:343
  33.0 1.0 collective-permute-start.4
  34.1 1.4 %collective-permute-start.5 = (bf16[128,2048]{1,0:T(8,128)(2,1)}, bf16[128,2048]{1,0:T(8,128)(2,1)S(1)}, u32[]{:S(2)}, u32[]{:S(2)}) collective-permute-start(bf16[128,2048]{1,0:T(8,128)(2,1)} %get-tuple-element.30), channel_id=1, source_target_pairs={{0,3},{1,2},{2,1},{3,0},{4,7},{5,6},{6,5},{7,4},{8,11},{9,10},{10,... | collective-permute-start | bytes 1572872 | tf_op jit(solution)/shard_map/ppermute | solution.py:343
  35.5 8.0 %shard_map.85 = (f32[512,128]{1,0:T(8,128)}, f32[512,128]{1,0:T(8,128)}, bf16[8,512,512]{2,1,0:T(8,128)(2,1)}, bf16[8,512,512]{2,1,0:T(8,128)(2,1)}) custom-call(bf16[512,1024]{1,0:T(8,128)(2,1)} %refs_3_.1, bf16[512,1024]{1,0:T(8,128)(2,1)} %refs_4_.1, bf16[512,1024]{1,0:T(8,128)(2,1)} %refs_5_.1, bf16[512,1024]{1,0:T(8,128)(2,1)} %refs_6_.1), custom_call_target="tpu_custom_call" | custom-call | flops 1073741824 | bytes 12582912 | tf_op jit(solution)/shard_map/pallas_call | solution.py:349
  43.4 10.3 %collective-permute-done.3.refs_9_.refs_22_ = bf16[128,2048]{1,0:T(8,128)(2,1)S(1)} collective-permute-done((bf16[128,2048]{1,0:T(8,128)(2,1)}, bf16[128,2048]{1,0:T(8,128)(2,1)S(1)}, u32[]{:S(2)}, u32[]{:S(2)}) %collective-permute-start.3) | collective-permute-done | bytes 524320 | tf_op jit(solution)/shard_map/ppermute | solution.py:343
  53.7 0.0 copy-start
  53.7 17.8 %collective-permute-done.4.refs_10_.refs_23_ = bf16[128,2048]{1,0:T(8,128)(2,1)S(1)} collective-permute-done((bf16[128,2048]{1,0:T(8,128)(2,1)}, bf16[128,2048]{1,0:T(8,128)(2,1)S(1)}, u32[]{:S(2)}, u32[]{:S(2)}) %collective-permute-start.4) | collective-permute-done | bytes 524320 | tf_op jit(solution)/shard_map/ppermute | solution.py:343
  71.5 0.0 copy-start.1
  71.5 0.0 collective-permute-done.5.refs_11_.refs_24_
  71.5 0.0 copy-start.2
  71.5 0.0 all-gather.3.cloned.1.call-done
  71.5 0.0 copy-done
  71.5 0.8 copy-done.1
  72.3 0.2 copy-done.2
  72.5 7.7 %shard_map.87 = (f32[512,128]{1,0:T(8,128)}, f32[512,128]{1,0:T(8,128)}, f32[128,128]{1,0:T(8,128)}, f32[128,128]{1,0:T(8,128)}, f32[16,128]{1,0:T(8,128)}, /*in...) custom-call(s32[2]{0:T(128)} %pad_add_fusion.place.refs_0_, s32[8]{0:T(128)} %refs_1_.3, s32[8]{0:T(128)} %refs_2_.3, ...), custom_call_target="tpu_custom_call" | custom-call | flops 536870912 | bytes 8388608 | tf_op jit(solution)/shard_map/pallas_call | solution.py:349
  80.1 1.7 %reshape.7 = f32[32,1,256]{2,1,0:T(1,128)} reshape(f32[32,16,16]{2,1,0:T(8,128)} %get-tuple-element.38) | data formatting | bytes 65536
  81.8 12.4 %all-to-all-start = ((f32[32,1,256]{2,1,0:T(1,128)}), f32[32,1,256]{2,1,0:T(1,128)S(1)}, u32[]{:S(2)}, u32[]{:S(2)}) async-start(f32[32,1,256]{2,1,0:T(1,128)} %reshape.7), calls=%async_computation | async-start | bytes 65536 | tf_op jit(solution)/shard_map/all_to_all | solution.py:440
  94.3 3.7 %collective-permute-start.8 = (f32[16,128]{1,0:T(8,128)}, f32[16,128]{1,0:T(8,128)S(1)}, u32[]{:S(2)}, u32[]{:S(2)}) collective-permute-start(f32[16,128]{1,0:T(8,128)} %get-tuple-element.37.refs_20_), channel_id=1, source_target_pairs={{0,3},{1,2},{2,1},{3,0},{4,7},{5,6},{6,5},{7,4},{8,11},{9,10},{10,... | collective-permute-start | bytes 24584 | tf_op jit(solution)/shard_map/ppermute | solution.py:343
  98.0 0.0 collective-permute-start.7
  98.0 0.8 collective-permute-start.6
  98.7 2.8 %all-to-all-done = f32[32,1,256]{2,1,0:T(1,128)S(1)} async-done(((f32[32,1,256]{2,1,0:T(1,128)}), f32[32,1,256]{2,1,0:T(1,128)S(1)}, u32[]{:S(2)}, u32[]{:S(2)}) %all-to-all-start) | async-done | bytes 32800 | tf_op jit(solution)/shard_map/all_to_all | solution.py:440
  101.6 0.5 broadcast
  102.1 0.7 reduce
  102.8 0.8 reshape.8.refs_21_
  103.6 0.0 collective-permute-done.8.refs_27_
  103.6 0.0 copy-start.3
  103.6 0.0 collective-permute-done.7.refs_26_
  103.6 0.0 copy-start.4
  103.6 0.0 collective-permute-done.6.refs_25_
  103.7 0.0 copy-start.5
  103.7 0.6 copy-done.3
  104.2 0.0 copy-done.4
  104.2 0.0 copy-done.5
  104.2 16.9 %shard_map.88 = (bf16[512,1024]{1,0:T(8,128)(2,1)}, bf16[512,1024]{1,0:T(8,128)(2,1)}, bf16[512,1024]{1,0:T(8,128)(2,1)}) custom-call(s32[2]{0:T(128)} %pad_add_fusion.place.refs_0_, s32[8]{0:T(128)} %refs_1_.3, s32[8]{0:T(128)} %refs_2_.3, bf16[512,1024]{1,0:T(8,128)(2,1)} %refs_3_.1, bf16[512,1024]{1,0:T(8,128)(2,1)} %refs_4_.1, ...), custom_call_target="tpu_custom_call" | custom-call | flops 3221225472 | bytes 20971520 | tf_op jit(solution)/shard_map/pallas_call | solution.py:349
Async XLA Ops:
  7.2 64.3 %all-gather.3.cloned.1.call-start = ((), (), s32[]{:S(2)}) async-start(), calls=%async_computation.1 | async-start | bytes 4718592 | tf_op jit(solution)/shard_map/all_gather | solution.py:402
  12.9 8.3 %collective-permute-start.2 = (bf16[2,16,2048]{2,1,0:T(8,128)(2,1)}, bf16[2,16,2048]{2,1,0:T(8,128)(2,1)S(1)}, u32[]{:S(2)}, u32[]{:S(2)}) collective-permute-start(bf16[2,16,2048]{2,1,0:T(8,128)(2,1)} %get-tuple-element.25.refs_5_.refs_11_), channel_id=1, source_target_pairs={{0,1},{1,0},{2,3},{3,2},{4,5},{5,4},{6,7},{7,6},{8,9},{9,8},{10,11... | collective-permute-start | bytes 393224 | tf_op jit(solution)/shard_map/ppermute | solution.py:343
  16.0 13.2 %collective-permute-start.1 = (bf16[2,16,2048]{2,1,0:T(8,128)(2,1)}, bf16[2,16,2048]{2,1,0:T(8,128)(2,1)S(1)}, u32[]{:S(2)}, u32[]{:S(2)}) collective-permute-start(bf16[2,16,2048]{2,1,0:T(8,128)(2,1)} %get-tuple-element.25.refs_5_.refs_11_), channel_id=1, source_target_pairs={{0,2},{1,3},{2,0},{3,1},{4,6},{5,7},{6,4},{7,5},{8,10},{9,11},{10,... | collective-permute-start | bytes 393224 | tf_op jit(solution)/shard_map/ppermute | solution.py:343
  18.6 10.6 %collective-permute-start = (bf16[2,16,2048]{2,1,0:T(8,128)(2,1)}, bf16[2,16,2048]{2,1,0:T(8,128)(2,1)S(1)}, u32[]{:S(2)}, u32[]{:S(2)}) collective-permute-start(bf16[2,16,2048]{2,1,0:T(8,128)(2,1)} %get-tuple-element.25.refs_5_.refs_11_), channel_id=1, source_target_pairs={{0,3},{1,2},{2,1},{3,0},{4,7},{5,6},{6,5},{7,4},{8,11},{9,10},{10,... | collective-permute-start | bytes 393224 | tf_op jit(solution)/shard_map/ppermute | solution.py:343
  31.0 22.7 %collective-permute-start.3 = (bf16[128,2048]{1,0:T(8,128)(2,1)}, bf16[128,2048]{1,0:T(8,128)(2,1)S(1)}, u32[]{:S(2)}, u32[]{:S(2)}) collective-permute-start(bf16[128,2048]{1,0:T(8,128)(2,1)} %get-tuple-element.28), channel_id=1, source_target_pairs={{0,1},{1,0},{2,3},{3,2},{4,5},{5,4},{6,7},{7,6},{8,9},{9,8},{10,11... | collective-permute-start | bytes 1572872 | tf_op jit(solution)/shard_map/ppermute | solution.py:343
  33.0 38.4 %collective-permute-start.4 = (bf16[128,2048]{1,0:T(8,128)(2,1)}, bf16[128,2048]{1,0:T(8,128)(2,1)S(1)}, u32[]{:S(2)}, u32[]{:S(2)}) collective-permute-start(bf16[128,2048]{1,0:T(8,128)(2,1)} %get-tuple-element.29), channel_id=1, source_target_pairs={{0,2},{1,3},{2,0},{3,1},{4,6},{5,7},{6,4},{7,5},{8,10},{9,11},{10,... | collective-permute-start | bytes 1572872 | tf_op jit(solution)/shard_map/ppermute | solution.py:343
  34.1 37.4 %collective-permute-start.5 = (bf16[128,2048]{1,0:T(8,128)(2,1)}, bf16[128,2048]{1,0:T(8,128)(2,1)S(1)}, u32[]{:S(2)}, u32[]{:S(2)}) collective-permute-start(bf16[128,2048]{1,0:T(8,128)(2,1)} %get-tuple-element.30), channel_id=1, source_target_pairs={{0,3},{1,2},{2,1},{3,0},{4,7},{5,6},{6,5},{7,4},{8,11},{9,10},{10,... | collective-permute-start | bytes 1572872 | tf_op jit(solution)/shard_map/ppermute | solution.py:343
  53.7 17.8 %copy-start = (bf16[128,2048]{1,0:T(8,128)(2,1)}, bf16[128,2048]{1,0:T(8,128)(2,1)S(1)}, u32[]{:S(2)}) copy-start(bf16[128,2048]{1,0:T(8,128)(2,1)S(1)} %collective-permute-done.3.refs_9_.refs_22_) | copy-start | bytes 1572868
  71.5 0.8 copy-start.1
  71.5 1.0 copy-start.2
  81.8 19.7 %all-to-all-start = ((f32[32,1,256]{2,1,0:T(1,128)}), f32[32,1,256]{2,1,0:T(1,128)S(1)}, u32[]{:S(2)}, u32[]{:S(2)}) async-start(f32[32,1,256]{2,1,0:T(1,128)} %reshape.7), calls=%async_computation | async-start | bytes 65536 | tf_op jit(solution)/shard_map/all_to_all | solution.py:440
  94.3 9.3 %collective-permute-start.8 = (f32[16,128]{1,0:T(8,128)}, f32[16,128]{1,0:T(8,128)S(1)}, u32[]{:S(2)}, u32[]{:S(2)}) collective-permute-start(f32[16,128]{1,0:T(8,128)} %get-tuple-element.37.refs_20_), channel_id=1, source_target_pairs={{0,3},{1,2},{2,1},{3,0},{4,7},{5,6},{6,5},{7,4},{8,11},{9,10},{10,... | collective-permute-start | bytes 24584 | tf_op jit(solution)/shard_map/ppermute | solution.py:343
  98.0 5.7 %collective-permute-start.7 = (f32[16,128]{1,0:T(8,128)}, f32[16,128]{1,0:T(8,128)S(1)}, u32[]{:S(2)}, u32[]{:S(2)}) collective-permute-start(f32[16,128]{1,0:T(8,128)} %get-tuple-element.37.refs_20_), channel_id=1, source_target_pairs={{0,2},{1,3},{2,0},{3,1},{4,6},{5,7},{6,4},{7,5},{8,10},{9,11},{10,... | collective-permute-start | bytes 24584 | tf_op jit(solution)/shard_map/ppermute | solution.py:343
  98.0 5.7 %collective-permute-start.6 = (f32[16,128]{1,0:T(8,128)}, f32[16,128]{1,0:T(8,128)S(1)}, u32[]{:S(2)}, u32[]{:S(2)}) collective-permute-start(f32[16,128]{1,0:T(8,128)} %get-tuple-element.37.refs_20_), channel_id=1, source_target_pairs={{0,1},{1,0},{2,3},{3,2},{4,5},{5,4},{6,7},{7,6},{8,9},{9,8},{10,11... | collective-permute-start | bytes 24584 | tf_op jit(solution)/shard_map/ppermute | solution.py:343
  103.6 0.6 copy-start.3
  103.6 0.6 copy-start.4
  103.7 0.6 copy-start.5
Sparse Core Ops, SparseCore 0:
  31.1 37.2 all-gather.2

commit v3 on v2

v3 whole, which is shorter than its diff:
```python
import functools

import jax
import jax.numpy as jnp
from jax import lax
from jax.experimental import pallas as pl
from jax.experimental.pallas import tpu as pltpu
from jax.sharding import PartitionSpec as P

F32 = jnp.float32
BF16 = jnp.bfloat16
LANES = 128
LOW = -1e30
MIB = 1024 * 1024
GROUP = 4
LIMIT = 28


def mm(a, b):
    return lax.dot_general(a, b, (((1,), (0,)), ((), ())), preferred_element_type=F32)


def mm_t(a, b):
    return lax.dot_general(a, b, (((1,), (1,)), ((), ())), preferred_element_type=F32)


def t_mm(a, b):
    return lax.dot_general(a, b, (((0,), (0,)), ((), ())), preferred_element_type=F32)


def exact(a, b):
    return lax.dot_general(
        a, b, (((1,), (0,)), ((), ())), preferred_element_type=F32, precision=lax.Precision.HIGHEST
    )


def iota(shape, axis):
    return lax.broadcasted_iota(jnp.int32, shape, axis)


def params(limit):
    return pltpu.CompilerParams(
        vmem_limit_bytes=limit * MIB, dimension_semantics=("arbitrary",)
    )


def smem():
    return pl.BlockSpec(memory_space=pltpu.SMEM)


def columns(rows, width):
    return pl.BlockSpec((rows, width), lambda h: (0, h))


def fixed(shape):
    return pl.BlockSpec(shape, lambda h: (0,) * len(shape))


def pick_lane(ref, head):
    block = ref[...]
    return jnp.sum(jnp.where(iota(block.shape, 1) == head, block, 0.0), axis=1, keepdims=True)


def put_lane(ref, rows, head, value):
    block = ref[rows, :]
    ref[rows, :] = jnp.where(iota(block.shape, 1) == head, value, block)


def select_kernel(place, mid_off, far_off, q, k, v, g, kv, qg, far, *pays):
    level = place[1]
    rows = q.shape[0]
    for at in range(GROUP):
        head = pl.program_id(0) * GROUP + at
        cut = slice(at * LANES, (at + 1) * LANES)
        wide = slice(2 * at * LANES, 2 * (at + 1) * LANES)
        whole = jnp.concatenate([k[:, cut], v[:, cut], q[:, cut], g[:, cut]], axis=1)

        def picked(count, offset):
            stride = rows // count
            table = iota((count, rows), 1) == iota((count, rows), 0) * stride + offset
            return mm(table.astype(BF16), whole).astype(BF16)

        mid = picked(kv.shape[0], mid_off[head])
        half = 2 * LANES
        kv[:, wide] = mid[:, :half]
        qg[:, wide] = mid[:, half:]
        picks = picked(far.shape[1], far_off[head])
        far[0, :, wide] = picks[:, :half]
        far[1, :, wide] = picks[:, half:]
    for step, pay in enumerate(pays, 1):
        upward = (level ^ step) > level

        @pl.when(upward)
        def _():
            pay[...] = kv[...]

        @pl.when(jnp.logical_not(upward))
        def _():
            pay[...] = qg[...]


def near_kernel(scale, parts, q, k, v, g, logs, dots, soft_out, slope_out):
    @pl.when(pl.program_id(0) == 0)
    def _():
        logs[...] = jnp.zeros_like(logs)
        dots[...] = jnp.zeros_like(dots)

    size = q.shape[0] // parts
    for at in range(GROUP):
        head = pl.program_id(0) * GROUP + at
        cut = slice(at * LANES, (at + 1) * LANES)
        for part in range(parts):
            rows = slice(part * size, (part + 1) * size)
            width = (part + 1) * size
            scores = mm_t(q[rows, cut], k[:width, cut]) * scale
            grads = mm_t(g[rows, cut], v[:width, cut])
            seen = iota((size, width), 1) <= iota((size, width), 0) + part * size
            scores = jnp.where(seen, scores, LOW)
            peak = jnp.max(scores, axis=1, keepdims=True)
            weights = jnp.exp(scores - peak)
            total = jnp.sum(weights, axis=1, keepdims=True)
            soft = weights / total
            dot_part = jnp.sum(soft * grads, axis=1, keepdims=True)
            soft_out[at, rows, :width] = soft.astype(BF16)
            slope_out[at, rows, :width] = (soft * (grads - dot_part)).astype(BF16)
            put_lane(logs, rows, head, peak + jnp.log(total))
            put_lane(dots, rows, head, dot_part)


def row_stats(scores, grads):
    peak = jnp.max(scores, axis=1, keepdims=True)
    weights = jnp.exp(scores - peak)
    total = jnp.sum(weights, axis=1, keepdims=True)
    return peak + jnp.log(total), jnp.sum(weights * grads, axis=1, keepdims=True) / total


def mid_places(count, total, level):
    col = iota((count, total), 1)
    other = ((col >> (count.bit_length() - 1)) ^ level) * count + (col & (count - 1))
    return other, level * count + iota((count, total), 0)


def far_places(count, total, levels, level, ring):
    col = iota((count, total), 1)
    bits, level_bits = count.bit_length() - 1, levels.bit_length() - 1
    slot, ring_slot = (col >> bits) & (levels - 1), col >> (bits + level_bits)
    other = ((ring_slot ^ ring) * levels + (slot ^ level)) * count + (col & (count - 1))
    return other, (ring * levels + level) * count + iota((count, total), 0)


def bias(seen):
    return jnp.where(seen, 0.0, LOW)


def stack(refs, cut):
    return jnp.concatenate([ref[:, cut] for ref in refs], axis=0)


def repeat_table(rows, count):
    return (iota((rows, count), 0) // (rows // count) == iota((rows, count), 1)).astype(F32)


def gather_table(rows, count):
    return (iota((count, rows), 1) // (rows // count) == iota((count, rows), 0)).astype(F32)


def lane_offsets(offsets, heads):
    lane = iota((1, LANES), 1)
    values = jnp.zeros((1, LANES), jnp.int32)
    for head in range(heads):
        values = jnp.where(lane == head, offsets[head], values)
    return values


def column_kernel(levels, bits, *refs):
    place = refs[0]
    pieces = refs[1 : 1 + levels]
    col_kv, col_qg = refs[1 + levels : 3 + levels]
    pays = refs[3 + levels :]
    col_kv[...] = jnp.concatenate([piece[0] for piece in pieces], axis=0)
    col_qg[...] = jnp.concatenate([piece[1] for piece in pieces], axis=0)
    for bit in range(bits):
        upward = ((place[0] >> bit) & 1) == 0

        @pl.when(upward)
        def _():
            pays[bit][...] = col_kv[...]

        @pl.when(jnp.logical_not(upward))
        def _():
            pays[bit][...] = col_qg[...]


def cuts(at):
    low = slice(2 * at * LANES, (2 * at + 1) * LANES)
    return low, slice((2 * at + 1) * LANES, (2 * at + 2) * LANES)


def level_stats_kernel(scale, heads, levels, mids, fars, *refs):
    place, mid_off, far_off, kv, qg, far_own, near_logs, near_dots = refs[:8]
    mid_in, far_in = refs[8 : 8 + mids], refs[8 + mids : 8 + mids + fars]
    factors, shifts, mid_log, mid_dot, far_log, far_dot, sent = refs[8 + mids + fars :][:7]
    mlog, mdot, flog, fdot = refs[15 + mids + fars :]
    ring, level = place[0], place[1]
    mid_count, far_count = kv.shape[0], far_own.shape[1]
    total = mid_count * levels

    @pl.when(pl.program_id(0) == 0)
    def _():
        for ref in (mlog, mdot, flog, fdot):
            ref[...] = jnp.zeros_like(ref)

    other, own = mid_places(mid_count, total, level)
    mid_bias = bias(other <= own)
    other, own = far_places(far_count, total, levels, level, ring)
    far_bias = bias(other <= own)
    every = slice(None)
    for at in range(GROUP):
        head = pl.program_id(0) * GROUP + at
        low, high = cuts(at)
        scores = mm_t(qg[:, low], stack((kv,) + mid_in, low)) * scale + mid_bias
        grads = mm_t(qg[:, high], stack((kv,) + mid_in, high))
        log_part, dot_part = row_stats(scores, grads)
        put_lane(mlog, every, head, log_part)
        put_lane(mdot, every, head, dot_part)
        scores = mm_t(far_own[1, :, low], stack(far_in, low)) * scale + far_bias
        grads = mm_t(far_own[1, :, high], stack(far_in, high))
        log_part, dot_part = row_stats(scores, grads)
        put_lane(flog, every, head, log_part)
        put_lane(fdot, every, head, dot_part)

    @pl.when(pl.program_id(0) == pl.num_programs(0) - 1)
    def _():
        rows = near_logs.shape[0]
        row = iota((rows, LANES), 0)
        mid_here = (row & (rows // mid_count - 1)) == lane_offsets(mid_off, heads)
        far_here = (row & (rows // far_count - 1)) == lane_offsets(far_off, heads)
        mid_table, far_table = repeat_table(rows, mid_count), repeat_table(rows, far_count)
        near = near_logs[...]
        mid = jnp.where(mid_here, exact(mid_table, mlog[...]), LOW)
        far = jnp.where(far_here, exact(far_table, flog[...]), LOW)
        peak = jnp.maximum(near, jnp.maximum(mid, far))
        near_part = jnp.exp(near - peak)
        mid, far = jnp.exp(mid - peak), jnp.exp(far - peak)
        whole = near_part + mid + far
        logs = peak + jnp.log(whole)
        dots = (
            near_part * near_dots[...]
            + mid * exact(mid_table, mdot[...])
            + far * exact(far_table, fdot[...])
        ) / whole
        factors[...] = jnp.exp(near - logs)
        shifts[...] = dots - near_dots[...]
        for here, count, log_out, dot_out, first in (
            (mid_here, mid_count, mid_log, mid_dot, 0),
            (far_here, far_count, far_log, far_dot, mid_count),
        ):
            table = gather_table(rows, count)
            log_out[...] = exact(table, jnp.where(here, logs, 0.0))
            dot_out[...] = exact(table, jnp.where(here, dots, 0.0))
            sent[:heads, first : first + count] = log_out[...].T[:heads, :]
            sent[heads:, first : first + count] = dot_out[...].T[:heads, :]


def row_side(scale, queries, cots, keys, vals, hide, logs, dots):
    scores = mm_t(queries, keys) * scale + hide
    soft = jnp.exp(scores - logs)
    slopes = soft * (mm_t(cots, vals) - dots)
    return soft.astype(BF16), slopes.astype(BF16)


def level_queries_kernel(scale, levels, mids, fars, *refs):
    place, kv, qg, far_own, mid_log, mid_dot, far_log, far_dot = refs[:8]
    mid_in, far_in = refs[8 : 8 + mids], refs[8 + mids : 8 + mids + fars]
    mid_dq, far_dq = refs[8 + mids + fars :]
    ring, level = place[0], place[1]
    mid_count, far_count = kv.shape[0], far_own.shape[1]
    total = mid_count * levels
    other, own = mid_places(mid_count, total, level)
    mid_bias = bias(other <= own)
    other, own = far_places(far_count, total, levels, level, ring)
    far_bias = bias(other <= own)
    for at in range(GROUP):
        head = pl.program_id(0) * GROUP + at
        cut = slice(at * LANES, (at + 1) * LANES)
        low, high = cuts(at)
        keys, vals = stack((kv,) + mid_in, low), stack((kv,) + mid_in, high)
        logs, dots = pick_lane(mid_log, head), pick_lane(mid_dot, head)
        _, slopes = row_side(scale, qg[:, low], qg[:, high], keys, vals, mid_bias, logs, dots)
        mid_dq[:, cut] = mm(slopes, keys)
        keys, vals = stack(far_in, low), stack(far_in, high)
        logs, dots = pick_lane(far_log, head), pick_lane(far_dot, head)
        _, slopes = row_side(
            scale, far_own[1, :, low], far_own[1, :, high], keys, vals, far_bias, logs, dots
        )
        far_dq[:, cut] = mm(slopes, keys)


def spread(rows, offset, piece):
    count = piece.shape[0]
    table = (iota((rows, count), 0) == iota((rows, count), 1) * (rows // count) + offset).astype(BF16)
    high = piece.astype(BF16)
    low = (piece - high.astype(F32)).astype(BF16)
    return mm(table, high) + mm(table, low)


def near_grads_kernel(scale, parts, mid_off, far_off, q, k, g, soft_in, slope_in, *refs):
    factors, shifts, mid_dq, far_dq, out_q, out_k, out_v = refs
    rows = q.shape[0]
    size = rows // parts
    for at in range(GROUP):
        head = pl.program_id(0) * GROUP + at
        cut = slice(at * LANES, (at + 1) * LANES)
        dq = spread(rows, mid_off[head], mid_dq[:, cut]) + spread(rows, far_off[head], far_dq[:, cut])
        factor, shift = pick_lane(factors, head), pick_lane(shifts, head)
        for part in reversed(range(parts)):
            part_rows = slice(part * size, (part + 1) * size)
            width = (part + 1) * size
            soft = soft_in[at, part_rows, :width].astype(F32)
            slopes = slope_in[at, part_rows, :width].astype(F32)
            slopes = (factor[part_rows] * (slopes - soft * shift[part_rows])).astype(BF16)
            soft = (factor[part_rows] * soft).astype(BF16)
            near_dq = mm(slopes, k[:width, cut])
            out_q[part_rows, cut] = ((dq[part_rows] + near_dq) * scale).astype(BF16)
            key_part = t_mm(slopes, q[part_rows, cut])
            value_part = t_mm(soft, g[part_rows, cut])
            if part == parts - 1:
                out_k[:, cut] = key_part
                out_v[:, cut] = value_part
            else:
                out_k[:width, cut] += key_part
                out_v[:width, cut] += value_part


def level_keys_kernel(scale, heads, levels, mids, fars, *refs):
    place, mid_off, far_off, kv, qg, far_own, near_dk, near_dv = refs[:8]
    mid_in, far_in = refs[8 : 8 + mids], refs[8 + mids : 8 + mids + fars]
    mid_stats = refs[8 + mids + fars :][: mids + 1]
    far_stats = refs[9 + 2 * mids + fars : 9 + 2 * mids + 2 * fars]
    out_k, out_v, mid_rows, far_rows = refs[9 + 2 * mids + 2 * fars :]
    ring, level = place[0], place[1]
    rows = out_k.shape[0]
    mid_count, far_count = kv.shape[0], far_own.shape[1]
    total = mid_count * levels

    @pl.when(pl.program_id(0) == 0)
    def _():
        mid_rows[...] = jnp.concatenate([ref[:, :mid_count] for ref in mid_stats], axis=1)
        far_rows[...] = jnp.concatenate([ref[...] for ref in far_stats], axis=1)

    other, own = mid_places(mid_count, total, level)
    mid_bias = bias(other >= own)
    other, own = far_places(far_count, total, levels, level, ring)
    far_bias = bias(other >= own)
    for at in range(GROUP):
        head = pl.program_id(0) * GROUP + at
        cut = slice(at * LANES, (at + 1) * LANES)
        low, high = cuts(at)

        def one(keys, vals, queries, cots, hide, stats):
            logs, dots = stats[pl.ds(head, 1), :], stats[pl.ds(head + heads, 1), :]
            soft, slopes = row_side(scale, keys, vals, queries, cots, hide, logs, dots)
            return jnp.concatenate([mm(slopes, queries), mm(soft, cots)], axis=1)

        queries, cots = stack((qg,) + mid_in, low), stack((qg,) + mid_in, high)
        mid = one(kv[:, low], kv[:, high], queries, cots, mid_bias, mid_rows)
        queries, cots = stack(far_in, low), stack(far_in, high)
        far = one(far_own[0, :, low], far_own[0, :, high], queries, cots, far_bias, far_rows)
        whole = spread(rows, mid_off[head], mid) + spread(rows, far_off[head], far)
        out_k[:, cut] = ((near_dk[:, cut] + whole[:, :LANES]) * scale).astype(BF16)
        out_v[:, cut] = (near_dv[:, cut] + whole[:, LANES:]).astype(BF16)


def swap(array, axis, size, step):
    return lax.ppermute(array, axis, [(i, i ^ step) for i in range(size)])


def call(kernel, steps, ins, outs, scratch, limit=LIMIT):
    specs, arrays = zip(*ins)
    out_specs, out_shapes = zip(*outs)
    return pl.pallas_call(
        kernel,
        grid=(steps,),
        in_specs=list(specs),
        out_specs=list(out_specs),
        out_shape=list(out_shapes),
        scratch_shapes=scratch,
        compiler_params=params(limit),
        cost_estimate=pl.CostEstimate(flops=0, bytes_accessed=0, transcendentals=0),
    )(*arrays)


def local(queries, keys, values, grad_out, mid_offset, far_offset):
    rows, flat = queries.shape
    heads = mid_offset.shape[0]
    width = flat // heads
    scale = width ** (-0.5)
    levels, rings = lax.axis_size("lvl"), lax.axis_size("seq")
    mid_count, far_count = rows // levels, rows // (levels * rings)
    block = far_count * levels
    level = lax.axis_index("lvl")
    place = jnp.stack([lax.axis_index("seq"), level]).astype(jnp.int32)
    shape = jax.ShapeDtypeStruct
    parts = 2
    steps = heads // GROUP
    tile = columns(rows, GROUP * width)
    mid_spec = columns(mid_count, GROUP * 2 * width)
    far_spec = pl.BlockSpec((2, far_count, GROUP * 2 * width), lambda h: (0, 0, h))
    sources = [(tile, queries), (tile, keys), (tile, values), (tile, grad_out)]
    scalars = [(smem(), place), (smem(), mid_offset), (smem(), far_offset)]
    mid_shape = shape((mid_count, 2 * flat), BF16)

    kv, qg, far, *pays = call(
        select_kernel,
        steps,
        scalars + sources,
        [(mid_spec, mid_shape)] * 2
        + [(far_spec, shape((2, far_count, 2 * flat), BF16))]
        + [(mid_spec, mid_shape)] * (levels - 1),
        [],
        60,
    )
    far_level = [far] + [swap(far, "lvl", levels, step) for step in range(1, levels)]
    mid_in = [swap(pays[step - 1], "lvl", levels, step) for step in range(1, levels)]
    stat, stat_spec = shape((rows, LANES), F32), fixed((rows, LANES))
    square = shape((heads, rows, rows), BF16)
    square_spec = pl.BlockSpec((GROUP, rows, rows), lambda h: (h, 0, 0))
    near_logs, near_dots, near_soft, near_slopes = call(
        functools.partial(near_kernel, scale, parts),
        steps,
        sources,
        [(stat_spec, stat)] * 2 + [(square_spec, square)] * 2,
        [],
    )
    far_level, near_logs = lax.optimization_barrier((far_level, near_logs))
    ring_bits = rings.bit_length() - 1
    col_shape = shape((block, 2 * flat), BF16)
    col_kv, col_qg, *ring_pays = call(
        functools.partial(column_kernel, levels, ring_bits),
        1,
        scalars[:1] + [(fixed(piece.shape), piece) for piece in far_level],
        [(fixed(col_shape.shape), col_shape)] * (2 + ring_bits),
        [],
    )
    far_ring = [None] * rings
    for step in range(2, rings, 2):
        far_ring[step] = swap(ring_pays[step.bit_length() - 1], "seq", rings, step)
    far_ring[1] = swap(ring_pays[0], "seq", rings, 1)
    for step in range(3, rings, 2):
        far_ring[step] = swap(far_ring[step - 1], "seq", rings, 1)

    col_spec = columns(block, GROUP * 2 * width)
    mid_list = [(mid_spec, piece) for piece in mid_in]
    far_rest = [(col_spec, piece) for piece in far_ring[1:]]
    far_kv, far_qg = [(col_spec, col_kv)] + far_rest, [(col_spec, col_qg)] + far_rest
    own = [(mid_spec, kv), (mid_spec, qg), (far_spec, far)]
    mid_stat, far_stat = shape((mid_count, LANES), F32), shape((far_count, LANES), F32)
    sent_shape = shape((2 * heads, mid_count + far_count), F32)
    stat_outs = [stat] * 2 + [mid_stat] * 2 + [far_stat] * 2 + [sent_shape]
    factors, shifts, mid_log, mid_dot, far_log, far_dot, sent = call(
        functools.partial(level_stats_kernel, scale, heads, levels, levels - 1, rings),
        steps,
        scalars + own + [(stat_spec, near_logs), (stat_spec, near_dots)] + mid_list + far_kv,
        [(fixed(out.shape), out) for out in stat_outs],
        [pltpu.VMEM((mid_count, LANES), F32)] * 2 + [pltpu.VMEM((far_count, LANES), F32)] * 2,
    )

    sent_in = [sent] + [swap(sent, "lvl", levels, step) for step in range(1, levels)]
    mid_dq, far_dq = call(
        functools.partial(level_queries_kernel, scale, levels, levels - 1, rings),
        steps,
        scalars[:1]
        + own
        + [(fixed(mid_stat.shape), mid_log), (fixed(mid_stat.shape), mid_dot)]
        + [(fixed(far_stat.shape), far_log), (fixed(far_stat.shape), far_dot)]
        + mid_list
        + far_kv,
        [
            (columns(mid_count, GROUP * width), shape((mid_count, flat), F32)),
            (columns(far_count, GROUP * width), shape((far_count, flat), F32)),
        ],
        [],
    )
    sent_in, mid_dq = lax.optimization_barrier((sent_in, mid_dq))
    far_sent = jnp.concatenate([piece[:, mid_count:] for piece in sent_in], axis=1)
    far_sent_in = [far_sent] + [swap(far_sent, "seq", rings, step) for step in range(1, rings)]

    out, grad = shape((rows, flat), BF16), shape((rows, flat), F32)
    grad_query, near_dk, near_dv = call(
        functools.partial(near_grads_kernel, scale, parts),
        steps,
        scalars[1:]
        + [(tile, queries), (tile, keys), (tile, grad_out)]
        + [(square_spec, near_soft), (square_spec, near_slopes)]
        + [(stat_spec, factors), (stat_spec, shifts)]
        + [(columns(mid_count, GROUP * width), mid_dq), (columns(far_count, GROUP * width), far_dq)],
        [(tile, out), (tile, grad), (tile, grad)],
        [],
    )
    grad_key, grad_value = call(
        functools.partial(level_keys_kernel, scale, heads, levels, levels - 1, rings),
        steps,
        scalars
        + own
        + [(tile, near_dk), (tile, near_dv)]
        + mid_list
        + far_qg
        + [(fixed(piece.shape), piece) for piece in sent_in + far_sent_in],
        [(tile, out)] * 2,
        [pltpu.VMEM((2 * heads, rows), F32)] * 2,
    )
    return grad_query, grad_key, grad_value


def solution(mesh):
    row_spec = P(("seq", "lvl"), None)
    return jax.shard_map(
        local,
        mesh=mesh,
        in_specs=(row_spec, row_spec, row_spec, row_spec, P(), P()),
        out_specs=(row_spec, row_spec, row_spec),
        check_vma=False,
    )
```

time: 128 us -> 106 us (0.83)
  between operations: 14.1 us -> 0.88 us
  starting transfers between devices: 27.1 us -> 34.5 us
  waiting for transfers between devices: 41.5 us -> 35.2 us
  Pallas kernels: 37.6 us -> 33.5 us
  local copies, waits for them, and re-layouts: 4.57 us -> 1.29 us
  other arithmetic: 3.1 us -> 0.72 us
    ppermute x9 -> x23, starting transfers between devices: 14.6 us -> 34.5 us  [swap(): return lax.ppermute(array, axis, [(i, i ^ step) for i in range(size)])]
    all_to_all x1 -> x0, starting transfers between devices: 12.4 us -> none  [local(): far_pack = lax.all_to_all(far_pack, ('seq', 'lvl'), 0, 0, tiled=True)]
    pallas_call x4 -> x7, Pallas kernels: 37.6 us -> 33.5 us  [call(): pl.pallas_call(kernel, grid=(steps,), in_specs=list(specs), out_specs=lis...]
    ppermute x9 -> x23, waiting for transfers between devices: 38.6 us -> 35.2 us  [swap(): return lax.ppermute(array, axis, [(i, i ^ step) for i in range(size)])]
    all_to_all x1 -> x0, waiting for transfers between devices: 2.84 us -> none  [local(): far_pack = lax.all_to_all(far_pack, ('seq', 'lvl'), 0, 0, tiled=True)]
    unnamed x14 -> x26, local copies, waits for them, and re-layouts: 4.06 us -> 1.28 us
  transfers between devices with their start and end apart: 11 -> 23, of which waited for: 5 -> 6; matrix products, arithmetic and copies ran while one was open for 2% -> 0% of each run, Pallas kernels for 6% -> 15%
where the time goes in v3:
time: 106 us
  waiting for transfers between devices  35.2 us (33%)
  starting transfers between devices  34.5 us (33%)
  Pallas kernels  33.5 us (32%)
  local copies, waits for them, and re-layouts  1.29 us (1%)
    ppermute x23, waiting for transfers between devices, swap(): return lax.ppermute(array, axis, [(i, i ^ step) for i in range(size)])  35.2 us
    ppermute x23, starting transfers between devices, swap(): return lax.ppermute(array, axis, [(i, i ^ step) for i in range(size)])  34.5 us
    pallas_call x7, Pallas kernels, call(): pl.pallas_call(kernel, grid=(steps,), in_specs=list(specs), out_specs=lis...  33.5 us
  transfers between devices with their start and end apart: 23, of which 6 were waited for; matrix products, arithmetic and copies ran while one was open for 0% of the time, Pallas kernels for 15%

profile of v3, /device:TPU:0, one launch (start us, length us, event | category | flops | bytes accessed | tf_op | source)
XLA Modules:
  0.0 106.0 jit_solution(13751753709912142127)
XLA Ops:
  0.6 0.0 copy-start.2
  0.6 0.0 copy-start.1
  0.7 0.0 copy-start
  0.7 0.6 pad_add_fusion.place.refs_0_
  1.3 4.6 %shard_map.86 = (bf16[128,2048]{1,0:T(8,128)(2,1)}, bf16[128,2048]{1,0:T(8,128)(2,1)}, bf16[2,16,2048]{2,1,0:T(8,128)(2,1)}, bf16[128,2048]{1,0:T(8,128)(2,1)}, ...) custom-call(s32[2]{0:T(128)} %pad_add_fusion.place.refs_0_, s32[8]{0:T(128)} %refs_1_.3, s32[8]{0:T(128)} %refs_2_.3, ...), custom_call_target="tpu_custom_call" | custom-call | tf_op jit(solution)/shard_map/pallas_call | solution.py:381
  5.9 0.0 copy-start.4
  5.9 5.1 %collective-permute-start.2 = (bf16[2,16,2048]{2,1,0:T(8,128)(2,1)}, bf16[2,16,2048]{2,1,0:T(8,128)(2,1)S(1)}, u32[]{:S(2)}, u32[]{:S(2)}) collective-permute-start(bf16[2,16,2048]{2,1,0:T(8,128)(2,1)} %get-tuple-element.53.refs_1_.refs_5_.refs_3_), channel_id=1, source_target_pairs={{0,3},{1,2},{2,1},{3,0},{4,7},{5,6},{6,5},{7,4},{8,11},{9,10},{10,... | collective-permute-start | bytes 393224 | tf_op jit(solution)/shard_map/ppermute | solution.py:375
  11.1 0.0 collective-permute-start.1
  11.1 0.6 collective-permute-start
  11.7 0.0 copy-done.2
  11.7 0.0 copy-done
  11.7 1.2 %copy-done.5 = bf16[512,1024]{1,0:T(8,128)(2,1)S(1)} copy-done((bf16[512,1024]{1,0:T(8,128)(2,1)S(1)}, bf16[512,1024]{1,0:T(8,128)(2,1)}, u32[]{:S(2)}) %copy-start.5) | copy-done | bytes 1048600
  13.0 4.6 %shard_map.85 = (f32[512,128]{1,0:T(8,128)S(1)}, f32[512,128]{1,0:T(8,128)S(1)}, bf16[8,512,512]{2,1,0:T(8,128)(2,1)S(1)}, bf16[8,512,512]{2,1,0:T(8,128)(2,1)S(1)}) custom-call(bf16[512,1024]{1,0:T(8,128)(2,1)S(1)} %copy-done, bf16[512,1024]{1,0:T(8,128)(2,1)S(1)} %copy-done.1, bf16[512,1024]{1,0:T(8,128)(2,1)S(1)} %copy-done.5, bf16[512,1024]{1,0:T(8,128)(2,1)S(1)} %copy-done.2), custom_call_target="tpu_custom_call" | custom-call | tf_op jit(solution)/shard_map/pallas_call | solution.py:381
  17.6 0.0 collective-permute-done.2.refs_4_
  17.6 4.8 %collective-permute-done.1.refs_3_ = bf16[2,16,2048]{2,1,0:T(8,128)(2,1)S(1)} collective-permute-done((bf16[2,16,2048]{2,1,0:T(8,128)(2,1)}, bf16[2,16,2048]{2,1,0:T(8,128)(2,1)S(1)}, u32[]{:S(2)}, u32[]{:S(2)}) %collective-permute-start.1) | collective-permute-done | bytes 131104 | tf_op jit(solution)/shard_map/ppermute | solution.py:375
  22.4 0.0 collective-permute-done.refs_2_
  22.4 0.0 copy-done.7
  22.4 0.8 shard_map.87
  23.2 0.1 collective-permute-start.6
  23.3 1.6 %collective-permute-start.7 = (bf16[64,2048]{1,0:T(8,128)(2,1)S(1)}, bf16[64,2048]{1,0:T(8,128)(2,1)S(1)}, u32[]{:S(2)}, u32[]{:S(2)}) collective-permute-start(bf16[64,2048]{1,0:T(8,128)(2,1)S(1)} %get-tuple-element.59), channel_id=1, source_target_pairs={{0,8},{4,12},{8,0},{12,4},{16,24},{20,28},{24,16},{28,20},{1,9},{5... | collective-permute-start | bytes 786440 | tf_op jit(solution)/shard_map/ppermute | solution.py:375
  24.9 0.0 copy-done.12
  24.9 0.0 collective-permute-start.3
  24.9 3.0 %collective-permute-start.4 = (bf16[128,2048]{1,0:T(8,128)(2,1)S(1)}, bf16[128,2048]{1,0:T(8,128)(2,1)S(1)}, u32[]{:S(2)}, u32[]{:S(2)}) collective-permute-start(bf16[128,2048]{1,0:T(8,128)(2,1)S(1)} %copy-done.11), channel_id=1, source_target_pairs={{0,2},{1,3},{2,0},{3,1},{4,6},{5,7},{6,4},{7,5},{8,10},{9,11},{10,... | collective-permute-start | bytes 1572872 | tf_op jit(solution)/shard_map/ppermute | solution.py:375
  27.9 1.4 %collective-permute-start.5 = (bf16[128,2048]{1,0:T(8,128)(2,1)S(1)}, bf16[128,2048]{1,0:T(8,128)(2,1)S(1)}, u32[]{:S(2)}, u32[]{:S(2)}) collective-permute-start(bf16[128,2048]{1,0:T(8,128)(2,1)S(1)} %copy-done.10), channel_id=1, source_target_pairs={{0,3},{1,2},{2,1},{3,0},{4,7},{5,6},{6,5},{7,4},{8,11},{9,10},{10,... | collective-permute-start | bytes 1572872 | tf_op jit(solution)/shard_map/ppermute | solution.py:375
  29.3 0.0 collective-permute-done.6.refs_12_
  29.3 1.5 %collective-permute-start.11 = (bf16[64,2048]{1,0:T(8,128)(2,1)S(1)}, bf16[64,2048]{1,0:T(8,128)(2,1)S(1)}, u32[]{:S(2)}, u32[]{:S(2)}) collective-permute-start(bf16[64,2048]{1,0:T(8,128)(2,1)S(1)} %get-tuple-element.60), channel_id=1, source_target_pairs={{0,24},{4,28},{8,16},{12,20},{16,8},{20,12},{24,0},{28,4},{1,25},{... | collective-permute-start | bytes 786440 | tf_op jit(solution)/shard_map/ppermute | solution.py:375
  30.8 1.3 %collective-permute-done.7.refs_13_ = bf16[64,2048]{1,0:T(8,128)(2,1)S(1)} collective-permute-done((bf16[64,2048]{1,0:T(8,128)(2,1)S(1)}, bf16[64,2048]{1,0:T(8,128)(2,1)S(1)}, u32[]{:S(2)}, u32[]{:S(2)}) %collective-permute-start.7) | collective-permute-done | bytes 262176 | tf_op jit(solution)/shard_map/ppermute | solution.py:375
  32.0 2.0 %collective-permute-start.9 = (bf16[64,2048]{1,0:T(8,128)(2,1)S(1)}, bf16[64,2048]{1,0:T(8,128)(2,1)S(1)}, u32[]{:S(2)}, u32[]{:S(2)}) collective-permute-start(bf16[64,2048]{1,0:T(8,128)(2,1)S(1)} %get-tuple-element.60), channel_id=1, source_target_pairs={{0,16},{4,20},{8,24},{12,28},{16,0},{20,4},{24,8},{28,12},{1,17},{... | collective-permute-start | bytes 786440 | tf_op jit(solution)/shard_map/ppermute | solution.py:375
  34.0 4.7 %collective-permute-done.11.refs_17_ = bf16[64,2048]{1,0:T(8,128)(2,1)S(1)} collective-permute-done((bf16[64,2048]{1,0:T(8,128)(2,1)S(1)}, bf16[64,2048]{1,0:T(8,128)(2,1)S(1)}, u32[]{:S(2)}, u32[]{:S(2)}) %collective-permute-start.11) | collective-permute-done | bytes 262176 | tf_op jit(solution)/shard_map/ppermute | solution.py:375
  38.7 0.0 collective-permute-start.8
  38.7 5.5 %collective-permute-done.9.refs_15_ = bf16[64,2048]{1,0:T(8,128)(2,1)S(1)} collective-permute-done((bf16[64,2048]{1,0:T(8,128)(2,1)S(1)}, bf16[64,2048]{1,0:T(8,128)(2,1)S(1)}, u32[]{:S(2)}, u32[]{:S(2)}) %collective-permute-start.9) | collective-permute-done | bytes 262176 | tf_op jit(solution)/shard_map/ppermute | solution.py:375
  44.2 0.0 collective-permute-start.12
  44.2 5.3 %collective-permute-done.3.refs_8_ = bf16[128,2048]{1,0:T(8,128)(2,1)S(1)} collective-permute-done((bf16[128,2048]{1,0:T(8,128)(2,1)S(1)}, bf16[128,2048]{1,0:T(8,128)(2,1)S(1)}, u32[]{:S(2)}, u32[]{:S(2)}) %collective-permute-start.3) | collective-permute-done | bytes 524320 | tf_op jit(solution)/shard_map/ppermute | solution.py:375
  49.6 0.0 collective-permute-start.10
  49.6 13.5 %collective-permute-done.4.refs_9_ = bf16[128,2048]{1,0:T(8,128)(2,1)S(1)} collective-permute-done((bf16[128,2048]{1,0:T(8,128)(2,1)S(1)}, bf16[128,2048]{1,0:T(8,128)(2,1)S(1)}, u32[]{:S(2)}, u32[]{:S(2)}) %collective-permute-start.4) | collective-permute-done | bytes 524320 | tf_op jit(solution)/shard_map/ppermute | solution.py:375
  63.1 0.0 collective-permute-done.5.refs_10_
  63.1 0.0 collective-permute-done.8.refs_14_
  63.1 0.0 collective-permute-done.12.refs_18_
  63.1 0.0 collective-permute-done.10.refs_16_
  63.2 4.9 %shard_map.88 = (f32[512,128]{1,0:T(8,128)S(1)}, f32[512,128]{1,0:T(8,128)S(1)}, f32[128,128]{1,0:T(8,128)S(1)}, f32[128,128]{1,0:T(8,128)S(1)}, f32[16,128]{1,0...) custom-call(s32[2]{0:T(128)S(1)} %copy-done.7, s32[8]{0:T(128)S(1)} %copy-done.8, s32[8]{0:T(128)S(1)} %copy-done.9, ...), custom_call_target="tpu_custom_call" | custom-call | tf_op jit(solution)/shard_map/pallas_call | solution.py:381
  68.1 2.5 %collective-permute-start.15 = (f32[16,144]{1,0:T(8,128)S(1)}, f32[16,144]{1,0:T(8,128)S(1)}, u32[]{:S(2)}, u32[]{:S(2)}) collective-permute-start(f32[16,144]{1,0:T(8,128)S(1)} %get-tuple-element.75.refs_19_), channel_id=1, source_target_pairs={{0,3},{1,2},{2,1},{3,0},{4,7},{5,6},{6,5},{7,4},{8,11},{9,10},{10,... | collective-permute-start | bytes 27656 | tf_op jit(solution)/shard_map/ppermute | solution.py:375
  70.6 10.4 %collective-permute-start.14 = (f32[16,144]{1,0:T(8,128)S(1)}, f32[16,144]{1,0:T(8,128)S(1)}, u32[]{:S(2)}, u32[]{:S(2)}) collective-permute-start(f32[16,144]{1,0:T(8,128)S(1)} %get-tuple-element.75.refs_19_), channel_id=1, source_target_pairs={{0,2},{1,3},{2,0},{3,1},{4,6},{5,7},{6,4},{7,5},{8,10},{9,11},{10,... | collective-permute-start | bytes 27656 | tf_op jit(solution)/shard_map/ppermute | solution.py:375
  81.0 0.1 collective-permute-start.13
  81.0 4.4 %shard_map.89 = (f32[128,1024]{1,0:T(8,128)S(1)}, f32[16,1024]{1,0:T(8,128)S(1)}) custom-call(s32[2]{0:T(128)S(1)} %copy-done.7, bf16[128,2048]{1,0:T(8,128)(2,1)S(1)} %copy-done.3, bf16[128,2048]{1,0:T(8,128)(2,1)S(1)} %copy-done.4, bf16[2,16,2048]{2,1,0:T(8,128)(2,1)S(1)} %copy-done.6, f32[128,128]{1,0:T(8,128)S(1)} %get-tuple-element.64.refs_4_, ...), custom_call_target="tpu_custom_call" | custom-call | tf_op jit(solution)/shard_map/pallas_call | solution.py:381
  85.5 0.0 collective-permute-done.15.refs_22_
  85.5 0.0 collective-permute-done.14.refs_21_
  85.5 0.0 collective-permute-done.13.refs_20_
  85.6 0.1 pad_maximum_fusion.refs_23_
  85.6 0.0 collective-permute-start.22
  85.7 1.5 %collective-permute-start.21 = (f32[16,64]{1,0:T(8,128)S(1)}, f32[16,64]{1,0:T(8,128)S(1)}, u32[]{:S(2)}, u32[]{:S(2)}) collective-permute-start(f32[16,64]{1,0:T(8,128)S(1)} %pad_maximum_fusion.refs_23_), channel_id=1, source_target_pairs={{0,24},{4,28},{8,16},{12,20},{16,8},{20,12},{24,0},{28,4},{1,25},{... | collective-permute-start | bytes 12296 | tf_op jit(solution)/shard_map/ppermute | solution.py:375
  87.2 2.3 %collective-permute-start.20 = (f32[16,64]{1,0:T(8,128)S(1)}, f32[16,64]{1,0:T(8,128)S(1)}, u32[]{:S(2)}, u32[]{:S(2)}) collective-permute-start(f32[16,64]{1,0:T(8,128)S(1)} %pad_maximum_fusion.refs_23_), channel_id=1, source_target_pairs={{0,20},{4,16},{8,28},{12,24},{16,4},{20,0},{24,12},{28,8},{1,21},{... | collective-permute-start | bytes 12296 | tf_op jit(solution)/shard_map/ppermute | solution.py:375
  89.5 0.5 collective-permute-start.19
  90.0 0.1 collective-permute-start.18
  90.2 0.0 collective-permute-done.22.refs_30_
  90.2 1.1 %collective-permute-start.17 = (f32[16,64]{1,0:T(8,128)S(1)}, f32[16,64]{1,0:T(8,128)S(1)}, u32[]{:S(2)}, u32[]{:S(2)}) collective-permute-start(f32[16,64]{1,0:T(8,128)S(1)} %pad_maximum_fusion.refs_23_), channel_id=1, source_target_pairs={{0,8},{4,12},{8,0},{12,4},{16,24},{20,28},{24,16},{28,20},{1,9},{5... | collective-permute-start | bytes 12296 | tf_op jit(solution)/shard_map/ppermute | solution.py:375
  91.3 0.0 collective-permute-done.21.refs_29_
  91.3 0.6 collective-permute-start.16
  91.9 6.4 %shard_map.90 = (bf16[512,1024]{1,0:T(8,128)(2,1)}, f32[512,1024]{1,0:T(8,128)S(1)}, f32[512,1024]{1,0:T(8,128)S(1)}) custom-call(s32[8]{0:T(128)S(1)} %copy-done.8, s32[8]{0:T(128)S(1)} %copy-done.9, bf16[512,1024]{1,0:T(8,128)(2,1)S(1)} %copy-done, bf16[512,1024]{1,0:T(8,128)(2,1)S(1)} %copy-done.1, bf16[512,1024]{1,0:T(8,128)(2,1)S(1)} %copy-done.2, ...), custom_call_target="tpu_custom_call" | custom-call | tf_op jit(solution)/shard_map/pallas_call | solution.py:381
  98.3 0.0 collective-permute-done.20.refs_28_
  98.3 0.0 collective-permute-done.19.refs_27_
  98.3 0.0 collective-permute-done.18.refs_26_
  98.3 0.0 collective-permute-done.17.refs_25_
  98.3 0.0 collective-permute-done.16.refs_24_
  98.3 7.7 %shard_map.91 = (bf16[512,1024]{1,0:T(8,128)(2,1)}, bf16[512,1024]{1,0:T(8,128)(2,1)}) custom-call(s32[2]{0:T(128)S(1)} %copy-done.7, s32[8]{0:T(128)S(1)} %copy-done.8, s32[8]{0:T(128)S(1)} %copy-done.9, bf16[128,2048]{1,0:T(8,128)(2,1)S(1)} %copy-done.3, bf16[128,2048]{1,0:T(8,128)(2,1)S(1)} %copy-done.4, bf16[2,16,2048]{2,1,0:T(8,128)(2,1)S(1)} %copy-done.6, ...), custom_call_target="tpu_custom_call" | custom-call | tf_op jit(solution)/shard_map/pallas_call | solution.py:381
  (21 shorter events, 0.0 us)
Async XLA Ops:
  0.6 11.1 %copy-start.2 = (bf16[512,1024]{1,0:T(8,128)(2,1)S(1)}, bf16[512,1024]{1,0:T(8,128)(2,1)}, u32[]{:S(2)}) copy-start(bf16[512,1024]{1,0:T(8,128)(2,1)} %g.5) | copy-start | bytes 3145732
  0.6 11.1 %copy-start.1 = (bf16[512,1024]{1,0:T(8,128)(2,1)S(1)}, bf16[512,1024]{1,0:T(8,128)(2,1)}, u32[]{:S(2)}) copy-start(bf16[512,1024]{1,0:T(8,128)(2,1)} %k.5) | copy-start | bytes 3145732
  0.7 11.1 %copy-start = (bf16[512,1024]{1,0:T(8,128)(2,1)S(1)}, bf16[512,1024]{1,0:T(8,128)(2,1)}, u32[]{:S(2)}) copy-start(bf16[512,1024]{1,0:T(8,128)(2,1)} %q.5) | copy-start | bytes 3145732
  1.3 21.1 %copy-start.7 = (s32[2]{0:T(128)S(1)}, s32[2]{0:T(128)}, u32[]{:S(2)}) copy-start(s32[2]{0:T(128)} %pad_add_fusion.place.refs_0_) | copy-start | bytes 28
  1.3 61.8 %copy-start.8 = (s32[8]{0:T(128)S(1)}, s32[8]{0:T(128)}, u32[]{:S(2)}) copy-start(s32[8]{0:T(128)} %refs_1_.3) | copy-start | bytes 100
  1.3 61.9 %copy-start.9 = (s32[8]{0:T(128)S(1)}, s32[8]{0:T(128)}, u32[]{:S(2)}) copy-start(s32[8]{0:T(128)} %refs_2_.3) | copy-start | bytes 100
  5.9 57.3 %copy-start.3 = (bf16[128,2048]{1,0:T(8,128)(2,1)S(1)}, bf16[128,2048]{1,0:T(8,128)(2,1)}, u32[]{:S(2)}) copy-start(bf16[128,2048]{1,0:T(8,128)(2,1)} %get-tuple-element.44.refs_3_.refs_1_) | copy-start | bytes 1572868
  5.9 57.3 %copy-start.4 = (bf16[128,2048]{1,0:T(8,128)(2,1)S(1)}, bf16[128,2048]{1,0:T(8,128)(2,1)}, u32[]{:S(2)}) copy-start(bf16[128,2048]{1,0:T(8,128)(2,1)} %get-tuple-element.45.refs_4_.refs_2_) | copy-start | bytes 1572868
  5.9 11.7 %collective-permute-start.2 = (bf16[2,16,2048]{2,1,0:T(8,128)(2,1)}, bf16[2,16,2048]{2,1,0:T(8,128)(2,1)S(1)}, u32[]{:S(2)}, u32[]{:S(2)}) collective-permute-start(bf16[2,16,2048]{2,1,0:T(8,128)(2,1)} %get-tuple-element.53.refs_1_.refs_5_.refs_3_), channel_id=1, source_target_pairs={{0,3},{1,2},{2,1},{3,0},{4,7},{5,6},{6,5},{7,4},{8,11},{9,10},{10,... | collective-permute-start | bytes 393224 | tf_op jit(solution)/shard_map/ppermute | solution.py:375
  11.1 11.3 %collective-permute-start.1 = (bf16[2,16,2048]{2,1,0:T(8,128)(2,1)}, bf16[2,16,2048]{2,1,0:T(8,128)(2,1)S(1)}, u32[]{:S(2)}, u32[]{:S(2)}) collective-permute-start(bf16[2,16,2048]{2,1,0:T(8,128)(2,1)} %get-tuple-element.53.refs_1_.refs_5_.refs_3_), channel_id=1, source_target_pairs={{0,2},{1,3},{2,0},{3,1},{4,6},{5,7},{6,4},{7,5},{8,10},{9,11},{10,... | collective-permute-start | bytes 393224 | tf_op jit(solution)/shard_map/ppermute | solution.py:375
  11.1 11.3 %collective-permute-start = (bf16[2,16,2048]{2,1,0:T(8,128)(2,1)}, bf16[2,16,2048]{2,1,0:T(8,128)(2,1)S(1)}, u32[]{:S(2)}, u32[]{:S(2)}) collective-permute-start(bf16[2,16,2048]{2,1,0:T(8,128)(2,1)} %get-tuple-element.53.refs_1_.refs_5_.refs_3_), channel_id=1, source_target_pairs={{0,1},{1,0},{2,3},{3,2},{4,5},{5,4},{6,7},{7,6},{8,9},{9,8},{10,11... | collective-permute-start | bytes 393224 | tf_op jit(solution)/shard_map/ppermute | solution.py:375
  11.7 1.2 %copy-start.5 = (bf16[512,1024]{1,0:T(8,128)(2,1)S(1)}, bf16[512,1024]{1,0:T(8,128)(2,1)}, u32[]{:S(2)}) copy-start(bf16[512,1024]{1,0:T(8,128)(2,1)} %v.3) | copy-start | bytes 3145732
  13.0 9.4 %copy-start.6 = (bf16[2,16,2048]{2,1,0:T(8,128)(2,1)S(1)}, bf16[2,16,2048]{2,1,0:T(8,128)(2,1)}, u32[]{:S(2)}) copy-start(bf16[2,16,2048]{2,1,0:T(8,128)(2,1)} %get-tuple-element.53.refs_1_.refs_5_.refs_3_) | copy-start | bytes 393220
  13.0 11.9 %copy-start.12 = (bf16[128,2048]{1,0:T(8,128)(2,1)S(1)}, bf16[128,2048]{1,0:T(8,128)(2,1)}, u32[]{:S(2)}) copy-start(bf16[128,2048]{1,0:T(8,128)(2,1)} %get-tuple-element.50) | copy-start | bytes 1572868
  13.0 11.9 %copy-start.11 = (bf16[128,2048]{1,0:T(8,128)(2,1)S(1)}, bf16[128,2048]{1,0:T(8,128)(2,1)}, u32[]{:S(2)}) copy-start(bf16[128,2048]{1,0:T(8,128)(2,1)} %get-tuple-element.51) | copy-start | bytes 1572868
  13.0 14.9 %copy-start.10 = (bf16[128,2048]{1,0:T(8,128)(2,1)S(1)}, bf16[128,2048]{1,0:T(8,128)(2,1)}, u32[]{:S(2)}) copy-start(bf16[128,2048]{1,0:T(8,128)(2,1)} %get-tuple-element.52) | copy-start | bytes 1572868
  23.2 6.0 %collective-permute-start.6 = (bf16[64,2048]{1,0:T(8,128)(2,1)S(1)}, bf16[64,2048]{1,0:T(8,128)(2,1)S(1)}, u32[]{:S(2)}, u32[]{:S(2)}) collective-permute-start(bf16[64,2048]{1,0:T(8,128)(2,1)S(1)} %get-tuple-element.58), channel_id=1, source_target_pairs={{0,4},{4,0},{8,12},{12,8},{16,20},{20,16},{24,28},{28,24},{1,5},{5... | collective-permute-start | bytes 786440 | tf_op jit(solution)/shard_map/ppermute | solution.py:375
  23.3 8.7 %collective-permute-start.7 = (bf16[64,2048]{1,0:T(8,128)(2,1)S(1)}, bf16[64,2048]{1,0:T(8,128)(2,1)S(1)}, u32[]{:S(2)}, u32[]{:S(2)}) collective-permute-start(bf16[64,2048]{1,0:T(8,128)(2,1)S(1)} %get-tuple-element.59), channel_id=1, source_target_pairs={{0,8},{4,12},{8,0},{12,4},{16,24},{20,28},{24,16},{28,20},{1,9},{5... | collective-permute-start | bytes 786440 | tf_op jit(solution)/shard_map/ppermute | solution.py:375
  24.9 24.7 %collective-permute-start.3 = (bf16[128,2048]{1,0:T(8,128)(2,1)S(1)}, bf16[128,2048]{1,0:T(8,128)(2,1)S(1)}, u32[]{:S(2)}, u32[]{:S(2)}) collective-permute-start(bf16[128,2048]{1,0:T(8,128)(2,1)S(1)} %copy-done.12), channel_id=1, source_target_pairs={{0,1},{1,0},{2,3},{3,2},{4,5},{5,4},{6,7},{7,6},{8,9},{9,8},{10,11... | collective-permute-start | bytes 1572872 | tf_op jit(solution)/shard_map/ppermute | solution.py:375
  24.9 38.3 %collective-permute-start.4 = (bf16[128,2048]{1,0:T(8,128)(2,1)S(1)}, bf16[128,2048]{1,0:T(8,128)(2,1)S(1)}, u32[]{:S(2)}, u32[]{:S(2)}) collective-permute-start(bf16[128,2048]{1,0:T(8,128)(2,1)S(1)} %copy-done.11), channel_id=1, source_target_pairs={{0,2},{1,3},{2,0},{3,1},{4,6},{5,7},{6,4},{7,5},{8,10},{9,11},{10,... | collective-permute-start | bytes 1572872 | tf_op jit(solution)/shard_map/ppermute | solution.py:375
  27.9 35.3 %collective-permute-start.5 = (bf16[128,2048]{1,0:T(8,128)(2,1)S(1)}, bf16[128,2048]{1,0:T(8,128)(2,1)S(1)}, u32[]{:S(2)}, u32[]{:S(2)}) collective-permute-start(bf16[128,2048]{1,0:T(8,128)(2,1)S(1)} %copy-done.10), channel_id=1, source_target_pairs={{0,3},{1,2},{2,1},{3,0},{4,7},{5,6},{6,5},{7,4},{8,11},{9,10},{10,... | collective-permute-start | bytes 1572872 | tf_op jit(solution)/shard_map/ppermute | solution.py:375
  29.3 9.5 %collective-permute-start.11 = (bf16[64,2048]{1,0:T(8,128)(2,1)S(1)}, bf16[64,2048]{1,0:T(8,128)(2,1)S(1)}, u32[]{:S(2)}, u32[]{:S(2)}) collective-permute-start(bf16[64,2048]{1,0:T(8,128)(2,1)S(1)} %get-tuple-element.60), channel_id=1, source_target_pairs={{0,24},{4,28},{8,16},{12,20},{16,8},{20,12},{24,0},{28,4},{1,25},{... | collective-permute-start | bytes 786440 | tf_op jit(solution)/shard_map/ppermute | solution.py:375
  32.0 12.2 %collective-permute-start.9 = (bf16[64,2048]{1,0:T(8,128)(2,1)S(1)}, bf16[64,2048]{1,0:T(8,128)(2,1)S(1)}, u32[]{:S(2)}, u32[]{:S(2)}) collective-permute-start(bf16[64,2048]{1,0:T(8,128)(2,1)S(1)} %get-tuple-element.60), channel_id=1, source_target_pairs={{0,16},{4,20},{8,24},{12,28},{16,0},{20,4},{24,8},{28,12},{1,17},{... | collective-permute-start | bytes 786440 | tf_op jit(solution)/shard_map/ppermute | solution.py:375
  38.7 24.4 %collective-permute-start.8 = (bf16[64,2048]{1,0:T(8,128)(2,1)S(1)}, bf16[64,2048]{1,0:T(8,128)(2,1)S(1)}, u32[]{:S(2)}, u32[]{:S(2)}) collective-permute-start(bf16[64,2048]{1,0:T(8,128)(2,1)S(1)} %collective-permute-done.7.refs_13_), channel_id=1, source_target_pairs={{0,4},{4,0},{8,12},{12,8},{16,20},{20,16},{24,28},{28,24},{1,5},{5... | collective-permute-start | bytes 786440 | tf_op jit(solution)/shard_map/ppermute | solution.py:375
  44.2 18.9 %collective-permute-start.12 = (bf16[64,2048]{1,0:T(8,128)(2,1)S(1)}, bf16[64,2048]{1,0:T(8,128)(2,1)S(1)}, u32[]{:S(2)}, u32[]{:S(2)}) collective-permute-start(bf16[64,2048]{1,0:T(8,128)(2,1)S(1)} %collective-permute-done.11.refs_17_), channel_id=1, source_target_pairs={{0,4},{4,0},{8,12},{12,8},{16,20},{20,16},{24,28},{28,24},{1,5},{5... | collective-permute-start | bytes 786440 | tf_op jit(solution)/shard_map/ppermute | solution.py:375
  49.6 13.6 %collective-permute-start.10 = (bf16[64,2048]{1,0:T(8,128)(2,1)S(1)}, bf16[64,2048]{1,0:T(8,128)(2,1)S(1)}, u32[]{:S(2)}, u32[]{:S(2)}) collective-permute-start(bf16[64,2048]{1,0:T(8,128)(2,1)S(1)} %collective-permute-done.9.refs_15_), channel_id=1, source_target_pairs={{0,4},{4,0},{8,12},{12,8},{16,20},{20,16},{24,28},{28,24},{1,5},{5... | collective-permute-start | bytes 786440 | tf_op jit(solution)/shard_map/ppermute | solution.py:375
  68.1 17.4 %collective-permute-start.15 = (f32[16,144]{1,0:T(8,128)S(1)}, f32[16,144]{1,0:T(8,128)S(1)}, u32[]{:S(2)}, u32[]{:S(2)}) collective-permute-start(f32[16,144]{1,0:T(8,128)S(1)} %get-tuple-element.75.refs_19_), channel_id=1, source_target_pairs={{0,3},{1,2},{2,1},{3,0},{4,7},{5,6},{6,5},{7,4},{8,11},{9,10},{10,... | collective-permute-start | bytes 27656 | tf_op jit(solution)/shard_map/ppermute | solution.py:375
  70.6 14.9 %collective-permute-start.14 = (f32[16,144]{1,0:T(8,128)S(1)}, f32[16,144]{1,0:T(8,128)S(1)}, u32[]{:S(2)}, u32[]{:S(2)}) collective-permute-start(f32[16,144]{1,0:T(8,128)S(1)} %get-tuple-element.75.refs_19_), channel_id=1, source_target_pairs={{0,2},{1,3},{2,0},{3,1},{4,6},{5,7},{6,4},{7,5},{8,10},{9,11},{10,... | collective-permute-start | bytes 27656 | tf_op jit(solution)/shard_map/ppermute | solution.py:375
  81.0 4.5 %collective-permute-start.13 = (f32[16,144]{1,0:T(8,128)S(1)}, f32[16,144]{1,0:T(8,128)S(1)}, u32[]{:S(2)}, u32[]{:S(2)}) collective-permute-start(f32[16,144]{1,0:T(8,128)S(1)} %get-tuple-element.75.refs_19_), channel_id=1, source_target_pairs={{0,1},{1,0},{2,3},{3,2},{4,5},{5,4},{6,7},{7,6},{8,9},{9,8},{10,11... | collective-permute-start | bytes 27656 | tf_op jit(solution)/shard_map/ppermute | solution.py:375
  85.6 4.5 %collective-permute-start.22 = (f32[16,64]{1,0:T(8,128)S(1)}, f32[16,64]{1,0:T(8,128)S(1)}, u32[]{:S(2)}, u32[]{:S(2)}) collective-permute-start(f32[16,64]{1,0:T(8,128)S(1)} %pad_maximum_fusion.refs_23_), channel_id=1, source_target_pairs={{0,28},{4,24},{8,20},{12,16},{16,12},{20,8},{24,4},{28,0},{1,29},{... | collective-permute-start | bytes 12296 | tf_op jit(solution)/shard_map/ppermute | solution.py:375
  85.7 5.6 %collective-permute-start.21 = (f32[16,64]{1,0:T(8,128)S(1)}, f32[16,64]{1,0:T(8,128)S(1)}, u32[]{:S(2)}, u32[]{:S(2)}) collective-permute-start(f32[16,64]{1,0:T(8,128)S(1)} %pad_maximum_fusion.refs_23_), channel_id=1, source_target_pairs={{0,24},{4,28},{8,16},{12,20},{16,8},{20,12},{24,0},{28,4},{1,25},{... | collective-permute-start | bytes 12296 | tf_op jit(solution)/shard_map/ppermute | solution.py:375
  87.2 11.1 %collective-permute-start.20 = (f32[16,64]{1,0:T(8,128)S(1)}, f32[16,64]{1,0:T(8,128)S(1)}, u32[]{:S(2)}, u32[]{:S(2)}) collective-permute-start(f32[16,64]{1,0:T(8,128)S(1)} %pad_maximum_fusion.refs_23_), channel_id=1, source_target_pairs={{0,20},{4,16},{8,28},{12,24},{16,4},{20,0},{24,12},{28,8},{1,21},{... | collective-permute-start | bytes 12296 | tf_op jit(solution)/shard_map/ppermute | solution.py:375
  89.5 8.8 %collective-permute-start.19 = (f32[16,64]{1,0:T(8,128)S(1)}, f32[16,64]{1,0:T(8,128)S(1)}, u32[]{:S(2)}, u32[]{:S(2)}) collective-permute-start(f32[16,64]{1,0:T(8,128)S(1)} %pad_maximum_fusion.refs_23_), channel_id=1, source_target_pairs={{0,16},{4,20},{8,24},{12,28},{16,0},{20,4},{24,8},{28,12},{1,17},{... | collective-permute-start | bytes 12296 | tf_op jit(solution)/shard_map/ppermute | solution.py:375
  90.0 8.2 %collective-permute-start.18 = (f32[16,64]{1,0:T(8,128)S(1)}, f32[16,64]{1,0:T(8,128)S(1)}, u32[]{:S(2)}, u32[]{:S(2)}) collective-permute-start(f32[16,64]{1,0:T(8,128)S(1)} %pad_maximum_fusion.refs_23_), channel_id=1, source_target_pairs={{0,12},{4,8},{8,4},{12,0},{16,28},{20,24},{24,20},{28,16},{1,13},{... | collective-permute-start | bytes 12296 | tf_op jit(solution)/shard_map/ppermute | solution.py:375
  90.2 8.1 %collective-permute-start.17 = (f32[16,64]{1,0:T(8,128)S(1)}, f32[16,64]{1,0:T(8,128)S(1)}, u32[]{:S(2)}, u32[]{:S(2)}) collective-permute-start(f32[16,64]{1,0:T(8,128)S(1)} %pad_maximum_fusion.refs_23_), channel_id=1, source_target_pairs={{0,8},{4,12},{8,0},{12,4},{16,24},{20,28},{24,16},{28,20},{1,9},{5... | collective-permute-start | bytes 12296 | tf_op jit(solution)/shard_map/ppermute | solution.py:375
  91.3 7.0 %collective-permute-start.16 = (f32[16,64]{1,0:T(8,128)S(1)}, f32[16,64]{1,0:T(8,128)S(1)}, u32[]{:S(2)}, u32[]{:S(2)}) collective-permute-start(f32[16,64]{1,0:T(8,128)S(1)} %pad_maximum_fusion.refs_23_), channel_id=1, source_target_pairs={{0,4},{4,0},{8,12},{12,8},{16,20},{20,16},{24,28},{28,24},{1,5},{5... | collective-permute-start | bytes 12296 | tf_op jit(solution)/shard_map/ppermute | solution.py:375

commit v4 on v3

v4 whole, which is shorter than its diff:
```python
import functools

import jax
import jax.numpy as jnp
from jax import lax
from jax.experimental import pallas as pl
from jax.experimental.pallas import tpu as pltpu
from jax.sharding import PartitionSpec as P

F32 = jnp.float32
BF16 = jnp.bfloat16
LANES = 128
LOW = -1e30
MIB = 1024 * 1024
GROUP = 4
LIMIT = 22


def mm(a, b):
    return lax.dot_general(a, b, (((1,), (0,)), ((), ())), preferred_element_type=F32)


def mm_t(a, b):
    return lax.dot_general(a, b, (((1,), (1,)), ((), ())), preferred_element_type=F32)


def t_mm(a, b):
    return lax.dot_general(a, b, (((0,), (0,)), ((), ())), preferred_element_type=F32)


def exact(a, b):
    return lax.dot_general(
        a, b, (((1,), (0,)), ((), ())), preferred_element_type=F32, precision=lax.Precision.HIGHEST
    )


def iota(shape, axis):
    return lax.broadcasted_iota(jnp.int32, shape, axis)


def params(limit):
    return pltpu.CompilerParams(
        vmem_limit_bytes=limit * MIB, dimension_semantics=("arbitrary",)
    )


def smem():
    return pl.BlockSpec(memory_space=pltpu.SMEM)


def columns(rows, width):
    return pl.BlockSpec((rows, width), lambda h: (0, h))


def fixed(shape):
    return pl.BlockSpec(shape, lambda h: (0,) * len(shape))


def pick_lane(ref, head):
    block = ref[...]
    return jnp.sum(jnp.where(iota(block.shape, 1) == head, block, 0.0), axis=1, keepdims=True)


def put_lane(ref, rows, head, value):
    block = ref[rows, :]
    ref[rows, :] = jnp.where(iota(block.shape, 1) == head, value, block)


def select_kernel(mid_off, far_off, q, k, v, g, kv, qg, far, *pays):
    level = lax.axis_index("lvl")
    rows = q.shape[0]
    for at in range(GROUP):
        head = pl.program_id(0) * GROUP + at
        cut = slice(at * LANES, (at + 1) * LANES)
        wide = slice(2 * at * LANES, 2 * (at + 1) * LANES)
        whole = jnp.concatenate([k[:, cut], v[:, cut], q[:, cut], g[:, cut]], axis=1)

        def picked(count, offset):
            stride = rows // count
            table = iota((count, rows), 1) == iota((count, rows), 0) * stride + offset
            return mm(table.astype(BF16), whole).astype(BF16)

        mid = picked(kv.shape[0], mid_off[head])
        half = 2 * LANES
        kv[:, wide] = mid[:, :half]
        qg[:, wide] = mid[:, half:]
        picks = picked(far.shape[1], far_off[head])
        far[0, :, wide] = picks[:, :half]
        far[1, :, wide] = picks[:, half:]
    firsts, seconds = pays[: len(pays) // 2], pays[len(pays) // 2 :]
    for step, (first, second) in enumerate(zip(firsts, seconds), 1):
        upward = (level ^ step) > level

        @pl.when(upward & (pl.program_id(0) == 0))
        def _():
            first[...] = kv[...]

        @pl.when(upward & (pl.program_id(0) == 1))
        def _():
            second[...] = kv[...]

        @pl.when(jnp.logical_not(upward) & (pl.program_id(0) == 0))
        def _():
            second[...] = qg[...]

        @pl.when(jnp.logical_not(upward) & (pl.program_id(0) == 1))
        def _():
            first[...] = qg[...]


def near_kernel(scale, parts, group, q, k, v, g, logs, dots, soft_out, slope_out, base):
    logs[...] = jnp.zeros_like(logs)
    dots[...] = jnp.zeros_like(dots)
    size = q.shape[0] // parts
    for at in range(GROUP):
        cut = slice(at * LANES, (at + 1) * LANES)
        low, high = cuts(at)
        for part in range(parts):
            rows = slice(part * size, (part + 1) * size)
            width = (part + 1) * size
            scores = mm_t(q[rows, cut], k[:width, cut]) * scale
            grads = mm_t(g[rows, cut], v[:width, cut])
            seen = iota((size, width), 1) <= iota((size, width), 0) + part * size
            scores = jnp.where(seen, scores, LOW)
            peak = jnp.max(scores, axis=1, keepdims=True)
            weights = jnp.exp(scores - peak)
            total = jnp.sum(weights, axis=1, keepdims=True)
            soft = weights / total
            dot_part = jnp.sum(soft * grads, axis=1, keepdims=True)
            slopes = (soft * (grads - dot_part)).astype(BF16)
            soft = soft.astype(BF16)
            base[rows, low] = mm(slopes, k[:width, cut])
            base[rows, high] = mm(soft, k[:width, cut])
            soft_out[at, :width, rows] = soft.T
            slope_out[at, :width, rows] = slopes.T
            put_lane(logs, rows, group * GROUP + at, peak + jnp.log(total))
            put_lane(dots, rows, group * GROUP + at, dot_part)


def row_stats(scores, grads):
    peak = jnp.max(scores, axis=1, keepdims=True)
    weights = jnp.exp(scores - peak)
    total = jnp.sum(weights, axis=1, keepdims=True)
    return peak + jnp.log(total), jnp.sum(weights * grads, axis=1, keepdims=True) / total


def mid_places(count, total, level):
    col = iota((count, total), 1)
    other = ((col >> (count.bit_length() - 1)) ^ level) * count + (col & (count - 1))
    return other, level * count + iota((count, total), 0)


def far_places(count, total, levels, level, ring):
    col = iota((count, total), 1)
    bits, level_bits = count.bit_length() - 1, levels.bit_length() - 1
    slot, ring_slot = (col >> bits) & (levels - 1), col >> (bits + level_bits)
    other = ((ring_slot ^ ring) * levels + (slot ^ level)) * count + (col & (count - 1))
    return other, (ring * levels + level) * count + iota((count, total), 0)


def bias(seen):
    return jnp.where(seen, 0.0, LOW)


def stack(refs, cut):
    return jnp.concatenate([ref[:, cut] for ref in refs], axis=0)


def repeat_table(rows, count):
    return (iota((rows, count), 0) // (rows // count) == iota((rows, count), 1)).astype(F32)


def gather_table(rows, count):
    return (iota((count, rows), 1) // (rows // count) == iota((count, rows), 0)).astype(F32)


def lane_offsets(offsets, heads):
    lane = iota((1, LANES), 1)
    values = jnp.zeros((1, LANES), jnp.int32)
    for head in range(heads):
        values = jnp.where(lane == head, offsets[head], values)
    return values


def column_kernel(levels, bits, *refs):
    pieces = refs[:levels]
    col_kv, col_qg = refs[levels : 2 + levels]
    pays = refs[2 + levels :]
    ring = lax.axis_index("seq")
    col_kv[...] = jnp.concatenate([piece[0] for piece in pieces], axis=0)
    col_qg[...] = jnp.concatenate([piece[1] for piece in pieces], axis=0)
    for bit in range(bits):
        upward = ((ring >> bit) & 1) == 0

        @pl.when(upward)
        def _():
            pays[bit][...] = col_kv[...]

        @pl.when(jnp.logical_not(upward))
        def _():
            pays[bit][...] = col_qg[...]


def cuts(at):
    low = slice(2 * at * LANES, (2 * at + 1) * LANES)
    return low, slice((2 * at + 1) * LANES, (2 * at + 2) * LANES)


def column_stats(scores, grads):
    peak = jnp.max(scores, axis=0, keepdims=True)
    weights = jnp.exp(scores - peak)
    total = jnp.sum(weights, axis=0, keepdims=True)
    return peak + jnp.log(total), jnp.sum(weights * grads, axis=0, keepdims=True) / total


def level_stats_kernel(scale, levels, mids, fars, *refs):
    kv, qg, far_own = refs[:3]
    mid_in, far_in = refs[3 : 3 + mids], refs[3 + mids : 3 + mids + fars]
    mlog, mdot, flog, fdot = refs[3 + mids + fars :][:4]
    backs = refs[7 + mids + fars :]
    step = pl.program_id(0)
    ring, level = lax.axis_index("seq"), lax.axis_index("lvl")
    mid_count, far_count = kv.shape[0], far_own.shape[1]
    total = mid_count * levels
    every = slice(None)

    @pl.when(step == 0)
    def _():
        for ref in (mlog, mdot, flog, fdot):
            ref[...] = jnp.zeros_like(ref)
        other, own = mid_places(mid_count, total, level)
        hide = bias(other <= own)
        for at in range(GROUP):
            low, high = cuts(at)
            scores = mm_t(qg[:, low], stack((kv,) + mid_in, low)) * scale + hide
            grads = mm_t(qg[:, high], stack((kv,) + mid_in, high))
            log_part, dot_part = row_stats(scores, grads)
            put_lane(mlog, every, at, log_part)
            put_lane(mdot, every, at, dot_part)

    @pl.when(step == 1)
    def _():
        other, own = mid_places(mid_count, mid_count, level)
        hide = bias(other <= own)
        for at in range(GROUP):
            low, high = cuts(at)
            scores = mm_t(qg[:, low], kv[:, low]) * scale + hide
            log_part, dot_part = row_stats(scores, mm_t(qg[:, high], kv[:, high]))
            put_lane(mlog, every, GROUP + at, log_part)
            put_lane(mdot, every, GROUP + at, dot_part)
            scores = mm_t(kv[:, low], stack(mid_in, low)) * scale
            log_part, dot_part = column_stats(scores, mm_t(kv[:, high], stack(mid_in, high)))
            for slot, back in enumerate(backs):
                where = slice(slot * mid_count, (slot + 1) * mid_count)
                back[at : at + 1, :] = log_part[:, where]
                back[GROUP + at : GROUP + at + 1, :] = dot_part[:, where]

    other, own = far_places(far_count, total, levels, level, ring)
    hide = bias(other <= own)
    for at in range(GROUP):
        head = step * GROUP + at
        low, high = cuts(at)
        scores = mm_t(far_own[1, :, low], stack(far_in, low)) * scale + hide
        grads = mm_t(far_own[1, :, high], stack(far_in, high))
        log_part, dot_part = row_stats(scores, grads)
        put_lane(flog, every, head, log_part)
        put_lane(fdot, every, head, dot_part)


def merge_kernel(heads, mids, *refs):
    mid_off, far_off, logs_a, dots_a, logs_b, dots_b, mlog, mdot, flog, fdot = refs[:10]
    backs = refs[10 : 10 + mids]
    outs = refs[10 + mids :]
    factors, shifts, mid_factor, mid_shift, far_factor, far_shift, mid_log, mid_dot = outs[:8]
    level = lax.axis_index("lvl")
    rows, mid_count, far_count = logs_a.shape[0], mlog.shape[0], flog.shape[0]

    lane = iota((mid_count, LANES), 1)
    theirs = (lane >= GROUP) & (lane < 2 * GROUP)
    logs, dots = [mlog[...]], [mdot[...]]
    head_rows, tail_rows = GROUP, LANES - 2 * GROUP
    for slot, back in enumerate(backs, 1):
        lower = theirs & ((iota((mid_count, LANES), 0) * 0 + (slot ^ level)) < level)
        parts = []
        for first in (0, GROUP):
            block = [jnp.zeros((head_rows, mid_count), F32), back[first : first + GROUP, :]]
            block.append(jnp.zeros((tail_rows, mid_count), F32))
            parts.append(jnp.concatenate(block, axis=0).T)
        logs.append(jnp.where(lower, parts[0], LOW))
        dots.append(parts[1])
    peak = functools.reduce(jnp.maximum, logs)
    weights = [jnp.exp(part - peak) for part in logs]
    whole = functools.reduce(jnp.add, weights)
    mid_logs = peak + jnp.log(whole)
    mid_dots = functools.reduce(jnp.add, [w * d for w, d in zip(weights, dots)]) / whole

    row = iota((rows, LANES), 0)
    mid_here = (row & (rows // mid_count - 1)) == lane_offsets(mid_off, heads)
    far_here = (row & (rows // far_count - 1)) == lane_offsets(far_off, heads)
    mid_table, far_table = repeat_table(rows, mid_count), repeat_table(rows, far_count)
    near, near_dots = logs_a[...] + logs_b[...], dots_a[...] + dots_b[...]
    mid = jnp.where(mid_here, exact(mid_table, mid_logs), LOW)
    far = jnp.where(far_here, exact(far_table, flog[...]), LOW)
    peak = jnp.maximum(near, jnp.maximum(mid, far))
    near_part = jnp.exp(near - peak)
    mid, far = jnp.exp(mid - peak), jnp.exp(far - peak)
    whole = near_part + mid + far
    logs = peak + jnp.log(whole)
    dots = (
        near_part * near_dots
        + mid * exact(mid_table, mid_dots)
        + far * exact(far_table, fdot[...])
    ) / whole
    factors[...] = jnp.exp(near - logs)
    shifts[...] = dots - near_dots
    for here, count, sent in ((mid_here, mid_count, outs[8]), (far_here, far_count, outs[9])):
        table = gather_table(rows, count)
        log_rows = exact(table, jnp.where(here, logs, 0.0))
        dot_rows = exact(table, jnp.where(here, dots, 0.0))
        sent[:heads, :] = log_rows.T[:heads, :]
        sent[heads:, :] = dot_rows.T[:heads, :]
        if count == mid_count:
            mid_log[...], mid_dot[...] = log_rows, dot_rows
            mid_factor[...] = jnp.exp(mid_logs - log_rows)
            mid_shift[...] = dot_rows - mid_dots
        else:
            far_factor[...] = jnp.exp(flog[...] - log_rows)
            far_shift[...] = dot_rows - fdot[...]


def row_side(scale, queries, cots, keys, vals, hide, logs, dots):
    scores = mm_t(queries, keys) * scale + hide
    soft = jnp.exp(scores - logs)
    slopes = soft * (mm_t(cots, vals) - dots)
    return soft.astype(BF16), slopes.astype(BF16)


def mid_queries(scale, levels, level, kv, qg, mid_in, mid_log, mid_dot, at, head):
    other, own = mid_places(kv.shape[0], kv.shape[0] * levels, level)
    low, high = cuts(at)
    keys, vals = stack((kv,) + mid_in, low), stack((kv,) + mid_in, high)
    logs, dots = pick_lane(mid_log, head), pick_lane(mid_dot, head)
    hide = bias(other <= own)
    _, slopes = row_side(scale, qg[:, low], qg[:, high], keys, vals, hide, logs, dots)
    return mm(slopes, keys)


def key_side(scale, keys, vals, queries, cots, hide, stats, head, heads):
    logs, dots = stats[pl.ds(head, 1), :], stats[pl.ds(head + heads, 1), :]
    soft, slopes = row_side(scale, keys, vals, queries, cots, hide, logs, dots)
    return jnp.concatenate([mm(slopes, queries), mm(soft, cots)], axis=1)


def mid_keys(scale, levels, level, kv, qg, mid_in, stats, at, head, heads):
    other, own = mid_places(kv.shape[0], kv.shape[0] * levels, level)
    low, high = cuts(at)
    queries, cots = stack((qg,) + mid_in, low), stack((qg,) + mid_in, high)
    return key_side(
        scale, kv[:, low], kv[:, high], queries, cots, bias(other >= own), stats, head, heads
    )


def level_base_kernel(scale, levels, mids, fars, *refs):
    kv, qg, far_own, mlog, mdot, flog, fdot = refs[:7]
    mid_in, far_in = refs[7 : 7 + mids], refs[7 + mids : 7 + mids + fars]
    mid_base, far_base = refs[7 + mids + fars :]
    step = pl.program_id(0)
    ring, level = lax.axis_index("seq"), lax.axis_index("lvl")
    far_count = far_own.shape[1]

    @pl.when(step == 0)
    def _():
        other, own = mid_places(kv.shape[0], kv.shape[0] * levels, level)
        hide = bias(other <= own)
        for at in range(GROUP):
            low, high = cuts(at)
            keys, vals = stack((kv,) + mid_in, low), stack((kv,) + mid_in, high)
            logs, dots = pick_lane(mlog, at), pick_lane(mdot, at)
            soft, slopes = row_side(scale, qg[:, low], qg[:, high], keys, vals, hide, logs, dots)
            mid_base[:, low] = mm(slopes, keys)
            mid_base[:, high] = mm(soft, keys)

    other, own = far_places(far_count, kv.shape[0] * levels, levels, level, ring)
    hide = bias(other <= own)
    for at in range(GROUP):
        head = step * GROUP + at
        low, high = cuts(at)
        keys, vals = stack(far_in, low), stack(far_in, high)
        logs, dots = pick_lane(flog, head), pick_lane(fdot, head)
        soft, slopes = row_side(
            scale, far_own[1, :, low], far_own[1, :, high], keys, vals, hide, logs, dots
        )
        far_base[:, low] = mm(slopes, keys)
        far_base[:, high] = mm(soft, keys)


def spread(rows, offsets, pieces):
    tables = []
    for offset, piece in zip(offsets, pieces):
        count = piece.shape[0]
        at = iota((rows, count), 0) - iota((rows, count), 1) * (rows // count)
        tables.append((at == offset).astype(BF16))
    table = tables[0] if len(tables) == 1 else jnp.concatenate(tables, axis=1)
    whole = pieces[0] if len(pieces) == 1 else jnp.concatenate(pieces, axis=0)
    return mm(table, whole.astype(BF16))


def rescaled(base, at, factors, shifts, head):
    low, high = cuts(at)
    return pick_lane(factors, head) * (base[:, low] - pick_lane(shifts, head) * base[:, high])


def near_grads_kernel(parts, group, mid_off, far_off, q, g, soft_in, slope_in, base, *refs):
    factors, shifts, mid_factor, mid_shift, far_factor, far_shift = refs[:6]
    mid_base, far_base, out_q, out_k, out_v = refs[6:]
    rows = q.shape[0]
    size = rows // parts
    for at in range(GROUP):
        head = group * GROUP + at
        cut = slice(at * LANES, (at + 1) * LANES)
        low, high = cuts(at)
        factor, shift = pick_lane(factors, head), pick_lane(shifts, head)
        far = rescaled(far_base, at, far_factor, far_shift, head)
        offsets, pieces = [far_off[head]], [far]
        if group == 0:
            offsets.insert(0, mid_off[head])
            pieces.insert(0, rescaled(mid_base, at, mid_factor, mid_shift, head))
        near = factor * (base[:, low] - shift * base[:, high])
        out_q[:, cut] = near + spread(rows, offsets, pieces)
        queries = factor * q[:, cut].astype(F32)
        shifted = (shift * queries).astype(BF16)
        queries = queries.astype(BF16)
        both = jnp.concatenate([(factor * g[:, cut].astype(F32)).astype(BF16), shifted], axis=1)
        for part in range(parts):
            keys = slice(part * size, (part + 1) * size)
            first = part * size
            value = mm(soft_in[at, keys, first:], both[first:])
            out_v[keys, cut] = value[:, :LANES]
            out_k[keys, cut] = mm(slope_in[at, keys, first:], queries[first:]) - value[:, LANES:]


def queries_kernel(scale, levels, mids, *refs):
    mid_off, kv, qg, dq_a, dq_b, mid_log, mid_dot = refs[:7]
    mid_in, out_q = refs[7 : 7 + mids], refs[7 + mids]
    level = lax.axis_index("lvl")
    rows = out_q.shape[0]

    @pl.when(pl.program_id(0) == 0)
    def _():
        out_q[...] = (dq_a[...] * scale).astype(BF16)

    @pl.when(pl.program_id(0) == 1)
    def _():
        for at in range(GROUP):
            head = GROUP + at
            cut = slice(at * LANES, (at + 1) * LANES)
            part = mid_queries(scale, levels, level, kv, qg, mid_in, mid_log, mid_dot, at, head)
            whole = dq_b[:, cut] + spread(rows, [mid_off[head]], [part])
            out_q[:, cut] = (whole * scale).astype(BF16)


def keys_kernel(scale, heads, levels, mids, fars, *refs):
    mid_off, far_off, kv, qg, far_own, dk_a, dv_a, dk_b, dv_b = refs[:9]
    first_in, second_in = refs[9 : 9 + mids], refs[9 + mids : 9 + 2 * mids]
    far_in = refs[9 + 2 * mids : 9 + 2 * mids + fars]
    stats = refs[9 + 2 * mids + fars : 10 + 3 * mids + fars]
    out_k, out_v, mid_rows, far_rows = refs[10 + 3 * mids + fars :]
    step = pl.program_id(0)
    ring, level = lax.axis_index("seq"), lax.axis_index("lvl")
    rows = out_k.shape[0]
    mid_count, far_count = kv.shape[0], far_own.shape[1]

    @pl.when(step == 0)
    def _():
        mid_rows[...] = jnp.concatenate([ref[:, :mid_count] for ref in stats], axis=1)
        for slot in range(fars):
            source = mid_count + (slot // 2 + slot % 2 * (fars // 2)) * far_count
            for low, ref in enumerate(stats):
                place = (slot * levels + low) * far_count
                far_rows[:, place : place + far_count] = ref[:, source : source + far_count]

    other, own = far_places(far_count, mid_count * levels, levels, level, ring)
    hide = bias(other >= own)

    def finish(group, mid_in, dk, dv):
        for at in range(GROUP):
            head = group * GROUP + at
            cut = slice(at * LANES, (at + 1) * LANES)
            low, high = cuts(at)
            mid = mid_keys(scale, levels, level, kv, qg, mid_in, mid_rows, at, head, heads)
            queries, cots = stack(far_in, low), stack(far_in, high)
            keys, vals = far_own[0, :, low], far_own[0, :, high]
            far = key_side(scale, keys, vals, queries, cots, hide, far_rows, head, heads)
            whole = spread(rows, [mid_off[head], far_off[head]], [mid, far])
            out_k[:, cut] = ((dk[:, cut] + whole[:, :LANES]) * scale).astype(BF16)
            out_v[:, cut] = (dv[:, cut] + whole[:, LANES:]).astype(BF16)

    @pl.when(step == 0)
    def _():
        finish(0, second_in, dk_a, dv_a)

    @pl.when(step == 1)
    def _():
        finish(1, first_in, dk_b, dv_b)


def pack_kernel(*refs):
    out, first = refs[-1], 0
    for ref in refs[:-1]:
        out[:, first : first + ref.shape[1]] = ref[...]
        first += ref.shape[1]


def pack(pieces):
    width = sum(piece.shape[1] for piece in pieces)
    out = jax.ShapeDtypeStruct((pieces[0].shape[0], width), F32)
    ins = [(fixed(piece.shape), piece) for piece in pieces]
    return call(pack_kernel, 1, ins, [(fixed(out.shape), out)], [])[0]


def swap(array, axis, size, step):
    return lax.ppermute(array, axis, [(i, i ^ step) for i in range(size)])


def call(kernel, steps, ins, outs, scratch, limit=LIMIT):
    specs, arrays = zip(*ins)
    out_specs, out_shapes = zip(*outs)
    return pl.pallas_call(
        kernel,
        grid=(steps,),
        in_specs=list(specs),
        out_specs=list(out_specs),
        out_shape=list(out_shapes),
        scratch_shapes=scratch,
        compiler_params=params(limit),
        cost_estimate=pl.CostEstimate(flops=0, bytes_accessed=0, transcendentals=0),
    )(*arrays)


def local(queries, keys, values, grad_out, mid_offset, far_offset):
    rows, flat = queries.shape
    heads = mid_offset.shape[0]
    width = flat // heads
    scale = width ** (-0.5)
    levels, rings = lax.axis_size("lvl"), lax.axis_size("seq")
    mid_count, far_count = rows // levels, rows // (levels * rings)
    block = far_count * levels
    shape = jax.ShapeDtypeStruct
    parts = 2
    steps = heads // GROUP
    tile = columns(rows, GROUP * width)
    mid_spec = columns(mid_count, GROUP * 2 * width)
    far_spec = pl.BlockSpec((2, far_count, GROUP * 2 * width), lambda h: (0, 0, h))
    sources = [(tile, queries), (tile, keys), (tile, values), (tile, grad_out)]
    scalars = [(smem(), mid_offset), (smem(), far_offset)]
    mid_shape = shape((mid_count, 2 * flat), BF16)

    half_shape, half_spec = shape((mid_count, flat), BF16), fixed((mid_count, flat))
    mids = levels - 1

    kv, qg, far, *pays = call(
        select_kernel,
        steps,
        scalars + [(spec, pltpu.with_memory_space_constraint(x, pltpu.HBM)) for spec, x in sources],
        [(mid_spec, mid_shape)] * 2
        + [(far_spec, shape((2, far_count, 2 * flat), BF16))]
        + [(half_spec, half_shape)] * (2 * mids),
        [],
    )
    far_level = [far] + [swap(far, "lvl", levels, step) for step in range(1, levels)]
    first_in = [swap(pays[step - 1], "lvl", levels, step) for step in range(1, levels)]

    stat, stat_spec = shape((rows, LANES), F32), fixed((rows, LANES))
    half = shape((rows, flat // 2), F32)
    square = shape((GROUP, rows, rows), BF16)

    def group_tile(group):
        return pl.BlockSpec((rows, GROUP * width), lambda h: (0, group))

    def group_sources(group, arrays):
        return [(group_tile(group), array) for array in arrays]

    def whole(array):
        return (fixed(array.shape), array)

    def result(*dims):
        return (fixed(dims), shape(dims, F32))

    def near_call(group, arrays):
        return call(
            functools.partial(near_kernel, scale, parts, group),
            1,
            group_sources(group, arrays),
            [(stat_spec, stat)] * 2
            + [(fixed(square.shape), square)] * 2
            + [result(rows, flat)],
            [],
        )

    inputs = (queries, keys, values, grad_out)
    near_a = near_call(0, inputs)
    far_level, near_a = lax.optimization_barrier((far_level, near_a))
    ring_bits = rings.bit_length() - 1
    col_shape = shape((block, 2 * flat), BF16)
    col_kv, col_qg, *ring_pays = call(
        functools.partial(column_kernel, levels, ring_bits),
        1,
        [(fixed(piece.shape), piece) for piece in far_level],
        [(fixed(col_shape.shape), col_shape)] * (2 + ring_bits),
        [],
    )
    far_ring = [None] * rings
    for step in range(2, rings, 2):
        far_ring[step] = swap(ring_pays[step.bit_length() - 1], "seq", rings, step)
    inputs, col_kv = lax.optimization_barrier((inputs, col_kv))
    near_b = near_call(1, inputs)
    far_ring[2::2], near_b = lax.optimization_barrier((far_ring[2::2], near_b))
    far_ring[1] = swap(ring_pays[0], "seq", rings, 1)
    for step in range(3, rings, 2):
        far_ring[step] = swap(far_ring[step - 1], "seq", rings, 1)

    col_spec = columns(block, GROUP * 2 * width)
    first_list = [(half_spec, piece) for piece in first_in]
    far_rest = [(col_spec, piece) for piece in far_ring[1:]]
    far_kv, far_qg = [(col_spec, col_kv)] + far_rest, [(col_spec, col_qg)] + far_rest
    mid_own = [(mid_spec, kv), (mid_spec, qg)]
    own = mid_own + [(far_spec, far)]
    mid_stat, far_stat = result(mid_count, LANES), result(far_count, LANES)
    level_stats = call(
        functools.partial(level_stats_kernel, scale, levels, mids, rings),
        steps,
        own + first_list + far_kv,
        [mid_stat] * 2 + [far_stat] * 2 + [result(2 * GROUP, mid_count)] * mids,
        [],
    )
    backs = [swap(level_stats[3 + step], "lvl", levels, step) for step in range(1, levels)]
    level_stats = level_stats[:4]
    later, backs = lax.optimization_barrier((pays[mids + 1 :], backs))
    second = [pays[mids]] + list(later)
    second[0], first_in[-1] = lax.optimization_barrier((second[0], first_in[-1]))
    second_in = [swap(second[step - 1], "lvl", levels, step) for step in range(1, levels)]
    second_list = [(half_spec, piece) for piece in second_in]
    mid_base, far_base = call(
        functools.partial(level_base_kernel, scale, levels, mids, rings),
        steps,
        own + [whole(array) for array in level_stats] + first_list + far_kv,
        [
            (fixed((mid_count, flat)), shape((mid_count, flat), F32)),
            (columns(far_count, GROUP * 2 * width), shape((far_count, 2 * flat), F32)),
        ],
        [],
    )
    backs, mid_base = lax.optimization_barrier((backs, mid_base))
    merged = call(
        functools.partial(merge_kernel, heads, mids),
        1,
        scalars + [whole(array) for array in [*near_a[:2], *near_b[:2], *level_stats, *backs]],
        [(stat_spec, stat)] * 2
        + [mid_stat] * 2
        + [far_stat] * 2
        + [mid_stat] * 2
        + [result(2 * heads, mid_count), result(2 * heads, far_count)],
        [],
    )
    mid_log, mid_dot, mid_sent, far_sent = merged[6:]
    near_sent = [far_sent] + [swap(far_sent, "seq", rings, step) for step in range(2, rings, 2)]

    def near_grads(group, near):
        far_spec = pl.BlockSpec((far_count, GROUP * 2 * width), lambda h: (0, group))
        return call(
            functools.partial(near_grads_kernel, parts, group),
            1,
            scalars
            + group_sources(group, (queries, grad_out))
            + [whole(array) for array in near[2:]]
            + [whole(array) for array in merged[:6]]
            + [whole(mid_base), (far_spec, far_base)],
            [result(rows, flat // 2)] * 3,
            [],
        )

    grads_a = near_grads(0, near_a)
    near_sent, grads_a = lax.optimization_barrier((near_sent, grads_a))
    near_sent = pack(near_sent)
    other_sent = swap(near_sent, "seq", rings, 1)
    grads_b = near_grads(1, near_b)
    other_sent, grads_b = lax.optimization_barrier((other_sent, grads_b))
    sent = pack([mid_sent, near_sent, other_sent])
    sent_in = [sent] + [swap(sent, "lvl", levels, step) for step in range(1, levels)]
    out = shape((rows, flat), BF16)
    group_mid = pl.BlockSpec((mid_count, GROUP * 2 * width), lambda h: (0, 1))
    (grad_query,) = call(
        functools.partial(queries_kernel, scale, levels, mids),
        steps,
        scalars[:1]
        + [(group_mid, kv), (group_mid, qg)]
        + [whole(array) for array in (grads_a[0], grads_b[0], mid_log, mid_dot)]
        + second_list,
        [(tile, out)],
        [],
    )
    sent_in, grad_query = lax.optimization_barrier((sent_in, grad_query))
    grad_key, grad_value = call(
        functools.partial(keys_kernel, scale, heads, levels, mids, rings),
        steps,
        scalars
        + own
        + [whole(array) for array in (*grads_a[1:], *grads_b[1:])]
        + first_list
        + second_list
        + far_qg
        + [whole(piece) for piece in sent_in],
        [(tile, out)] * 2,
        [pltpu.VMEM((2 * heads, rows), F32)] * 2,
    )
    return grad_query, grad_key, grad_value


def solution(mesh):
    row_spec = P(("seq", "lvl"), None)
    return jax.shard_map(
        local,
        mesh=mesh,
        in_specs=(row_spec, row_spec, row_spec, row_spec, P(), P()),
        out_specs=(row_spec, row_spec, row_spec),
        check_vma=False,
    )
```

time: 106 us -> 96.6 us (0.911)
  waiting for transfers between devices: 35.2 us -> 27.5 us
  starting transfers between devices: 34.5 us -> 28.9 us
  Pallas kernels: 33.5 us -> 37.6 us
    ppermute x23 -> x26, waiting for transfers between devices: 35.2 us -> 27.5 us  [swap(): return lax.ppermute(array, axis, [(i, i ^ step) for i in range(size)])]
    ppermute x23 -> x26, starting transfers between devices: 34.5 us -> 28.9 us  [swap(): return lax.ppermute(array, axis, [(i, i ^ step) for i in range(size)])]
    pallas_call x7 -> x13, Pallas kernels: 33.5 us -> 37.6 us  [call(): pl.pallas_call(kernel, grid=(steps,), in_specs=list(specs), out_specs=lis...]
  transfers between devices with their start and end apart: 23 -> 26, of which waited for: 6 -> 8; matrix products, arithmetic and copies ran while one was open for 0% -> 0% of each run, Pallas kernels for 15% -> 28%
where the time goes in v4:
time: 96.6 us; the launch traced here: 96.4 us
  Pallas kernels  37.6 us (39%)
  starting transfers between devices  28.9 us (30%)
  waiting for transfers between devices  27.5 us (28%)
  local copies, waits for them, and re-layouts  1.6 us (2%)
    pallas_call x13, Pallas kernels, call(): pl.pallas_call(kernel, grid=(steps,), in_specs=list(specs), out_specs=lis...  37.6 us
    ppermute x26, starting transfers between devices, swap(): return lax.ppermute(array, axis, [(i, i ^ step) for i in range(size)])  28.9 us
    ppermute x26, waiting for transfers between devices, swap(): return lax.ppermute(array, axis, [(i, i ^ step) for i in range(size)])  27.5 us
  transfers between devices with their start and end apart: 26, of which 8 were waited for; matrix products, arithmetic and copies ran while one was open for 0% of the time, Pallas kernels for 28%

profile of v4, /device:TPU:0, one launch (start us, length us, event | category | flops | bytes accessed | tf_op | source)
XLA Modules:
  0.0 96.4 jit_solution(843386300828973189)
XLA Ops:
  0.7 0.0 copy-start.4
  0.7 0.8 copy-done.4
  1.5 0.8 copy-done.6
  2.3 3.5 %shard_map.85 = (bf16[128,2048]{1,0:T(8,128)(2,1)S(1)}, bf16[128,2048]{1,0:T(8,128)(2,1)S(1)}, bf16[2,16,2048]{2,1,0:T(8,128)(2,1)S(1)}, bf16[128,1024]{1,0:T(8,...) custom-call(s32[8]{0:T(128)S(1)} %copy-done.4, ...), custom_call_target="tpu_custom_call" | custom-call | tf_op jit(solution)/shard_map/pallas_call | solution.py:528
  5.8 5.1 %collective-permute-start.2 = (bf16[2,16,2048]{2,1,0:T(8,128)(2,1)S(1)}, bf16[2,16,2048]{2,1,0:T(8,128)(2,1)S(1)}, u32[]{:S(2)}, u32[]{:S(2)}) collective-permute-start(bf16[2,16,2048]{2,1,0:T(8,128)(2,1)S(1)} %get-tuple-element.110.refs_0_.refs_2_.refs_4_), channel_id=1, source_target_pairs={{0,3},{1,2},{2,1},{3,0},{4,7},{5,6},{6,5},{7,4},{8,11},{9,10},{10,... | collective-permute-start | bytes 393224 | tf_op jit(solution)/shard_map/ppermute | solution.py:522
  10.9 0.0 collective-permute-start.1
  10.9 0.6 collective-permute-start
  11.5 5.0 %shard_map.86 = (f32[512,128]{1,0:T(8,128)S(1)}, f32[512,128]{1,0:T(8,128)S(1)}, bf16[4,512,512]{2,1,0:T(8,128)(2,1)S(1)}, bf16[4,512,512]{2,1,0:T(8,128)(2,1)S(1)}, f32[512,1024]{1,0:T(8,128)S(1)}) custom-call(bf16[512,1024]{1,0:T(8,128)(2,1)S(1)} %copy-done, bf16[512,1024]{1,0:T(8,128)(2,1)S(1)} %copy-done.2, bf16[512,1024]{1,0:T(8,128)(2,1)S(1)} %copy-done.3, ...), custom_call_target="tpu_custom_call" | custom-call | tf_op jit(solution)/shard_map/pallas_call | solution.py:528
  16.5 0.0 collective-permute-done.2.refs_3_
  16.5 5.4 %collective-permute-done.1.refs_2_ = bf16[2,16,2048]{2,1,0:T(8,128)(2,1)S(1)} collective-permute-done((bf16[2,16,2048]{2,1,0:T(8,128)(2,1)S(1)}, bf16[2,16,2048]{2,1,0:T(8,128)(2,1)S(1)}, u32[]{:S(2)}, u32[]{:S(2)}) %collective-permute-start.1) | collective-permute-done | bytes 131104 | tf_op jit(solution)/shard_map/ppermute | solution.py:522
  22.0 0.0 collective-permute-done.refs_1_
  22.0 0.1 shard_map.87
  22.1 1.6 %collective-permute-start.3 = (bf16[64,2048]{1,0:T(8,128)(2,1)S(1)}, bf16[64,2048]{1,0:T(8,128)(2,1)S(1)}, u32[]{:S(2)}, u32[]{:S(2)}) collective-permute-start(bf16[64,2048]{1,0:T(8,128)(2,1)S(1)} %get-tuple-element.114), channel_id=1, source_target_pairs={{0,8},{4,12},{8,0},{12,4},{16,24},{20,28},{24,16},{28,20},{1,9},{5... | collective-permute-start | bytes 786440 | tf_op jit(solution)/shard_map/ppermute | solution.py:522
  23.6 1.5 %collective-permute-start.5 = (bf16[64,2048]{1,0:T(8,128)(2,1)S(1)}, bf16[64,2048]{1,0:T(8,128)(2,1)S(1)}, u32[]{:S(2)}, u32[]{:S(2)}) collective-permute-start(bf16[64,2048]{1,0:T(8,128)(2,1)S(1)} %get-tuple-element.115), channel_id=1, source_target_pairs={{0,24},{4,28},{8,16},{12,20},{16,8},{20,12},{24,0},{28,4},{1,25},{... | collective-permute-start | bytes 786440 | tf_op jit(solution)/shard_map/ppermute | solution.py:522
  25.1 0.5 collective-permute-start.4
  25.6 0.0 collective-permute-start.6
  25.6 2.5 %collective-permute-start.8 = (bf16[128,1024]{1,0:T(8,128)(2,1)S(1)}, bf16[128,1024]{1,0:T(8,128)(2,1)S(1)}, u32[]{:S(2)}, u32[]{:S(2)}) collective-permute-start(bf16[128,1024]{1,0:T(8,128)(2,1)S(1)} %get-tuple-element.132), channel_id=1, source_target_pairs={{0,3},{1,2},{2,1},{3,0},{4,7},{5,6},{6,5},{7,4},{8,11},{9,10},{10,... | collective-permute-start | bytes 786440 | tf_op jit(solution)/shard_map/ppermute | solution.py:522
  28.1 3.3 %collective-permute-done.3.refs_8_.refs_12_.refs_17_ = bf16[64,2048]{1,0:T(8,128)(2,1)S(1)} collective-permute-done((bf16[64,2048]{1,0:T(8,128)(2,1)S(1)}, bf16[64,2048]{1,0:T(8,128)(2,1)S(1)}, u32[]{:S(2)}, u32[]{:S(2)}) %collective-permute-start.3) | collective-permute-done | bytes 262176 | tf_op jit(solution)/shard_map/ppermute | solution.py:522
  31.4 0.0 collective-permute-start.7
  31.4 5.0 %shard_map.88 = (f32[512,128]{1,0:T(8,128)S(1)}, f32[512,128]{1,0:T(8,128)S(1)}, bf16[4,512,512]{2,1,0:T(8,128)(2,1)S(1)}, bf16[4,512,512]{2,1,0:T(8,128)(2,1)S(1)}, f32[512,1024]{1,0:T(8,128)S(1)}) custom-call(bf16[512,1024]{1,0:T(8,128)(2,1)S(1)} %copy-done, bf16[512,1024]{1,0:T(8,128)(2,1)S(1)} %copy-done.2, bf16[512,1024]{1,0:T(8,128)(2,1)S(1)} %copy-done.3, ...), custom_call_target="tpu_custom_call" | custom-call | tf_op jit(solution)/shard_map/pallas_call | solution.py:528
  36.4 0.0 collective-permute-done.5.refs_12_.refs_16_.refs_21_
  36.4 0.1 collective-permute-start.9
  36.5 1.1 %collective-permute-done.4.refs_10_.refs_14_.refs_19_ = bf16[64,2048]{1,0:T(8,128)(2,1)S(1)} collective-permute-done((bf16[64,2048]{1,0:T(8,128)(2,1)S(1)}, bf16[64,2048]{1,0:T(8,128)(2,1)S(1)}, u32[]{:S(2)}, u32[]{:S(2)}) %collective-permute-start.4) | collective-permute-done | bytes 262176 | tf_op jit(solution)/shard_map/ppermute | solution.py:522
  37.5 0.0 collective-permute-start.10
  37.5 0.0 collective-permute-done.6.refs_3_.refs_7_.refs_9_
  37.6 0.5 collective-permute-start.11
  38.1 3.0 %collective-permute-done.8.refs_5_.refs_9_.refs_11_ = bf16[128,1024]{1,0:T(8,128)(2,1)S(1)} collective-permute-done((bf16[128,1024]{1,0:T(8,128)(2,1)S(1)}, bf16[128,1024]{1,0:T(8,128)(2,1)S(1)}, u32[]{:S(2)}, u32[]{:S(2)}) %collective-permute-start.8) | collective-permute-done | bytes 262176 | tf_op jit(solution)/shard_map/ppermute | solution.py:522
  41.0 0.0 collective-permute-start.12
  41.0 9.1 %collective-permute-done.7.refs_4_.refs_8_.refs_10_ = bf16[128,1024]{1,0:T(8,128)(2,1)S(1)} collective-permute-done((bf16[128,1024]{1,0:T(8,128)(2,1)S(1)}, bf16[128,1024]{1,0:T(8,128)(2,1)S(1)}, u32[]{:S(2)}, u32[]{:S(2)}) %collective-permute-start.7) | collective-permute-done | bytes 262176 | tf_op jit(solution)/shard_map/ppermute | solution.py:522
  50.2 0.0 collective-permute-start.23
  50.2 0.0 collective-permute-done.9.refs_7_.refs_11_.refs_16_
  50.2 0.0 collective-permute-done.10.refs_9_.refs_13_.refs_18_
  50.2 0.0 collective-permute-done.11.refs_11_.refs_15_.refs_20_
  50.2 0.0 collective-permute-done.12.refs_13_.refs_17_.refs_22_
  50.2 3.2 %shard_map.89 = (f32[128,128]{1,0:T(8,128)S(1)}, f32[128,128]{1,0:T(8,128)S(1)}, f32[16,128]{1,0:T(8,128)S(1)}, f32[16,128]{1,0:T(8,128)S(1)}, f32[8,128]{1,0:T(...) custom-call(bf16[128,2048]{1,0:T(8,128)(2,1)S(1)} %get-tuple-element.128.refs_0_.refs_1_.refs_2_, ...), custom_call_target="tpu_custom_call" | custom-call | tf_op jit(solution)/shard_map/pallas_call | solution.py:528
  53.4 2.1 %collective-permute-start.13 = (f32[8,128]{1,0:T(8,128)S(1)}, f32[8,128]{1,0:T(8,128)S(1)}, u32[]{:S(2)}, u32[]{:S(2)}) collective-permute-start(f32[8,128]{1,0:T(8,128)S(1)} %get-tuple-element.144), channel_id=1, source_target_pairs={{0,1},{1,0},{2,3},{3,2},{4,5},{5,4},{6,7},{7,6},{8,9},{9,8},{10,11... | collective-permute-start | bytes 12296 | tf_op jit(solution)/shard_map/ppermute | solution.py:522
  55.5 0.9 collective-permute-start.14
  56.4 1.6 %collective-permute-start.15 = (f32[8,128]{1,0:T(8,128)S(1)}, f32[8,128]{1,0:T(8,128)S(1)}, u32[]{:S(2)}, u32[]{:S(2)}) collective-permute-start(f32[8,128]{1,0:T(8,128)S(1)} %get-tuple-element.146), channel_id=1, source_target_pairs={{0,3},{1,2},{2,1},{3,0},{4,7},{5,6},{6,5},{7,4},{8,11},{9,10},{10,... | collective-permute-start | bytes 12296 | tf_op jit(solution)/shard_map/ppermute | solution.py:522
  58.0 2.1 %collective-permute-done.14.refs_11_ = f32[8,128]{1,0:T(8,128)S(1)} collective-permute-done((f32[8,128]{1,0:T(8,128)S(1)}, f32[8,128]{1,0:T(8,128)S(1)}, u32[]{:S(2)}, u32[]{:S(2)}) %collective-permute-start.14) | collective-permute-done | bytes 4128 | tf_op jit(solution)/shard_map/ppermute | solution.py:522
  60.0 1.9 %collective-permute-done.15.refs_12_ = f32[8,128]{1,0:T(8,128)S(1)} collective-permute-done((f32[8,128]{1,0:T(8,128)S(1)}, f32[8,128]{1,0:T(8,128)S(1)}, u32[]{:S(2)}, u32[]{:S(2)}) %collective-permute-start.15) | collective-permute-done | bytes 4128 | tf_op jit(solution)/shard_map/ppermute | solution.py:522
  62.0 0.9 collective-permute-start.24
  62.8 2.2 %collective-permute-start.25 = (bf16[128,1024]{1,0:T(8,128)(2,1)S(1)}, bf16[128,1024]{1,0:T(8,128)(2,1)S(1)}, u32[]{:S(2)}, u32[]{:S(2)}) collective-permute-start(bf16[128,1024]{1,0:T(8,128)(2,1)S(1)} %get-tuple-element.188), channel_id=1, source_target_pairs={{0,3},{1,2},{2,1},{3,0},{4,7},{5,6},{6,5},{7,4},{8,11},{9,10},{10,... | collective-permute-start | bytes 786440 | tf_op jit(solution)/shard_map/ppermute | solution.py:522
  65.1 3.5 %shard_map.90 = (f32[128,1024]{1,0:T(8,128)S(1)}, f32[16,2048]{1,0:T(8,128)S(1)}) custom-call(bf16[128,2048]{1,0:T(8,128)(2,1)S(1)} %get-tuple-element.128.refs_0_.refs_1_.refs_2_, bf16[128,2048]{1,0:T(8,128)(2,1)S(1)} %get-tuple-element.129.refs_1_.refs_2_.refs_3_, bf16[2,16,2048]{2,1,0:T(8,128)(2,1)S(1)} %get-tuple-element.110.refs_0_.refs_2_.refs_4_, ...), custom_call_target="tpu_custom_call" | custom-call | tf_op jit(solution)/shard_map/pallas_call | solution.py:528
  68.6 2.6 %shard_map.91 = (f32[512,128]{1,0:T(8,128)S(1)}, f32[512,128]{1,0:T(8,128)S(1)}, f32[128,128]{1,0:T(8,128)S(1)}, f32[128,128]{1,0:T(8,128)S(1)}, f32[16,128]{1,0...) custom-call(s32[8]{0:T(128)S(1)} %copy-done.5, ...), custom_call_target="tpu_custom_call" | custom-call | tf_op jit(solution)/shard_map/pallas_call | solution.py:528
  71.2 2.5 %collective-permute-start.18 = (f32[16,16]{1,0:T(8,128)S(1)}, f32[16,16]{1,0:T(8,128)S(1)}, u32[]{:S(2)}, u32[]{:S(2)}) collective-permute-start(f32[16,16]{1,0:T(8,128)S(1)} %get-tuple-element.170.refs_0_), channel_id=1, source_target_pairs={{0,24},{4,28},{8,16},{12,20},{16,8},{20,12},{24,0},{28,4},{1,25},{... | collective-permute-start | bytes 3080 | tf_op jit(solution)/shard_map/ppermute | solution.py:522
  73.6 0.5 collective-permute-start.17
  74.2 1.6 %collective-permute-done.18.refs_3_ = f32[16,16]{1,0:T(8,128)S(1)} collective-permute-done((f32[16,16]{1,0:T(8,128)S(1)}, f32[16,16]{1,0:T(8,128)S(1)}, u32[]{:S(2)}, u32[]{:S(2)}) %collective-permute-start.18) | collective-permute-done | bytes 1056 | tf_op jit(solution)/shard_map/ppermute | solution.py:522
  75.7 1.5 %collective-permute-start.16 = (f32[16,16]{1,0:T(8,128)S(1)}, f32[16,16]{1,0:T(8,128)S(1)}, u32[]{:S(2)}, u32[]{:S(2)}) collective-permute-start(f32[16,16]{1,0:T(8,128)S(1)} %get-tuple-element.170.refs_0_), channel_id=1, source_target_pairs={{0,8},{4,12},{8,0},{12,4},{16,24},{20,28},{24,16},{28,20},{1,9},{5... | collective-permute-start | bytes 3080 | tf_op jit(solution)/shard_map/ppermute | solution.py:522
  77.3 2.2 %shard_map.92 = (f32[512,512]{1,0:T(8,128)S(1)}, f32[512,512]{1,0:T(8,128)S(1)}, f32[512,512]{1,0:T(8,128)S(1)}) custom-call(s32[8]{0:T(128)S(1)} %copy-done.5, s32[8]{0:T(128)S(1)} %copy-done.6, bf16[512,1024]{1,0:T(8,128)(2,1)S(1)} %copy-done, bf16[512,1024]{1,0:T(8,128)(2,1)S(1)} %copy-done.1, bf16[4,512,512]{2,1,0:T(8,128)(2,1)S(1)} %get-tuple-element.156.soft_in, ...), custom_call_target="tpu_custom_call" | custom-call | tf_op jit(solution)/shard_map/pallas_call | solution.py:528
  79.4 0.0 collective-permute-done.17.refs_2_
  79.4 0.0 collective-permute-done.16.refs_1_
  79.4 0.1 shard_map.93.refs_1_
  79.5 0.0 collective-permute-start.19
  79.5 1.9 %shard_map.94 = (f32[512,512]{1,0:T(8,128)S(1)}, f32[512,512]{1,0:T(8,128)S(1)}, f32[512,512]{1,0:T(8,128)S(1)}) custom-call(s32[8]{0:T(128)S(1)} %copy-done.5, s32[8]{0:T(128)S(1)} %copy-done.6, bf16[512,1024]{1,0:T(8,128)(2,1)S(1)} %copy-done, bf16[512,1024]{1,0:T(8,128)(2,1)S(1)} %copy-done.1, bf16[4,512,512]{2,1,0:T(8,128)(2,1)S(1)} %get-tuple-element.174.soft_in, ...), custom_call_target="tpu_custom_call" | custom-call | tf_op jit(solution)/shard_map/pallas_call | solution.py:528
  81.5 0.1 shard_map.95.refs_23_
  81.5 1.6 %collective-permute-start.22 = (f32[16,256]{1,0:T(8,128)S(1)}, f32[16,256]{1,0:T(8,128)S(1)}, u32[]{:S(2)}, u32[]{:S(2)}) collective-permute-start(f32[16,256]{1,0:T(8,128)S(1)} %shard_map.95.refs_23_), channel_id=1, source_target_pairs={{0,3},{1,2},{2,1},{3,0},{4,7},{5,6},{6,5},{7,4},{8,11},{9,10},{10,... | collective-permute-start | bytes 49160 | tf_op jit(solution)/shard_map/ppermute | solution.py:522
  83.1 0.2 collective-permute-start.21
  83.4 2.6 %collective-permute-start.20 = (f32[16,256]{1,0:T(8,128)S(1)}, f32[16,256]{1,0:T(8,128)S(1)}, u32[]{:S(2)}, u32[]{:S(2)}) collective-permute-start(f32[16,256]{1,0:T(8,128)S(1)} %shard_map.95.refs_23_), channel_id=1, source_target_pairs={{0,1},{1,0},{2,3},{3,2},{4,5},{5,4},{6,7},{7,6},{8,9},{9,8},{10,11... | collective-permute-start | bytes 49160 | tf_op jit(solution)/shard_map/ppermute | solution.py:522
  85.9 0.0 collective-permute-done.25.refs_9_.refs_14_
  85.9 3.1 %shard_map.96 = bf16[512,1024]{1,0:T(8,128)(2,1)} custom-call(s32[8]{0:T(128)S(1)} %copy-done.5, bf16[128,2048]{1,0:T(8,128)(2,1)S(1)} %get-tuple-element.128.refs_0_.refs_1_.refs_2_, bf16[128,2048]{1,0:T(8,128)(2,1)S(1)} %get-tuple-element.129.refs_1_.refs_2_.refs_3_, f32[512,512]{1,0:T(8,128)S(1)} %get-tuple-element.181.refs_3_, ...), custom_call_target="tpu_custom_call" | custom-call | tf_op jit(solution)/shard_map/pallas_call | solution.py:528
  89.0 0.0 collective-permute-done.22.refs_26_
  89.0 0.0 collective-permute-done.21.refs_25_
  89.0 0.0 collective-permute-done.20.refs_24_
  89.0 7.4 %shard_map.97 = (bf16[512,1024]{1,0:T(8,128)(2,1)}, bf16[512,1024]{1,0:T(8,128)(2,1)}) custom-call(s32[8]{0:T(128)S(1)} %copy-done.5, s32[8]{0:T(128)S(1)} %copy-done.6, bf16[128,2048]{1,0:T(8,128)(2,1)S(1)} %get-tuple-element.128.refs_0_.refs_1_.refs_2_, bf16[128,2048]{1,0:T(8,128)(2,1)S(1)} %get-tuple-element.129.refs_1_.refs_2_.refs_3_, ...), custom_call_target="tpu_custom_call" | custom-call | tf_op jit(solution)/shard_map/pallas_call | solution.py:528
  (15 shorter events, 0.0 us)
Async XLA Ops:
  0.6 10.9 %copy-start.1 = (bf16[512,1024]{1,0:T(8,128)(2,1)S(1)}, bf16[512,1024]{1,0:T(8,128)(2,1)}, u32[]{:S(2)}) copy-start(bf16[512,1024]{1,0:T(8,128)(2,1)} %g.8) | copy-start | bytes 3145732
  0.6 10.9 %copy-start = (bf16[512,1024]{1,0:T(8,128)(2,1)S(1)}, bf16[512,1024]{1,0:T(8,128)(2,1)}, u32[]{:S(2)}) copy-start(bf16[512,1024]{1,0:T(8,128)(2,1)} %q.8) | copy-start | bytes 3145732
  0.7 10.9 %copy-start.3 = (bf16[512,1024]{1,0:T(8,128)(2,1)S(1)}, bf16[512,1024]{1,0:T(8,128)(2,1)}, u32[]{:S(2)}) copy-start(bf16[512,1024]{1,0:T(8,128)(2,1)} %v.4) | copy-start | bytes 3145732
  0.7 0.8 copy-start.4
  1.5 0.8 copy-start.6
  2.2 9.3 %copy-start.2 = (bf16[512,1024]{1,0:T(8,128)(2,1)S(1)}, bf16[512,1024]{1,0:T(8,128)(2,1)}, u32[]{:S(2)}) copy-start(bf16[512,1024]{1,0:T(8,128)(2,1)} %k.4) | copy-start | bytes 3145732
  5.8 10.8 %collective-permute-start.2 = (bf16[2,16,2048]{2,1,0:T(8,128)(2,1)S(1)}, bf16[2,16,2048]{2,1,0:T(8,128)(2,1)S(1)}, u32[]{:S(2)}, u32[]{:S(2)}) collective-permute-start(bf16[2,16,2048]{2,1,0:T(8,128)(2,1)S(1)} %get-tuple-element.110.refs_0_.refs_2_.refs_4_), channel_id=1, source_target_pairs={{0,3},{1,2},{2,1},{3,0},{4,7},{5,6},{6,5},{7,4},{8,11},{9,10},{10,... | collective-permute-start | bytes 393224 | tf_op jit(solution)/shard_map/ppermute | solution.py:522
  10.9 11.1 %collective-permute-start.1 = (bf16[2,16,2048]{2,1,0:T(8,128)(2,1)S(1)}, bf16[2,16,2048]{2,1,0:T(8,128)(2,1)S(1)}, u32[]{:S(2)}, u32[]{:S(2)}) collective-permute-start(bf16[2,16,2048]{2,1,0:T(8,128)(2,1)S(1)} %get-tuple-element.110.refs_0_.refs_2_.refs_4_), channel_id=1, source_target_pairs={{0,2},{1,3},{2,0},{3,1},{4,6},{5,7},{6,4},{7,5},{8,10},{9,11},{10,... | collective-permute-start | bytes 393224 | tf_op jit(solution)/shard_map/ppermute | solution.py:522
  10.9 11.1 %collective-permute-start = (bf16[2,16,2048]{2,1,0:T(8,128)(2,1)S(1)}, bf16[2,16,2048]{2,1,0:T(8,128)(2,1)S(1)}, u32[]{:S(2)}, u32[]{:S(2)}) collective-permute-start(bf16[2,16,2048]{2,1,0:T(8,128)(2,1)S(1)} %get-tuple-element.110.refs_0_.refs_2_.refs_4_), channel_id=1, source_target_pairs={{0,1},{1,0},{2,3},{3,2},{4,5},{5,4},{6,7},{7,6},{8,9},{9,8},{10,11... | collective-permute-start | bytes 393224 | tf_op jit(solution)/shard_map/ppermute | solution.py:522
  22.1 9.3 %collective-permute-start.3 = (bf16[64,2048]{1,0:T(8,128)(2,1)S(1)}, bf16[64,2048]{1,0:T(8,128)(2,1)S(1)}, u32[]{:S(2)}, u32[]{:S(2)}) collective-permute-start(bf16[64,2048]{1,0:T(8,128)(2,1)S(1)} %get-tuple-element.114), channel_id=1, source_target_pairs={{0,8},{4,12},{8,0},{12,4},{16,24},{20,28},{24,16},{28,20},{1,9},{5... | collective-permute-start | bytes 786440 | tf_op jit(solution)/shard_map/ppermute | solution.py:522
  23.6 12.8 %collective-permute-start.5 = (bf16[64,2048]{1,0:T(8,128)(2,1)S(1)}, bf16[64,2048]{1,0:T(8,128)(2,1)S(1)}, u32[]{:S(2)}, u32[]{:S(2)}) collective-permute-start(bf16[64,2048]{1,0:T(8,128)(2,1)S(1)} %get-tuple-element.115), channel_id=1, source_target_pairs={{0,24},{4,28},{8,16},{12,20},{16,8},{20,12},{24,0},{28,4},{1,25},{... | collective-permute-start | bytes 786440 | tf_op jit(solution)/shard_map/ppermute | solution.py:522
  25.1 12.4 %collective-permute-start.4 = (bf16[64,2048]{1,0:T(8,128)(2,1)S(1)}, bf16[64,2048]{1,0:T(8,128)(2,1)S(1)}, u32[]{:S(2)}, u32[]{:S(2)}) collective-permute-start(bf16[64,2048]{1,0:T(8,128)(2,1)S(1)} %get-tuple-element.115), channel_id=1, source_target_pairs={{0,16},{4,20},{8,24},{12,28},{16,0},{20,4},{24,8},{28,12},{1,17},{... | collective-permute-start | bytes 786440 | tf_op jit(solution)/shard_map/ppermute | solution.py:522
  25.6 11.9 %collective-permute-start.6 = (bf16[128,1024]{1,0:T(8,128)(2,1)S(1)}, bf16[128,1024]{1,0:T(8,128)(2,1)S(1)}, u32[]{:S(2)}, u32[]{:S(2)}) collective-permute-start(bf16[128,1024]{1,0:T(8,128)(2,1)S(1)} %get-tuple-element.130), channel_id=1, source_target_pairs={{0,1},{1,0},{2,3},{3,2},{4,5},{5,4},{6,7},{7,6},{8,9},{9,8},{10,11... | collective-permute-start | bytes 786440 | tf_op jit(solution)/shard_map/ppermute | solution.py:522
  25.6 15.4 %collective-permute-start.8 = (bf16[128,1024]{1,0:T(8,128)(2,1)S(1)}, bf16[128,1024]{1,0:T(8,128)(2,1)S(1)}, u32[]{:S(2)}, u32[]{:S(2)}) collective-permute-start(bf16[128,1024]{1,0:T(8,128)(2,1)S(1)} %get-tuple-element.132), channel_id=1, source_target_pairs={{0,3},{1,2},{2,1},{3,0},{4,7},{5,6},{6,5},{7,4},{8,11},{9,10},{10,... | collective-permute-start | bytes 786440 | tf_op jit(solution)/shard_map/ppermute | solution.py:522
  31.4 18.8 %collective-permute-start.7 = (bf16[128,1024]{1,0:T(8,128)(2,1)S(1)}, bf16[128,1024]{1,0:T(8,128)(2,1)S(1)}, u32[]{:S(2)}, u32[]{:S(2)}) collective-permute-start(bf16[128,1024]{1,0:T(8,128)(2,1)S(1)} %get-tuple-element.131), channel_id=1, source_target_pairs={{0,2},{1,3},{2,0},{3,1},{4,6},{5,7},{6,4},{7,5},{8,10},{9,11},{10,... | collective-permute-start | bytes 786440 | tf_op jit(solution)/shard_map/ppermute | solution.py:522
  36.4 13.8 %collective-permute-start.9 = (bf16[64,2048]{1,0:T(8,128)(2,1)S(1)}, bf16[64,2048]{1,0:T(8,128)(2,1)S(1)}, u32[]{:S(2)}, u32[]{:S(2)}) collective-permute-start(bf16[64,2048]{1,0:T(8,128)(2,1)S(1)} %get-tuple-element.134), channel_id=1, source_target_pairs={{0,4},{4,0},{8,12},{12,8},{16,20},{20,16},{24,28},{28,24},{1,5},{5... | collective-permute-start | bytes 786440 | tf_op jit(solution)/shard_map/ppermute | solution.py:522
  37.5 12.6 %collective-permute-start.10 = (bf16[64,2048]{1,0:T(8,128)(2,1)S(1)}, bf16[64,2048]{1,0:T(8,128)(2,1)S(1)}, u32[]{:S(2)}, u32[]{:S(2)}) collective-permute-start(bf16[64,2048]{1,0:T(8,128)(2,1)S(1)} %collective-permute-done.3.refs_8_.refs_12_.refs_17_), channel_id=1, source_target_pairs={{0,4},{4,0},{8,12},{12,8},{16,20},{20,16},{24,28},{28,24},{1,5},{5... | collective-permute-start | bytes 786440 | tf_op jit(solution)/shard_map/ppermute | solution.py:522
  37.6 12.6 %collective-permute-start.11 = (bf16[64,2048]{1,0:T(8,128)(2,1)S(1)}, bf16[64,2048]{1,0:T(8,128)(2,1)S(1)}, u32[]{:S(2)}, u32[]{:S(2)}) collective-permute-start(bf16[64,2048]{1,0:T(8,128)(2,1)S(1)} %collective-permute-done.4.refs_10_.refs_14_.refs_19_), channel_id=1, source_target_pairs={{0,4},{4,0},{8,12},{12,8},{16,20},{20,16},{24,28},{28,24},{1,5},{5... | collective-permute-start | bytes 786440 | tf_op jit(solution)/shard_map/ppermute | solution.py:522
  41.0 9.2 %collective-permute-start.12 = (bf16[64,2048]{1,0:T(8,128)(2,1)S(1)}, bf16[64,2048]{1,0:T(8,128)(2,1)S(1)}, u32[]{:S(2)}, u32[]{:S(2)}) collective-permute-start(bf16[64,2048]{1,0:T(8,128)(2,1)S(1)} %collective-permute-done.5.refs_12_.refs_16_.refs_21_), channel_id=1, source_target_pairs={{0,4},{4,0},{8,12},{12,8},{16,20},{20,16},{24,28},{28,24},{1,5},{5... | collective-permute-start | bytes 786440 | tf_op jit(solution)/shard_map/ppermute | solution.py:522
  50.2 33.2 %collective-permute-start.23 = (bf16[128,1024]{1,0:T(8,128)(2,1)S(1)}, bf16[128,1024]{1,0:T(8,128)(2,1)S(1)}, u32[]{:S(2)}, u32[]{:S(2)}) collective-permute-start(bf16[128,1024]{1,0:T(8,128)(2,1)S(1)} %get-tuple-element.186), channel_id=1, source_target_pairs={{0,1},{1,0},{2,3},{3,2},{4,5},{5,4},{6,7},{7,6},{8,9},{9,8},{10,11... | collective-permute-start | bytes 786440 | tf_op jit(solution)/shard_map/ppermute | solution.py:522
  53.4 4.5 %collective-permute-start.13 = (f32[8,128]{1,0:T(8,128)S(1)}, f32[8,128]{1,0:T(8,128)S(1)}, u32[]{:S(2)}, u32[]{:S(2)}) collective-permute-start(f32[8,128]{1,0:T(8,128)S(1)} %get-tuple-element.144), channel_id=1, source_target_pairs={{0,1},{1,0},{2,3},{3,2},{4,5},{5,4},{6,7},{7,6},{8,9},{9,8},{10,11... | collective-permute-start | bytes 12296 | tf_op jit(solution)/shard_map/ppermute | solution.py:522
  55.5 4.5 %collective-permute-start.14 = (f32[8,128]{1,0:T(8,128)S(1)}, f32[8,128]{1,0:T(8,128)S(1)}, u32[]{:S(2)}, u32[]{:S(2)}) collective-permute-start(f32[8,128]{1,0:T(8,128)S(1)} %get-tuple-element.145), channel_id=1, source_target_pairs={{0,2},{1,3},{2,0},{3,1},{4,6},{5,7},{6,4},{7,5},{8,10},{9,11},{10,... | collective-permute-start | bytes 12296 | tf_op jit(solution)/shard_map/ppermute | solution.py:522
  56.4 5.6 %collective-permute-start.15 = (f32[8,128]{1,0:T(8,128)S(1)}, f32[8,128]{1,0:T(8,128)S(1)}, u32[]{:S(2)}, u32[]{:S(2)}) collective-permute-start(f32[8,128]{1,0:T(8,128)S(1)} %get-tuple-element.146), channel_id=1, source_target_pairs={{0,3},{1,2},{2,1},{3,0},{4,7},{5,6},{6,5},{7,4},{8,11},{9,10},{10,... | collective-permute-start | bytes 12296 | tf_op jit(solution)/shard_map/ppermute | solution.py:522
  62.0 24.0 %collective-permute-start.24 = (bf16[128,1024]{1,0:T(8,128)(2,1)S(1)}, bf16[128,1024]{1,0:T(8,128)(2,1)S(1)}, u32[]{:S(2)}, u32[]{:S(2)}) collective-permute-start(bf16[128,1024]{1,0:T(8,128)(2,1)S(1)} %get-tuple-element.187), channel_id=1, source_target_pairs={{0,2},{1,3},{2,0},{3,1},{4,6},{5,7},{6,4},{7,5},{8,10},{9,11},{10,... | collective-permute-start | bytes 786440 | tf_op jit(solution)/shard_map/ppermute | solution.py:522
  62.8 23.1 %collective-permute-start.25 = (bf16[128,1024]{1,0:T(8,128)(2,1)S(1)}, bf16[128,1024]{1,0:T(8,128)(2,1)S(1)}, u32[]{:S(2)}, u32[]{:S(2)}) collective-permute-start(bf16[128,1024]{1,0:T(8,128)(2,1)S(1)} %get-tuple-element.188), channel_id=1, source_target_pairs={{0,3},{1,2},{2,1},{3,0},{4,7},{5,6},{6,5},{7,4},{8,11},{9,10},{10,... | collective-permute-start | bytes 786440 | tf_op jit(solution)/shard_map/ppermute | solution.py:522
  65.1 3.5 %copy-start.5 = (s32[8]{0:T(128)S(1)}, s32[8]{0:T(128)}, u32[]{:S(2)}) copy-start(s32[8]{0:T(128)} %refs_0_.5) | copy-start | bytes 100
  71.2 4.6 %collective-permute-start.18 = (f32[16,16]{1,0:T(8,128)S(1)}, f32[16,16]{1,0:T(8,128)S(1)}, u32[]{:S(2)}, u32[]{:S(2)}) collective-permute-start(f32[16,16]{1,0:T(8,128)S(1)} %get-tuple-element.170.refs_0_), channel_id=1, source_target_pairs={{0,24},{4,28},{8,16},{12,20},{16,8},{20,12},{24,0},{28,4},{1,25},{... | collective-permute-start | bytes 3080 | tf_op jit(solution)/shard_map/ppermute | solution.py:522
  73.6 5.8 %collective-permute-start.17 = (f32[16,16]{1,0:T(8,128)S(1)}, f32[16,16]{1,0:T(8,128)S(1)}, u32[]{:S(2)}, u32[]{:S(2)}) collective-permute-start(f32[16,16]{1,0:T(8,128)S(1)} %get-tuple-element.170.refs_0_), channel_id=1, source_target_pairs={{0,16},{4,20},{8,24},{12,28},{16,0},{20,4},{24,8},{28,12},{1,17},{... | collective-permute-start | bytes 3080 | tf_op jit(solution)/shard_map/ppermute | solution.py:522
  75.7 3.7 %collective-permute-start.16 = (f32[16,16]{1,0:T(8,128)S(1)}, f32[16,16]{1,0:T(8,128)S(1)}, u32[]{:S(2)}, u32[]{:S(2)}) collective-permute-start(f32[16,16]{1,0:T(8,128)S(1)} %get-tuple-element.170.refs_0_), channel_id=1, source_target_pairs={{0,8},{4,12},{8,0},{12,4},{16,24},{20,28},{24,16},{28,20},{1,9},{5... | collective-permute-start | bytes 3080 | tf_op jit(solution)/shard_map/ppermute | solution.py:522
  79.5 1.9 %collective-permute-start.19 = (f32[16,64]{1,0:T(8,128)S(1)}, f32[16,64]{1,0:T(8,128)S(1)}, u32[]{:S(2)}, u32[]{:S(2)}) collective-permute-start(f32[16,64]{1,0:T(8,128)S(1)} %shard_map.93.refs_1_), channel_id=1, source_target_pairs={{0,4},{4,0},{8,12},{12,8},{16,20},{20,16},{24,28},{28,24},{1,5},{5... | collective-permute-start | bytes 12296 | tf_op jit(solution)/shard_map/ppermute | solution.py:522
  81.5 7.5 %collective-permute-start.22 = (f32[16,256]{1,0:T(8,128)S(1)}, f32[16,256]{1,0:T(8,128)S(1)}, u32[]{:S(2)}, u32[]{:S(2)}) collective-permute-start(f32[16,256]{1,0:T(8,128)S(1)} %shard_map.95.refs_23_), channel_id=1, source_target_pairs={{0,3},{1,2},{2,1},{3,0},{4,7},{5,6},{6,5},{7,4},{8,11},{9,10},{10,... | collective-permute-start | bytes 49160 | tf_op jit(solution)/shard_map/ppermute | solution.py:522
  83.1 5.9 %collective-permute-start.21 = (f32[16,256]{1,0:T(8,128)S(1)}, f32[16,256]{1,0:T(8,128)S(1)}, u32[]{:S(2)}, u32[]{:S(2)}) collective-permute-start(f32[16,256]{1,0:T(8,128)S(1)} %shard_map.95.refs_23_), channel_id=1, source_target_pairs={{0,2},{1,3},{2,0},{3,1},{4,6},{5,7},{6,4},{7,5},{8,10},{9,11},{10,... | collective-permute-start | bytes 49160 | tf_op jit(solution)/shard_map/ppermute | solution.py:522
  83.4 5.7 %collective-permute-start.20 = (f32[16,256]{1,0:T(8,128)S(1)}, f32[16,256]{1,0:T(8,128)S(1)}, u32[]{:S(2)}, u32[]{:S(2)}) collective-permute-start(f32[16,256]{1,0:T(8,128)S(1)} %shard_map.95.refs_23_), channel_id=1, source_target_pairs={{0,1},{1,0},{2,3},{3,2},{4,5},{5,4},{6,7},{7,6},{8,9},{9,8},{10,11... | collective-permute-start | bytes 49160 | tf_op jit(solution)/shard_map/ppermute | solution.py:522

commit v5 on v4

--- a/solution.py
+++ b/solution.py
@@ -154,6 +154,8 @@
     col = iota((count, total), 1)
     bits, level_bits = count.bit_length() - 1, levels.bit_length() - 1
     slot, ring_slot = (col >> bits) & (levels - 1), col >> (bits + level_bits)
+    evens = total >> (bits + level_bits + 1)
+    ring_slot = (ring_slot & (evens - 1)) * 2 + (ring_slot >> (evens.bit_length() - 1))
     other = ((ring_slot ^ ring) * levels + (slot ^ level)) * count + (col & (count - 1))
     return other, (ring * levels + level) * count + iota((count, total), 0)
 
@@ -213,22 +215,21 @@
     return peak + jnp.log(total), jnp.sum(weights * grads, axis=0, keepdims=True) / total
 
 
-def level_stats_kernel(scale, levels, mids, fars, *refs):
-    kv, qg, far_own = refs[:3]
-    mid_in, far_in = refs[3 : 3 + mids], refs[3 + mids : 3 + mids + fars]
-    mlog, mdot, flog, fdot = refs[3 + mids + fars :][:4]
-    backs = refs[7 + mids + fars :]
+def mid_stats_kernel(scale, levels, mids, *refs):
+    kv, qg = refs[:2]
+    mid_in = refs[2 : 2 + mids]
+    mlog, mdot = refs[2 + mids : 4 + mids]
+    backs = refs[4 + mids :]
     step = pl.program_id(0)
-    ring, level = lax.axis_index("seq"), lax.axis_index("lvl")
-    mid_count, far_count = kv.shape[0], far_own.shape[1]
-    total = mid_count * levels
+    level = lax.axis_index("lvl")
+    mid_count = kv.shape[0]
     every = slice(None)
 
     @pl.when(step == 0)
     def _():
-        for ref in (mlog, mdot, flog, fdot):
+        for ref in (mlog, mdot):
             ref[...] = jnp.zeros_like(ref)
-        other, own = mid_places(mid_count, total, level)
+        other, own = mid_places(mid_count, mid_count * levels, level)
         hide = bias(other <= own)
         for at in range(GROUP):
             low, high = cuts(at)
@@ -254,17 +255,6 @@
                 where = slice(slot * mid_count, (slot + 1) * mid_count)
                 back[at : at + 1, :] = log_part[:, where]
                 back[GROUP + at : GROUP + at + 1, :] = dot_part[:, where]
-
-    other, own = far_places(far_count, total, levels, level, ring)
-    hide = bias(other <= own)
-    for at in range(GROUP):
-        head = step * GROUP + at
-        low, high = cuts(at)
-        scores = mm_t(far_own[1, :, low], stack(far_in, low)) * scale + hide
-        grads = mm_t(far_own[1, :, high], stack(far_in, high))
-        log_part, dot_part = row_stats(scores, grads)
-        put_lane(flog, every, head, log_part)
-        put_lane(fdot, every, head, dot_part)
 
 
 def merge_kernel(heads, mids, *refs):
@@ -297,10 +287,11 @@
     row = iota((rows, LANES), 0)
     mid_here = (row & (rows // mid_count - 1)) == lane_offsets(mid_off, heads)
     far_here = (row & (rows // far_count - 1)) == lane_offsets(far_off, heads)
-    mid_table, far_table = repeat_table(rows, mid_count), repeat_table(rows, far_count)
+    mid_wide = exact(repeat_table(rows, mid_count), jnp.concatenate([mid_logs, mid_dots], axis=1))
+    far_wide = exact(repeat_table(rows, far_count), jnp.concatenate([flog[...], fdot[...]], axis=1))
     near, near_dots = logs_a[...] + logs_b[...], dots_a[...] + dots_b[...]
-    mid = jnp.where(mid_here, exact(mid_table, mid_logs), LOW)
-    far = jnp.where(far_here, exact(far_table, flog[...]), LOW)
+    mid = jnp.where(mid_here, mid_wide[:, :LANES], LOW)
+    far = jnp.where(far_here, far_wide[:, :LANES], LOW)
     peak = jnp.maximum(near, jnp.maximum(mid, far))
     near_part = jnp.exp(near - peak)
     mid, far = jnp.exp(mid - peak), jnp.exp(far - peak)
@@ -308,15 +299,16 @@
     logs = peak + jnp.log(whole)
     dots = (
         near_part * near_dots
-        + mid * exact(mid_table, mid_dots)
-        + far * exact(far_table, fdot[...])
+        + mid * mid_wide[:, LANES:]
+        + far * far_wide[:, LANES:]
     ) / whole
     factors[...] = jnp.exp(near - logs)
     shifts[...] = dots - near_dots
     for here, count, sent in ((mid_here, mid_count, outs[8]), (far_here, far_count, outs[9])):
         table = gather_table(rows, count)
-        log_rows = exact(table, jnp.where(here, logs, 0.0))
-        dot_rows = exact(table, jnp.where(here, dots, 0.0))
+        chosen = [jnp.where(here, logs, 0.0), jnp.where(here, dots, 0.0)]
+        chosen = exact(table, jnp.concatenate(chosen, axis=1))
+        log_rows, dot_rows = chosen[:, :LANES], chosen[:, LANES:]
         sent[:heads, :] = log_rows.T[:heads, :]
         sent[heads:, :] = dot_rows.T[:heads, :]
         if count == mid_count:
@@ -361,15 +353,18 @@
 
 
 def level_base_kernel(scale, levels, mids, fars, *refs):
-    kv, qg, far_own, mlog, mdot, flog, fdot = refs[:7]
-    mid_in, far_in = refs[7 : 7 + mids], refs[7 + mids : 7 + mids + fars]
-    mid_base, far_base = refs[7 + mids + fars :]
+    kv, qg, far_own, mlog, mdot = refs[:5]
+    mid_in, far_in = refs[5 : 5 + mids], refs[5 + mids : 5 + mids + fars]
+    mid_base, far_base, flog, fdot = refs[5 + mids + fars :]
     step = pl.program_id(0)
     ring, level = lax.axis_index("seq"), lax.axis_index("lvl")
     far_count = far_own.shape[1]
+    every = slice(None)
 
     @pl.when(step == 0)
     def _():
+        for ref in (flog, fdot):
+            ref[...] = jnp.zeros_like(ref)
         other, own = mid_places(kv.shape[0], kv.shape[0] * levels, level)
         hide = bias(other <= own)
         for at in range(GROUP):
@@ -385,24 +380,24 @@
     for at in range(GROUP):
         head = step * GROUP + at
         low, high = cuts(at)
-        keys, vals = stack(far_in, low), stack(far_in, high)
-        logs, dots = pick_lane(flog, head), pick_lane(fdot, head)
-        soft, slopes = row_side(
-            scale, far_own[1, :, low], far_own[1, :, high], keys, vals, hide, logs, dots
-        )
-        far_base[:, low] = mm(slopes, keys)
-        far_base[:, high] = mm(soft, keys)
-
-
-def spread(rows, offsets, pieces):
-    tables = []
-    for offset, piece in zip(offsets, pieces):
-        count = piece.shape[0]
-        at = iota((rows, count), 0) - iota((rows, count), 1) * (rows // count)
-        tables.append((at == offset).astype(BF16))
-    table = tables[0] if len(tables) == 1 else jnp.concatenate(tables, axis=1)
-    whole = pieces[0] if len(pieces) == 1 else jnp.concatenate(pieces, axis=0)
-    return mm(table, whole.astype(BF16))
+        keys = stack(far_in, low)
+        scores = mm_t(far_own[1, :, low], keys) * scale + hide
+        grads = mm_t(far_own[1, :, high], stack(far_in, high))
+        peak = jnp.max(scores, axis=1, keepdims=True)
+        weights = jnp.exp(scores - peak)
+        total = jnp.sum(weights, axis=1, keepdims=True)
+        soft = weights / total
+        dots = jnp.sum(soft * grads, axis=1, keepdims=True)
+        put_lane(flog, every, head, peak + jnp.log(total))
+        put_lane(fdot, every, head, dots)
+        far_base[:, low] = mm((soft * (grads - dots)).astype(BF16), keys)
+        far_base[:, high] = mm(soft.astype(BF16), keys)
+
+
+def put_rows(ref, at, offset, piece):
+    count = piece.shape[0]
+    rows = pl.ds(offset, count, stride=ref.shape[1] // count)
+    ref[at, rows, :] += piece
 
 
 def rescaled(base, at, factors, shifts, head):
@@ -412,7 +407,7 @@
 
 def near_grads_kernel(parts, group, mid_off, far_off, q, g, soft_in, slope_in, base, *refs):
     factors, shifts, mid_factor, mid_shift, far_factor, far_shift = refs[:6]
-    mid_base, far_base, out_q, out_k, out_v = refs[6:]
+    mid_base, far_base, out_q, out_k, out_v, work = refs[6:]
     rows = q.shape[0]
     size = rows // parts
     for at in range(GROUP):
@@ -421,12 +416,12 @@
         low, high = cuts(at)
         factor, shift = pick_lane(factors, head), pick_lane(shifts, head)
         far = rescaled(far_base, at, far_factor, far_shift, head)
-        offsets, pieces = [far_off[head]], [far]
+        work[at] = factor * (base[:, low] - shift * base[:, high])
+        put_rows(work, at, far_off[head], far)
         if group == 0:
-            offsets.insert(0, mid_off[head])
-            pieces.insert(0, rescaled(mid_base, at, mid_factor, mid_shift, head))
-        near = factor * (base[:, low] - shift * base[:, high])
-        out_q[:, cut] = near + spread(rows, offsets, pieces)
+            mid = rescaled(mid_base, at, mid_factor, mid_shift, head)
+            put_rows(work, at, mid_off[head], mid)
+        out_q[:, cut] = work[at]
         queries = factor * q[:, cut].astype(F32)
         shifted = (shift * queries).astype(BF16)
         queries = queries.astype(BF16)
@@ -441,9 +436,8 @@
 
 def queries_kernel(scale, levels, mids, *refs):
     mid_off, kv, qg, dq_a, dq_b, mid_log, mid_dot = refs[:7]
-    mid_in, out_q = refs[7 : 7 + mids], refs[7 + mids]
+    mid_in, out_q, work = refs[7 : 7 + mids], refs[7 + mids], refs[8 + mids]
     level = lax.axis_index("lvl")
-    rows = out_q.shape[0]
 
     @pl.when(pl.program_id(0) == 0)
     def _():
@@ -455,26 +449,26 @@
             head = GROUP + at
             cut = slice(at * LANES, (at + 1) * LANES)
             part = mid_queries(scale, levels, level, kv, qg, mid_in, mid_log, mid_dot, at, head)
-            whole = dq_b[:, cut] + spread(rows, [mid_off[head]], [part])
-            out_q[:, cut] = (whole * scale).astype(BF16)
-
-
-def keys_kernel(scale, heads, levels, mids, fars, *refs):
+            work[at] = dq_b[:, cut]
+            put_rows(work, at, mid_off[head], part)
+            out_q[:, cut] = (work[at] * scale).astype(BF16)
+
+
+def keys_kernel(scale, heads, levels, rings, mids, fars, *refs):
     mid_off, far_off, kv, qg, far_own, dk_a, dv_a, dk_b, dv_b = refs[:9]
     first_in, second_in = refs[9 : 9 + mids], refs[9 + mids : 9 + 2 * mids]
     far_in = refs[9 + 2 * mids : 9 + 2 * mids + fars]
     stats = refs[9 + 2 * mids + fars : 10 + 3 * mids + fars]
-    out_k, out_v, mid_rows, far_rows = refs[10 + 3 * mids + fars :]
+    out_k, out_v, mid_rows, far_rows, work = refs[10 + 3 * mids + fars :]
     step = pl.program_id(0)
     ring, level = lax.axis_index("seq"), lax.axis_index("lvl")
-    rows = out_k.shape[0]
     mid_count, far_count = kv.shape[0], far_own.shape[1]
 
     @pl.when(step == 0)
     def _():
         mid_rows[...] = jnp.concatenate([ref[:, :mid_count] for ref in stats], axis=1)
-        for slot in range(fars):
-            source = mid_count + (slot // 2 + slot % 2 * (fars // 2)) * far_count
+        for slot in range(rings):
+            source = mid_count + slot * far_count
             for low, ref in enumerate(stats):
                 place = (slot * levels + low) * far_count
                 far_rows[:, place : place + far_count] = ref[:, source : source + far_count]
@@ -491,9 +485,13 @@
             queries, cots = stack(far_in, low), stack(far_in, high)
             keys, vals = far_own[0, :, low], far_own[0, :, high]
             far = key_side(scale, keys, vals, queries, cots, hide, far_rows, head, heads)
-            whole = spread(rows, [mid_off[head], far_off[head]], [mid, far])
-            out_k[:, cut] = ((dk[:, cut] + whole[:, :LANES]) * scale).astype(BF16)
-            out_v[:, cut] = (dv[:, cut] + whole[:, LANES:]).astype(BF16)
+            one, two = 2 * at, 2 * at + 1
+            work[one], work[two] = dk[:, cut], dv[:, cut]
+            for where, first in ((one, 0), (two, LANES)):
+                put_rows(work, where, mid_off[head], mid[:, first : first + LANES])
+                put_rows(work, where, far_off[head], far[:, first : first + LANES])
+            out_k[:, cut] = (work[one] * scale).astype(BF16)
+            out_v[:, cut] = work[two].astype(BF16)
 
     @pl.when(step == 0)
     def _():
@@ -502,6 +500,20 @@
     @pl.when(step == 1)
     def _():
         finish(1, first_in, dk_b, dv_b)
+
+
+def join_kernel(*refs):
+    out, first = refs[-1], 0
+    for ref in refs[:-2]:
+        out[first : first + ref.shape[0], :] = ref[...]
+        first += ref.shape[0]
+
+
+def join(pieces, after):
+    rows = sum(piece.shape[0] for piece in pieces)
+    out = jax.ShapeDtypeStruct((rows, pieces[0].shape[1]), BF16)
+    ins = [(fixed(piece.shape), piece) for piece in pieces + [after]]
+    return call(join_kernel, 1, ins, [(fixed(out.shape), out)], [])[0]
 
 
 def pack_kernel(*refs):
@@ -522,7 +534,7 @@
     return lax.ppermute(array, axis, [(i, i ^ step) for i in range(size)])
 
 
-def call(kernel, steps, ins, outs, scratch, limit=LIMIT):
+def call(kernel, steps, ins, outs, scratch, limit=LIMIT, flops=0):
     specs, arrays = zip(*ins)
     out_specs, out_shapes = zip(*outs)
     return pl.pallas_call(
@@ -533,7 +545,7 @@
         out_shape=list(out_shapes),
         scratch_shapes=scratch,
         compiler_params=params(limit),
-        cost_estimate=pl.CostEstimate(flops=0, bytes_accessed=0, transcendentals=0),
+        cost_estimate=pl.CostEstimate(flops=flops, bytes_accessed=0, transcendentals=0),
     )(*arrays)
 
 
@@ -568,7 +580,12 @@
         [],
     )
     far_level = [far] + [swap(far, "lvl", levels, step) for step in range(1, levels)]
-    first_in = [swap(pays[step - 1], "lvl", levels, step) for step in range(1, levels)]
+    first = list(pays[:mids])
+    first_in = [None] * mids
+    first_in[1] = swap(first[1], "lvl", levels, 2)
+    for step in range(1, levels):
+        if step != 2:
+            first_in[step - 1] = swap(first[step - 1], "lvl", levels, step)
 
     stat, stat_spec = shape((rows, LANES), F32), fixed((rows, LANES))
     half = shape((rows, flat // 2), F32)
@@ -599,7 +616,9 @@
 
     inputs = (queries, keys, values, grad_out)
     near_a = near_call(0, inputs)
-    far_level, near_a = lax.optimization_barrier((far_level, near_a))
+    inputs, near_a = lax.optimization_barrier((inputs, near_a))
+    near_b = near_call(1, inputs)
+    far_level, near_b = lax.optimization_barrier((far_level, near_b))
     ring_bits = rings.bit_length() - 1
     col_shape = shape((block, 2 * flat), BF16)
     col_kv, col_qg, *ring_pays = call(
@@ -608,49 +627,49 @@
         [(fixed(piece.shape), piece) for piece in far_level],
         [(fixed(col_shape.shape), col_shape)] * (2 + ring_bits),
         [],
+        flops=4000000000,
     )
     far_ring = [None] * rings
     for step in range(2, rings, 2):
         far_ring[step] = swap(ring_pays[step.bit_length() - 1], "seq", rings, step)
-    inputs, col_kv = lax.optimization_barrier((inputs, col_kv))
-    near_b = near_call(1, inputs)
-    far_ring[2::2], near_b = lax.optimization_barrier((far_ring[2::2], near_b))
-    far_ring[1] = swap(ring_pays[0], "seq", rings, 1)
-    for step in range(3, rings, 2):
-        far_ring[step] = swap(far_ring[step - 1], "seq", rings, 1)
+    pieces = [ring_pays[0]] + far_ring[2::2]
+    here = first_in[0][:16, :LANES] + first_in[1][:16, :LANES] + first_in[2][:16, :LANES]
+    across = swap(join(pieces, swap(here, "seq", rings, 1)), "seq", rings, 1)
 
     col_spec = columns(block, GROUP * 2 * width)
     first_list = [(half_spec, piece) for piece in first_in]
-    far_rest = [(col_spec, piece) for piece in far_ring[1:]]
+    far_rest = [(col_spec, piece) for piece in far_ring[2::2]]
+    across_spec = columns(across.shape[0], GROUP * 2 * width)
+    far_rest.append((across_spec, across))
     far_kv, far_qg = [(col_spec, col_kv)] + far_rest, [(col_spec, col_qg)] + far_rest
+    fars = len(far_kv)
     mid_own = [(mid_spec, kv), (mid_spec, qg)]
     own = mid_own + [(far_spec, far)]
     mid_stat, far_stat = result(mid_count, LANES), result(far_count, LANES)
-    level_stats = call(
-        functools.partial(level_stats_kernel, scale, levels, mids, rings),
+    mid_stats = call(
+        functools.partial(mid_stats_kernel, scale, levels, mids),
         steps,
-        own + first_list + far_kv,
-        [mid_stat] * 2 + [far_stat] * 2 + [result(2 * GROUP, mid_count)] * mids,
+        mid_own + first_list,
+        [mid_stat] * 2 + [result(2 * GROUP, mid_count)] * mids,
         [],
     )
-    backs = [swap(level_stats[3 + step], "lvl", levels, step) for step in range(1, levels)]
-    level_stats = level_stats[:4]
-    later, backs = lax.optimization_barrier((pays[mids + 1 :], backs))
-    second = [pays[mids]] + list(later)
-    second[0], first_in[-1] = lax.optimization_barrier((second[0], first_in[-1]))
-    second_in = [swap(second[step - 1], "lvl", levels, step) for step in range(1, levels)]
-    second_list = [(half_spec, piece) for piece in second_in]
-    mid_base, far_base = call(
-        functools.partial(level_base_kernel, scale, levels, mids, rings),
+    backs = [swap(mid_stats[1 + step], "lvl", levels, step) for step in range(1, levels)]
+    second = list(pays[mids:])
+    mid_base, far_base, *far_stats = call(
+        functools.partial(level_base_kernel, scale, levels, mids, fars),
         steps,
-        own + [whole(array) for array in level_stats] + first_list + far_kv,
+        own + [whole(array) for array in mid_stats[:2]] + first_list + far_kv,
         [
             (fixed((mid_count, flat)), shape((mid_count, flat), F32)),
             (columns(far_count, GROUP * 2 * width), shape((far_count, 2 * flat), F32)),
-        ],
+        ]
+        + [far_stat] * 2,
         [],
     )
-    backs, mid_base = lax.optimization_barrier((backs, mid_base))
+    level_stats = [*mid_stats[:2], *far_stats]
+    second, backs, mid_base = lax.optimization_barrier((second, backs, mid_base))
+    second_in = [swap(second[step - 1], "lvl", levels, step) for step in range(1, levels)]
+    second_list = [(half_spec, piece) for piece in second_in]
     merged = call(
         functools.partial(merge_kernel, heads, mids),
         1,
@@ -676,7 +695,7 @@
             + [whole(array) for array in merged[:6]]
             + [whole(mid_base), (far_spec, far_base)],
             [result(rows, flat // 2)] * 3,
-            [],
+            [pltpu.VMEM((GROUP, rows, LANES), F32)],
         )
 
     grads_a = near_grads(0, near_a)
@@ -697,11 +716,11 @@
         + [whole(array) for array in (grads_a[0], grads_b[0], mid_log, mid_dot)]
         + second_list,
         [(tile, out)],
-        [],
+        [pltpu.VMEM((GROUP, rows, LANES), F32)],
     )
     sent_in, grad_query = lax.optimization_barrier((sent_in, grad_query))
     grad_key, grad_value = call(
-        functools.partial(keys_kernel, scale, heads, levels, mids, rings),
+        functools.partial(keys_kernel, scale, heads, levels, rings, mids, fars),
         steps,
         scalars
         + own
@@ -711,7 +730,7 @@
         + far_qg
         + [whole(piece) for piece in sent_in],
         [(tile, out)] * 2,
-        [pltpu.VMEM((2 * heads, rows), F32)] * 2,
+        [pltpu.VMEM((2 * heads, rows), F32)] * 2 + [pltpu.VMEM((2 * GROUP, rows, LANES), F32)],
     )
     return grad_query, grad_key, grad_value
 

time: 96.6 us -> 90.9 us (0.941)
  waiting for transfers between devices: 27.5 us -> 16.5 us
  starting transfers between devices: 28.9 us -> 34.6 us
    ppermute x26 -> x24, waiting for transfers between devices: 27.5 us -> 16.5 us  [swap(): return lax.ppermute(array, axis, [(i, i ^ step) for i in range(size)])]
    ppermute x26 -> x24, starting transfers between devices: 28.9 us -> 34.6 us  [swap(): return lax.ppermute(array, axis, [(i, i ^ step) for i in range(size)])]
    pallas_call x13 -> x14, Pallas kernels: 37.6 us -> 37.1 us  [call(): pl.pallas_call(kernel, grid=(steps,), in_specs=list(specs), out_specs=lis...]
  transfers between devices with their start and end apart: 26 -> 24, of which waited for: 8 -> 7; matrix products, arithmetic and copies ran while one was open for 0% -> 0% of each run, Pallas kernels for 28% -> 29%
where the time goes in v5:
time: 90.9 us; the launch traced here: 90.6 us
  Pallas kernels  37.1 us (41%)
  starting transfers between devices  34.6 us (38%)
  waiting for transfers between devices  16.5 us (18%)
  local copies, waits for them, and re-layouts  1.6 us (2%)
    pallas_call x14, Pallas kernels, call(): pl.pallas_call(kernel, grid=(steps,), in_specs=list(specs), out_specs=lis...  37.1 us
    ppermute x24, starting transfers between devices, swap(): return lax.ppermute(array, axis, [(i, i ^ step) for i in range(size)])  34.6 us
    ppermute x24, waiting for transfers between devices, swap(): return lax.ppermute(array, axis, [(i, i ^ step) for i in range(size)])  16.5 us
  transfers between devices with their start and end apart: 24, of which 7 were waited for; matrix products, arithmetic and copies ran while one was open for 0% of the time, Pallas kernels for 29%

profile of v5, /device:TPU:0, one launch (start us, length us, event | category | flops | bytes accessed | tf_op | source)
XLA Modules:
  0.0 90.6 jit_solution(1141907424316342664)
XLA Ops:
  0.7 0.0 copy-start.4
  0.7 0.8 copy-done.4
  1.5 0.8 copy-done.6
  2.3 3.5 %shard_map.86 = (bf16[128,2048]{1,0:T(8,128)(2,1)S(1)}, bf16[128,2048]{1,0:T(8,128)(2,1)S(1)}, bf16[2,16,2048]{2,1,0:T(8,128)(2,1)S(1)}, bf16[128,1024]{1,0:T(8,...) custom-call(s32[8]{0:T(128)S(1)} %copy-done.4, ...), custom_call_target="tpu_custom_call" | custom-call | tf_op jit(solution)/shard_map/pallas_call | solution.py:540
  5.8 5.1 %collective-permute-start.2 = (bf16[2,16,2048]{2,1,0:T(8,128)(2,1)S(1)}, bf16[2,16,2048]{2,1,0:T(8,128)(2,1)S(1)}, u32[]{:S(2)}, u32[]{:S(2)}) collective-permute-start(bf16[2,16,2048]{2,1,0:T(8,128)(2,1)S(1)} %get-tuple-element.121.refs_0_.refs_2_.refs_4_), channel_id=1, source_target_pairs={{0,3},{1,2},{2,1},{3,0},{4,7},{5,6},{6,5},{7,4},{8,11},{9,10},{10,... | collective-permute-start | bytes 393224 | tf_op jit(solution)/shard_map/ppermute | solution.py:534
  10.9 0.0 collective-permute-start.1
  10.9 0.6 collective-permute-start
  11.5 1.4 %collective-permute-start.3 = (bf16[128,1024]{1,0:T(8,128)(2,1)S(1)}, bf16[128,1024]{1,0:T(8,128)(2,1)S(1)}, u32[]{:S(2)}, u32[]{:S(2)}) collective-permute-start(bf16[128,1024]{1,0:T(8,128)(2,1)S(1)} %get-tuple-element.116), channel_id=1, source_target_pairs={{0,1},{1,0},{2,3},{3,2},{4,5},{5,4},{6,7},{7,6},{8,9},{9,8},{10,11... | collective-permute-start | bytes 786440 | tf_op jit(solution)/shard_map/ppermute | solution.py:534
  12.9 2.9 %collective-permute-start.4 = (bf16[128,1024]{1,0:T(8,128)(2,1)S(1)}, bf16[128,1024]{1,0:T(8,128)(2,1)S(1)}, u32[]{:S(2)}, u32[]{:S(2)}) collective-permute-start(bf16[128,1024]{1,0:T(8,128)(2,1)S(1)} %get-tuple-element.117), channel_id=1, source_target_pairs={{0,2},{1,3},{2,0},{3,1},{4,6},{5,7},{6,4},{7,5},{8,10},{9,11},{10,... | collective-permute-start | bytes 786440 | tf_op jit(solution)/shard_map/ppermute | solution.py:534
  15.8 5.0 %shard_map.85 = (f32[512,128]{1,0:T(8,128)S(1)}, f32[512,128]{1,0:T(8,128)S(1)}, bf16[4,512,512]{2,1,0:T(8,128)(2,1)S(1)}, bf16[4,512,512]{2,1,0:T(8,128)(2,1)S(1)}, f32[512,1024]{1,0:T(8,128)S(1)}) custom-call(bf16[512,1024]{1,0:T(8,128)(2,1)S(1)} %copy-done, bf16[512,1024]{1,0:T(8,128)(2,1)S(1)} %copy-done.2, bf16[512,1024]{1,0:T(8,128)(2,1)S(1)} %copy-done.3, ...), custom_call_target="tpu_custom_call" | custom-call | tf_op jit(solution)/shard_map/pallas_call | solution.py:540
  20.8 5.0 %shard_map.87 = (f32[512,128]{1,0:T(8,128)S(1)}, f32[512,128]{1,0:T(8,128)S(1)}, bf16[4,512,512]{2,1,0:T(8,128)(2,1)S(1)}, bf16[4,512,512]{2,1,0:T(8,128)(2,1)S(1)}, f32[512,1024]{1,0:T(8,128)S(1)}) custom-call(bf16[512,1024]{1,0:T(8,128)(2,1)S(1)} %copy-done, bf16[512,1024]{1,0:T(8,128)(2,1)S(1)} %copy-done.2, bf16[512,1024]{1,0:T(8,128)(2,1)S(1)} %copy-done.3, ...), custom_call_target="tpu_custom_call" | custom-call | tf_op jit(solution)/shard_map/pallas_call | solution.py:540
  25.8 0.0 collective-permute-done.2.refs_3_
  25.8 0.1 collective-permute-start.5
  26.0 0.0 collective-permute-done.1.refs_2_
  26.0 0.0 collective-permute-done.refs_1_
  26.0 0.3 shard_map.89
  26.3 1.7 %collective-permute-start.6 = (bf16[64,2048]{1,0:T(8,128)(2,1)S(1)}, bf16[64,2048]{1,0:T(8,128)(2,1)S(1)}, u32[]{:S(2)}, u32[]{:S(2)}) collective-permute-start(bf16[64,2048]{1,0:T(8,128)(2,1)S(1)} %get-tuple-element.126), channel_id=1, source_target_pairs={{0,8},{4,12},{8,0},{12,4},{16,24},{20,28},{24,16},{28,20},{1,9},{5... | collective-permute-start | bytes 786440 | tf_op jit(solution)/shard_map/ppermute | solution.py:534
  28.0 1.5 %collective-permute-start.8 = (bf16[64,2048]{1,0:T(8,128)(2,1)S(1)}, bf16[64,2048]{1,0:T(8,128)(2,1)S(1)}, u32[]{:S(2)}, u32[]{:S(2)}) collective-permute-start(bf16[64,2048]{1,0:T(8,128)(2,1)S(1)} %get-tuple-element.127), channel_id=1, source_target_pairs={{0,24},{4,28},{8,16},{12,20},{16,8},{20,12},{24,0},{28,4},{1,25},{... | collective-permute-start | bytes 786440 | tf_op jit(solution)/shard_map/ppermute | solution.py:534
  29.5 0.0 collective-permute-done.3.refs_2_.refs_5_.refs_9_
  29.5 1.5 %collective-permute-start.7 = (bf16[64,2048]{1,0:T(8,128)(2,1)S(1)}, bf16[64,2048]{1,0:T(8,128)(2,1)S(1)}, u32[]{:S(2)}, u32[]{:S(2)}) collective-permute-start(bf16[64,2048]{1,0:T(8,128)(2,1)S(1)} %get-tuple-element.127), channel_id=1, source_target_pairs={{0,16},{4,20},{8,24},{12,28},{16,0},{20,4},{24,8},{28,12},{1,17},{... | collective-permute-start | bytes 786440 | tf_op jit(solution)/shard_map/ppermute | solution.py:534
  31.0 8.8 %collective-permute-done.4.refs_3_.refs_6_.refs_10_ = bf16[128,1024]{1,0:T(8,128)(2,1)S(1)} collective-permute-done((bf16[128,1024]{1,0:T(8,128)(2,1)S(1)}, bf16[128,1024]{1,0:T(8,128)(2,1)S(1)}, u32[]{:S(2)}, u32[]{:S(2)}) %collective-permute-start.4) | collective-permute-done | bytes 262176 | tf_op jit(solution)/shard_map/ppermute | solution.py:534
  39.8 0.0 collective-permute-done.5.refs_4_.refs_7_.refs_11_
  39.8 0.1 collective-permute-start.9
  39.9 1.2 %collective-permute-done.9.refs_4_ = bf16[16,128]{1,0:T(8,128)(2,1)S(1)} collective-permute-done((bf16[16,128]{1,0:T(8,128)(2,1)S(1)}, bf16[16,128]{1,0:T(8,128)(2,1)S(1)}, u32[]{:S(2)}, u32[]{:S(2)}) %collective-permute-start.9) | collective-permute-done | bytes 4128 | tf_op jit(solution)/shard_map/ppermute | solution.py:534
  41.1 0.0 collective-permute-done.6.refs_1_.refs_9_.refs_16_
  41.1 0.0 collective-permute-done.8.refs_3_.refs_11_.refs_18_
  41.1 1.6 %collective-permute-done.7.refs_2_.refs_10_.refs_17_ = bf16[64,2048]{1,0:T(8,128)(2,1)S(1)} collective-permute-done((bf16[64,2048]{1,0:T(8,128)(2,1)S(1)}, bf16[64,2048]{1,0:T(8,128)(2,1)S(1)}, u32[]{:S(2)}, u32[]{:S(2)}) %collective-permute-start.7) | collective-permute-done | bytes 262176 | tf_op jit(solution)/shard_map/ppermute | solution.py:534
  42.7 0.1 shard_map.90
  42.8 0.1 collective-permute-start.10
  42.9 1.7 %shard_map.88 = (f32[128,128]{1,0:T(8,128)S(1)}, f32[128,128]{1,0:T(8,128)S(1)}, f32[8,128]{1,0:T(8,128)S(1)}, f32[8,128]{1,0:T(8,128)S(1)}, f32[8,128]{1,0:T(8,128)S(1)}) custom-call(bf16[128,2048]{1,0:T(8,128)(2,1)S(1)} %get-tuple-element.114.refs_0_.refs_1_.refs_2_, bf16[128,2048]{1,0:T(8,128)(2,1)S(1)} %get-tuple-element.115.refs_1_.refs_2_.refs_3_, ...), custom_call_target="tpu_custom_call" | custom-call | tf_op jit(solution)/shard_map/pallas_call | solution.py:540
  44.6 3.7 %collective-permute-start.11 = (f32[8,128]{1,0:T(8,128)S(1)}, f32[8,128]{1,0:T(8,128)S(1)}, u32[]{:S(2)}, u32[]{:S(2)}) collective-permute-start(f32[8,128]{1,0:T(8,128)S(1)} %get-tuple-element.134), channel_id=1, source_target_pairs={{0,1},{1,0},{2,3},{3,2},{4,5},{5,4},{6,7},{7,6},{8,9},{9,8},{10,11... | collective-permute-start | bytes 12296 | tf_op jit(solution)/shard_map/ppermute | solution.py:534
  48.3 1.1 %collective-permute-start.12 = (f32[8,128]{1,0:T(8,128)S(1)}, f32[8,128]{1,0:T(8,128)S(1)}, u32[]{:S(2)}, u32[]{:S(2)}) collective-permute-start(f32[8,128]{1,0:T(8,128)S(1)} %get-tuple-element.135), channel_id=1, source_target_pairs={{0,2},{1,3},{2,0},{3,1},{4,6},{5,7},{6,4},{7,5},{8,10},{9,11},{10,... | collective-permute-start | bytes 12296 | tf_op jit(solution)/shard_map/ppermute | solution.py:534
  49.4 1.4 %collective-permute-start.13 = (f32[8,128]{1,0:T(8,128)S(1)}, f32[8,128]{1,0:T(8,128)S(1)}, u32[]{:S(2)}, u32[]{:S(2)}) collective-permute-start(f32[8,128]{1,0:T(8,128)S(1)} %get-tuple-element.136), channel_id=1, source_target_pairs={{0,3},{1,2},{2,1},{3,0},{4,7},{5,6},{6,5},{7,4},{8,11},{9,10},{10,... | collective-permute-start | bytes 12296 | tf_op jit(solution)/shard_map/ppermute | solution.py:534
  50.7 0.0 collective-permute-done.10.refs_12_.refs_19_
  50.8 5.2 %shard_map.91 = (f32[128,1024]{1,0:T(8,128)S(1)}, f32[16,2048]{1,0:T(8,128)S(1)}, f32[16,128]{1,0:T(8,128)S(1)}, f32[16,128]{1,0:T(8,128)S(1)}) custom-call(bf16[128,2048]{1,0:T(8,128)(2,1)S(1)} %get-tuple-element.114.refs_0_.refs_1_.refs_2_, bf16[128,2048]{1,0:T(8,128)(2,1)S(1)} %get-tuple-element.115.refs_1_.refs_2_.refs_3_, ...), custom_call_target="tpu_custom_call" | custom-call | tf_op jit(solution)/shard_map/pallas_call | solution.py:540
  56.0 0.0 collective-permute-done.11.refs_10_
  56.0 0.0 collective-permute-done.12.refs_11_
  56.0 0.0 collective-permute-done.13.refs_12_
  56.0 1.1 %collective-permute-start.21 = (bf16[128,1024]{1,0:T(8,128)(2,1)S(1)}, bf16[128,1024]{1,0:T(8,128)(2,1)S(1)}, u32[]{:S(2)}, u32[]{:S(2)}) collective-permute-start(bf16[128,1024]{1,0:T(8,128)(2,1)S(1)} %get-tuple-element.172), channel_id=1, source_target_pairs={{0,1},{1,0},{2,3},{3,2},{4,5},{5,4},{6,7},{7,6},{8,9},{9,8},{10,11... | collective-permute-start | bytes 786440 | tf_op jit(solution)/shard_map/ppermute | solution.py:534
  57.1 2.0 %collective-permute-start.22 = (bf16[128,1024]{1,0:T(8,128)(2,1)S(1)}, bf16[128,1024]{1,0:T(8,128)(2,1)S(1)}, u32[]{:S(2)}, u32[]{:S(2)}) collective-permute-start(bf16[128,1024]{1,0:T(8,128)(2,1)S(1)} %get-tuple-element.173), channel_id=1, source_target_pairs={{0,2},{1,3},{2,0},{3,1},{4,6},{5,7},{6,4},{7,5},{8,10},{9,11},{10,... | collective-permute-start | bytes 786440 | tf_op jit(solution)/shard_map/ppermute | solution.py:534
  59.1 1.4 %collective-permute-start.23 = (bf16[128,1024]{1,0:T(8,128)(2,1)S(1)}, bf16[128,1024]{1,0:T(8,128)(2,1)S(1)}, u32[]{:S(2)}, u32[]{:S(2)}) collective-permute-start(bf16[128,1024]{1,0:T(8,128)(2,1)S(1)} %get-tuple-element.174), channel_id=1, source_target_pairs={{0,3},{1,2},{2,1},{3,0},{4,7},{5,6},{6,5},{7,4},{8,11},{9,10},{10,... | collective-permute-start | bytes 786440 | tf_op jit(solution)/shard_map/ppermute | solution.py:534
  60.5 2.6 %shard_map.92 = (f32[512,128]{1,0:T(8,128)S(1)}, f32[512,128]{1,0:T(8,128)S(1)}, f32[128,128]{1,0:T(8,128)S(1)}, f32[128,128]{1,0:T(8,128)S(1)}, f32[16,128]{1,0...) custom-call(s32[8]{0:T(128)S(1)} %copy-done.4, ...), custom_call_target="tpu_custom_call" | custom-call | tf_op jit(solution)/shard_map/pallas_call | solution.py:540
  63.1 2.5 %collective-permute-start.16 = (f32[16,16]{1,0:T(8,128)S(1)}, f32[16,16]{1,0:T(8,128)S(1)}, u32[]{:S(2)}, u32[]{:S(2)}) collective-permute-start(f32[16,16]{1,0:T(8,128)S(1)} %get-tuple-element.157.refs_0_), channel_id=1, source_target_pairs={{0,24},{4,28},{8,16},{12,20},{16,8},{20,12},{24,0},{28,4},{1,25},{... | collective-permute-start | bytes 3080 | tf_op jit(solution)/shard_map/ppermute | solution.py:534
  65.5 0.5 collective-permute-start.15
  66.0 1.6 %collective-permute-done.16.refs_3_ = f32[16,16]{1,0:T(8,128)S(1)} collective-permute-done((f32[16,16]{1,0:T(8,128)S(1)}, f32[16,16]{1,0:T(8,128)S(1)}, u32[]{:S(2)}, u32[]{:S(2)}) %collective-permute-start.16) | collective-permute-done | bytes 1056 | tf_op jit(solution)/shard_map/ppermute | solution.py:534
  67.6 1.5 %collective-permute-start.14 = (f32[16,16]{1,0:T(8,128)S(1)}, f32[16,16]{1,0:T(8,128)S(1)}, u32[]{:S(2)}, u32[]{:S(2)}) collective-permute-start(f32[16,16]{1,0:T(8,128)S(1)} %get-tuple-element.157.refs_0_), channel_id=1, source_target_pairs={{0,8},{4,12},{8,0},{12,4},{16,24},{20,28},{24,16},{28,20},{1,9},{5... | collective-permute-start | bytes 3080 | tf_op jit(solution)/shard_map/ppermute | solution.py:534
  69.1 2.0 %shard_map.93 = (f32[512,512]{1,0:T(8,128)S(1)}, f32[512,512]{1,0:T(8,128)S(1)}, f32[512,512]{1,0:T(8,128)S(1)}) custom-call(s32[8]{0:T(128)S(1)} %copy-done.4, s32[8]{0:T(128)S(1)} %copy-done.7, bf16[512,1024]{1,0:T(8,128)(2,1)S(1)} %copy-done, bf16[512,1024]{1,0:T(8,128)(2,1)S(1)} %copy-done.1, bf16[4,512,512]{2,1,0:T(8,128)(2,1)S(1)} %get-tuple-element.143.soft_in, ...), custom_call_target="tpu_custom_call" | custom-call | tf_op jit(solution)/shard_map/pallas_call | solution.py:540
  71.2 0.0 collective-permute-done.15.refs_2_
  71.2 0.1 collective-permute-done.14.refs_1_
  71.3 0.1 shard_map.94.refs_1_
  71.4 0.0 collective-permute-start.17
  71.4 2.0 %shard_map.95 = (f32[512,512]{1,0:T(8,128)S(1)}, f32[512,512]{1,0:T(8,128)S(1)}, f32[512,512]{1,0:T(8,128)S(1)}) custom-call(s32[8]{0:T(128)S(1)} %copy-done.5, s32[8]{0:T(128)S(1)} %copy-done.7, bf16[512,1024]{1,0:T(8,128)(2,1)S(1)} %copy-done, bf16[512,1024]{1,0:T(8,128)(2,1)S(1)} %copy-done.1, bf16[4,512,512]{2,1,0:T(8,128)(2,1)S(1)} %get-tuple-element.161.soft_in, ...), custom_call_target="tpu_custom_call" | custom-call | tf_op jit(solution)/shard_map/pallas_call | solution.py:540
  73.4 0.0 collective-permute-done.17.refs_2_
  73.4 0.1 shard_map.96.refs_20_
  73.5 2.4 %collective-permute-start.20 = (f32[16,256]{1,0:T(8,128)S(1)}, f32[16,256]{1,0:T(8,128)S(1)}, u32[]{:S(2)}, u32[]{:S(2)}) collective-permute-start(f32[16,256]{1,0:T(8,128)S(1)} %shard_map.96.refs_20_), channel_id=1, source_target_pairs={{0,3},{1,2},{2,1},{3,0},{4,7},{5,6},{6,5},{7,4},{8,11},{9,10},{10,... | collective-permute-start | bytes 49160 | tf_op jit(solution)/shard_map/ppermute | solution.py:534
  75.9 0.0 collective-permute-start.19
  75.9 0.0 collective-permute-done.21.refs_7_.refs_12_
  75.9 1.9 %collective-permute-start.18 = (f32[16,256]{1,0:T(8,128)S(1)}, f32[16,256]{1,0:T(8,128)S(1)}, u32[]{:S(2)}, u32[]{:S(2)}) collective-permute-start(f32[16,256]{1,0:T(8,128)S(1)} %shard_map.96.refs_20_), channel_id=1, source_target_pairs={{0,1},{1,0},{2,3},{3,2},{4,5},{5,4},{6,7},{7,6},{8,9},{9,8},{10,11... | collective-permute-start | bytes 49160 | tf_op jit(solution)/shard_map/ppermute | solution.py:534
  77.9 0.9 %collective-permute-done.22.refs_8_.refs_13_ = bf16[128,1024]{1,0:T(8,128)(2,1)S(1)} collective-permute-done((bf16[128,1024]{1,0:T(8,128)(2,1)S(1)}, bf16[128,1024]{1,0:T(8,128)(2,1)S(1)}, u32[]{:S(2)}, u32[]{:S(2)}) %collective-permute-start.22) | collective-permute-done | bytes 262176 | tf_op jit(solution)/shard_map/ppermute | solution.py:534
  78.8 0.0 collective-permute-done.23.refs_9_.refs_14_
  78.8 2.7 %shard_map.97 = bf16[512,1024]{1,0:T(8,128)(2,1)} custom-call(s32[8]{0:T(128)S(1)} %copy-done.5, bf16[128,2048]{1,0:T(8,128)(2,1)S(1)} %get-tuple-element.114.refs_0_.refs_1_.refs_2_, bf16[128,2048]{1,0:T(8,128)(2,1)S(1)} %get-tuple-element.115.refs_1_.refs_2_.refs_3_, f32[512,512]{1,0:T(8,128)S(1)} %get-tuple-element.168.refs_3_, ...), custom_call_target="tpu_custom_call" | custom-call | tf_op jit(solution)/shard_map/pallas_call | solution.py:540
  81.6 0.0 collective-permute-done.20.refs_23_
  81.6 2.2 %collective-permute-done.19.refs_22_ = f32[16,256]{1,0:T(8,128)S(1)} collective-permute-done((f32[16,256]{1,0:T(8,128)S(1)}, f32[16,256]{1,0:T(8,128)S(1)}, u32[]{:S(2)}, u32[]{:S(2)}) %collective-permute-start.19) | collective-permute-done | bytes 16416 | tf_op jit(solution)/shard_map/ppermute | solution.py:534
  83.7 6.8 %shard_map.98 = (bf16[512,1024]{1,0:T(8,128)(2,1)}, bf16[512,1024]{1,0:T(8,128)(2,1)}) custom-call(s32[8]{0:T(128)S(1)} %copy-done.5, s32[8]{0:T(128)S(1)} %copy-done.7, bf16[128,2048]{1,0:T(8,128)(2,1)S(1)} %get-tuple-element.114.refs_0_.refs_1_.refs_2_, bf16[128,2048]{1,0:T(8,128)(2,1)S(1)} %get-tuple-element.115.refs_1_.refs_2_.refs_3_, ...), custom_call_target="tpu_custom_call" | custom-call | tf_op jit(solution)/shard_map/pallas_call | solution.py:540
  (15 shorter events, 0.0 us)
Async XLA Ops:
  0.6 15.2 %copy-start.1 = (bf16[512,1024]{1,0:T(8,128)(2,1)S(1)}, bf16[512,1024]{1,0:T(8,128)(2,1)}, u32[]{:S(2)}) copy-start(bf16[512,1024]{1,0:T(8,128)(2,1)} %g.8) | copy-start | bytes 3145732
  0.6 15.2 %copy-start = (bf16[512,1024]{1,0:T(8,128)(2,1)S(1)}, bf16[512,1024]{1,0:T(8,128)(2,1)}, u32[]{:S(2)}) copy-start(bf16[512,1024]{1,0:T(8,128)(2,1)} %q.8) | copy-start | bytes 3145732
  0.7 15.2 %copy-start.3 = (bf16[512,1024]{1,0:T(8,128)(2,1)S(1)}, bf16[512,1024]{1,0:T(8,128)(2,1)}, u32[]{:S(2)}) copy-start(bf16[512,1024]{1,0:T(8,128)(2,1)} %v.4) | copy-start | bytes 3145732
  0.7 0.8 copy-start.4
  1.5 0.8 copy-start.6
  2.2 13.6 %copy-start.2 = (bf16[512,1024]{1,0:T(8,128)(2,1)S(1)}, bf16[512,1024]{1,0:T(8,128)(2,1)}, u32[]{:S(2)}) copy-start(bf16[512,1024]{1,0:T(8,128)(2,1)} %k.4) | copy-start | bytes 3145732
  5.8 20.1 %collective-permute-start.2 = (bf16[2,16,2048]{2,1,0:T(8,128)(2,1)S(1)}, bf16[2,16,2048]{2,1,0:T(8,128)(2,1)S(1)}, u32[]{:S(2)}, u32[]{:S(2)}) collective-permute-start(bf16[2,16,2048]{2,1,0:T(8,128)(2,1)S(1)} %get-tuple-element.121.refs_0_.refs_2_.refs_4_), channel_id=1, source_target_pairs={{0,3},{1,2},{2,1},{3,0},{4,7},{5,6},{6,5},{7,4},{8,11},{9,10},{10,... | collective-permute-start | bytes 393224 | tf_op jit(solution)/shard_map/ppermute | solution.py:534
  10.9 15.1 %collective-permute-start.1 = (bf16[2,16,2048]{2,1,0:T(8,128)(2,1)S(1)}, bf16[2,16,2048]{2,1,0:T(8,128)(2,1)S(1)}, u32[]{:S(2)}, u32[]{:S(2)}) collective-permute-start(bf16[2,16,2048]{2,1,0:T(8,128)(2,1)S(1)} %get-tuple-element.121.refs_0_.refs_2_.refs_4_), channel_id=1, source_target_pairs={{0,2},{1,3},{2,0},{3,1},{4,6},{5,7},{6,4},{7,5},{8,10},{9,11},{10,... | collective-permute-start | bytes 393224 | tf_op jit(solution)/shard_map/ppermute | solution.py:534
  10.9 15.1 %collective-permute-start = (bf16[2,16,2048]{2,1,0:T(8,128)(2,1)S(1)}, bf16[2,16,2048]{2,1,0:T(8,128)(2,1)S(1)}, u32[]{:S(2)}, u32[]{:S(2)}) collective-permute-start(bf16[2,16,2048]{2,1,0:T(8,128)(2,1)S(1)} %get-tuple-element.121.refs_0_.refs_2_.refs_4_), channel_id=1, source_target_pairs={{0,1},{1,0},{2,3},{3,2},{4,5},{5,4},{6,7},{7,6},{8,9},{9,8},{10,11... | collective-permute-start | bytes 393224 | tf_op jit(solution)/shard_map/ppermute | solution.py:534
  11.5 18.0 %collective-permute-start.3 = (bf16[128,1024]{1,0:T(8,128)(2,1)S(1)}, bf16[128,1024]{1,0:T(8,128)(2,1)S(1)}, u32[]{:S(2)}, u32[]{:S(2)}) collective-permute-start(bf16[128,1024]{1,0:T(8,128)(2,1)S(1)} %get-tuple-element.116), channel_id=1, source_target_pairs={{0,1},{1,0},{2,3},{3,2},{4,5},{5,4},{6,7},{7,6},{8,9},{9,8},{10,11... | collective-permute-start | bytes 786440 | tf_op jit(solution)/shard_map/ppermute | solution.py:534
  12.9 26.9 %collective-permute-start.4 = (bf16[128,1024]{1,0:T(8,128)(2,1)S(1)}, bf16[128,1024]{1,0:T(8,128)(2,1)S(1)}, u32[]{:S(2)}, u32[]{:S(2)}) collective-permute-start(bf16[128,1024]{1,0:T(8,128)(2,1)S(1)} %get-tuple-element.117), channel_id=1, source_target_pairs={{0,2},{1,3},{2,0},{3,1},{4,6},{5,7},{6,4},{7,5},{8,10},{9,11},{10,... | collective-permute-start | bytes 786440 | tf_op jit(solution)/shard_map/ppermute | solution.py:534
  25.8 14.0 %collective-permute-start.5 = (bf16[128,1024]{1,0:T(8,128)(2,1)S(1)}, bf16[128,1024]{1,0:T(8,128)(2,1)S(1)}, u32[]{:S(2)}, u32[]{:S(2)}) collective-permute-start(bf16[128,1024]{1,0:T(8,128)(2,1)S(1)} %get-tuple-element.118), channel_id=1, source_target_pairs={{0,3},{1,2},{2,1},{3,0},{4,7},{5,6},{6,5},{7,4},{8,11},{9,10},{10,... | collective-permute-start | bytes 786440 | tf_op jit(solution)/shard_map/ppermute | solution.py:534
  26.3 14.8 %collective-permute-start.6 = (bf16[64,2048]{1,0:T(8,128)(2,1)S(1)}, bf16[64,2048]{1,0:T(8,128)(2,1)S(1)}, u32[]{:S(2)}, u32[]{:S(2)}) collective-permute-start(bf16[64,2048]{1,0:T(8,128)(2,1)S(1)} %get-tuple-element.126), channel_id=1, source_target_pairs={{0,8},{4,12},{8,0},{12,4},{16,24},{20,28},{24,16},{28,20},{1,9},{5... | collective-permute-start | bytes 786440 | tf_op jit(solution)/shard_map/ppermute | solution.py:534
  28.0 13.1 %collective-permute-start.8 = (bf16[64,2048]{1,0:T(8,128)(2,1)S(1)}, bf16[64,2048]{1,0:T(8,128)(2,1)S(1)}, u32[]{:S(2)}, u32[]{:S(2)}) collective-permute-start(bf16[64,2048]{1,0:T(8,128)(2,1)S(1)} %get-tuple-element.127), channel_id=1, source_target_pairs={{0,24},{4,28},{8,16},{12,20},{16,8},{20,12},{24,0},{28,4},{1,25},{... | collective-permute-start | bytes 786440 | tf_op jit(solution)/shard_map/ppermute | solution.py:534
  29.5 13.2 %collective-permute-start.7 = (bf16[64,2048]{1,0:T(8,128)(2,1)S(1)}, bf16[64,2048]{1,0:T(8,128)(2,1)S(1)}, u32[]{:S(2)}, u32[]{:S(2)}) collective-permute-start(bf16[64,2048]{1,0:T(8,128)(2,1)S(1)} %get-tuple-element.127), channel_id=1, source_target_pairs={{0,16},{4,20},{8,24},{12,28},{16,0},{20,4},{24,8},{28,12},{1,17},{... | collective-permute-start | bytes 786440 | tf_op jit(solution)/shard_map/ppermute | solution.py:534
  39.8 1.2 %collective-permute-start.9 = (bf16[16,128]{1,0:T(8,128)(2,1)S(1)}, bf16[16,128]{1,0:T(8,128)(2,1)S(1)}, u32[]{:S(2)}, u32[]{:S(2)}) collective-permute-start(bf16[16,128]{1,0:T(8,128)(2,1)S(1)} %slice_add_fusion), channel_id=1, source_target_pairs={{0,4},{4,0},{8,12},{12,8},{16,20},{20,16},{24,28},{28,24},{1,5},{5... | collective-permute-start | bytes 12296 | tf_op jit(solution)/shard_map/ppermute | solution.py:534
  42.8 8.0 %collective-permute-start.10 = (bf16[256,2048]{1,0:T(8,128)(2,1)S(1)}, bf16[256,2048]{1,0:T(8,128)(2,1)S(1)}, u32[]{:S(2)}, u32[]{:S(2)}) collective-permute-start(bf16[256,2048]{1,0:T(8,128)(2,1)S(1)} %shard_map.90), channel_id=1, source_target_pairs={{0,4},{4,0},{8,12},{12,8},{16,20},{20,16},{24,28},{28,24},{1,5},{5... | collective-permute-start | bytes 3145736 | tf_op jit(solution)/shard_map/ppermute | solution.py:534
  44.6 11.4 %collective-permute-start.11 = (f32[8,128]{1,0:T(8,128)S(1)}, f32[8,128]{1,0:T(8,128)S(1)}, u32[]{:S(2)}, u32[]{:S(2)}) collective-permute-start(f32[8,128]{1,0:T(8,128)S(1)} %get-tuple-element.134), channel_id=1, source_target_pairs={{0,1},{1,0},{2,3},{3,2},{4,5},{5,4},{6,7},{7,6},{8,9},{9,8},{10,11... | collective-permute-start | bytes 12296 | tf_op jit(solution)/shard_map/ppermute | solution.py:534
  48.3 7.7 %collective-permute-start.12 = (f32[8,128]{1,0:T(8,128)S(1)}, f32[8,128]{1,0:T(8,128)S(1)}, u32[]{:S(2)}, u32[]{:S(2)}) collective-permute-start(f32[8,128]{1,0:T(8,128)S(1)} %get-tuple-element.135), channel_id=1, source_target_pairs={{0,2},{1,3},{2,0},{3,1},{4,6},{5,7},{6,4},{7,5},{8,10},{9,11},{10,... | collective-permute-start | bytes 12296 | tf_op jit(solution)/shard_map/ppermute | solution.py:534
  49.4 6.7 %collective-permute-start.13 = (f32[8,128]{1,0:T(8,128)S(1)}, f32[8,128]{1,0:T(8,128)S(1)}, u32[]{:S(2)}, u32[]{:S(2)}) collective-permute-start(f32[8,128]{1,0:T(8,128)S(1)} %get-tuple-element.136), channel_id=1, source_target_pairs={{0,3},{1,2},{2,1},{3,0},{4,7},{5,6},{6,5},{7,4},{8,11},{9,10},{10,... | collective-permute-start | bytes 12296 | tf_op jit(solution)/shard_map/ppermute | solution.py:534
  50.8 9.7 %copy-start.7 = (s32[8]{0:T(128)S(1)}, s32[8]{0:T(128)}, u32[]{:S(2)}) copy-start(s32[8]{0:T(128)} %refs_1_.3) | copy-start | bytes 100
  56.0 19.9 %collective-permute-start.21 = (bf16[128,1024]{1,0:T(8,128)(2,1)S(1)}, bf16[128,1024]{1,0:T(8,128)(2,1)S(1)}, u32[]{:S(2)}, u32[]{:S(2)}) collective-permute-start(bf16[128,1024]{1,0:T(8,128)(2,1)S(1)} %get-tuple-element.172), channel_id=1, source_target_pairs={{0,1},{1,0},{2,3},{3,2},{4,5},{5,4},{6,7},{7,6},{8,9},{9,8},{10,11... | collective-permute-start | bytes 786440 | tf_op jit(solution)/shard_map/ppermute | solution.py:534
  57.1 21.7 %collective-permute-start.22 = (bf16[128,1024]{1,0:T(8,128)(2,1)S(1)}, bf16[128,1024]{1,0:T(8,128)(2,1)S(1)}, u32[]{:S(2)}, u32[]{:S(2)}) collective-permute-start(bf16[128,1024]{1,0:T(8,128)(2,1)S(1)} %get-tuple-element.173), channel_id=1, source_target_pairs={{0,2},{1,3},{2,0},{3,1},{4,6},{5,7},{6,4},{7,5},{8,10},{9,11},{10,... | collective-permute-start | bytes 786440 | tf_op jit(solution)/shard_map/ppermute | solution.py:534
  59.1 19.7 %collective-permute-start.23 = (bf16[128,1024]{1,0:T(8,128)(2,1)S(1)}, bf16[128,1024]{1,0:T(8,128)(2,1)S(1)}, u32[]{:S(2)}, u32[]{:S(2)}) collective-permute-start(bf16[128,1024]{1,0:T(8,128)(2,1)S(1)} %get-tuple-element.174), channel_id=1, source_target_pairs={{0,3},{1,2},{2,1},{3,0},{4,7},{5,6},{6,5},{7,4},{8,11},{9,10},{10,... | collective-permute-start | bytes 786440 | tf_op jit(solution)/shard_map/ppermute | solution.py:534
  63.1 4.6 %collective-permute-start.16 = (f32[16,16]{1,0:T(8,128)S(1)}, f32[16,16]{1,0:T(8,128)S(1)}, u32[]{:S(2)}, u32[]{:S(2)}) collective-permute-start(f32[16,16]{1,0:T(8,128)S(1)} %get-tuple-element.157.refs_0_), channel_id=1, source_target_pairs={{0,24},{4,28},{8,16},{12,20},{16,8},{20,12},{24,0},{28,4},{1,25},{... | collective-permute-start | bytes 3080 | tf_op jit(solution)/shard_map/ppermute | solution.py:534
  65.5 5.7 %collective-permute-start.15 = (f32[16,16]{1,0:T(8,128)S(1)}, f32[16,16]{1,0:T(8,128)S(1)}, u32[]{:S(2)}, u32[]{:S(2)}) collective-permute-start(f32[16,16]{1,0:T(8,128)S(1)} %get-tuple-element.157.refs_0_), channel_id=1, source_target_pairs={{0,16},{4,20},{8,24},{12,28},{16,0},{20,4},{24,8},{28,12},{1,17},{... | collective-permute-start | bytes 3080 | tf_op jit(solution)/shard_map/ppermute | solution.py:534
  67.6 3.7 %collective-permute-start.14 = (f32[16,16]{1,0:T(8,128)S(1)}, f32[16,16]{1,0:T(8,128)S(1)}, u32[]{:S(2)}, u32[]{:S(2)}) collective-permute-start(f32[16,16]{1,0:T(8,128)S(1)} %get-tuple-element.157.refs_0_), channel_id=1, source_target_pairs={{0,8},{4,12},{8,0},{12,4},{16,24},{20,28},{24,16},{28,20},{1,9},{5... | collective-permute-start | bytes 3080 | tf_op jit(solution)/shard_map/ppermute | solution.py:534
  69.1 2.3 %copy-start.5 = (s32[8]{0:T(128)S(1)}, s32[8]{0:T(128)}, u32[]{:S(2)}) copy-start(s32[8]{0:T(128)} %refs_0_.5) | copy-start | bytes 100
  71.4 2.0 %collective-permute-start.17 = (f32[16,64]{1,0:T(8,128)S(1)}, f32[16,64]{1,0:T(8,128)S(1)}, u32[]{:S(2)}, u32[]{:S(2)}) collective-permute-start(f32[16,64]{1,0:T(8,128)S(1)} %shard_map.94.refs_1_), channel_id=1, source_target_pairs={{0,4},{4,0},{8,12},{12,8},{16,20},{20,16},{24,28},{28,24},{1,5},{5... | collective-permute-start | bytes 12296 | tf_op jit(solution)/shard_map/ppermute | solution.py:534
  73.5 8.1 %collective-permute-start.20 = (f32[16,256]{1,0:T(8,128)S(1)}, f32[16,256]{1,0:T(8,128)S(1)}, u32[]{:S(2)}, u32[]{:S(2)}) collective-permute-start(f32[16,256]{1,0:T(8,128)S(1)} %shard_map.96.refs_20_), channel_id=1, source_target_pairs={{0,3},{1,2},{2,1},{3,0},{4,7},{5,6},{6,5},{7,4},{8,11},{9,10},{10,... | collective-permute-start | bytes 49160 | tf_op jit(solution)/shard_map/ppermute | solution.py:534
  75.9 7.8 %collective-permute-start.19 = (f32[16,256]{1,0:T(8,128)S(1)}, f32[16,256]{1,0:T(8,128)S(1)}, u32[]{:S(2)}, u32[]{:S(2)}) collective-permute-start(f32[16,256]{1,0:T(8,128)S(1)} %shard_map.96.refs_20_), channel_id=1, source_target_pairs={{0,2},{1,3},{2,0},{3,1},{4,6},{5,7},{6,4},{7,5},{8,10},{9,11},{10,... | collective-permute-start | bytes 49160 | tf_op jit(solution)/shard_map/ppermute | solution.py:534
  75.9 7.8 %collective-permute-start.18 = (f32[16,256]{1,0:T(8,128)S(1)}, f32[16,256]{1,0:T(8,128)S(1)}, u32[]{:S(2)}, u32[]{:S(2)}) collective-permute-start(f32[16,256]{1,0:T(8,128)S(1)} %shard_map.96.refs_20_), channel_id=1, source_target_pairs={{0,1},{1,0},{2,3},{3,2},{4,5},{5,4},{6,7},{7,6},{8,9},{9,8},{10,11... | collective-permute-start | bytes 49160 | tf_op jit(solution)/shard_map/ppermute | solution.py:534

commit v6 on v5

v6 whole, which is shorter than its diff:
```python
import functools

import jax
import jax.numpy as jnp
from jax import lax
from jax.experimental import pallas as pl
from jax.experimental.pallas import tpu as pltpu
from jax.sharding import PartitionSpec as P

F32 = jnp.float32
BF16 = jnp.bfloat16
LANES = 128
LOW = -1e30
MIB = 1024 * 1024
LIMIT = 22


def mm(a, b):
    return lax.dot_general(a, b, (((1,), (0,)), ((), ())), preferred_element_type=F32)


def mm_t(a, b):
    return lax.dot_general(a, b, (((1,), (1,)), ((), ())), preferred_element_type=F32)


def iota(shape, axis):
    return lax.broadcasted_iota(jnp.int32, shape, axis)


def params(limit):
    return pltpu.CompilerParams(
        vmem_limit_bytes=limit * MIB, dimension_semantics=("arbitrary",)
    )


def smem():
    return pl.BlockSpec(memory_space=pltpu.SMEM)


def columns(rows, width):
    return pl.BlockSpec((rows, width), lambda h: (0, h))


def fixed(shape):
    return pl.BlockSpec(shape, lambda h: (0,) * len(shape))


def pick_lane(ref, head):
    block = ref[...]
    return jnp.sum(jnp.where(iota(block.shape, 1) == head, block, 0.0), axis=1, keepdims=True)


def put_lane(ref, rows, head, value):
    block = ref[rows, :]
    ref[rows, :] = jnp.where(iota(block.shape, 1) == head, value, block)


def select_kernel(mid_off, far_off, q, k, v, g, kv, qg, far, *refs):
    per = q.shape[1] // LANES
    pays, work = refs[:-1], refs[-1]
    level = lax.axis_index("lvl")
    rows = q.shape[0]
    mid_count, far_count = kv.shape[0], far.shape[1]
    for at in range(per):
        head = pl.program_id(0) * per + at
        cut = slice(at * LANES, (at + 1) * LANES)
        mid_rows = pl.ds(mid_off[head], mid_count, stride=rows // mid_count)
        far_rows = pl.ds(far_off[head], far_count, stride=rows // far_count)
        for place, source in enumerate((k, v, q, g)):
            side, slot = divmod(place, 2)
            spot = 4 * at + place
            work[spot] = source[:, cut].astype(F32)
            wide = slice((2 * at + slot) * LANES, (2 * at + slot + 1) * LANES)
            (kv, qg)[side][:, wide] = work[spot, mid_rows, :].astype(BF16)
            far[side, :, wide] = work[spot, far_rows, :].astype(BF16)
    firsts, seconds = pays[: len(pays) // 2], pays[len(pays) // 2 :]
    for step, (first, second) in enumerate(zip(firsts, seconds), 1):
        upward = (level ^ step) > level

        @pl.when(upward & (pl.program_id(0) == 0))
        def _():
            first[...] = kv[...]

        @pl.when(upward & (pl.program_id(0) == 1))
        def _():
            second[...] = kv[...]

        @pl.when(jnp.logical_not(upward) & (pl.program_id(0) == 0))
        def _():
            second[...] = qg[...]

        @pl.when(jnp.logical_not(upward) & (pl.program_id(0) == 1))
        def _():
            first[...] = qg[...]


def near_kernel(scale, parts, q, k, v, g, stats, soft_out, slope_out, base, work):
    per = q.shape[1] // LANES
    work[...] = jnp.zeros_like(work)
    size = q.shape[0] // parts
    for at in range(per):
        cut = slice(at * LANES, (at + 1) * LANES)
        low, high = cuts(at)
        for part in range(parts):
            rows = slice(part * size, (part + 1) * size)
            width = (part + 1) * size
            scores = mm_t(q[rows, cut], k[:width, cut]) * scale
            grads = mm_t(g[rows, cut], v[:width, cut])
            seen = iota((size, width), 1) <= iota((size, width), 0) + part * size
            scores = jnp.where(seen, scores, LOW)
            peak = jnp.max(scores, axis=1, keepdims=True)
            weights = jnp.exp(scores - peak)
            total = jnp.sum(weights, axis=1, keepdims=True)
            soft = weights / total
            dot_part = jnp.sum(soft * grads, axis=1, keepdims=True)
            slopes = (soft * (grads - dot_part)).astype(BF16)
            soft = soft.astype(BF16)
            base[rows, low] = mm(slopes, k[:width, cut])
            base[rows, high] = mm(soft, k[:width, cut])
            soft_out[at, :width, rows] = soft.T
            slope_out[at, :width, rows] = slopes.T
            put_lane(work, rows, at, peak + jnp.log(total))
            put_lane(work, rows, per + at, dot_part)
    stats[...] = work[...].T[: 2 * per, :]


def row_stats(scores, grads):
    peak = jnp.max(scores, axis=1, keepdims=True)
    weights = jnp.exp(scores - peak)
    total = jnp.sum(weights, axis=1, keepdims=True)
    return peak + jnp.log(total), jnp.sum(weights * grads, axis=1, keepdims=True) / total


def mid_places(count, total, level):
    col = iota((count, total), 1)
    other = ((col >> (count.bit_length() - 1)) ^ level) * count + (col & (count - 1))
    return other, level * count + iota((count, total), 0)


def far_places(count, total, levels, level, ring):
    col = iota((count, total), 1)
    bits, level_bits = count.bit_length() - 1, levels.bit_length() - 1
    slot, ring_slot = (col >> bits) & (levels - 1), col >> (bits + level_bits)
    evens = total >> (bits + level_bits + 1)
    ring_slot = (ring_slot & (evens - 1)) * 2 + (ring_slot >> (evens.bit_length() - 1))
    other = ((ring_slot ^ ring) * levels + (slot ^ level)) * count + (col & (count - 1))
    return other, (ring * levels + level) * count + iota((count, total), 0)


def bias(seen):
    return jnp.where(seen, 0.0, LOW)


def stack(refs, cut):
    return jnp.concatenate([ref[:, cut] for ref in refs], axis=0)


def repeat_table(rows, count):
    return (iota((rows, count), 0) // (rows // count) == iota((rows, count), 1)).astype(F32)


def gather_table(rows, count):
    return (iota((count, rows), 1) // (rows // count) == iota((count, rows), 0)).astype(F32)


def column_kernel(levels, bits, *refs):
    pieces = refs[:levels]
    col_kv, col_qg = refs[levels : 2 + levels]
    pays = refs[2 + levels :]
    ring = lax.axis_index("seq")
    col_kv[...] = jnp.concatenate([piece[0] for piece in pieces], axis=0)
    col_qg[...] = jnp.concatenate([piece[1] for piece in pieces], axis=0)
    for bit in range(bits):
        upward = ((ring >> bit) & 1) == 0

        @pl.when(upward)
        def _():
            pays[bit][...] = col_kv[...]

        @pl.when(jnp.logical_not(upward))
        def _():
            pays[bit][...] = col_qg[...]


def cuts(at):
    low = slice(2 * at * LANES, (2 * at + 1) * LANES)
    return low, slice((2 * at + 1) * LANES, (2 * at + 2) * LANES)


def column_stats(scores, grads):
    peak = jnp.max(scores, axis=0, keepdims=True)
    weights = jnp.exp(scores - peak)
    total = jnp.sum(weights, axis=0, keepdims=True)
    return peak + jnp.log(total), jnp.sum(weights * grads, axis=0, keepdims=True) / total


def mid_stats_kernel(scale, levels, mids, *refs):
    per = refs[0].shape[1] // (2 * LANES)
    kv, qg = refs[:2]
    mid_in = refs[2 : 2 + mids]
    mlog, mdot = refs[2 + mids : 4 + mids]
    backs = refs[4 + mids :]
    step = pl.program_id(0)
    level = lax.axis_index("lvl")
    mid_count = kv.shape[0]
    every = slice(None)

    @pl.when(step == 0)
    def _():
        for ref in (mlog, mdot):
            ref[...] = jnp.zeros_like(ref)
        other, own = mid_places(mid_count, mid_count * levels, level)
        hide = bias(other <= own)
        for at in range(per):
            low, high = cuts(at)
            scores = mm_t(qg[:, low], stack((kv,) + mid_in, low)) * scale + hide
            grads = mm_t(qg[:, high], stack((kv,) + mid_in, high))
            log_part, dot_part = row_stats(scores, grads)
            put_lane(mlog, every, at, log_part)
            put_lane(mdot, every, at, dot_part)

    @pl.when(step == 1)
    def _():
        other, own = mid_places(mid_count, mid_count, level)
        hide = bias(other <= own)
        for at in range(per):
            low, high = cuts(at)
            scores = mm_t(qg[:, low], kv[:, low]) * scale + hide
            log_part, dot_part = row_stats(scores, mm_t(qg[:, high], kv[:, high]))
            put_lane(mlog, every, per + at, log_part)
            put_lane(mdot, every, per + at, dot_part)
            scores = mm_t(kv[:, low], stack(mid_in, low)) * scale
            log_part, dot_part = column_stats(scores, mm_t(kv[:, high], stack(mid_in, high)))
            for slot, back in enumerate(backs):
                where = slice(slot * mid_count, (slot + 1) * mid_count)
                back[at : at + 1, :] = log_part[:, where]
                back[per + at : per + at + 1, :] = dot_part[:, where]


def parts_of(block):
    high = block.astype(BF16)
    rest = block - high.astype(F32)
    middle = rest.astype(BF16)
    return jnp.concatenate([high, middle, (rest - middle.astype(F32)).astype(BF16)], axis=0)


def move(block, table):
    moved = mm(parts_of(block), table.astype(BF16))
    count = block.shape[0]
    return moved[:count] + moved[count : 2 * count] + moved[2 * count :]


def head_column(offsets, heads):
    row = iota((heads, 1), 0)
    values = jnp.zeros((heads, 1), jnp.int32)
    for head in range(heads):
        values = jnp.where(row == head, offsets[head], values)
    return values


def as_columns(blocks):
    height = sum(block.shape[0] for block in blocks)
    width = blocks[0].shape[1]
    fill = jnp.zeros((LANES - height, width), F32)
    whole = jnp.concatenate(blocks + [fill], axis=0)
    if width < LANES:
        whole = jnp.concatenate([whole, jnp.zeros((LANES, LANES - width), F32)], axis=1)
    return whole.T[:width, :]


def merge_kernel(heads, mids, *refs):
    per = heads // 2
    mid_off, far_off, rows_a, rows_b, mlog, mdot, flog, fdot = refs[:8]
    backs = refs[8 : 8 + mids]
    near_cols, mid_cols, far_cols, mid_sent, far_sent = refs[8 + mids :]
    level = lax.axis_index("lvl")
    rows, mid_count, far_count = rows_a.shape[1], mlog.shape[0], flog.shape[0]

    logs, dots = [mlog[...].T[:heads, :]], [mdot[...].T[:heads, :]]
    empty = jnp.zeros((heads - per, mid_count), F32)
    for slot, back in enumerate(backs, 1):
        hidden = jnp.where((slot ^ level) < level, 0.0, LOW)
        logs.append(jnp.concatenate([empty + LOW, back[:per, :] + hidden], axis=0))
        dots.append(jnp.concatenate([empty, back[per:, :]], axis=0))
    peak = functools.reduce(jnp.maximum, logs)
    weights = [jnp.exp(part - peak) for part in logs]
    whole = functools.reduce(jnp.add, weights)
    mid_logs = peak + jnp.log(whole)
    mid_dots = functools.reduce(jnp.add, [w * d for w, d in zip(weights, dots)]) / whole
    far_logs, far_dots = flog[...].T[:heads, :], fdot[...].T[:heads, :]

    lane = iota((heads, rows), 1)
    mid_here = (lane & (rows // mid_count - 1)) == head_column(mid_off, heads)
    far_here = (lane & (rows // far_count - 1)) == head_column(far_off, heads)
    mid_wide = move(jnp.concatenate([mid_logs, mid_dots], axis=0), gather_table(rows, mid_count))
    far_wide = move(jnp.concatenate([far_logs, far_dots], axis=0), gather_table(rows, far_count))
    near = jnp.concatenate([rows_a[:per, :], rows_b[:per, :]], axis=0)
    near_dots = jnp.concatenate([rows_a[per:, :], rows_b[per:, :]], axis=0)
    mid = jnp.where(mid_here, mid_wide[:heads], LOW)
    far = jnp.where(far_here, far_wide[:heads], LOW)
    peak = jnp.maximum(near, jnp.maximum(mid, far))
    near_part = jnp.exp(near - peak)
    mid, far = jnp.exp(mid - peak), jnp.exp(far - peak)
    whole = near_part + mid + far
    logs = peak + jnp.log(whole)
    dots = (near_part * near_dots + mid * mid_wide[heads:] + far * far_wide[heads:]) / whole
    near_cols[...] = as_columns([jnp.exp(near - logs), dots - near_dots])
    both = []
    for here, count in ((mid_here, mid_count), (far_here, far_count)):
        chosen = [jnp.where(here, logs, 0.0), jnp.where(here, dots, 0.0)]
        both.append(move(jnp.concatenate(chosen, axis=0), repeat_table(rows, count)))
    mid_sent[...], far_sent[...] = both
    log_rows, dot_rows = both[0][:heads], both[0][heads:]
    mid_cols[...] = as_columns(
        [jnp.exp(mid_logs - log_rows), dot_rows - mid_dots, log_rows, dot_rows]
    )
    log_rows, dot_rows = both[1][:heads], both[1][heads:]
    far_cols[...] = as_columns([jnp.exp(far_logs - log_rows), dot_rows - far_dots])


def row_side(scale, queries, cots, keys, vals, hide, logs, dots):
    scores = mm_t(queries, keys) * scale + hide
    soft = jnp.exp(scores - logs)
    slopes = soft * (mm_t(cots, vals) - dots)
    return soft.astype(BF16), slopes.astype(BF16)


def mid_queries(scale, levels, level, kv, qg, mid_in, mid_cols, at, head, heads):
    other, own = mid_places(kv.shape[0], kv.shape[0] * levels, level)
    low, high = cuts(at)
    keys, vals = stack((kv,) + mid_in, low), stack((kv,) + mid_in, high)
    logs, dots = pick_lane(mid_cols, 2 * heads + head), pick_lane(mid_cols, 3 * heads + head)
    hide = bias(other <= own)
    _, slopes = row_side(scale, qg[:, low], qg[:, high], keys, vals, hide, logs, dots)
    return mm(slopes, keys)


def key_side(scale, keys, vals, queries, cots, hide, stats, head, heads):
    logs, dots = stats[pl.ds(head, 1), :], stats[pl.ds(head + heads, 1), :]
    soft, slopes = row_side(scale, keys, vals, queries, cots, hide, logs, dots)
    return jnp.concatenate([mm(slopes, queries), mm(soft, cots)], axis=1)


def mid_keys(scale, levels, level, kv, qg, mid_in, stats, at, head, heads):
    other, own = mid_places(kv.shape[0], kv.shape[0] * levels, level)
    low, high = cuts(at)
    queries, cots = stack((qg,) + mid_in, low), stack((qg,) + mid_in, high)
    return key_side(
        scale, kv[:, low], kv[:, high], queries, cots, bias(other >= own), stats, head, heads
    )


def far_stats_kernel(scale, levels, total, fars, far_own, *refs):
    per = far_own.shape[2] // (2 * LANES)
    far_in = refs[:fars]
    far_base, flog, fdot = refs[fars:]
    step = pl.program_id(0)
    ring, level = lax.axis_index("seq"), lax.axis_index("lvl")
    every = slice(None)

    @pl.when(step == 0)
    def _():
        for ref in (flog, fdot):
            ref[...] = jnp.zeros_like(ref)

    other, own = far_places(far_own.shape[1], total, levels, level, ring)
    hide = bias(other <= own)
    for at in range(per):
        head = step * per + at
        low, high = cuts(at)
        keys = stack(far_in, low)
        scores = mm_t(far_own[1, :, low], keys) * scale + hide
        grads = mm_t(far_own[1, :, high], stack(far_in, high))
        peak = jnp.max(scores, axis=1, keepdims=True)
        weights = jnp.exp(scores - peak)
        whole = jnp.sum(weights, axis=1, keepdims=True)
        soft = weights / whole
        dots = jnp.sum(soft * grads, axis=1, keepdims=True)
        put_lane(flog, every, head, peak + jnp.log(whole))
        put_lane(fdot, every, head, dots)
        far_base[:, low] = mm((soft * (grads - dots)).astype(BF16), keys)
        far_base[:, high] = mm(soft.astype(BF16), keys)


def mid_base_kernel(scale, levels, mids, kv, qg, mlog, mdot, *refs):
    per = kv.shape[1] // (2 * LANES)
    mid_in, mid_base = refs[:mids], refs[mids]
    level = lax.axis_index("lvl")
    other, own = mid_places(kv.shape[0], kv.shape[0] * levels, level)
    hide = bias(other <= own)
    for at in range(per):
        low, high = cuts(at)
        keys, vals = stack((kv,) + mid_in, low), stack((kv,) + mid_in, high)
        logs, dots = pick_lane(mlog, at), pick_lane(mdot, at)
        soft, slopes = row_side(scale, qg[:, low], qg[:, high], keys, vals, hide, logs, dots)
        mid_base[:, low] = mm(slopes, keys)
        mid_base[:, high] = mm(soft, keys)


def far_raw_kernel(scale, levels, total, fars, far_own, *refs):
    per = far_own.shape[2] // (2 * LANES)
    far_in = refs[:fars]
    raw_scores, raw_grads = refs[fars:]
    ring, level = lax.axis_index("seq"), lax.axis_index("lvl")
    far_count = far_own.shape[1]
    other, own = far_places(far_count, total, levels, level, ring)
    hide = bias(other >= own)
    for at in range(per):
        low, high = cuts(at)
        rows = slice(at * far_count, (at + 1) * far_count)
        raw_scores[rows, :] = mm_t(far_own[0, :, low], stack(far_in, low)) * scale + hide
        raw_grads[rows, :] = mm_t(far_own[0, :, high], stack(far_in, high))


def put_rows(ref, at, offset, piece):
    count = piece.shape[0]
    rows = pl.ds(offset, count, stride=ref.shape[1] // count)
    ref[at, rows, :] += piece


def rescaled(base, at, cols, head, heads):
    low, high = cuts(at)
    factor, shift = pick_lane(cols, head), pick_lane(cols, heads + head)
    return factor * (base[:, low] - shift * base[:, high])


def near_grads_kernel(parts, group, heads, mid_off, far_off, q, g, soft_in, slope_in, base, *refs):
    per = q.shape[1] // LANES
    near_cols, mid_cols, far_cols = refs[:3]
    mid_base, far_base, out_q, out_k, out_v, work = refs[3:]
    rows = q.shape[0]
    size = rows // parts
    for at in range(per):
        head = group * per + at
        cut = slice(at * LANES, (at + 1) * LANES)
        low, high = cuts(at)
        factor, shift = pick_lane(near_cols, head), pick_lane(near_cols, heads + head)
        far = rescaled(far_base, at, far_cols, head, heads)
        work[at] = factor * (base[:, low] - shift * base[:, high])
        put_rows(work, at, far_off[head], far)
        if group == 0:
            mid = rescaled(mid_base, at, mid_cols, head, heads)
            put_rows(work, at, mid_off[head], mid)
        out_q[:, cut] = work[at]
        queries = factor * q[:, cut].astype(F32)
        shifted = (shift * queries).astype(BF16)
        queries = queries.astype(BF16)
        both = jnp.concatenate([(factor * g[:, cut].astype(F32)).astype(BF16), shifted], axis=1)
        for part in range(parts):
            keys = slice(part * size, (part + 1) * size)
            first = part * size
            value = mm(soft_in[at, keys, first:], both[first:])
            out_v[keys, cut] = value[:, :LANES]
            out_k[keys, cut] = mm(slope_in[at, keys, first:], queries[first:]) - value[:, LANES:]


def queries_kernel(scale, heads, levels, mids, *refs):
    per = heads // 2
    mid_off, kv, qg, dq_a, dq_b, mid_cols = refs[:6]
    mid_in, out_q, work = refs[6 : 6 + mids], refs[6 + mids], refs[7 + mids]
    level = lax.axis_index("lvl")

    @pl.when(pl.program_id(0) == 0)
    def _():
        out_q[...] = (dq_a[...] * scale).astype(BF16)

    @pl.when(pl.program_id(0) == 1)
    def _():
        for at in range(per):
            head = per + at
            cut = slice(at * LANES, (at + 1) * LANES)
            part = mid_queries(scale, levels, level, kv, qg, mid_in, mid_cols, at, head, heads)
            work[at] = dq_b[:, cut]
            put_rows(work, at, mid_off[head], part)
            out_q[:, cut] = (work[at] * scale).astype(BF16)


def keys_kernel(scale, heads, levels, rings, mids, seconds, fars, *refs):
    per = heads // 2
    mid_off, far_off, kv, qg, raw_scores, raw_grads, dk_a, dv_a, dk_b, dv_b = refs[:10]
    first_in, refs = refs[10 : 10 + mids], refs[10 + mids :]
    second_in, refs = refs[:seconds], refs[seconds:]
    far_in, refs = refs[:fars], refs[fars:]
    stats, refs = refs[: mids + 1], refs[mids + 1 :]
    out_k, out_v, mid_rows, far_rows, work = refs
    step = pl.program_id(0)
    level = lax.axis_index("lvl")
    mid_count, far_count = kv.shape[0], raw_scores.shape[0] // per

    @pl.when(step == 0)
    def _():
        mid_rows[...] = jnp.concatenate([ref[:, :mid_count] for ref in stats], axis=1)
        for slot in range(rings):
            source = mid_count + slot * far_count
            for low, ref in enumerate(stats):
                place = (slot * levels + low) * far_count
                far_rows[:, place : place + far_count] = ref[:, source : source + far_count]

    def finish(group, mid_in, dk, dv):
        for at in range(per):
            head = group * per + at
            cut = slice(at * LANES, (at + 1) * LANES)
            low, high = cuts(at)
            mid = mid_keys(scale, levels, level, kv, qg, mid_in, mid_rows, at, head, heads)
            queries, cots = stack(far_in, low), stack(far_in, high)
            rows = slice(at * far_count, (at + 1) * far_count)
            soft = jnp.exp(raw_scores[rows, :] - far_rows[pl.ds(head, 1), :])
            slopes = soft * (raw_grads[rows, :] - far_rows[pl.ds(head + heads, 1), :])
            far = [mm(slopes.astype(BF16), queries), mm(soft.astype(BF16), cots)]
            far = jnp.concatenate(far, axis=1)
            one, two = 2 * at, 2 * at + 1
            work[one], work[two] = dk[:, cut], dv[:, cut]
            for where, first in ((one, 0), (two, LANES)):
                put_rows(work, where, mid_off[head], mid[:, first : first + LANES])
                put_rows(work, where, far_off[head], far[:, first : first + LANES])
            out_k[:, cut] = (work[one] * scale).astype(BF16)
            out_v[:, cut] = work[two].astype(BF16)

    @pl.when(step == 0)
    def _():
        finish(0, second_in, dk_a, dv_a)

    @pl.when(step == 1)
    def _():
        finish(1, first_in, dk_b, dv_b)


def join_kernel(*refs):
    out, first = refs[-1], 0
    for ref in refs[:-2]:
        out[first : first + ref.shape[0], :] = ref[...]
        first += ref.shape[0]


def join(pieces, after):
    rows = sum(piece.shape[0] for piece in pieces)
    out = jax.ShapeDtypeStruct((rows, pieces[0].shape[1]), BF16)
    ins = [(fixed(piece.shape), piece) for piece in pieces + [after]]
    return call(join_kernel, 1, ins, [(fixed(out.shape), out)], [])[0]


def pack_kernel(*refs):
    out, first = refs[-1], 0
    for ref in refs[:-1]:
        out[:, first : first + ref.shape[1]] = ref[...]
        first += ref.shape[1]


def pack(pieces):
    width = sum(piece.shape[1] for piece in pieces)
    out = jax.ShapeDtypeStruct((pieces[0].shape[0], width), F32)
    ins = [(fixed(piece.shape), piece) for piece in pieces]
    return call(pack_kernel, 1, ins, [(fixed(out.shape), out)], [])[0]


def swap(array, axis, size, step):
    return lax.ppermute(array, axis, [(i, i ^ step) for i in range(size)])


def call(kernel, steps, ins, outs, scratch, limit=LIMIT, flops=0):
    specs, arrays = zip(*ins)
    out_specs, out_shapes = zip(*outs)
    return pl.pallas_call(
        kernel,
        grid=(steps,),
        in_specs=list(specs),
        out_specs=list(out_specs),
        out_shape=list(out_shapes),
        scratch_shapes=scratch,
        compiler_params=params(limit),
        cost_estimate=pl.CostEstimate(flops=flops, bytes_accessed=0, transcendentals=0),
    )(*arrays)


def local(queries, keys, values, grad_out, mid_offset, far_offset):
    rows, flat = queries.shape
    heads = mid_offset.shape[0]
    per = heads // 2
    width = flat // heads
    scale = width ** (-0.5)
    levels, rings = lax.axis_size("lvl"), lax.axis_size("seq")
    mid_count, far_count = rows // levels, rows // (levels * rings)
    block = far_count * levels
    shape = jax.ShapeDtypeStruct
    if width != LANES:
        raise ValueError("head width")
    parts = 2
    steps = heads // per
    tile = columns(rows, per * width)
    mid_spec = columns(mid_count, per * 2 * width)
    far_spec = pl.BlockSpec((2, far_count, per * 2 * width), lambda h: (0, 0, h))
    sources = [(tile, queries), (tile, keys), (tile, values), (tile, grad_out)]
    scalars = [(smem(), mid_offset), (smem(), far_offset)]
    mid_shape = shape((mid_count, 2 * flat), BF16)

    half_shape, half_spec = shape((mid_count, flat), BF16), fixed((mid_count, flat))
    mids = levels - 1

    kv, qg, far, *pays = call(
        select_kernel,
        steps,
        scalars + [(spec, pltpu.with_memory_space_constraint(x, pltpu.HBM)) for spec, x in sources],
        [(mid_spec, mid_shape)] * 2
        + [(far_spec, shape((2, far_count, 2 * flat), BF16))]
        + [(half_spec, half_shape)] * (2 * mids),
        [pltpu.VMEM((4 * per, rows, LANES), F32)],
    )
    far_level = [far] + [swap(far, "lvl", levels, step) for step in range(1, levels)]
    first = list(pays[:mids])
    first_in = [None] * mids
    first_in[1] = swap(first[1], "lvl", levels, 2)
    for step in range(1, levels):
        if step != 2:
            first_in[step - 1] = swap(first[step - 1], "lvl", levels, step)

    half = shape((rows, flat // 2), F32)
    square = shape((per, rows, rows), BF16)

    def group_tile(group):
        return pl.BlockSpec((rows, per * width), lambda h: (0, group))

    def group_sources(group, arrays):
        return [(group_tile(group), array) for array in arrays]

    def whole(array):
        return (fixed(array.shape), array)

    def result(*dims):
        return (fixed(dims), shape(dims, F32))

    def near_call(group, arrays):
        return call(
            functools.partial(near_kernel, scale, parts),
            1,
            group_sources(group, arrays),
            [result(2 * per, rows)]
            + [(fixed(square.shape), square)] * 2
            + [result(rows, flat)],
            [pltpu.VMEM((rows, LANES), F32)],
        )

    inputs = (queries, keys, values, grad_out)
    near_a = near_call(0, inputs)
    inputs, near_a = lax.optimization_barrier((inputs, near_a))
    near_b = near_call(1, inputs)
    far_level, near_b = lax.optimization_barrier((far_level, near_b))
    ring_bits = rings.bit_length() - 1
    col_shape = shape((block, 2 * flat), BF16)
    col_kv, col_qg, *ring_pays = call(
        functools.partial(column_kernel, levels, ring_bits),
        1,
        [(fixed(piece.shape), piece) for piece in far_level],
        [(fixed(col_shape.shape), col_shape)] * (2 + ring_bits),
        [],
        flops=4000000000,
    )
    far_ring = [None] * rings
    for step in range(2, rings, 2):
        far_ring[step] = swap(ring_pays[step.bit_length() - 1], "seq", rings, step)
    pieces = [ring_pays[0]] + far_ring[2::2]
    here = first_in[0][:16, :LANES] + first_in[1][:16, :LANES] + first_in[2][:16, :LANES]
    across = swap(join(pieces, swap(here, "seq", rings, 1)), "seq", rings, 1)

    col_spec = columns(block, per * 2 * width)
    first_list = [(half_spec, piece) for piece in first_in]
    far_rest = [(col_spec, piece) for piece in far_ring[2::2]]
    across_spec = columns(across.shape[0], per * 2 * width)
    far_rest.append((across_spec, across))
    far_kv, far_qg = [(col_spec, col_kv)] + far_rest, [(col_spec, col_qg)] + far_rest
    fars = len(far_kv)
    mid_own = [(mid_spec, kv), (mid_spec, qg)]
    own = mid_own + [(far_spec, far)]
    mid_stat, far_stat = result(mid_count, LANES), result(far_count, LANES)
    mid_stats = call(
        functools.partial(mid_stats_kernel, scale, levels, mids),
        steps,
        mid_own + first_list,
        [mid_stat] * 2 + [result(2 * per, mid_count)] * mids,
        [],
    )
    backs = [swap(mid_stats[1 + step], "lvl", levels, step) for step in range(1, levels)]
    second = list(pays[mids:])
    early, first_in = lax.optimization_barrier((second[1][: mid_count // 2], first_in))
    early = swap(early, "lvl", levels, 2)
    second[1] = second[1][mid_count // 2 :]
    far_base, *far_stats = call(
        functools.partial(far_stats_kernel, scale, levels, rows, fars),
        steps,
        own[2:] + far_kv,
        [(columns(far_count, per * 2 * width), shape((far_count, 2 * flat), F32))]
        + [far_stat] * 2,
        [],
    )
    level_stats = [*mid_stats[:2], *far_stats]
    group_rows = pl.BlockSpec((per * far_count, rows), lambda h: (h, 0))
    half_a = pl.BlockSpec((mid_count, per * 2 * width), lambda h: (0, 0))
    (mid_base,) = call(
        functools.partial(mid_base_kernel, scale, levels, mids),
        1,
        [(half_a, kv), (half_a, qg)]
        + [whole(array) for array in mid_stats[:2]]
        + [whole(piece) for piece in first_in],
        [result(mid_count, flat)],
        [],
    )
    raw_scores, raw_grads = call(
        functools.partial(far_raw_kernel, scale, levels, rows, fars),
        steps,
        own[2:] + far_qg,
        [(group_rows, shape((heads * far_count, rows), F32))] * 2,
        [],
    )
    waited = (second, backs, far_base, early)
    second, backs, far_base, early = lax.optimization_barrier(waited)
    second_in = [swap(second[step - 1], "lvl", levels, step) for step in range(1, levels)]
    second_in.insert(1, early)
    second_list = [whole(piece) for piece in second_in]
    near_cols, mid_cols, far_cols, mid_sent, far_sent = call(
        functools.partial(merge_kernel, heads, mids),
        1,
        scalars + [whole(array) for array in [near_a[0], near_b[0], *level_stats, *backs]],
        [result(rows, LANES), mid_stat, far_stat]
        + [result(2 * heads, mid_count), result(2 * heads, far_count)],
        [],
    )
    near_sent = [far_sent] + [swap(far_sent, "seq", rings, step) for step in range(2, rings, 2)]

    def near_grads(group, near):
        far_spec = pl.BlockSpec((far_count, per * 2 * width), lambda h: (0, group))
        return call(
            functools.partial(near_grads_kernel, parts, group, heads),
            1,
            scalars
            + group_sources(group, (queries, grad_out))
            + [whole(array) for array in near[1:]]
            + [whole(array) for array in (near_cols, mid_cols, far_cols)]
            + [whole(mid_base), (far_spec, far_base)],
            [result(rows, flat // 2)] * 3,
            [pltpu.VMEM((per, rows, LANES), F32)],
        )

    grads_a = near_grads(0, near_a)
    near_sent, grads_a = lax.optimization_barrier((near_sent, grads_a))
    near_sent = pack(near_sent)
    other_sent = swap(near_sent, "seq", rings, 1)
    grads_b = near_grads(1, near_b)
    other_sent, grads_b = lax.optimization_barrier((other_sent, grads_b))
    sent = pack([mid_sent, near_sent, other_sent])
    sent_in = [sent] + [swap(sent, "lvl", levels, step) for step in range(1, levels)]
    out = shape((rows, flat), BF16)
    group_mid = pl.BlockSpec((mid_count, per * 2 * width), lambda h: (0, 1))
    (grad_query,) = call(
        functools.partial(queries_kernel, scale, heads, levels, len(second_in)),
        steps,
        scalars[:1]
        + [(group_mid, kv), (group_mid, qg)]
        + [whole(array) for array in (grads_a[0], grads_b[0], mid_cols)]
        + second_list,
        [(tile, out)],
        [pltpu.VMEM((per, rows, LANES), F32)],
    )
    sent_in, grad_query = lax.optimization_barrier((sent_in, grad_query))
    grad_key, grad_value = call(
        functools.partial(keys_kernel, scale, heads, levels, rings, mids, len(second_in), fars),
        steps,
        scalars
        + mid_own
        + [(group_rows, array) for array in (raw_scores, raw_grads)]
        + [whole(array) for array in (*grads_a[1:], *grads_b[1:])]
        + first_list
        + second_list
        + far_qg
        + [whole(piece) for piece in sent_in],
        [(tile, out)] * 2,
        [pltpu.VMEM((2 * heads, rows), F32)] * 2 + [pltpu.VMEM((2 * per, rows, LANES), F32)],
    )
    return grad_query, grad_key, grad_value


def solution(mesh):
    row_spec = P(("seq", "lvl"), None)
    return jax.shard_map(
        local,
        mesh=mesh,
        in_specs=(row_spec, row_spec, row_spec, row_spec, P(), P()),
        out_specs=(row_spec, row_spec, row_spec),
        check_vma=False,
    )
```

time: 90.9 us -> 87.6 us (0.964)
  Pallas kernels: 37.1 us -> 34.8 us
  waiting for transfers between devices: 16.5 us -> 14.9 us
    pallas_call x14 -> x16, Pallas kernels: 37.1 us -> 34.8 us  [call(): pl.pallas_call(kernel, grid=(steps,), in_specs=list(specs), out_specs=lis...]
    ppermute x24 -> x25, waiting for transfers between devices: 16.5 us -> 14.9 us  [swap(): return lax.ppermute(array, axis, [(i, i ^ step) for i in range(size)])]
    ppermute x24 -> x25, starting transfers between devices: 34.6 us -> 35.2 us  [swap(): return lax.ppermute(array, axis, [(i, i ^ step) for i in range(size)])]
  transfers between devices with their start and end apart: 24 -> 25, of which waited for: 7 -> 6; matrix products, arithmetic and copies ran while one was open for 0% -> 0% of each run, Pallas kernels for 29% -> 29%
where the time goes in v6:
time: 87.6 us; the launch traced here: 87.4 us
  starting transfers between devices  35.2 us (40%)
  Pallas kernels  34.8 us (40%)
  waiting for transfers between devices  14.9 us (17%)
  local copies, waits for them, and re-layouts  1.63 us (2%)
  between operations  0.91 us (1%)
    ppermute x25, starting transfers between devices, swap(): return lax.ppermute(array, axis, [(i, i ^ step) for i in range(size)])  35.2 us
    pallas_call x16, Pallas kernels, call(): pl.pallas_call(kernel, grid=(steps,), in_specs=list(specs), out_specs=lis...  34.8 us
    ppermute x25, waiting for transfers between devices, swap(): return lax.ppermute(array, axis, [(i, i ^ step) for i in range(size)])  14.9 us
  transfers between devices with their start and end apart: 25, of which 6 were waited for; matrix products, arithmetic and copies ran while one was open for 0% of the time, Pallas kernels for 29%

profile of v6, /device:TPU:0, one launch (start us, length us, event | category | flops | bytes accessed | tf_op | source)
XLA Modules:
  0.0 87.4 jit_solution(3908263544070670785)
XLA Ops:
  0.7 0.0 copy-start.4
  0.7 0.8 copy-done.4
  1.5 0.8 copy-done.6
  2.3 3.3 %shard_map.86 = (bf16[128,2048]{1,0:T(8,128)(2,1)S(1)}, bf16[128,2048]{1,0:T(8,128)(2,1)S(1)}, bf16[2,16,2048]{2,1,0:T(8,128)(2,1)S(1)}, bf16[128,1024]{1,0:T(8,...) custom-call(s32[8]{0:T(128)S(1)} %copy-done.4, ...), custom_call_target="tpu_custom_call" | custom-call | tf_op jit(solution)/shard_map/pallas_call | solution.py:563
  5.5 5.1 %collective-permute-start.2 = (bf16[2,16,2048]{2,1,0:T(8,128)(2,1)S(1)}, bf16[2,16,2048]{2,1,0:T(8,128)(2,1)S(1)}, u32[]{:S(2)}, u32[]{:S(2)}) collective-permute-start(bf16[2,16,2048]{2,1,0:T(8,128)(2,1)S(1)} %get-tuple-element.114.refs_0_.far_own), channel_id=1, source_target_pairs={{0,3},{1,2},{2,1},{3,0},{4,7},{5,6},{6,5},{7,4},{8,11},{9,10},{10,... | collective-permute-start | bytes 393224 | tf_op jit(solution)/shard_map/ppermute | solution.py:557
  10.7 0.0 collective-permute-start.1
  10.7 0.6 collective-permute-start
  11.3 1.4 %collective-permute-start.3 = (bf16[128,1024]{1,0:T(8,128)(2,1)S(1)}, bf16[128,1024]{1,0:T(8,128)(2,1)S(1)}, u32[]{:S(2)}, u32[]{:S(2)}) collective-permute-start(bf16[128,1024]{1,0:T(8,128)(2,1)S(1)} %get-tuple-element.109), channel_id=1, source_target_pairs={{0,1},{1,0},{2,3},{3,2},{4,5},{5,4},{6,7},{7,6},{8,9},{9,8},{10,11... | collective-permute-start | bytes 786440 | tf_op jit(solution)/shard_map/ppermute | solution.py:557
  12.7 2.9 %collective-permute-start.4 = (bf16[128,1024]{1,0:T(8,128)(2,1)S(1)}, bf16[128,1024]{1,0:T(8,128)(2,1)S(1)}, u32[]{:S(2)}, u32[]{:S(2)}) collective-permute-start(bf16[128,1024]{1,0:T(8,128)(2,1)S(1)} %get-tuple-element.110), channel_id=1, source_target_pairs={{0,2},{1,3},{2,0},{3,1},{4,6},{5,7},{6,4},{7,5},{8,10},{9,11},{10,... | collective-permute-start | bytes 786440 | tf_op jit(solution)/shard_map/ppermute | solution.py:557
  15.6 4.9 %shard_map.85 = (f32[8,512]{1,0:T(8,128)S(1)}, bf16[4,512,512]{2,1,0:T(8,128)(2,1)S(1)}, bf16[4,512,512]{2,1,0:T(8,128)(2,1)S(1)}, f32[512,1024]{1,0:T(8,128)S(1)}) custom-call(bf16[512,1024]{1,0:T(8,128)(2,1)S(1)} %copy-done, bf16[512,1024]{1,0:T(8,128)(2,1)S(1)} %copy-done.2, bf16[512,1024]{1,0:T(8,128)(2,1)S(1)} %copy-done.3, bf16[512,1024]{1,0:T(8,128)(2,1)S(1)} %copy-done.1), custom_call_target="tpu_custom_call" | custom-call | tf_op jit(solution)/shard_map/pallas_call | solution.py:563
  20.5 4.9 %shard_map.87 = (f32[8,512]{1,0:T(8,128)S(1)}, bf16[4,512,512]{2,1,0:T(8,128)(2,1)S(1)}, bf16[4,512,512]{2,1,0:T(8,128)(2,1)S(1)}, f32[512,1024]{1,0:T(8,128)S(1)}) custom-call(bf16[512,1024]{1,0:T(8,128)(2,1)S(1)} %copy-done, bf16[512,1024]{1,0:T(8,128)(2,1)S(1)} %copy-done.2, bf16[512,1024]{1,0:T(8,128)(2,1)S(1)} %copy-done.3, bf16[512,1024]{1,0:T(8,128)(2,1)S(1)} %copy-done.1), custom_call_target="tpu_custom_call" | custom-call | tf_op jit(solution)/shard_map/pallas_call | solution.py:563
  25.5 0.0 collective-permute-done.2.refs_3_
  25.5 0.1 collective-permute-start.5
  25.6 0.0 collective-permute-done.1.refs_2_
  25.6 0.3 shard_map.89
  25.9 1.7 %collective-permute-start.6 = (bf16[64,2048]{1,0:T(8,128)(2,1)S(1)}, bf16[64,2048]{1,0:T(8,128)(2,1)S(1)}, u32[]{:S(2)}, u32[]{:S(2)}) collective-permute-start(bf16[64,2048]{1,0:T(8,128)(2,1)S(1)} %get-tuple-element.119), channel_id=1, source_target_pairs={{0,8},{4,12},{8,0},{12,4},{16,24},{20,28},{24,16},{28,20},{1,9},{5... | collective-permute-start | bytes 786440 | tf_op jit(solution)/shard_map/ppermute | solution.py:557
  27.6 1.5 %collective-permute-start.8 = (bf16[64,2048]{1,0:T(8,128)(2,1)S(1)}, bf16[64,2048]{1,0:T(8,128)(2,1)S(1)}, u32[]{:S(2)}, u32[]{:S(2)}) collective-permute-start(bf16[64,2048]{1,0:T(8,128)(2,1)S(1)} %get-tuple-element.120), channel_id=1, source_target_pairs={{0,24},{4,28},{8,16},{12,20},{16,8},{20,12},{24,0},{28,4},{1,25},{... | collective-permute-start | bytes 786440 | tf_op jit(solution)/shard_map/ppermute | solution.py:557
  29.1 0.1 collective-permute-done.3.refs_2_.refs_0_.refs_10_
  29.2 1.5 %collective-permute-start.7 = (bf16[64,2048]{1,0:T(8,128)(2,1)S(1)}, bf16[64,2048]{1,0:T(8,128)(2,1)S(1)}, u32[]{:S(2)}, u32[]{:S(2)}) collective-permute-start(bf16[64,2048]{1,0:T(8,128)(2,1)S(1)} %get-tuple-element.120), channel_id=1, source_target_pairs={{0,16},{4,20},{8,24},{12,28},{16,0},{20,4},{24,8},{28,12},{1,17},{... | collective-permute-start | bytes 786440 | tf_op jit(solution)/shard_map/ppermute | solution.py:557
  30.8 8.8 %collective-permute-done.4.refs_3_.refs_1_.refs_11_ = bf16[128,1024]{1,0:T(8,128)(2,1)S(1)} collective-permute-done((bf16[128,1024]{1,0:T(8,128)(2,1)S(1)}, bf16[128,1024]{1,0:T(8,128)(2,1)S(1)}, u32[]{:S(2)}, u32[]{:S(2)}) %collective-permute-start.4) | collective-permute-done | bytes 262176 | tf_op jit(solution)/shard_map/ppermute | solution.py:557
  39.6 0.0 collective-permute-done.5.refs_4_.refs_2_.refs_12_
  39.6 0.1 collective-permute-start.9
  39.7 1.2 %collective-permute-done.9.refs_4_ = bf16[16,128]{1,0:T(8,128)(2,1)S(1)} collective-permute-done((bf16[16,128]{1,0:T(8,128)(2,1)S(1)}, bf16[16,128]{1,0:T(8,128)(2,1)S(1)}, u32[]{:S(2)}, u32[]{:S(2)}) %collective-permute-start.9) | collective-permute-done | bytes 4128 | tf_op jit(solution)/shard_map/ppermute | solution.py:557
  40.8 0.0 collective-permute-done.6.refs_1_.refs_18_
  40.8 1.6 %collective-permute-done.7.refs_2_.refs_19_ = bf16[64,2048]{1,0:T(8,128)(2,1)S(1)} collective-permute-done((bf16[64,2048]{1,0:T(8,128)(2,1)S(1)}, bf16[64,2048]{1,0:T(8,128)(2,1)S(1)}, u32[]{:S(2)}, u32[]{:S(2)}) %collective-permute-start.7) | collective-permute-done | bytes 262176 | tf_op jit(solution)/shard_map/ppermute | solution.py:557
  42.4 0.1 shard_map.90
  42.5 0.1 collective-permute-start.10
  42.6 0.0 copy-start.7
  42.6 4.8 %collective-permute-start.14 = (bf16[64,1024]{1,0:T(8,128)(2,1)S(1)}, bf16[64,1024]{1,0:T(8,128)(2,1)S(1)}, u32[]{:S(2)}, u32[]{:S(2)}) collective-permute-start(bf16[64,1024]{1,0:T(8,128)(2,1)S(1)} %get-tuple-element.131), channel_id=1, source_target_pairs={{0,2},{1,3},{2,0},{3,1},{4,6},{5,7},{6,4},{7,5},{8,10},{9,11},{10,... | collective-permute-start | bytes 393224 | tf_op jit(solution)/shard_map/ppermute | solution.py:557
  47.4 1.7 %shard_map.88 = (f32[128,128]{1,0:T(8,128)S(1)}, f32[128,128]{1,0:T(8,128)S(1)}, f32[8,128]{1,0:T(8,128)S(1)}, f32[8,128]{1,0:T(8,128)S(1)}, f32[8,128]{1,0:T(8,128)S(1)}) custom-call(bf16[128,2048]{1,0:T(8,128)(2,1)S(1)} %get-tuple-element.107.refs_0_.kv.refs_1_.refs_2_, bf16[128,2048]{1,0:T(8,128)(2,1)S(1)} %get-tuple-element.108.refs_1_.qg.refs_2_.refs_3_, ...), custom_call_target="tpu_custom_call" | custom-call | tf_op jit(solution)/shard_map/pallas_call | solution.py:563
  49.1 0.1 collective-permute-start.11
  49.2 1.9 %collective-permute-start.12 = (f32[8,128]{1,0:T(8,128)S(1)}, f32[8,128]{1,0:T(8,128)S(1)}, u32[]{:S(2)}, u32[]{:S(2)}) collective-permute-start(f32[8,128]{1,0:T(8,128)S(1)} %get-tuple-element.128), channel_id=1, source_target_pairs={{0,2},{1,3},{2,0},{3,1},{4,6},{5,7},{6,4},{7,5},{8,10},{9,11},{10,... | collective-permute-start | bytes 12296 | tf_op jit(solution)/shard_map/ppermute | solution.py:557
  51.1 2.5 %collective-permute-start.13 = (f32[8,128]{1,0:T(8,128)S(1)}, f32[8,128]{1,0:T(8,128)S(1)}, u32[]{:S(2)}, u32[]{:S(2)}) collective-permute-start(f32[8,128]{1,0:T(8,128)S(1)} %get-tuple-element.129), channel_id=1, source_target_pairs={{0,3},{1,2},{2,1},{3,0},{4,7},{5,6},{6,5},{7,4},{8,11},{9,10},{10,... | collective-permute-start | bytes 12296 | tf_op jit(solution)/shard_map/ppermute | solution.py:557
  53.5 3.9 %shard_map.91 = (f32[16,2048]{1,0:T(8,128)S(1)}, f32[16,128]{1,0:T(8,128)S(1)}, f32[16,128]{1,0:T(8,128)S(1)}) custom-call(bf16[2,16,2048]{2,1,0:T(8,128)(2,1)S(1)} %get-tuple-element.114.refs_0_.far_own, bf16[64,2048]{1,0:T(8,128)(2,1)S(1)} %get-tuple-element.118.refs_0_, bf16[64,2048]{1,0:T(8,128)(2,1)S(1)} %collective-permute-done.6.refs_1_.refs_18_, ...), custom_call_target="tpu_custom_call" | custom-call | tf_op jit(solution)/shard_map/pallas_call | solution.py:563
  57.4 0.0 collective-permute-done.11.refs_8_
  57.4 0.0 collective-permute-done.13.refs_10_
  57.4 0.0 collective-permute-done.14.refs_7_.refs_14_
  57.4 0.1 collective-permute-start.22
  57.5 1.4 %collective-permute-start.24 = (bf16[128,1024]{1,0:T(8,128)(2,1)S(1)}, bf16[128,1024]{1,0:T(8,128)(2,1)S(1)}, u32[]{:S(2)}, u32[]{:S(2)}) collective-permute-start(bf16[128,1024]{1,0:T(8,128)(2,1)S(1)} %get-tuple-element.166), channel_id=1, source_target_pairs={{0,3},{1,2},{2,1},{3,0},{4,7},{5,6},{6,5},{7,4},{8,11},{9,10},{10,... | collective-permute-start | bytes 786440 | tf_op jit(solution)/shard_map/ppermute | solution.py:557
  59.0 2.0 %collective-permute-start.23 = (bf16[64,1024]{1,0:T(8,128)(2,1)S(1)}, bf16[64,1024]{1,0:T(8,128)(2,1)S(1)}, u32[]{:S(2)}, u32[]{:S(2)}) collective-permute-start(bf16[64,1024]{1,0:T(8,128)(2,1)S(1)} %get-tuple-element.165), channel_id=1, source_target_pairs={{0,2},{1,3},{2,0},{3,1},{4,6},{5,7},{6,4},{7,5},{8,10},{9,11},{10,... | collective-permute-start | bytes 393224 | tf_op jit(solution)/shard_map/ppermute | solution.py:557
  61.0 1.1 %shard_map.92 = (f32[512,128]{1,0:T(8,128)S(1)}, f32[128,128]{1,0:T(8,128)S(1)}, f32[16,128]{1,0:T(8,128)S(1)}, f32[16,128]{1,0:T(8,128)S(1)}, f32[16,16]{1,0:T(8,128)S(1)}) custom-call(s32[8]{0:T(128)S(1)} %copy-done.4, s32[8]{0:T(128)S(1)} %copy-done.7, f32[8,512]{1,0:T(8,128)S(1)} %get-tuple-element.96.refs_2_, f32[8,512]{1,0:T(8,128)S(1)} %get-tuple-element.106.refs_3_, ...), custom_call_target="tpu_custom_call" | custom-call | tf_op jit(solution)/shard_map/pallas_call | solution.py:563
  62.1 2.5 %collective-permute-start.17 = (f32[16,16]{1,0:T(8,128)S(1)}, f32[16,16]{1,0:T(8,128)S(1)}, u32[]{:S(2)}, u32[]{:S(2)}) collective-permute-start(f32[16,16]{1,0:T(8,128)S(1)} %get-tuple-element.150.refs_0_), channel_id=1, source_target_pairs={{0,24},{4,28},{8,16},{12,20},{16,8},{20,12},{24,0},{28,4},{1,25},{... | collective-permute-start | bytes 3080 | tf_op jit(solution)/shard_map/ppermute | solution.py:557
  64.6 0.5 collective-permute-start.16
  65.1 1.6 %collective-permute-done.17.refs_3_ = f32[16,16]{1,0:T(8,128)S(1)} collective-permute-done((f32[16,16]{1,0:T(8,128)S(1)}, f32[16,16]{1,0:T(8,128)S(1)}, u32[]{:S(2)}, u32[]{:S(2)}) %collective-permute-start.17) | collective-permute-done | bytes 1056 | tf_op jit(solution)/shard_map/ppermute | solution.py:557
  66.7 1.5 %collective-permute-start.15 = (f32[16,16]{1,0:T(8,128)S(1)}, f32[16,16]{1,0:T(8,128)S(1)}, u32[]{:S(2)}, u32[]{:S(2)}) collective-permute-start(f32[16,16]{1,0:T(8,128)S(1)} %get-tuple-element.150.refs_0_), channel_id=1, source_target_pairs={{0,8},{4,12},{8,0},{12,4},{16,24},{20,28},{24,16},{28,20},{1,9},{5... | collective-permute-start | bytes 3080 | tf_op jit(solution)/shard_map/ppermute | solution.py:557
  68.2 1.2 %shard_map.93.refs_3_ = f32[128,1024]{1,0:T(8,128)S(1)} custom-call(bf16[128,2048]{1,0:T(8,128)(2,1)S(1)} %get-tuple-element.107.refs_0_.kv.refs_1_.refs_2_, bf16[128,2048]{1,0:T(8,128)(2,1)S(1)} %get-tuple-element.108.refs_1_.qg.refs_2_.refs_3_, f32[128,128]{1,0:T(8,128)S(1)} %get-tuple-element.112.refs_4_.mlog, ...), custom_call_target="tpu_custom_call" | custom-call | tf_op jit(solution)/shard_map/pallas_call | solution.py:563
  69.4 0.0 copy-start.5
  69.4 2.0 %shard_map.94 = (f32[512,512]{1,0:T(8,128)S(1)}, f32[512,512]{1,0:T(8,128)S(1)}, f32[512,512]{1,0:T(8,128)S(1)}) custom-call(s32[8]{0:T(128)S(1)} %copy-done.4, s32[8]{0:T(128)S(1)} %copy-done.7, bf16[512,1024]{1,0:T(8,128)(2,1)S(1)} %copy-done, bf16[512,1024]{1,0:T(8,128)(2,1)S(1)} %copy-done.1, bf16[4,512,512]{2,1,0:T(8,128)(2,1)S(1)} %get-tuple-element.137.soft_in, ...), custom_call_target="tpu_custom_call" | custom-call | tf_op jit(solution)/shard_map/pallas_call | solution.py:563
  71.4 0.0 collective-permute-done.15.refs_1_
  71.4 0.1 shard_map.95.refs_1_
  71.5 0.0 collective-permute-start.18
  71.5 1.9 %shard_map.96 = (f32[512,512]{1,0:T(8,128)S(1)}, f32[512,512]{1,0:T(8,128)S(1)}, f32[512,512]{1,0:T(8,128)S(1)}) custom-call(s32[8]{0:T(128)S(1)} %copy-done.5, s32[8]{0:T(128)S(1)} %copy-done.7, bf16[512,1024]{1,0:T(8,128)(2,1)S(1)} %copy-done, bf16[512,1024]{1,0:T(8,128)(2,1)S(1)} %copy-done.1, bf16[4,512,512]{2,1,0:T(8,128)(2,1)S(1)} %get-tuple-element.154.soft_in, ...), custom_call_target="tpu_custom_call" | custom-call | tf_op jit(solution)/shard_map/pallas_call | solution.py:563
  73.4 0.0 collective-permute-done.18.refs_2_
  73.4 0.1 shard_map.97.refs_22_
  73.5 1.4 %collective-permute-start.21 = (f32[16,256]{1,0:T(8,128)S(1)}, f32[16,256]{1,0:T(8,128)S(1)}, u32[]{:S(2)}, u32[]{:S(2)}) collective-permute-start(f32[16,256]{1,0:T(8,128)S(1)} %shard_map.97.refs_22_), channel_id=1, source_target_pairs={{0,3},{1,2},{2,1},{3,0},{4,7},{5,6},{6,5},{7,4},{8,11},{9,10},{10,... | collective-permute-start | bytes 49160 | tf_op jit(solution)/shard_map/ppermute | solution.py:557
  74.9 1.0 %collective-permute-start.20 = (f32[16,256]{1,0:T(8,128)S(1)}, f32[16,256]{1,0:T(8,128)S(1)}, u32[]{:S(2)}, u32[]{:S(2)}) collective-permute-start(f32[16,256]{1,0:T(8,128)S(1)} %shard_map.97.refs_22_), channel_id=1, source_target_pairs={{0,2},{1,3},{2,0},{3,1},{4,6},{5,7},{6,4},{7,5},{8,10},{9,11},{10,... | collective-permute-start | bytes 49160 | tf_op jit(solution)/shard_map/ppermute | solution.py:557
  75.9 1.6 %collective-permute-done.23.refs_8_.refs_15_ = bf16[64,1024]{1,0:T(8,128)(2,1)S(1)} collective-permute-done((bf16[64,1024]{1,0:T(8,128)(2,1)S(1)}, bf16[64,1024]{1,0:T(8,128)(2,1)S(1)}, u32[]{:S(2)}, u32[]{:S(2)}) %collective-permute-start.23) | collective-permute-done | bytes 131104 | tf_op jit(solution)/shard_map/ppermute | solution.py:557
  77.5 0.3 collective-permute-start.19
  77.9 0.9 %shard_map.99 = (f32[128,512]{1,0:T(8,128)S(1)}, f32[128,512]{1,0:T(8,128)S(1)}) custom-call(bf16[2,16,2048]{2,1,0:T(8,128)(2,1)S(1)} %get-tuple-element.114.refs_0_.far_own, bf16[64,2048]{1,0:T(8,128)(2,1)S(1)} %get-tuple-element.168.refs_0_.refs_17_, bf16[64,2048]{1,0:T(8,128)(2,1)S(1)} %collective-permute-done.6.refs_1_.refs_18_, ...), custom_call_target="tpu_custom_call" | custom-call | tf_op jit(solution)/shard_map/pallas_call | solution.py:563
  78.8 0.0 collective-permute-done.22.refs_6_.refs_13_
  78.8 0.0 collective-permute-done.24.refs_9_.refs_16_
  78.9 2.8 %shard_map.98 = bf16[512,1024]{1,0:T(8,128)(2,1)} custom-call(s32[8]{0:T(128)S(1)} %copy-done.5, bf16[128,2048]{1,0:T(8,128)(2,1)S(1)} %get-tuple-element.107.refs_0_.kv.refs_1_.refs_2_, bf16[128,2048]{1,0:T(8,128)(2,1)S(1)} %get-tuple-element.108.refs_1_.qg.refs_2_.refs_3_, f32[512,512]{1,0:T(8,128)S(1)} %get-tuple-element.161.refs_3_, ...), custom_call_target="tpu_custom_call" | custom-call | tf_op jit(solution)/shard_map/pallas_call | solution.py:563
  81.6 0.0 collective-permute-done.21.refs_25_
  81.6 5.8 %shard_map.100 = (bf16[512,1024]{1,0:T(8,128)(2,1)}, bf16[512,1024]{1,0:T(8,128)(2,1)}) custom-call(s32[8]{0:T(128)S(1)} %copy-done.5, s32[8]{0:T(128)S(1)} %copy-done.7, bf16[128,2048]{1,0:T(8,128)(2,1)S(1)} %get-tuple-element.107.refs_0_.kv.refs_1_.refs_2_, bf16[128,2048]{1,0:T(8,128)(2,1)S(1)} %get-tuple-element.108.refs_1_.qg.refs_2_.refs_3_, ...), custom_call_target="tpu_custom_call" | custom-call | tf_op jit(solution)/shard_map/pallas_call | solution.py:563
  (20 shorter events, 0.1 us)
Async XLA Ops:
  0.6 15.0 %copy-start.1 = (bf16[512,1024]{1,0:T(8,128)(2,1)S(1)}, bf16[512,1024]{1,0:T(8,128)(2,1)}, u32[]{:S(2)}) copy-start(bf16[512,1024]{1,0:T(8,128)(2,1)} %g.8) | copy-start | bytes 3145732
  0.6 15.0 %copy-start = (bf16[512,1024]{1,0:T(8,128)(2,1)S(1)}, bf16[512,1024]{1,0:T(8,128)(2,1)}, u32[]{:S(2)}) copy-start(bf16[512,1024]{1,0:T(8,128)(2,1)} %q.8) | copy-start | bytes 3145732
  0.7 15.0 %copy-start.3 = (bf16[512,1024]{1,0:T(8,128)(2,1)S(1)}, bf16[512,1024]{1,0:T(8,128)(2,1)}, u32[]{:S(2)}) copy-start(bf16[512,1024]{1,0:T(8,128)(2,1)} %v.4) | copy-start | bytes 3145732
  0.7 0.8 copy-start.4
  1.5 0.8 copy-start.6
  2.2 13.4 %copy-start.2 = (bf16[512,1024]{1,0:T(8,128)(2,1)S(1)}, bf16[512,1024]{1,0:T(8,128)(2,1)}, u32[]{:S(2)}) copy-start(bf16[512,1024]{1,0:T(8,128)(2,1)} %k.4) | copy-start | bytes 3145732
  5.5 19.9 %collective-permute-start.2 = (bf16[2,16,2048]{2,1,0:T(8,128)(2,1)S(1)}, bf16[2,16,2048]{2,1,0:T(8,128)(2,1)S(1)}, u32[]{:S(2)}, u32[]{:S(2)}) collective-permute-start(bf16[2,16,2048]{2,1,0:T(8,128)(2,1)S(1)} %get-tuple-element.114.refs_0_.far_own), channel_id=1, source_target_pairs={{0,3},{1,2},{2,1},{3,0},{4,7},{5,6},{6,5},{7,4},{8,11},{9,10},{10,... | collective-permute-start | bytes 393224 | tf_op jit(solution)/shard_map/ppermute | solution.py:557
  10.7 15.0 %collective-permute-start.1 = (bf16[2,16,2048]{2,1,0:T(8,128)(2,1)S(1)}, bf16[2,16,2048]{2,1,0:T(8,128)(2,1)S(1)}, u32[]{:S(2)}, u32[]{:S(2)}) collective-permute-start(bf16[2,16,2048]{2,1,0:T(8,128)(2,1)S(1)} %get-tuple-element.114.refs_0_.far_own), channel_id=1, source_target_pairs={{0,2},{1,3},{2,0},{3,1},{4,6},{5,7},{6,4},{7,5},{8,10},{9,11},{10,... | collective-permute-start | bytes 393224 | tf_op jit(solution)/shard_map/ppermute | solution.py:557
  10.7 15.0 %collective-permute-start = (bf16[2,16,2048]{2,1,0:T(8,128)(2,1)S(1)}, bf16[2,16,2048]{2,1,0:T(8,128)(2,1)S(1)}, u32[]{:S(2)}, u32[]{:S(2)}) collective-permute-start(bf16[2,16,2048]{2,1,0:T(8,128)(2,1)S(1)} %get-tuple-element.114.refs_0_.far_own), channel_id=1, source_target_pairs={{0,1},{1,0},{2,3},{3,2},{4,5},{5,4},{6,7},{7,6},{8,9},{9,8},{10,11... | collective-permute-start | bytes 393224 | tf_op jit(solution)/shard_map/ppermute | solution.py:557
  11.3 17.9 %collective-permute-start.3 = (bf16[128,1024]{1,0:T(8,128)(2,1)S(1)}, bf16[128,1024]{1,0:T(8,128)(2,1)S(1)}, u32[]{:S(2)}, u32[]{:S(2)}) collective-permute-start(bf16[128,1024]{1,0:T(8,128)(2,1)S(1)} %get-tuple-element.109), channel_id=1, source_target_pairs={{0,1},{1,0},{2,3},{3,2},{4,5},{5,4},{6,7},{7,6},{8,9},{9,8},{10,11... | collective-permute-start | bytes 786440 | tf_op jit(solution)/shard_map/ppermute | solution.py:557
  12.7 26.9 %collective-permute-start.4 = (bf16[128,1024]{1,0:T(8,128)(2,1)S(1)}, bf16[128,1024]{1,0:T(8,128)(2,1)S(1)}, u32[]{:S(2)}, u32[]{:S(2)}) collective-permute-start(bf16[128,1024]{1,0:T(8,128)(2,1)S(1)} %get-tuple-element.110), channel_id=1, source_target_pairs={{0,2},{1,3},{2,0},{3,1},{4,6},{5,7},{6,4},{7,5},{8,10},{9,11},{10,... | collective-permute-start | bytes 786440 | tf_op jit(solution)/shard_map/ppermute | solution.py:557
  25.5 14.1 %collective-permute-start.5 = (bf16[128,1024]{1,0:T(8,128)(2,1)S(1)}, bf16[128,1024]{1,0:T(8,128)(2,1)S(1)}, u32[]{:S(2)}, u32[]{:S(2)}) collective-permute-start(bf16[128,1024]{1,0:T(8,128)(2,1)S(1)} %get-tuple-element.111), channel_id=1, source_target_pairs={{0,3},{1,2},{2,1},{3,0},{4,7},{5,6},{6,5},{7,4},{8,11},{9,10},{10,... | collective-permute-start | bytes 786440 | tf_op jit(solution)/shard_map/ppermute | solution.py:557
  25.9 14.9 %collective-permute-start.6 = (bf16[64,2048]{1,0:T(8,128)(2,1)S(1)}, bf16[64,2048]{1,0:T(8,128)(2,1)S(1)}, u32[]{:S(2)}, u32[]{:S(2)}) collective-permute-start(bf16[64,2048]{1,0:T(8,128)(2,1)S(1)} %get-tuple-element.119), channel_id=1, source_target_pairs={{0,8},{4,12},{8,0},{12,4},{16,24},{20,28},{24,16},{28,20},{1,9},{5... | collective-permute-start | bytes 786440 | tf_op jit(solution)/shard_map/ppermute | solution.py:557
  27.6 13.2 %collective-permute-start.8 = (bf16[64,2048]{1,0:T(8,128)(2,1)S(1)}, bf16[64,2048]{1,0:T(8,128)(2,1)S(1)}, u32[]{:S(2)}, u32[]{:S(2)}) collective-permute-start(bf16[64,2048]{1,0:T(8,128)(2,1)S(1)} %get-tuple-element.120), channel_id=1, source_target_pairs={{0,24},{4,28},{8,16},{12,20},{16,8},{20,12},{24,0},{28,4},{1,25},{... | collective-permute-start | bytes 786440 | tf_op jit(solution)/shard_map/ppermute | solution.py:557
  29.2 13.2 %collective-permute-start.7 = (bf16[64,2048]{1,0:T(8,128)(2,1)S(1)}, bf16[64,2048]{1,0:T(8,128)(2,1)S(1)}, u32[]{:S(2)}, u32[]{:S(2)}) collective-permute-start(bf16[64,2048]{1,0:T(8,128)(2,1)S(1)} %get-tuple-element.120), channel_id=1, source_target_pairs={{0,16},{4,20},{8,24},{12,28},{16,0},{20,4},{24,8},{28,12},{1,17},{... | collective-permute-start | bytes 786440 | tf_op jit(solution)/shard_map/ppermute | solution.py:557
  39.6 1.2 %collective-permute-start.9 = (bf16[16,128]{1,0:T(8,128)(2,1)S(1)}, bf16[16,128]{1,0:T(8,128)(2,1)S(1)}, u32[]{:S(2)}, u32[]{:S(2)}) collective-permute-start(bf16[16,128]{1,0:T(8,128)(2,1)S(1)} %slice_add_fusion), channel_id=1, source_target_pairs={{0,4},{4,0},{8,12},{12,8},{16,20},{20,16},{24,28},{28,24},{1,5},{5... | collective-permute-start | bytes 12296 | tf_op jit(solution)/shard_map/ppermute | solution.py:557
  42.5 11.1 %collective-permute-start.10 = (bf16[256,2048]{1,0:T(8,128)(2,1)S(1)}, bf16[256,2048]{1,0:T(8,128)(2,1)S(1)}, u32[]{:S(2)}, u32[]{:S(2)}) collective-permute-start(bf16[256,2048]{1,0:T(8,128)(2,1)S(1)} %shard_map.90), channel_id=1, source_target_pairs={{0,4},{4,0},{8,12},{12,8},{16,20},{20,16},{24,28},{28,24},{1,5},{5... | collective-permute-start | bytes 3145736 | tf_op jit(solution)/shard_map/ppermute | solution.py:557
  42.6 18.4 %copy-start.7 = (s32[8]{0:T(128)S(1)}, s32[8]{0:T(128)}, u32[]{:S(2)}) copy-start(s32[8]{0:T(128)} %refs_1_.3) | copy-start | bytes 100
  42.6 14.8 %collective-permute-start.14 = (bf16[64,1024]{1,0:T(8,128)(2,1)S(1)}, bf16[64,1024]{1,0:T(8,128)(2,1)S(1)}, u32[]{:S(2)}, u32[]{:S(2)}) collective-permute-start(bf16[64,1024]{1,0:T(8,128)(2,1)S(1)} %get-tuple-element.131), channel_id=1, source_target_pairs={{0,2},{1,3},{2,0},{3,1},{4,6},{5,7},{6,4},{7,5},{8,10},{9,11},{10,... | collective-permute-start | bytes 393224 | tf_op jit(solution)/shard_map/ppermute | solution.py:557
  49.1 8.3 %collective-permute-start.11 = (f32[8,128]{1,0:T(8,128)S(1)}, f32[8,128]{1,0:T(8,128)S(1)}, u32[]{:S(2)}, u32[]{:S(2)}) collective-permute-start(f32[8,128]{1,0:T(8,128)S(1)} %get-tuple-element.127), channel_id=1, source_target_pairs={{0,1},{1,0},{2,3},{3,2},{4,5},{5,4},{6,7},{7,6},{8,9},{9,8},{10,11... | collective-permute-start | bytes 12296 | tf_op jit(solution)/shard_map/ppermute | solution.py:557
  49.2 8.3 %collective-permute-start.12 = (f32[8,128]{1,0:T(8,128)S(1)}, f32[8,128]{1,0:T(8,128)S(1)}, u32[]{:S(2)}, u32[]{:S(2)}) collective-permute-start(f32[8,128]{1,0:T(8,128)S(1)} %get-tuple-element.128), channel_id=1, source_target_pairs={{0,2},{1,3},{2,0},{3,1},{4,6},{5,7},{6,4},{7,5},{8,10},{9,11},{10,... | collective-permute-start | bytes 12296 | tf_op jit(solution)/shard_map/ppermute | solution.py:557
  51.1 6.4 %collective-permute-start.13 = (f32[8,128]{1,0:T(8,128)S(1)}, f32[8,128]{1,0:T(8,128)S(1)}, u32[]{:S(2)}, u32[]{:S(2)}) collective-permute-start(f32[8,128]{1,0:T(8,128)S(1)} %get-tuple-element.129), channel_id=1, source_target_pairs={{0,3},{1,2},{2,1},{3,0},{4,7},{5,6},{6,5},{7,4},{8,11},{9,10},{10,... | collective-permute-start | bytes 12296 | tf_op jit(solution)/shard_map/ppermute | solution.py:557
  57.4 21.4 %collective-permute-start.22 = (bf16[128,1024]{1,0:T(8,128)(2,1)S(1)}, bf16[128,1024]{1,0:T(8,128)(2,1)S(1)}, u32[]{:S(2)}, u32[]{:S(2)}) collective-permute-start(bf16[128,1024]{1,0:T(8,128)(2,1)S(1)} %get-tuple-element.163), channel_id=1, source_target_pairs={{0,1},{1,0},{2,3},{3,2},{4,5},{5,4},{6,7},{7,6},{8,9},{9,8},{10,11... | collective-permute-start | bytes 786440 | tf_op jit(solution)/shard_map/ppermute | solution.py:557
  57.5 21.3 %collective-permute-start.24 = (bf16[128,1024]{1,0:T(8,128)(2,1)S(1)}, bf16[128,1024]{1,0:T(8,128)(2,1)S(1)}, u32[]{:S(2)}, u32[]{:S(2)}) collective-permute-start(bf16[128,1024]{1,0:T(8,128)(2,1)S(1)} %get-tuple-element.166), channel_id=1, source_target_pairs={{0,3},{1,2},{2,1},{3,0},{4,7},{5,6},{6,5},{7,4},{8,11},{9,10},{10,... | collective-permute-start | bytes 786440 | tf_op jit(solution)/shard_map/ppermute | solution.py:557
  59.0 18.6 %collective-permute-start.23 = (bf16[64,1024]{1,0:T(8,128)(2,1)S(1)}, bf16[64,1024]{1,0:T(8,128)(2,1)S(1)}, u32[]{:S(2)}, u32[]{:S(2)}) collective-permute-start(bf16[64,1024]{1,0:T(8,128)(2,1)S(1)} %get-tuple-element.165), channel_id=1, source_target_pairs={{0,2},{1,3},{2,0},{3,1},{4,6},{5,7},{6,4},{7,5},{8,10},{9,11},{10,... | collective-permute-start | bytes 393224 | tf_op jit(solution)/shard_map/ppermute | solution.py:557
  62.1 4.6 %collective-permute-start.17 = (f32[16,16]{1,0:T(8,128)S(1)}, f32[16,16]{1,0:T(8,128)S(1)}, u32[]{:S(2)}, u32[]{:S(2)}) collective-permute-start(f32[16,16]{1,0:T(8,128)S(1)} %get-tuple-element.150.refs_0_), channel_id=1, source_target_pairs={{0,24},{4,28},{8,16},{12,20},{16,8},{20,12},{24,0},{28,4},{1,25},{... | collective-permute-start | bytes 3080 | tf_op jit(solution)/shard_map/ppermute | solution.py:557
  64.6 6.8 %collective-permute-start.16 = (f32[16,16]{1,0:T(8,128)S(1)}, f32[16,16]{1,0:T(8,128)S(1)}, u32[]{:S(2)}, u32[]{:S(2)}) collective-permute-start(f32[16,16]{1,0:T(8,128)S(1)} %get-tuple-element.150.refs_0_), channel_id=1, source_target_pairs={{0,16},{4,20},{8,24},{12,28},{16,0},{20,4},{24,8},{28,12},{1,17},{... | collective-permute-start | bytes 3080 | tf_op jit(solution)/shard_map/ppermute | solution.py:557
  66.7 4.7 %collective-permute-start.15 = (f32[16,16]{1,0:T(8,128)S(1)}, f32[16,16]{1,0:T(8,128)S(1)}, u32[]{:S(2)}, u32[]{:S(2)}) collective-permute-start(f32[16,16]{1,0:T(8,128)S(1)} %get-tuple-element.150.refs_0_), channel_id=1, source_target_pairs={{0,8},{4,12},{8,0},{12,4},{16,24},{20,28},{24,16},{28,20},{1,9},{5... | collective-permute-start | bytes 3080 | tf_op jit(solution)/shard_map/ppermute | solution.py:557
  69.4 2.1 %copy-start.5 = (s32[8]{0:T(128)S(1)}, s32[8]{0:T(128)}, u32[]{:S(2)}) copy-start(s32[8]{0:T(128)} %refs_0_.5) | copy-start | bytes 100
  71.5 1.9 %collective-permute-start.18 = (f32[16,64]{1,0:T(8,128)S(1)}, f32[16,64]{1,0:T(8,128)S(1)}, u32[]{:S(2)}, u32[]{:S(2)}) collective-permute-start(f32[16,64]{1,0:T(8,128)S(1)} %shard_map.95.refs_1_), channel_id=1, source_target_pairs={{0,4},{4,0},{8,12},{12,8},{16,20},{20,16},{24,28},{28,24},{1,5},{5... | collective-permute-start | bytes 12296 | tf_op jit(solution)/shard_map/ppermute | solution.py:557
  73.5 8.1 %collective-permute-start.21 = (f32[16,256]{1,0:T(8,128)S(1)}, f32[16,256]{1,0:T(8,128)S(1)}, u32[]{:S(2)}, u32[]{:S(2)}) collective-permute-start(f32[16,256]{1,0:T(8,128)S(1)} %shard_map.97.refs_22_), channel_id=1, source_target_pairs={{0,3},{1,2},{2,1},{3,0},{4,7},{5,6},{6,5},{7,4},{8,11},{9,10},{10,... | collective-permute-start | bytes 49160 | tf_op jit(solution)/shard_map/ppermute | solution.py:557
  74.9 6.7 %collective-permute-start.20 = (f32[16,256]{1,0:T(8,128)S(1)}, f32[16,256]{1,0:T(8,128)S(1)}, u32[]{:S(2)}, u32[]{:S(2)}) collective-permute-start(f32[16,256]{1,0:T(8,128)S(1)} %shard_map.97.refs_22_), channel_id=1, source_target_pairs={{0,2},{1,3},{2,0},{3,1},{4,6},{5,7},{6,4},{7,5},{8,10},{9,11},{10,... | collective-permute-start | bytes 49160 | tf_op jit(solution)/shard_map/ppermute | solution.py:557
  77.5 4.1 %collective-permute-start.19 = (f32[16,256]{1,0:T(8,128)S(1)}, f32[16,256]{1,0:T(8,128)S(1)}, u32[]{:S(2)}, u32[]{:S(2)}) collective-permute-start(f32[16,256]{1,0:T(8,128)S(1)} %shard_map.97.refs_22_), channel_id=1, source_target_pairs={{0,1},{1,0},{2,3},{3,2},{4,5},{5,4},{6,7},{7,6},{8,9},{9,8},{10,11... | collective-permute-start | bytes 49160 | tf_op jit(solution)/shard_map/ppermute | solution.py:557

commit v7 on v6

--- a/solution.py
+++ b/solution.py
@@ -680,9 +680,11 @@
     )
     backs = [swap(mid_stats[1 + step], "lvl", levels, step) for step in range(1, levels)]
     second = list(pays[mids:])
-    early, first_in = lax.optimization_barrier((second[1][: mid_count // 2], first_in))
+    early, first_in = lax.optimization_barrier((second[1][: mid_count * 3 // 4], first_in))
     early = swap(early, "lvl", levels, 2)
-    second[1] = second[1][mid_count // 2 :]
+    second[0], first_in = lax.optimization_barrier((second[0], first_in))
+    nearest = swap(second[0], "lvl", levels, 1)
+    second[1] = second[1][mid_count * 3 // 4 :]
     far_base, *far_stats = call(
         functools.partial(far_stats_kernel, scale, levels, rows, fars),
         steps,
@@ -710,10 +712,10 @@
         [(group_rows, shape((heads * far_count, rows), F32))] * 2,
         [],
     )
-    waited = (second, backs, far_base, early)
-    second, backs, far_base, early = lax.optimization_barrier(waited)
-    second_in = [swap(second[step - 1], "lvl", levels, step) for step in range(1, levels)]
-    second_in.insert(1, early)
+    waited = (second[1:], backs, far_base, early, nearest)
+    rest, backs, far_base, early, nearest = lax.optimization_barrier(waited)
+    second_in = [swap(rest[step - 2], "lvl", levels, step) for step in range(2, levels)]
+    second_in = [nearest, early] + second_in
     second_list = [whole(piece) for piece in second_in]
     near_cols, mid_cols, far_cols, mid_sent, far_sent = call(
         functools.partial(merge_kernel, heads, mids),

time: 87.6 us -> 86 us (0.982)
  transfers between devices with their start and end apart: 25 -> 25, of which waited for: 6 -> 6; matrix products, arithmetic and copies ran while one was open for 0% -> 0% of each run, Pallas kernels for 29% -> 30%
where the time goes in v7:
time: 86 us; the launch traced here: 85.8 us
  Pallas kernels  34.8 us (40%)
  starting transfers between devices  34.4 us (40%)
  waiting for transfers between devices  14.1 us (16%)
  local copies, waits for them, and re-layouts  1.63 us (2%)
  between operations  0.87 us (1%)
    pallas_call x16, Pallas kernels, call(): pl.pallas_call(kernel, grid=(steps,), in_specs=list(specs), out_specs=lis...  34.8 us
    ppermute x25, starting transfers between devices, swap(): return lax.ppermute(array, axis, [(i, i ^ step) for i in range(size)])  34.4 us
    ppermute x25, waiting for transfers between devices, swap(): return lax.ppermute(array, axis, [(i, i ^ step) for i in range(size)])  14.1 us
  transfers between devices with their start and end apart: 25, of which 6 were waited for; matrix products, arithmetic and copies ran while one was open for 0% of the time, Pallas kernels for 30%

profile of v7, /device:TPU:0, one launch (start us, length us, event | category | flops | bytes accessed | tf_op | source)
XLA Modules:
  0.0 85.8 jit_solution(642063347654203601)
XLA Ops:
  0.7 0.0 copy-start.4
  0.7 0.8 copy-done.4
  1.5 0.8 copy-done.6
  2.3 3.3 %shard_map.86 = (bf16[128,2048]{1,0:T(8,128)(2,1)S(1)}, bf16[128,2048]{1,0:T(8,128)(2,1)S(1)}, bf16[2,16,2048]{2,1,0:T(8,128)(2,1)S(1)}, bf16[128,1024]{1,0:T(8,...) custom-call(s32[8]{0:T(128)S(1)} %copy-done.4, ...), custom_call_target="tpu_custom_call" | custom-call | tf_op jit(solution)/shard_map/pallas_call | solution.py:563
  5.5 5.1 %collective-permute-start.2 = (bf16[2,16,2048]{2,1,0:T(8,128)(2,1)S(1)}, bf16[2,16,2048]{2,1,0:T(8,128)(2,1)S(1)}, u32[]{:S(2)}, u32[]{:S(2)}) collective-permute-start(bf16[2,16,2048]{2,1,0:T(8,128)(2,1)S(1)} %get-tuple-element.118.refs_0_.far_own), channel_id=1, source_target_pairs={{0,3},{1,2},{2,1},{3,0},{4,7},{5,6},{6,5},{7,4},{8,11},{9,10},{10,... | collective-permute-start | bytes 393224 | tf_op jit(solution)/shard_map/ppermute | solution.py:557
  10.7 0.6 collective-permute-start
  11.3 1.4 %collective-permute-start.3 = (bf16[128,1024]{1,0:T(8,128)(2,1)S(1)}, bf16[128,1024]{1,0:T(8,128)(2,1)S(1)}, u32[]{:S(2)}, u32[]{:S(2)}) collective-permute-start(bf16[128,1024]{1,0:T(8,128)(2,1)S(1)} %get-tuple-element.113), channel_id=1, source_target_pairs={{0,1},{1,0},{2,3},{3,2},{4,5},{5,4},{6,7},{7,6},{8,9},{9,8},{10,11... | collective-permute-start | bytes 786440 | tf_op jit(solution)/shard_map/ppermute | solution.py:557
  12.7 2.9 %collective-permute-start.4 = (bf16[128,1024]{1,0:T(8,128)(2,1)S(1)}, bf16[128,1024]{1,0:T(8,128)(2,1)S(1)}, u32[]{:S(2)}, u32[]{:S(2)}) collective-permute-start(bf16[128,1024]{1,0:T(8,128)(2,1)S(1)} %get-tuple-element.114), channel_id=1, source_target_pairs={{0,2},{1,3},{2,0},{3,1},{4,6},{5,7},{6,4},{7,5},{8,10},{9,11},{10,... | collective-permute-start | bytes 786440 | tf_op jit(solution)/shard_map/ppermute | solution.py:557
  15.6 4.9 %shard_map.85 = (f32[8,512]{1,0:T(8,128)S(1)}, bf16[4,512,512]{2,1,0:T(8,128)(2,1)S(1)}, bf16[4,512,512]{2,1,0:T(8,128)(2,1)S(1)}, f32[512,1024]{1,0:T(8,128)S(1)}) custom-call(bf16[512,1024]{1,0:T(8,128)(2,1)S(1)} %copy-done, bf16[512,1024]{1,0:T(8,128)(2,1)S(1)} %copy-done.2, bf16[512,1024]{1,0:T(8,128)(2,1)S(1)} %copy-done.3, bf16[512,1024]{1,0:T(8,128)(2,1)S(1)} %copy-done.1), custom_call_target="tpu_custom_call" | custom-call | tf_op jit(solution)/shard_map/pallas_call | solution.py:563
  20.6 4.9 %shard_map.87 = (f32[8,512]{1,0:T(8,128)S(1)}, bf16[4,512,512]{2,1,0:T(8,128)(2,1)S(1)}, bf16[4,512,512]{2,1,0:T(8,128)(2,1)S(1)}, f32[512,1024]{1,0:T(8,128)S(1)}) custom-call(bf16[512,1024]{1,0:T(8,128)(2,1)S(1)} %copy-done, bf16[512,1024]{1,0:T(8,128)(2,1)S(1)} %copy-done.2, bf16[512,1024]{1,0:T(8,128)(2,1)S(1)} %copy-done.3, bf16[512,1024]{1,0:T(8,128)(2,1)S(1)} %copy-done.1), custom_call_target="tpu_custom_call" | custom-call | tf_op jit(solution)/shard_map/pallas_call | solution.py:563
  25.5 0.1 collective-permute-start.5
  25.6 0.0 collective-permute-done.1.refs_2_
  25.6 0.0 collective-permute-done.refs_1_
  25.6 0.3 shard_map.89
  25.9 1.7 %collective-permute-start.6 = (bf16[64,2048]{1,0:T(8,128)(2,1)S(1)}, bf16[64,2048]{1,0:T(8,128)(2,1)S(1)}, u32[]{:S(2)}, u32[]{:S(2)}) collective-permute-start(bf16[64,2048]{1,0:T(8,128)(2,1)S(1)} %get-tuple-element.123), channel_id=1, source_target_pairs={{0,8},{4,12},{8,0},{12,4},{16,24},{20,28},{24,16},{28,20},{1,9},{5... | collective-permute-start | bytes 786440 | tf_op jit(solution)/shard_map/ppermute | solution.py:557
  27.6 1.5 %collective-permute-start.8 = (bf16[64,2048]{1,0:T(8,128)(2,1)S(1)}, bf16[64,2048]{1,0:T(8,128)(2,1)S(1)}, u32[]{:S(2)}, u32[]{:S(2)}) collective-permute-start(bf16[64,2048]{1,0:T(8,128)(2,1)S(1)} %get-tuple-element.124), channel_id=1, source_target_pairs={{0,24},{4,28},{8,16},{12,20},{16,8},{20,12},{24,0},{28,4},{1,25},{... | collective-permute-start | bytes 786440 | tf_op jit(solution)/shard_map/ppermute | solution.py:557
  29.1 0.1 collective-permute-done.3.refs_2_.refs_0_.refs_10_
  29.2 1.5 %collective-permute-start.7 = (bf16[64,2048]{1,0:T(8,128)(2,1)S(1)}, bf16[64,2048]{1,0:T(8,128)(2,1)S(1)}, u32[]{:S(2)}, u32[]{:S(2)}) collective-permute-start(bf16[64,2048]{1,0:T(8,128)(2,1)S(1)} %get-tuple-element.124), channel_id=1, source_target_pairs={{0,16},{4,20},{8,24},{12,28},{16,0},{20,4},{24,8},{28,12},{1,17},{... | collective-permute-start | bytes 786440 | tf_op jit(solution)/shard_map/ppermute | solution.py:557
  30.8 8.8 %collective-permute-done.4.refs_3_.refs_1_.refs_11_ = bf16[128,1024]{1,0:T(8,128)(2,1)S(1)} collective-permute-done((bf16[128,1024]{1,0:T(8,128)(2,1)S(1)}, bf16[128,1024]{1,0:T(8,128)(2,1)S(1)}, u32[]{:S(2)}, u32[]{:S(2)}) %collective-permute-start.4) | collective-permute-done | bytes 262176 | tf_op jit(solution)/shard_map/ppermute | solution.py:557
  39.6 0.1 collective-permute-start.9
  39.7 1.2 %collective-permute-done.9.refs_4_ = bf16[16,128]{1,0:T(8,128)(2,1)S(1)} collective-permute-done((bf16[16,128]{1,0:T(8,128)(2,1)S(1)}, bf16[16,128]{1,0:T(8,128)(2,1)S(1)}, u32[]{:S(2)}, u32[]{:S(2)}) %collective-permute-start.9) | collective-permute-done | bytes 4128 | tf_op jit(solution)/shard_map/ppermute | solution.py:557
  40.8 0.0 collective-permute-done.6.refs_1_.refs_18_
  40.8 0.0 collective-permute-done.8.refs_3_.refs_20_
  40.8 1.6 %collective-permute-done.7.refs_2_.refs_19_ = bf16[64,2048]{1,0:T(8,128)(2,1)S(1)} collective-permute-done((bf16[64,2048]{1,0:T(8,128)(2,1)S(1)}, bf16[64,2048]{1,0:T(8,128)(2,1)S(1)}, u32[]{:S(2)}, u32[]{:S(2)}) %collective-permute-start.7) | collective-permute-done | bytes 262176 | tf_op jit(solution)/shard_map/ppermute | solution.py:557
  42.4 0.1 shard_map.90
  42.5 0.1 collective-permute-start.10
  42.6 3.8 %collective-permute-start.15 = (bf16[128,1024]{1,0:T(8,128)(2,1)S(1)}, bf16[128,1024]{1,0:T(8,128)(2,1)S(1)}, u32[]{:S(2)}, u32[]{:S(2)}) collective-permute-start(bf16[128,1024]{1,0:T(8,128)(2,1)S(1)} %get-tuple-element.139), channel_id=1, source_target_pairs={{0,1},{1,0},{2,3},{3,2},{4,5},{5,4},{6,7},{7,6},{8,9},{9,8},{10,11... | collective-permute-start | bytes 786440 | tf_op jit(solution)/shard_map/ppermute | solution.py:557
  46.4 1.1 %collective-permute-start.14 = (bf16[96,1024]{1,0:T(8,128)(2,1)S(1)}, bf16[96,1024]{1,0:T(8,128)(2,1)S(1)}, u32[]{:S(2)}, u32[]{:S(2)}) collective-permute-start(bf16[96,1024]{1,0:T(8,128)(2,1)S(1)} %slice.19), channel_id=1, source_target_pairs={{0,2},{1,3},{2,0},{3,1},{4,6},{5,7},{6,4},{7,5},{8,10},{9,11},{10,... | collective-permute-start | bytes 589832 | tf_op jit(solution)/shard_map/ppermute | solution.py:557
  47.5 1.7 %shard_map.88 = (f32[128,128]{1,0:T(8,128)S(1)}, f32[128,128]{1,0:T(8,128)S(1)}, f32[8,128]{1,0:T(8,128)S(1)}, f32[8,128]{1,0:T(8,128)S(1)}, f32[8,128]{1,0:T(8,128)S(1)}) custom-call(bf16[128,2048]{1,0:T(8,128)(2,1)S(1)} %get-tuple-element.111.refs_0_.kv.refs_1_.refs_2_, bf16[128,2048]{1,0:T(8,128)(2,1)S(1)} %get-tuple-element.112.refs_1_.qg.refs_2_.refs_3_, ...), custom_call_target="tpu_custom_call" | custom-call | tf_op jit(solution)/shard_map/pallas_call | solution.py:563
  49.2 2.0 %collective-permute-start.11 = (f32[8,128]{1,0:T(8,128)S(1)}, f32[8,128]{1,0:T(8,128)S(1)}, u32[]{:S(2)}, u32[]{:S(2)}) collective-permute-start(f32[8,128]{1,0:T(8,128)S(1)} %get-tuple-element.130), channel_id=1, source_target_pairs={{0,1},{1,0},{2,3},{3,2},{4,5},{5,4},{6,7},{7,6},{8,9},{9,8},{10,11... | collective-permute-start | bytes 12296 | tf_op jit(solution)/shard_map/ppermute | solution.py:557
  51.2 0.0 collective-permute-start.12
  51.2 0.0 collective-permute-done.10.refs_4_.refs_21_
  51.2 2.4 %collective-permute-start.13 = (f32[8,128]{1,0:T(8,128)S(1)}, f32[8,128]{1,0:T(8,128)S(1)}, u32[]{:S(2)}, u32[]{:S(2)}) collective-permute-start(f32[8,128]{1,0:T(8,128)S(1)} %get-tuple-element.132), channel_id=1, source_target_pairs={{0,3},{1,2},{2,1},{3,0},{4,7},{5,6},{6,5},{7,4},{8,11},{9,10},{10,... | collective-permute-start | bytes 12296 | tf_op jit(solution)/shard_map/ppermute | solution.py:557
  53.6 3.9 %shard_map.91 = (f32[16,2048]{1,0:T(8,128)S(1)}, f32[16,128]{1,0:T(8,128)S(1)}, f32[16,128]{1,0:T(8,128)S(1)}) custom-call(bf16[2,16,2048]{2,1,0:T(8,128)(2,1)S(1)} %get-tuple-element.118.refs_0_.far_own, bf16[64,2048]{1,0:T(8,128)(2,1)S(1)} %get-tuple-element.122.refs_0_, bf16[64,2048]{1,0:T(8,128)(2,1)S(1)} %collective-permute-done.6.refs_1_.refs_18_, ...), custom_call_target="tpu_custom_call" | custom-call | tf_op jit(solution)/shard_map/pallas_call | solution.py:563
  57.5 0.1 collective-permute-done.11.refs_8_
  57.6 0.0 collective-permute-done.12.refs_9_
  57.6 2.3 %collective-permute-done.13.refs_10_ = f32[8,128]{1,0:T(8,128)S(1)} collective-permute-done((f32[8,128]{1,0:T(8,128)S(1)}, f32[8,128]{1,0:T(8,128)S(1)}, u32[]{:S(2)}, u32[]{:S(2)}) %collective-permute-start.13) | collective-permute-done | bytes 4128 | tf_op jit(solution)/shard_map/ppermute | solution.py:557
  59.9 0.0 collective-permute-done.14.refs_7_.refs_14_
  59.9 1.4 %collective-permute-start.24 = (bf16[128,1024]{1,0:T(8,128)(2,1)S(1)}, bf16[128,1024]{1,0:T(8,128)(2,1)S(1)}, u32[]{:S(2)}, u32[]{:S(2)}) collective-permute-start(bf16[128,1024]{1,0:T(8,128)(2,1)S(1)} %get-tuple-element.174), channel_id=1, source_target_pairs={{0,3},{1,2},{2,1},{3,0},{4,7},{5,6},{6,5},{7,4},{8,11},{9,10},{10,... | collective-permute-start | bytes 786440 | tf_op jit(solution)/shard_map/ppermute | solution.py:557
  61.3 0.7 collective-permute-start.23
  61.9 1.1 %shard_map.92 = (f32[512,128]{1,0:T(8,128)S(1)}, f32[128,128]{1,0:T(8,128)S(1)}, f32[16,128]{1,0:T(8,128)S(1)}, f32[16,128]{1,0:T(8,128)S(1)}, f32[16,16]{1,0:T(8,128)S(1)}) custom-call(s32[8]{0:T(128)S(1)} %copy-done.4, s32[8]{0:T(128)S(1)} %copy-done.7, f32[8,512]{1,0:T(8,128)S(1)} %get-tuple-element.100.refs_2_, f32[8,512]{1,0:T(8,128)S(1)} %get-tuple-element.110.refs_3_, ...), custom_call_target="tpu_custom_call" | custom-call | tf_op jit(solution)/shard_map/pallas_call | solution.py:563
  63.0 2.5 %collective-permute-start.18 = (f32[16,16]{1,0:T(8,128)S(1)}, f32[16,16]{1,0:T(8,128)S(1)}, u32[]{:S(2)}, u32[]{:S(2)}) collective-permute-start(f32[16,16]{1,0:T(8,128)S(1)} %get-tuple-element.158.refs_0_), channel_id=1, source_target_pairs={{0,24},{4,28},{8,16},{12,20},{16,8},{20,12},{24,0},{28,4},{1,25},{... | collective-permute-start | bytes 3080 | tf_op jit(solution)/shard_map/ppermute | solution.py:557
  65.5 0.5 collective-permute-start.17
  66.0 0.5 collective-permute-start.16
  66.6 1.2 %shard_map.93.refs_3_ = f32[128,1024]{1,0:T(8,128)S(1)} custom-call(bf16[128,2048]{1,0:T(8,128)(2,1)S(1)} %get-tuple-element.111.refs_0_.kv.refs_1_.refs_2_, bf16[128,2048]{1,0:T(8,128)(2,1)S(1)} %get-tuple-element.112.refs_1_.qg.refs_2_.refs_3_, f32[128,128]{1,0:T(8,128)S(1)} %get-tuple-element.116.refs_4_.mlog, ...), custom_call_target="tpu_custom_call" | custom-call | tf_op jit(solution)/shard_map/pallas_call | solution.py:563
  67.8 0.0 copy-start.5
  67.8 2.0 %shard_map.94 = (f32[512,512]{1,0:T(8,128)S(1)}, f32[512,512]{1,0:T(8,128)S(1)}, f32[512,512]{1,0:T(8,128)S(1)}) custom-call(s32[8]{0:T(128)S(1)} %copy-done.4, s32[8]{0:T(128)S(1)} %copy-done.7, bf16[512,1024]{1,0:T(8,128)(2,1)S(1)} %copy-done, bf16[512,1024]{1,0:T(8,128)(2,1)S(1)} %copy-done.1, bf16[4,512,512]{2,1,0:T(8,128)(2,1)S(1)} %get-tuple-element.145.soft_in, ...), custom_call_target="tpu_custom_call" | custom-call | tf_op jit(solution)/shard_map/pallas_call | solution.py:563
  69.8 0.0 collective-permute-done.17.refs_2_
  69.8 0.0 collective-permute-done.16.refs_1_
  69.8 0.1 shard_map.95.refs_1_
  69.9 0.0 collective-permute-start.19
  69.9 1.9 %shard_map.96 = (f32[512,512]{1,0:T(8,128)S(1)}, f32[512,512]{1,0:T(8,128)S(1)}, f32[512,512]{1,0:T(8,128)S(1)}) custom-call(s32[8]{0:T(128)S(1)} %copy-done.5, s32[8]{0:T(128)S(1)} %copy-done.7, bf16[512,1024]{1,0:T(8,128)(2,1)S(1)} %copy-done, bf16[512,1024]{1,0:T(8,128)(2,1)S(1)} %copy-done.1, bf16[4,512,512]{2,1,0:T(8,128)(2,1)S(1)} %get-tuple-element.162.soft_in, ...), custom_call_target="tpu_custom_call" | custom-call | tf_op jit(solution)/shard_map/pallas_call | solution.py:563
  71.8 0.0 collective-permute-done.19.refs_2_
  71.8 0.1 shard_map.97.refs_22_
  71.9 1.8 %collective-permute-start.22 = (f32[16,256]{1,0:T(8,128)S(1)}, f32[16,256]{1,0:T(8,128)S(1)}, u32[]{:S(2)}, u32[]{:S(2)}) collective-permute-start(f32[16,256]{1,0:T(8,128)S(1)} %shard_map.97.refs_22_), channel_id=1, source_target_pairs={{0,3},{1,2},{2,1},{3,0},{4,7},{5,6},{6,5},{7,4},{8,11},{9,10},{10,... | collective-permute-start | bytes 49160 | tf_op jit(solution)/shard_map/ppermute | solution.py:557
  73.7 2.0 %collective-permute-start.21 = (f32[16,256]{1,0:T(8,128)S(1)}, f32[16,256]{1,0:T(8,128)S(1)}, u32[]{:S(2)}, u32[]{:S(2)}) collective-permute-start(f32[16,256]{1,0:T(8,128)S(1)} %shard_map.97.refs_22_), channel_id=1, source_target_pairs={{0,2},{1,3},{2,0},{3,1},{4,6},{5,7},{6,4},{7,5},{8,10},{9,11},{10,... | collective-permute-start | bytes 49160 | tf_op jit(solution)/shard_map/ppermute | solution.py:557
  75.7 0.6 collective-permute-start.20
  76.3 0.9 %shard_map.99 = (f32[128,512]{1,0:T(8,128)S(1)}, f32[128,512]{1,0:T(8,128)S(1)}) custom-call(bf16[2,16,2048]{2,1,0:T(8,128)(2,1)S(1)} %get-tuple-element.118.refs_0_.far_own, bf16[64,2048]{1,0:T(8,128)(2,1)S(1)} %get-tuple-element.176.refs_0_.refs_17_, bf16[64,2048]{1,0:T(8,128)(2,1)S(1)} %collective-permute-done.6.refs_1_.refs_18_, ...), custom_call_target="tpu_custom_call" | custom-call | tf_op jit(solution)/shard_map/pallas_call | solution.py:563
  77.2 0.0 collective-permute-done.23.refs_8_.refs_15_
  77.2 0.0 collective-permute-done.24.refs_9_.refs_16_
  77.2 2.8 %shard_map.98 = bf16[512,1024]{1,0:T(8,128)(2,1)} custom-call(s32[8]{0:T(128)S(1)} %copy-done.5, bf16[128,2048]{1,0:T(8,128)(2,1)S(1)} %get-tuple-element.111.refs_0_.kv.refs_1_.refs_2_, bf16[128,2048]{1,0:T(8,128)(2,1)S(1)} %get-tuple-element.112.refs_1_.qg.refs_2_.refs_3_, f32[512,512]{1,0:T(8,128)S(1)} %get-tuple-element.169.refs_3_, ...), custom_call_target="tpu_custom_call" | custom-call | tf_op jit(solution)/shard_map/pallas_call | solution.py:563
  80.0 0.0 collective-permute-done.22.refs_25_
  80.0 0.0 collective-permute-done.21.refs_24_
  80.0 5.8 %shard_map.100 = (bf16[512,1024]{1,0:T(8,128)(2,1)}, bf16[512,1024]{1,0:T(8,128)(2,1)}) custom-call(s32[8]{0:T(128)S(1)} %copy-done.5, s32[8]{0:T(128)S(1)} %copy-done.7, bf16[128,2048]{1,0:T(8,128)(2,1)S(1)} %get-tuple-element.111.refs_0_.kv.refs_1_.refs_2_, bf16[128,2048]{1,0:T(8,128)(2,1)S(1)} %get-tuple-element.112.refs_1_.qg.refs_2_.refs_3_, ...), custom_call_target="tpu_custom_call" | custom-call | tf_op jit(solution)/shard_map/pallas_call | solution.py:563
  (21 shorter events, 0.1 us)
Async XLA Ops:
  0.6 15.0 %copy-start.1 = (bf16[512,1024]{1,0:T(8,128)(2,1)S(1)}, bf16[512,1024]{1,0:T(8,128)(2,1)}, u32[]{:S(2)}) copy-start(bf16[512,1024]{1,0:T(8,128)(2,1)} %g.8) | copy-start | bytes 3145732
  0.6 15.0 %copy-start = (bf16[512,1024]{1,0:T(8,128)(2,1)S(1)}, bf16[512,1024]{1,0:T(8,128)(2,1)}, u32[]{:S(2)}) copy-start(bf16[512,1024]{1,0:T(8,128)(2,1)} %q.8) | copy-start | bytes 3145732
  0.7 15.0 %copy-start.3 = (bf16[512,1024]{1,0:T(8,128)(2,1)S(1)}, bf16[512,1024]{1,0:T(8,128)(2,1)}, u32[]{:S(2)}) copy-start(bf16[512,1024]{1,0:T(8,128)(2,1)} %v.4) | copy-start | bytes 3145732
  0.7 0.8 copy-start.4
  1.5 0.8 copy-start.6
  2.2 13.4 %copy-start.2 = (bf16[512,1024]{1,0:T(8,128)(2,1)S(1)}, bf16[512,1024]{1,0:T(8,128)(2,1)}, u32[]{:S(2)}) copy-start(bf16[512,1024]{1,0:T(8,128)(2,1)} %k.4) | copy-start | bytes 3145732
  5.5 19.9 %collective-permute-start.2 = (bf16[2,16,2048]{2,1,0:T(8,128)(2,1)S(1)}, bf16[2,16,2048]{2,1,0:T(8,128)(2,1)S(1)}, u32[]{:S(2)}, u32[]{:S(2)}) collective-permute-start(bf16[2,16,2048]{2,1,0:T(8,128)(2,1)S(1)} %get-tuple-element.118.refs_0_.far_own), channel_id=1, source_target_pairs={{0,3},{1,2},{2,1},{3,0},{4,7},{5,6},{6,5},{7,4},{8,11},{9,10},{10,... | collective-permute-start | bytes 393224 | tf_op jit(solution)/shard_map/ppermute | solution.py:557
  10.7 15.0 %collective-permute-start.1 = (bf16[2,16,2048]{2,1,0:T(8,128)(2,1)S(1)}, bf16[2,16,2048]{2,1,0:T(8,128)(2,1)S(1)}, u32[]{:S(2)}, u32[]{:S(2)}) collective-permute-start(bf16[2,16,2048]{2,1,0:T(8,128)(2,1)S(1)} %get-tuple-element.118.refs_0_.far_own), channel_id=1, source_target_pairs={{0,2},{1,3},{2,0},{3,1},{4,6},{5,7},{6,4},{7,5},{8,10},{9,11},{10,... | collective-permute-start | bytes 393224 | tf_op jit(solution)/shard_map/ppermute | solution.py:557
  10.7 15.0 %collective-permute-start = (bf16[2,16,2048]{2,1,0:T(8,128)(2,1)S(1)}, bf16[2,16,2048]{2,1,0:T(8,128)(2,1)S(1)}, u32[]{:S(2)}, u32[]{:S(2)}) collective-permute-start(bf16[2,16,2048]{2,1,0:T(8,128)(2,1)S(1)} %get-tuple-element.118.refs_0_.far_own), channel_id=1, source_target_pairs={{0,1},{1,0},{2,3},{3,2},{4,5},{5,4},{6,7},{7,6},{8,9},{9,8},{10,11... | collective-permute-start | bytes 393224 | tf_op jit(solution)/shard_map/ppermute | solution.py:557
  11.3 17.9 %collective-permute-start.3 = (bf16[128,1024]{1,0:T(8,128)(2,1)S(1)}, bf16[128,1024]{1,0:T(8,128)(2,1)S(1)}, u32[]{:S(2)}, u32[]{:S(2)}) collective-permute-start(bf16[128,1024]{1,0:T(8,128)(2,1)S(1)} %get-tuple-element.113), channel_id=1, source_target_pairs={{0,1},{1,0},{2,3},{3,2},{4,5},{5,4},{6,7},{7,6},{8,9},{9,8},{10,11... | collective-permute-start | bytes 786440 | tf_op jit(solution)/shard_map/ppermute | solution.py:557
  12.7 26.9 %collective-permute-start.4 = (bf16[128,1024]{1,0:T(8,128)(2,1)S(1)}, bf16[128,1024]{1,0:T(8,128)(2,1)S(1)}, u32[]{:S(2)}, u32[]{:S(2)}) collective-permute-start(bf16[128,1024]{1,0:T(8,128)(2,1)S(1)} %get-tuple-element.114), channel_id=1, source_target_pairs={{0,2},{1,3},{2,0},{3,1},{4,6},{5,7},{6,4},{7,5},{8,10},{9,11},{10,... | collective-permute-start | bytes 786440 | tf_op jit(solution)/shard_map/ppermute | solution.py:557
  25.5 14.1 %collective-permute-start.5 = (bf16[128,1024]{1,0:T(8,128)(2,1)S(1)}, bf16[128,1024]{1,0:T(8,128)(2,1)S(1)}, u32[]{:S(2)}, u32[]{:S(2)}) collective-permute-start(bf16[128,1024]{1,0:T(8,128)(2,1)S(1)} %get-tuple-element.115), channel_id=1, source_target_pairs={{0,3},{1,2},{2,1},{3,0},{4,7},{5,6},{6,5},{7,4},{8,11},{9,10},{10,... | collective-permute-start | bytes 786440 | tf_op jit(solution)/shard_map/ppermute | solution.py:557
  25.9 14.9 %collective-permute-start.6 = (bf16[64,2048]{1,0:T(8,128)(2,1)S(1)}, bf16[64,2048]{1,0:T(8,128)(2,1)S(1)}, u32[]{:S(2)}, u32[]{:S(2)}) collective-permute-start(bf16[64,2048]{1,0:T(8,128)(2,1)S(1)} %get-tuple-element.123), channel_id=1, source_target_pairs={{0,8},{4,12},{8,0},{12,4},{16,24},{20,28},{24,16},{28,20},{1,9},{5... | collective-permute-start | bytes 786440 | tf_op jit(solution)/shard_map/ppermute | solution.py:557
  27.6 13.2 %collective-permute-start.8 = (bf16[64,2048]{1,0:T(8,128)(2,1)S(1)}, bf16[64,2048]{1,0:T(8,128)(2,1)S(1)}, u32[]{:S(2)}, u32[]{:S(2)}) collective-permute-start(bf16[64,2048]{1,0:T(8,128)(2,1)S(1)} %get-tuple-element.124), channel_id=1, source_target_pairs={{0,24},{4,28},{8,16},{12,20},{16,8},{20,12},{24,0},{28,4},{1,25},{... | collective-permute-start | bytes 786440 | tf_op jit(solution)/shard_map/ppermute | solution.py:557
  29.2 13.2 %collective-permute-start.7 = (bf16[64,2048]{1,0:T(8,128)(2,1)S(1)}, bf16[64,2048]{1,0:T(8,128)(2,1)S(1)}, u32[]{:S(2)}, u32[]{:S(2)}) collective-permute-start(bf16[64,2048]{1,0:T(8,128)(2,1)S(1)} %get-tuple-element.124), channel_id=1, source_target_pairs={{0,16},{4,20},{8,24},{12,28},{16,0},{20,4},{24,8},{28,12},{1,17},{... | collective-permute-start | bytes 786440 | tf_op jit(solution)/shard_map/ppermute | solution.py:557
  39.6 1.2 %collective-permute-start.9 = (bf16[16,128]{1,0:T(8,128)(2,1)S(1)}, bf16[16,128]{1,0:T(8,128)(2,1)S(1)}, u32[]{:S(2)}, u32[]{:S(2)}) collective-permute-start(bf16[16,128]{1,0:T(8,128)(2,1)S(1)} %slice_add_fusion), channel_id=1, source_target_pairs={{0,4},{4,0},{8,12},{12,8},{16,20},{20,16},{24,28},{28,24},{1,5},{5... | collective-permute-start | bytes 12296 | tf_op jit(solution)/shard_map/ppermute | solution.py:557
  42.5 8.7 %collective-permute-start.10 = (bf16[256,2048]{1,0:T(8,128)(2,1)S(1)}, bf16[256,2048]{1,0:T(8,128)(2,1)S(1)}, u32[]{:S(2)}, u32[]{:S(2)}) collective-permute-start(bf16[256,2048]{1,0:T(8,128)(2,1)S(1)} %shard_map.90), channel_id=1, source_target_pairs={{0,4},{4,0},{8,12},{12,8},{16,20},{20,16},{24,28},{28,24},{1,5},{5... | collective-permute-start | bytes 3145736 | tf_op jit(solution)/shard_map/ppermute | solution.py:557
  42.6 17.3 %collective-permute-start.15 = (bf16[128,1024]{1,0:T(8,128)(2,1)S(1)}, bf16[128,1024]{1,0:T(8,128)(2,1)S(1)}, u32[]{:S(2)}, u32[]{:S(2)}) collective-permute-start(bf16[128,1024]{1,0:T(8,128)(2,1)S(1)} %get-tuple-element.139), channel_id=1, source_target_pairs={{0,1},{1,0},{2,3},{3,2},{4,5},{5,4},{6,7},{7,6},{8,9},{9,8},{10,11... | collective-permute-start | bytes 786440 | tf_op jit(solution)/shard_map/ppermute | solution.py:557
  46.4 13.5 %collective-permute-start.14 = (bf16[96,1024]{1,0:T(8,128)(2,1)S(1)}, bf16[96,1024]{1,0:T(8,128)(2,1)S(1)}, u32[]{:S(2)}, u32[]{:S(2)}) collective-permute-start(bf16[96,1024]{1,0:T(8,128)(2,1)S(1)} %slice.19), channel_id=1, source_target_pairs={{0,2},{1,3},{2,0},{3,1},{4,6},{5,7},{6,4},{7,5},{8,10},{9,11},{10,... | collective-permute-start | bytes 589832 | tf_op jit(solution)/shard_map/ppermute | solution.py:557
  47.5 14.5 %copy-start.7 = (s32[8]{0:T(128)S(1)}, s32[8]{0:T(128)}, u32[]{:S(2)}) copy-start(s32[8]{0:T(128)} %refs_1_.3) | copy-start | bytes 100
  49.2 8.4 %collective-permute-start.11 = (f32[8,128]{1,0:T(8,128)S(1)}, f32[8,128]{1,0:T(8,128)S(1)}, u32[]{:S(2)}, u32[]{:S(2)}) collective-permute-start(f32[8,128]{1,0:T(8,128)S(1)} %get-tuple-element.130), channel_id=1, source_target_pairs={{0,1},{1,0},{2,3},{3,2},{4,5},{5,4},{6,7},{7,6},{8,9},{9,8},{10,11... | collective-permute-start | bytes 12296 | tf_op jit(solution)/shard_map/ppermute | solution.py:557
  51.2 6.4 %collective-permute-start.12 = (f32[8,128]{1,0:T(8,128)S(1)}, f32[8,128]{1,0:T(8,128)S(1)}, u32[]{:S(2)}, u32[]{:S(2)}) collective-permute-start(f32[8,128]{1,0:T(8,128)S(1)} %get-tuple-element.131), channel_id=1, source_target_pairs={{0,2},{1,3},{2,0},{3,1},{4,6},{5,7},{6,4},{7,5},{8,10},{9,11},{10,... | collective-permute-start | bytes 12296 | tf_op jit(solution)/shard_map/ppermute | solution.py:557
  51.2 8.7 %collective-permute-start.13 = (f32[8,128]{1,0:T(8,128)S(1)}, f32[8,128]{1,0:T(8,128)S(1)}, u32[]{:S(2)}, u32[]{:S(2)}) collective-permute-start(f32[8,128]{1,0:T(8,128)S(1)} %get-tuple-element.132), channel_id=1, source_target_pairs={{0,3},{1,2},{2,1},{3,0},{4,7},{5,6},{6,5},{7,4},{8,11},{9,10},{10,... | collective-permute-start | bytes 12296 | tf_op jit(solution)/shard_map/ppermute | solution.py:557
  59.9 17.3 %collective-permute-start.24 = (bf16[128,1024]{1,0:T(8,128)(2,1)S(1)}, bf16[128,1024]{1,0:T(8,128)(2,1)S(1)}, u32[]{:S(2)}, u32[]{:S(2)}) collective-permute-start(bf16[128,1024]{1,0:T(8,128)(2,1)S(1)} %get-tuple-element.174), channel_id=1, source_target_pairs={{0,3},{1,2},{2,1},{3,0},{4,7},{5,6},{6,5},{7,4},{8,11},{9,10},{10,... | collective-permute-start | bytes 786440 | tf_op jit(solution)/shard_map/ppermute | solution.py:557
  61.3 15.9 %collective-permute-start.23 = (bf16[32,1024]{1,0:T(8,128)(2,1)S(1)}, bf16[32,1024]{1,0:T(8,128)(2,1)S(1)}, u32[]{:S(2)}, u32[]{:S(2)}) collective-permute-start(bf16[32,1024]{1,0:T(8,128)(2,1)S(1)} %slice.18), channel_id=1, source_target_pairs={{0,2},{1,3},{2,0},{3,1},{4,6},{5,7},{6,4},{7,5},{8,10},{9,11},{10,... | collective-permute-start | bytes 196616 | tf_op jit(solution)/shard_map/ppermute | solution.py:557
  63.0 6.8 %collective-permute-start.18 = (f32[16,16]{1,0:T(8,128)S(1)}, f32[16,16]{1,0:T(8,128)S(1)}, u32[]{:S(2)}, u32[]{:S(2)}) collective-permute-start(f32[16,16]{1,0:T(8,128)S(1)} %get-tuple-element.158.refs_0_), channel_id=1, source_target_pairs={{0,24},{4,28},{8,16},{12,20},{16,8},{20,12},{24,0},{28,4},{1,25},{... | collective-permute-start | bytes 3080 | tf_op jit(solution)/shard_map/ppermute | solution.py:557
  65.5 4.3 %collective-permute-start.17 = (f32[16,16]{1,0:T(8,128)S(1)}, f32[16,16]{1,0:T(8,128)S(1)}, u32[]{:S(2)}, u32[]{:S(2)}) collective-permute-start(f32[16,16]{1,0:T(8,128)S(1)} %get-tuple-element.158.refs_0_), channel_id=1, source_target_pairs={{0,16},{4,20},{8,24},{12,28},{16,0},{20,4},{24,8},{28,12},{1,17},{... | collective-permute-start | bytes 3080 | tf_op jit(solution)/shard_map/ppermute | solution.py:557
  66.0 3.8 %collective-permute-start.16 = (f32[16,16]{1,0:T(8,128)S(1)}, f32[16,16]{1,0:T(8,128)S(1)}, u32[]{:S(2)}, u32[]{:S(2)}) collective-permute-start(f32[16,16]{1,0:T(8,128)S(1)} %get-tuple-element.158.refs_0_), channel_id=1, source_target_pairs={{0,8},{4,12},{8,0},{12,4},{16,24},{20,28},{24,16},{28,20},{1,9},{5... | collective-permute-start | bytes 3080 | tf_op jit(solution)/shard_map/ppermute | solution.py:557
  67.8 2.1 %copy-start.5 = (s32[8]{0:T(128)S(1)}, s32[8]{0:T(128)}, u32[]{:S(2)}) copy-start(s32[8]{0:T(128)} %refs_0_.5) | copy-start | bytes 100
  69.9 1.9 %collective-permute-start.19 = (f32[16,64]{1,0:T(8,128)S(1)}, f32[16,64]{1,0:T(8,128)S(1)}, u32[]{:S(2)}, u32[]{:S(2)}) collective-permute-start(f32[16,64]{1,0:T(8,128)S(1)} %shard_map.95.refs_1_), channel_id=1, source_target_pairs={{0,4},{4,0},{8,12},{12,8},{16,20},{20,16},{24,28},{28,24},{1,5},{5... | collective-permute-start | bytes 12296 | tf_op jit(solution)/shard_map/ppermute | solution.py:557
  71.9 8.1 %collective-permute-start.22 = (f32[16,256]{1,0:T(8,128)S(1)}, f32[16,256]{1,0:T(8,128)S(1)}, u32[]{:S(2)}, u32[]{:S(2)}) collective-permute-start(f32[16,256]{1,0:T(8,128)S(1)} %shard_map.97.refs_22_), channel_id=1, source_target_pairs={{0,3},{1,2},{2,1},{3,0},{4,7},{5,6},{6,5},{7,4},{8,11},{9,10},{10,... | collective-permute-start | bytes 49160 | tf_op jit(solution)/shard_map/ppermute | solution.py:557
  73.7 6.4 %collective-permute-start.21 = (f32[16,256]{1,0:T(8,128)S(1)}, f32[16,256]{1,0:T(8,128)S(1)}, u32[]{:S(2)}, u32[]{:S(2)}) collective-permute-start(f32[16,256]{1,0:T(8,128)S(1)} %shard_map.97.refs_22_), channel_id=1, source_target_pairs={{0,2},{1,3},{2,0},{3,1},{4,6},{5,7},{6,4},{7,5},{8,10},{9,11},{10,... | collective-permute-start | bytes 49160 | tf_op jit(solution)/shard_map/ppermute | solution.py:557
  75.7 4.3 %collective-permute-start.20 = (f32[16,256]{1,0:T(8,128)S(1)}, f32[16,256]{1,0:T(8,128)S(1)}, u32[]{:S(2)}, u32[]{:S(2)}) collective-permute-start(f32[16,256]{1,0:T(8,128)S(1)} %shard_map.97.refs_22_), channel_id=1, source_target_pairs={{0,1},{1,0},{2,3},{3,2},{4,5},{5,4},{6,7},{7,6},{8,9},{9,8},{10,11... | collective-permute-start | bytes 49160 | tf_op jit(solution)/shard_map/ppermute | solution.py:557

commit v8 on v7

--- a/solution.py
+++ b/solution.py
@@ -599,11 +599,12 @@
     kv, qg, far, *pays = call(
         select_kernel,
         steps,
-        scalars + [(spec, pltpu.with_memory_space_constraint(x, pltpu.HBM)) for spec, x in sources],
+        scalars + sources,
         [(mid_spec, mid_shape)] * 2
         + [(far_spec, shape((2, far_count, 2 * flat), BF16))]
         + [(half_spec, half_shape)] * (2 * mids),
         [pltpu.VMEM((4 * per, rows, LANES), F32)],
+        60,
     )
     far_level = [far] + [swap(far, "lvl", levels, step) for step in range(1, levels)]
     first = list(pays[:mids])

time: 86 us -> 85.9 us (level)
  Pallas kernels: 34.8 us -> 36.1 us
  starting transfers between devices: 34.4 us -> 33.4 us
    pallas_call x16, Pallas kernels: 34.8 us -> 36.1 us  [call(): pl.pallas_call(kernel, grid=(steps,), in_specs=list(specs), out_specs=lis...]
    ppermute x25, starting transfers between devices: 34.4 us -> 33.4 us  [swap(): return lax.ppermute(array, axis, [(i, i ^ step) for i in range(size)])]
  transfers between devices with their start and end apart: 25 -> 25, of which waited for: 6 -> 4; matrix products, arithmetic and copies ran while one was open for 0% -> 0% of each run, Pallas kernels for 30% -> 30%
where the time goes in v8:
time: 85.9 us; the launch traced here: 85.8 us
  Pallas kernels  36.1 us (42%)
  starting transfers between devices  33.4 us (39%)
  waiting for transfers between devices  14 us (16%)
  local copies, waits for them, and re-layouts  1.3 us (2%)
  between operations  0.95 us (1%)
    pallas_call x16, Pallas kernels, call(): pl.pallas_call(kernel, grid=(steps,), in_specs=list(specs), out_specs=lis...  36.1 us
    ppermute x25, starting transfers between devices, swap(): return lax.ppermute(array, axis, [(i, i ^ step) for i in range(size)])  33.4 us
    ppermute x25, waiting for transfers between devices, swap(): return lax.ppermute(array, axis, [(i, i ^ step) for i in range(size)])  14 us
  transfers between devices with their start and end apart: 25, of which 4 were waited for; matrix products, arithmetic and copies ran while one was open for 0% of the time, Pallas kernels for 30%

profile of v8, /device:TPU:0, one launch (start us, length us, event | category | flops | bytes accessed | tf_op | source)
XLA Modules:
  0.0 85.8 jit_solution(10408500129215444425)
XLA Ops:
  0.7 4.6 %shard_map.86 = (bf16[128,2048]{1,0:T(8,128)(2,1)}, bf16[128,2048]{1,0:T(8,128)(2,1)}, bf16[2,16,2048]{2,1,0:T(8,128)(2,1)}, bf16[128,1024]{1,0:T(8,128)(2,1)}, ...) custom-call(s32[8]{0:T(128)} %refs_0_.5, ...), custom_call_target="tpu_custom_call" | custom-call | tf_op jit(solution)/shard_map/pallas_call | solution.py:563
  5.3 5.1 %collective-permute-start.2 = (bf16[2,16,2048]{2,1,0:T(8,128)(2,1)}, bf16[2,16,2048]{2,1,0:T(8,128)(2,1)S(1)}, u32[]{:S(2)}, u32[]{:S(2)}) collective-permute-start(bf16[2,16,2048]{2,1,0:T(8,128)(2,1)} %get-tuple-element.118.refs_0_.far_own), channel_id=1, source_target_pairs={{0,3},{1,2},{2,1},{3,0},{4,7},{5,6},{6,5},{7,4},{8,11},{9,10},{10,... | collective-permute-start | bytes 393224 | tf_op jit(solution)/shard_map/ppermute | solution.py:557
  10.4 0.0 collective-permute-start.1
  10.4 0.6 collective-permute-start
  11.0 1.4 %collective-permute-start.3 = (bf16[128,1024]{1,0:T(8,128)(2,1)}, bf16[128,1024]{1,0:T(8,128)(2,1)S(1)}, u32[]{:S(2)}, u32[]{:S(2)}) collective-permute-start(bf16[128,1024]{1,0:T(8,128)(2,1)} %get-tuple-element.113), channel_id=1, source_target_pairs={{0,1},{1,0},{2,3},{3,2},{4,5},{5,4},{6,7},{7,6},{8,9},{9,8},{10,11... | collective-permute-start | bytes 786440 | tf_op jit(solution)/shard_map/ppermute | solution.py:557
  12.4 2.9 %collective-permute-start.4 = (bf16[128,1024]{1,0:T(8,128)(2,1)}, bf16[128,1024]{1,0:T(8,128)(2,1)S(1)}, u32[]{:S(2)}, u32[]{:S(2)}) collective-permute-start(bf16[128,1024]{1,0:T(8,128)(2,1)} %get-tuple-element.114), channel_id=1, source_target_pairs={{0,2},{1,3},{2,0},{3,1},{4,6},{5,7},{6,4},{7,5},{8,10},{9,11},{10,... | collective-permute-start | bytes 786440 | tf_op jit(solution)/shard_map/ppermute | solution.py:557
  15.3 1.2 %copy-done.3 = bf16[512,1024]{1,0:T(8,128)(2,1)S(1)} copy-done((bf16[512,1024]{1,0:T(8,128)(2,1)S(1)}, bf16[512,1024]{1,0:T(8,128)(2,1)}, u32[]{:S(2)}) %copy-start.3) | copy-done | bytes 1048600
  16.6 4.9 %shard_map.85 = (f32[8,512]{1,0:T(8,128)S(1)}, bf16[4,512,512]{2,1,0:T(8,128)(2,1)S(1)}, bf16[4,512,512]{2,1,0:T(8,128)(2,1)S(1)}, f32[512,1024]{1,0:T(8,128)S(1)}) custom-call(bf16[512,1024]{1,0:T(8,128)(2,1)S(1)} %copy-done, bf16[512,1024]{1,0:T(8,128)(2,1)S(1)} %copy-done.2, bf16[512,1024]{1,0:T(8,128)(2,1)S(1)} %copy-done.3, bf16[512,1024]{1,0:T(8,128)(2,1)S(1)} %copy-done.1), custom_call_target="tpu_custom_call" | custom-call | tf_op jit(solution)/shard_map/pallas_call | solution.py:563
  21.5 4.9 %shard_map.87 = (f32[8,512]{1,0:T(8,128)S(1)}, bf16[4,512,512]{2,1,0:T(8,128)(2,1)S(1)}, bf16[4,512,512]{2,1,0:T(8,128)(2,1)S(1)}, f32[512,1024]{1,0:T(8,128)S(1)}) custom-call(bf16[512,1024]{1,0:T(8,128)(2,1)S(1)} %copy-done, bf16[512,1024]{1,0:T(8,128)(2,1)S(1)} %copy-done.2, bf16[512,1024]{1,0:T(8,128)(2,1)S(1)} %copy-done.3, bf16[512,1024]{1,0:T(8,128)(2,1)S(1)} %copy-done.1), custom_call_target="tpu_custom_call" | custom-call | tf_op jit(solution)/shard_map/pallas_call | solution.py:563
  26.4 0.0 collective-permute-done.2.refs_3_
  26.5 0.1 collective-permute-start.5
  26.6 0.0 collective-permute-done.1.refs_2_
  26.6 0.0 collective-permute-done.refs_1_
  26.6 0.3 shard_map.89
  26.9 0.0 copy-start.4
  26.9 0.0 copy-start.5
  27.0 1.7 %collective-permute-start.6 = (bf16[64,2048]{1,0:T(8,128)(2,1)S(1)}, bf16[64,2048]{1,0:T(8,128)(2,1)S(1)}, u32[]{:S(2)}, u32[]{:S(2)}) collective-permute-start(bf16[64,2048]{1,0:T(8,128)(2,1)S(1)} %get-tuple-element.123), channel_id=1, source_target_pairs={{0,8},{4,12},{8,0},{12,4},{16,24},{20,28},{24,16},{28,20},{1,9},{5... | collective-permute-start | bytes 786440 | tf_op jit(solution)/shard_map/ppermute | solution.py:557
  28.7 1.5 %collective-permute-start.8 = (bf16[64,2048]{1,0:T(8,128)(2,1)S(1)}, bf16[64,2048]{1,0:T(8,128)(2,1)S(1)}, u32[]{:S(2)}, u32[]{:S(2)}) collective-permute-start(bf16[64,2048]{1,0:T(8,128)(2,1)S(1)} %get-tuple-element.124), channel_id=1, source_target_pairs={{0,24},{4,28},{8,16},{12,20},{16,8},{20,12},{24,0},{28,4},{1,25},{... | collective-permute-start | bytes 786440 | tf_op jit(solution)/shard_map/ppermute | solution.py:557
  30.2 0.0 collective-permute-done.3.refs_2_.refs_0_.refs_10_
  30.2 0.5 collective-permute-start.7
  30.7 8.8 %collective-permute-done.4.refs_3_.refs_1_.refs_11_ = bf16[128,1024]{1,0:T(8,128)(2,1)S(1)} collective-permute-done((bf16[128,1024]{1,0:T(8,128)(2,1)}, bf16[128,1024]{1,0:T(8,128)(2,1)S(1)}, u32[]{:S(2)}, u32[]{:S(2)}) %collective-permute-start.4) | collective-permute-done | bytes 262176 | tf_op jit(solution)/shard_map/ppermute | solution.py:557
  39.5 0.0 collective-permute-done.5.refs_4_.refs_2_.refs_12_
  39.5 0.1 collective-permute-start.9
  39.6 1.2 %collective-permute-done.9.refs_4_ = bf16[16,128]{1,0:T(8,128)(2,1)S(1)} collective-permute-done((bf16[16,128]{1,0:T(8,128)(2,1)S(1)}, bf16[16,128]{1,0:T(8,128)(2,1)S(1)}, u32[]{:S(2)}, u32[]{:S(2)}) %collective-permute-start.9) | collective-permute-done | bytes 4128 | tf_op jit(solution)/shard_map/ppermute | solution.py:557
  40.8 1.9 %collective-permute-done.7.refs_2_.refs_19_ = bf16[64,2048]{1,0:T(8,128)(2,1)S(1)} collective-permute-done((bf16[64,2048]{1,0:T(8,128)(2,1)S(1)}, bf16[64,2048]{1,0:T(8,128)(2,1)S(1)}, u32[]{:S(2)}, u32[]{:S(2)}) %collective-permute-start.7) | collective-permute-done | bytes 262176 | tf_op jit(solution)/shard_map/ppermute | solution.py:557
  42.7 0.1 shard_map.90
  42.7 0.1 collective-permute-start.10
  42.9 3.5 %collective-permute-start.15 = (bf16[128,1024]{1,0:T(8,128)(2,1)S(1)}, bf16[128,1024]{1,0:T(8,128)(2,1)S(1)}, u32[]{:S(2)}, u32[]{:S(2)}) collective-permute-start(bf16[128,1024]{1,0:T(8,128)(2,1)S(1)} %copy-done.11), channel_id=1, source_target_pairs={{0,1},{1,0},{2,3},{3,2},{4,5},{5,4},{6,7},{7,6},{8,9},{9,8},{10,11... | collective-permute-start | bytes 786440 | tf_op jit(solution)/shard_map/ppermute | solution.py:557
  46.3 1.3 %collective-permute-start.14 = (bf16[96,1024]{1,0:T(8,128)(2,1)S(1)}, bf16[96,1024]{1,0:T(8,128)(2,1)S(1)}, u32[]{:S(2)}, u32[]{:S(2)}) collective-permute-start(bf16[96,1024]{1,0:T(8,128)(2,1)S(1)} %slice.19), channel_id=1, source_target_pairs={{0,2},{1,3},{2,0},{3,1},{4,6},{5,7},{6,4},{7,5},{8,10},{9,11},{10,... | collective-permute-start | bytes 589832 | tf_op jit(solution)/shard_map/ppermute | solution.py:557
  47.7 0.0 copy-start.8
  47.7 1.7 %shard_map.88 = (f32[128,128]{1,0:T(8,128)S(1)}, f32[128,128]{1,0:T(8,128)S(1)}, f32[8,128]{1,0:T(8,128)S(1)}, f32[8,128]{1,0:T(8,128)S(1)}, f32[8,128]{1,0:T(8,128)S(1)}) custom-call(bf16[128,2048]{1,0:T(8,128)(2,1)S(1)} %copy-done.4, bf16[128,2048]{1,0:T(8,128)(2,1)S(1)} %copy-done.5, ...), custom_call_target="tpu_custom_call" | custom-call | tf_op jit(solution)/shard_map/pallas_call | solution.py:563
  49.4 1.8 %collective-permute-start.11 = (f32[8,128]{1,0:T(8,128)S(1)}, f32[8,128]{1,0:T(8,128)S(1)}, u32[]{:S(2)}, u32[]{:S(2)}) collective-permute-start(f32[8,128]{1,0:T(8,128)S(1)} %get-tuple-element.130), channel_id=1, source_target_pairs={{0,1},{1,0},{2,3},{3,2},{4,5},{5,4},{6,7},{7,6},{8,9},{9,8},{10,11... | collective-permute-start | bytes 12296 | tf_op jit(solution)/shard_map/ppermute | solution.py:557
  51.1 0.0 collective-permute-start.12
  51.2 0.0 collective-permute-done.10.refs_4_.refs_21_
  51.2 2.7 %collective-permute-start.13 = (f32[8,128]{1,0:T(8,128)S(1)}, f32[8,128]{1,0:T(8,128)S(1)}, u32[]{:S(2)}, u32[]{:S(2)}) collective-permute-start(f32[8,128]{1,0:T(8,128)S(1)} %get-tuple-element.132), channel_id=1, source_target_pairs={{0,3},{1,2},{2,1},{3,0},{4,7},{5,6},{6,5},{7,4},{8,11},{9,10},{10,... | collective-permute-start | bytes 12296 | tf_op jit(solution)/shard_map/ppermute | solution.py:557
  53.8 3.9 %shard_map.91 = (f32[16,2048]{1,0:T(8,128)S(1)}, f32[16,128]{1,0:T(8,128)S(1)}, f32[16,128]{1,0:T(8,128)S(1)}) custom-call(bf16[2,16,2048]{2,1,0:T(8,128)(2,1)S(1)} %copy-done.6, bf16[64,2048]{1,0:T(8,128)(2,1)S(1)} %get-tuple-element.122.refs_0_, bf16[64,2048]{1,0:T(8,128)(2,1)S(1)} %collective-permute-done.6.refs_1_.refs_18_, ...), custom_call_target="tpu_custom_call" | custom-call | tf_op jit(solution)/shard_map/pallas_call | solution.py:563
  57.7 0.0 collective-permute-done.11.refs_8_
  57.7 2.1 %collective-permute-done.13.refs_10_ = f32[8,128]{1,0:T(8,128)S(1)} collective-permute-done((f32[8,128]{1,0:T(8,128)S(1)}, f32[8,128]{1,0:T(8,128)S(1)}, u32[]{:S(2)}, u32[]{:S(2)}) %collective-permute-start.13) | collective-permute-done | bytes 4128 | tf_op jit(solution)/shard_map/ppermute | solution.py:557
  59.8 1.5 %collective-permute-start.24 = (bf16[128,1024]{1,0:T(8,128)(2,1)S(1)}, bf16[128,1024]{1,0:T(8,128)(2,1)S(1)}, u32[]{:S(2)}, u32[]{:S(2)}) collective-permute-start(bf16[128,1024]{1,0:T(8,128)(2,1)S(1)} %copy-done.10), channel_id=1, source_target_pairs={{0,3},{1,2},{2,1},{3,0},{4,7},{5,6},{6,5},{7,4},{8,11},{9,10},{10,... | collective-permute-start | bytes 786440 | tf_op jit(solution)/shard_map/ppermute | solution.py:557
  61.3 0.6 collective-permute-start.23
  61.9 1.1 %shard_map.92 = (f32[512,128]{1,0:T(8,128)S(1)}, f32[128,128]{1,0:T(8,128)S(1)}, f32[16,128]{1,0:T(8,128)S(1)}, f32[16,128]{1,0:T(8,128)S(1)}, f32[16,16]{1,0:T(8,128)S(1)}) custom-call(s32[8]{0:T(128)S(1)} %copy-done.7, s32[8]{0:T(128)S(1)} %copy-done.8, f32[8,512]{1,0:T(8,128)S(1)} %get-tuple-element.100.refs_2_, f32[8,512]{1,0:T(8,128)S(1)} %get-tuple-element.110.refs_3_, ...), custom_call_target="tpu_custom_call" | custom-call | tf_op jit(solution)/shard_map/pallas_call | solution.py:563
  63.0 2.5 %collective-permute-start.18 = (f32[16,16]{1,0:T(8,128)S(1)}, f32[16,16]{1,0:T(8,128)S(1)}, u32[]{:S(2)}, u32[]{:S(2)}) collective-permute-start(f32[16,16]{1,0:T(8,128)S(1)} %get-tuple-element.158.refs_0_), channel_id=1, source_target_pairs={{0,24},{4,28},{8,16},{12,20},{16,8},{20,12},{24,0},{28,4},{1,25},{... | collective-permute-start | bytes 3080 | tf_op jit(solution)/shard_map/ppermute | solution.py:557
  65.5 0.5 collective-permute-start.17
  66.0 0.5 collective-permute-start.16
  66.5 1.2 %shard_map.93.refs_3_ = f32[128,1024]{1,0:T(8,128)S(1)} custom-call(bf16[128,2048]{1,0:T(8,128)(2,1)S(1)} %copy-done.4, bf16[128,2048]{1,0:T(8,128)(2,1)S(1)} %copy-done.5, f32[128,128]{1,0:T(8,128)S(1)} %get-tuple-element.116.refs_4_.mlog, f32[128,128]{1,0:T(8,128)S(1)} %get-tuple-element.117.refs_5_.mdot, ...), custom_call_target="tpu_custom_call" | custom-call | tf_op jit(solution)/shard_map/pallas_call | solution.py:563
  67.7 2.0 %shard_map.94 = (f32[512,512]{1,0:T(8,128)S(1)}, f32[512,512]{1,0:T(8,128)S(1)}, f32[512,512]{1,0:T(8,128)S(1)}) custom-call(s32[8]{0:T(128)S(1)} %copy-done.7, s32[8]{0:T(128)S(1)} %copy-done.8, bf16[512,1024]{1,0:T(8,128)(2,1)S(1)} %copy-done, bf16[512,1024]{1,0:T(8,128)(2,1)S(1)} %copy-done.1, bf16[4,512,512]{2,1,0:T(8,128)(2,1)S(1)} %get-tuple-element.145.soft_in, ...), custom_call_target="tpu_custom_call" | custom-call | tf_op jit(solution)/shard_map/pallas_call | solution.py:563
  69.7 0.0 collective-permute-done.18.refs_3_
  69.7 0.0 collective-permute-done.17.refs_2_
  69.7 0.1 shard_map.95.refs_1_
  69.8 0.0 collective-permute-start.19
  69.8 1.9 %shard_map.96 = (f32[512,512]{1,0:T(8,128)S(1)}, f32[512,512]{1,0:T(8,128)S(1)}, f32[512,512]{1,0:T(8,128)S(1)}) custom-call(s32[8]{0:T(128)S(1)} %copy-done.7, s32[8]{0:T(128)S(1)} %copy-done.8, bf16[512,1024]{1,0:T(8,128)(2,1)S(1)} %copy-done, bf16[512,1024]{1,0:T(8,128)(2,1)S(1)} %copy-done.1, bf16[4,512,512]{2,1,0:T(8,128)(2,1)S(1)} %get-tuple-element.162.soft_in, ...), custom_call_target="tpu_custom_call" | custom-call | tf_op jit(solution)/shard_map/pallas_call | solution.py:563
  71.7 0.0 collective-permute-done.19.refs_2_
  71.7 0.1 shard_map.97.refs_22_
  71.8 1.8 %collective-permute-start.22 = (f32[16,256]{1,0:T(8,128)S(1)}, f32[16,256]{1,0:T(8,128)S(1)}, u32[]{:S(2)}, u32[]{:S(2)}) collective-permute-start(f32[16,256]{1,0:T(8,128)S(1)} %shard_map.97.refs_22_), channel_id=1, source_target_pairs={{0,3},{1,2},{2,1},{3,0},{4,7},{5,6},{6,5},{7,4},{8,11},{9,10},{10,... | collective-permute-start | bytes 49160 | tf_op jit(solution)/shard_map/ppermute | solution.py:557
  73.7 2.0 %collective-permute-start.21 = (f32[16,256]{1,0:T(8,128)S(1)}, f32[16,256]{1,0:T(8,128)S(1)}, u32[]{:S(2)}, u32[]{:S(2)}) collective-permute-start(f32[16,256]{1,0:T(8,128)S(1)} %shard_map.97.refs_22_), channel_id=1, source_target_pairs={{0,2},{1,3},{2,0},{3,1},{4,6},{5,7},{6,4},{7,5},{8,10},{9,11},{10,... | collective-permute-start | bytes 49160 | tf_op jit(solution)/shard_map/ppermute | solution.py:557
  75.7 0.5 collective-permute-start.20
  76.2 0.9 %shard_map.99 = (f32[128,512]{1,0:T(8,128)S(1)}, f32[128,512]{1,0:T(8,128)S(1)}) custom-call(bf16[2,16,2048]{2,1,0:T(8,128)(2,1)S(1)} %copy-done.6, bf16[64,2048]{1,0:T(8,128)(2,1)S(1)} %get-tuple-element.176.refs_0_.refs_17_, bf16[64,2048]{1,0:T(8,128)(2,1)S(1)} %collective-permute-done.6.refs_1_.refs_18_, ...), custom_call_target="tpu_custom_call" | custom-call | tf_op jit(solution)/shard_map/pallas_call | solution.py:563
  77.2 0.0 collective-permute-done.23.refs_8_.refs_15_
  77.2 0.0 collective-permute-done.24.refs_9_.refs_16_
  77.2 2.8 %shard_map.98 = bf16[512,1024]{1,0:T(8,128)(2,1)} custom-call(s32[8]{0:T(128)S(1)} %copy-done.7, bf16[128,2048]{1,0:T(8,128)(2,1)S(1)} %copy-done.4, bf16[128,2048]{1,0:T(8,128)(2,1)S(1)} %copy-done.5, f32[512,512]{1,0:T(8,128)S(1)} %get-tuple-element.169.refs_3_, f32[512,512]{1,0:T(8,128)S(1)} %get-tuple-element.170.refs_4_, ...), custom_call_target="tpu_custom_call" | custom-call | tf_op jit(solution)/shard_map/pallas_call | solution.py:563
  80.0 0.0 collective-permute-done.22.refs_25_
  80.0 0.0 collective-permute-done.21.refs_24_
  80.0 0.0 collective-permute-done.20.refs_23_
  80.0 5.8 %shard_map.100 = (bf16[512,1024]{1,0:T(8,128)(2,1)}, bf16[512,1024]{1,0:T(8,128)(2,1)}) custom-call(s32[8]{0:T(128)S(1)} %copy-done.7, s32[8]{0:T(128)S(1)} %copy-done.8, bf16[128,2048]{1,0:T(8,128)(2,1)S(1)} %copy-done.4, bf16[128,2048]{1,0:T(8,128)(2,1)S(1)} %copy-done.5, f32[128,512]{1,0:T(8,128)S(1)} %get-tuple-element.177.refs_4_, ...), custom_call_target="tpu_custom_call" | custom-call | tf_op jit(solution)/shard_map/pallas_call | solution.py:563
  (31 shorter events, 0.1 us)
Async XLA Ops:
  0.6 14.7 %copy-start.1 = (bf16[512,1024]{1,0:T(8,128)(2,1)S(1)}, bf16[512,1024]{1,0:T(8,128)(2,1)}, u32[]{:S(2)}) copy-start(bf16[512,1024]{1,0:T(8,128)(2,1)} %g.8) | copy-start | bytes 3145732
  0.6 14.7 %copy-start = (bf16[512,1024]{1,0:T(8,128)(2,1)S(1)}, bf16[512,1024]{1,0:T(8,128)(2,1)}, u32[]{:S(2)}) copy-start(bf16[512,1024]{1,0:T(8,128)(2,1)} %q.8) | copy-start | bytes 3145732
  0.7 14.7 %copy-start.2 = (bf16[512,1024]{1,0:T(8,128)(2,1)S(1)}, bf16[512,1024]{1,0:T(8,128)(2,1)}, u32[]{:S(2)}) copy-start(bf16[512,1024]{1,0:T(8,128)(2,1)} %k.4) | copy-start | bytes 3145732
  5.3 21.2 %collective-permute-start.2 = (bf16[2,16,2048]{2,1,0:T(8,128)(2,1)}, bf16[2,16,2048]{2,1,0:T(8,128)(2,1)S(1)}, u32[]{:S(2)}, u32[]{:S(2)}) collective-permute-start(bf16[2,16,2048]{2,1,0:T(8,128)(2,1)} %get-tuple-element.118.refs_0_.far_own), channel_id=1, source_target_pairs={{0,3},{1,2},{2,1},{3,0},{4,7},{5,6},{6,5},{7,4},{8,11},{9,10},{10,... | collective-permute-start | bytes 393224 | tf_op jit(solution)/shard_map/ppermute | solution.py:557
  10.4 16.2 %collective-permute-start.1 = (bf16[2,16,2048]{2,1,0:T(8,128)(2,1)}, bf16[2,16,2048]{2,1,0:T(8,128)(2,1)S(1)}, u32[]{:S(2)}, u32[]{:S(2)}) collective-permute-start(bf16[2,16,2048]{2,1,0:T(8,128)(2,1)} %get-tuple-element.118.refs_0_.far_own), channel_id=1, source_target_pairs={{0,2},{1,3},{2,0},{3,1},{4,6},{5,7},{6,4},{7,5},{8,10},{9,11},{10,... | collective-permute-start | bytes 393224 | tf_op jit(solution)/shard_map/ppermute | solution.py:557
  10.4 16.2 %collective-permute-start = (bf16[2,16,2048]{2,1,0:T(8,128)(2,1)}, bf16[2,16,2048]{2,1,0:T(8,128)(2,1)S(1)}, u32[]{:S(2)}, u32[]{:S(2)}) collective-permute-start(bf16[2,16,2048]{2,1,0:T(8,128)(2,1)} %get-tuple-element.118.refs_0_.far_own), channel_id=1, source_target_pairs={{0,1},{1,0},{2,3},{3,2},{4,5},{5,4},{6,7},{7,6},{8,9},{9,8},{10,11... | collective-permute-start | bytes 393224 | tf_op jit(solution)/shard_map/ppermute | solution.py:557
  11.0 19.1 %collective-permute-start.3 = (bf16[128,1024]{1,0:T(8,128)(2,1)}, bf16[128,1024]{1,0:T(8,128)(2,1)S(1)}, u32[]{:S(2)}, u32[]{:S(2)}) collective-permute-start(bf16[128,1024]{1,0:T(8,128)(2,1)} %get-tuple-element.113), channel_id=1, source_target_pairs={{0,1},{1,0},{2,3},{3,2},{4,5},{5,4},{6,7},{7,6},{8,9},{9,8},{10,11... | collective-permute-start | bytes 786440 | tf_op jit(solution)/shard_map/ppermute | solution.py:557
  12.4 27.1 %collective-permute-start.4 = (bf16[128,1024]{1,0:T(8,128)(2,1)}, bf16[128,1024]{1,0:T(8,128)(2,1)S(1)}, u32[]{:S(2)}, u32[]{:S(2)}) collective-permute-start(bf16[128,1024]{1,0:T(8,128)(2,1)} %get-tuple-element.114), channel_id=1, source_target_pairs={{0,2},{1,3},{2,0},{3,1},{4,6},{5,7},{6,4},{7,5},{8,10},{9,11},{10,... | collective-permute-start | bytes 786440 | tf_op jit(solution)/shard_map/ppermute | solution.py:557
  15.3 1.2 %copy-start.3 = (bf16[512,1024]{1,0:T(8,128)(2,1)S(1)}, bf16[512,1024]{1,0:T(8,128)(2,1)}, u32[]{:S(2)}) copy-start(bf16[512,1024]{1,0:T(8,128)(2,1)} %v.4) | copy-start | bytes 3145732
  21.5 5.0 %copy-start.12 = (bf16[128,1024]{1,0:T(8,128)(2,1)S(1)}, bf16[128,1024]{1,0:T(8,128)(2,1)}, u32[]{:S(2)}) copy-start(bf16[128,1024]{1,0:T(8,128)(2,1)} %get-tuple-element.115) | copy-start | bytes 786436
  21.5 5.1 %copy-start.6 = (bf16[2,16,2048]{2,1,0:T(8,128)(2,1)S(1)}, bf16[2,16,2048]{2,1,0:T(8,128)(2,1)}, u32[]{:S(2)}) copy-start(bf16[2,16,2048]{2,1,0:T(8,128)(2,1)} %get-tuple-element.118.refs_0_.far_own) | copy-start | bytes 393220
  26.5 13.1 %collective-permute-start.5 = (bf16[128,1024]{1,0:T(8,128)(2,1)S(1)}, bf16[128,1024]{1,0:T(8,128)(2,1)S(1)}, u32[]{:S(2)}, u32[]{:S(2)}) collective-permute-start(bf16[128,1024]{1,0:T(8,128)(2,1)S(1)} %copy-done.12), channel_id=1, source_target_pairs={{0,3},{1,2},{2,1},{3,0},{4,7},{5,6},{6,5},{7,4},{8,11},{9,10},{10,... | collective-permute-start | bytes 786440 | tf_op jit(solution)/shard_map/ppermute | solution.py:557
  26.9 15.9 %copy-start.9 = (bf16[128,1024]{1,0:T(8,128)(2,1)S(1)}, bf16[128,1024]{1,0:T(8,128)(2,1)}, u32[]{:S(2)}) copy-start(bf16[128,1024]{1,0:T(8,128)(2,1)} %get-tuple-element.128) | copy-start | bytes 786436
  26.9 15.9 %copy-start.11 = (bf16[128,1024]{1,0:T(8,128)(2,1)S(1)}, bf16[128,1024]{1,0:T(8,128)(2,1)}, u32[]{:S(2)}) copy-start(bf16[128,1024]{1,0:T(8,128)(2,1)} %get-tuple-element.139) | copy-start | bytes 786436
  26.9 20.8 %copy-start.4 = (bf16[128,2048]{1,0:T(8,128)(2,1)S(1)}, bf16[128,2048]{1,0:T(8,128)(2,1)}, u32[]{:S(2)}) copy-start(bf16[128,2048]{1,0:T(8,128)(2,1)} %get-tuple-element.111.refs_0_.kv.refs_1_.refs_2_) | copy-start | bytes 1572868
  26.9 20.7 %copy-start.5 = (bf16[128,2048]{1,0:T(8,128)(2,1)S(1)}, bf16[128,2048]{1,0:T(8,128)(2,1)}, u32[]{:S(2)}) copy-start(bf16[128,2048]{1,0:T(8,128)(2,1)} %get-tuple-element.112.refs_1_.qg.refs_2_.refs_3_) | copy-start | bytes 1572868
  27.0 13.8 %collective-permute-start.6 = (bf16[64,2048]{1,0:T(8,128)(2,1)S(1)}, bf16[64,2048]{1,0:T(8,128)(2,1)S(1)}, u32[]{:S(2)}, u32[]{:S(2)}) collective-permute-start(bf16[64,2048]{1,0:T(8,128)(2,1)S(1)} %get-tuple-element.123), channel_id=1, source_target_pairs={{0,8},{4,12},{8,0},{12,4},{16,24},{20,28},{24,16},{28,20},{1,9},{5... | collective-permute-start | bytes 786440 | tf_op jit(solution)/shard_map/ppermute | solution.py:557
  28.7 12.1 %collective-permute-start.8 = (bf16[64,2048]{1,0:T(8,128)(2,1)S(1)}, bf16[64,2048]{1,0:T(8,128)(2,1)S(1)}, u32[]{:S(2)}, u32[]{:S(2)}) collective-permute-start(bf16[64,2048]{1,0:T(8,128)(2,1)S(1)} %get-tuple-element.124), channel_id=1, source_target_pairs={{0,24},{4,28},{8,16},{12,20},{16,8},{20,12},{24,0},{28,4},{1,25},{... | collective-permute-start | bytes 786440 | tf_op jit(solution)/shard_map/ppermute | solution.py:557
  30.2 12.5 %collective-permute-start.7 = (bf16[64,2048]{1,0:T(8,128)(2,1)S(1)}, bf16[64,2048]{1,0:T(8,128)(2,1)S(1)}, u32[]{:S(2)}, u32[]{:S(2)}) collective-permute-start(bf16[64,2048]{1,0:T(8,128)(2,1)S(1)} %get-tuple-element.124), channel_id=1, source_target_pairs={{0,16},{4,20},{8,24},{12,28},{16,0},{20,4},{24,8},{28,12},{1,17},{... | collective-permute-start | bytes 786440 | tf_op jit(solution)/shard_map/ppermute | solution.py:557
  39.5 1.2 %collective-permute-start.9 = (bf16[16,128]{1,0:T(8,128)(2,1)S(1)}, bf16[16,128]{1,0:T(8,128)(2,1)S(1)}, u32[]{:S(2)}, u32[]{:S(2)}) collective-permute-start(bf16[16,128]{1,0:T(8,128)(2,1)S(1)} %slice_add_fusion), channel_id=1, source_target_pairs={{0,4},{4,0},{8,12},{12,8},{16,20},{20,16},{24,28},{28,24},{1,5},{5... | collective-permute-start | bytes 12296 | tf_op jit(solution)/shard_map/ppermute | solution.py:557
  42.7 8.4 %collective-permute-start.10 = (bf16[256,2048]{1,0:T(8,128)(2,1)S(1)}, bf16[256,2048]{1,0:T(8,128)(2,1)S(1)}, u32[]{:S(2)}, u32[]{:S(2)}) collective-permute-start(bf16[256,2048]{1,0:T(8,128)(2,1)S(1)} %shard_map.90), channel_id=1, source_target_pairs={{0,4},{4,0},{8,12},{12,8},{16,20},{20,16},{24,28},{28,24},{1,5},{5... | collective-permute-start | bytes 3145736 | tf_op jit(solution)/shard_map/ppermute | solution.py:557
  42.9 17.0 %collective-permute-start.15 = (bf16[128,1024]{1,0:T(8,128)(2,1)S(1)}, bf16[128,1024]{1,0:T(8,128)(2,1)S(1)}, u32[]{:S(2)}, u32[]{:S(2)}) collective-permute-start(bf16[128,1024]{1,0:T(8,128)(2,1)S(1)} %copy-done.11), channel_id=1, source_target_pairs={{0,1},{1,0},{2,3},{3,2},{4,5},{5,4},{6,7},{7,6},{8,9},{9,8},{10,11... | collective-permute-start | bytes 786440 | tf_op jit(solution)/shard_map/ppermute | solution.py:557
  46.3 13.5 %collective-permute-start.14 = (bf16[96,1024]{1,0:T(8,128)(2,1)S(1)}, bf16[96,1024]{1,0:T(8,128)(2,1)S(1)}, u32[]{:S(2)}, u32[]{:S(2)}) collective-permute-start(bf16[96,1024]{1,0:T(8,128)(2,1)S(1)} %slice.19), channel_id=1, source_target_pairs={{0,2},{1,3},{2,0},{3,1},{4,6},{5,7},{6,4},{7,5},{8,10},{9,11},{10,... | collective-permute-start | bytes 589832 | tf_op jit(solution)/shard_map/ppermute | solution.py:557
  47.7 12.1 %copy-start.10 = (bf16[128,1024]{1,0:T(8,128)(2,1)S(1)}, bf16[128,1024]{1,0:T(8,128)(2,1)}, u32[]{:S(2)}) copy-start(bf16[128,1024]{1,0:T(8,128)(2,1)} %get-tuple-element.174) | copy-start | bytes 786436
  47.7 14.2 %copy-start.7 = (s32[8]{0:T(128)S(1)}, s32[8]{0:T(128)}, u32[]{:S(2)}) copy-start(s32[8]{0:T(128)} %refs_0_.5) | copy-start | bytes 100
  47.7 14.2 %copy-start.8 = (s32[8]{0:T(128)S(1)}, s32[8]{0:T(128)}, u32[]{:S(2)}) copy-start(s32[8]{0:T(128)} %refs_1_.3) | copy-start | bytes 100
  49.4 8.3 %collective-permute-start.11 = (f32[8,128]{1,0:T(8,128)S(1)}, f32[8,128]{1,0:T(8,128)S(1)}, u32[]{:S(2)}, u32[]{:S(2)}) collective-permute-start(f32[8,128]{1,0:T(8,128)S(1)} %get-tuple-element.130), channel_id=1, source_target_pairs={{0,1},{1,0},{2,3},{3,2},{4,5},{5,4},{6,7},{7,6},{8,9},{9,8},{10,11... | collective-permute-start | bytes 12296 | tf_op jit(solution)/shard_map/ppermute | solution.py:557
  51.1 6.6 %collective-permute-start.12 = (f32[8,128]{1,0:T(8,128)S(1)}, f32[8,128]{1,0:T(8,128)S(1)}, u32[]{:S(2)}, u32[]{:S(2)}) collective-permute-start(f32[8,128]{1,0:T(8,128)S(1)} %get-tuple-element.131), channel_id=1, source_target_pairs={{0,2},{1,3},{2,0},{3,1},{4,6},{5,7},{6,4},{7,5},{8,10},{9,11},{10,... | collective-permute-start | bytes 12296 | tf_op jit(solution)/shard_map/ppermute | solution.py:557
  51.2 8.6 %collective-permute-start.13 = (f32[8,128]{1,0:T(8,128)S(1)}, f32[8,128]{1,0:T(8,128)S(1)}, u32[]{:S(2)}, u32[]{:S(2)}) collective-permute-start(f32[8,128]{1,0:T(8,128)S(1)} %get-tuple-element.132), channel_id=1, source_target_pairs={{0,3},{1,2},{2,1},{3,0},{4,7},{5,6},{6,5},{7,4},{8,11},{9,10},{10,... | collective-permute-start | bytes 12296 | tf_op jit(solution)/shard_map/ppermute | solution.py:557
  59.8 17.3 %collective-permute-start.24 = (bf16[128,1024]{1,0:T(8,128)(2,1)S(1)}, bf16[128,1024]{1,0:T(8,128)(2,1)S(1)}, u32[]{:S(2)}, u32[]{:S(2)}) collective-permute-start(bf16[128,1024]{1,0:T(8,128)(2,1)S(1)} %copy-done.10), channel_id=1, source_target_pairs={{0,3},{1,2},{2,1},{3,0},{4,7},{5,6},{6,5},{7,4},{8,11},{9,10},{10,... | collective-permute-start | bytes 786440 | tf_op jit(solution)/shard_map/ppermute | solution.py:557
  61.3 15.9 %collective-permute-start.23 = (bf16[32,1024]{1,0:T(8,128)(2,1)S(1)}, bf16[32,1024]{1,0:T(8,128)(2,1)S(1)}, u32[]{:S(2)}, u32[]{:S(2)}) collective-permute-start(bf16[32,1024]{1,0:T(8,128)(2,1)S(1)} %slice.18), channel_id=1, source_target_pairs={{0,2},{1,3},{2,0},{3,1},{4,6},{5,7},{6,4},{7,5},{8,10},{9,11},{10,... | collective-permute-start | bytes 196616 | tf_op jit(solution)/shard_map/ppermute | solution.py:557
  63.0 6.8 %collective-permute-start.18 = (f32[16,16]{1,0:T(8,128)S(1)}, f32[16,16]{1,0:T(8,128)S(1)}, u32[]{:S(2)}, u32[]{:S(2)}) collective-permute-start(f32[16,16]{1,0:T(8,128)S(1)} %get-tuple-element.158.refs_0_), channel_id=1, source_target_pairs={{0,24},{4,28},{8,16},{12,20},{16,8},{20,12},{24,0},{28,4},{1,25},{... | collective-permute-start | bytes 3080 | tf_op jit(solution)/shard_map/ppermute | solution.py:557
  65.5 4.3 %collective-permute-start.17 = (f32[16,16]{1,0:T(8,128)S(1)}, f32[16,16]{1,0:T(8,128)S(1)}, u32[]{:S(2)}, u32[]{:S(2)}) collective-permute-start(f32[16,16]{1,0:T(8,128)S(1)} %get-tuple-element.158.refs_0_), channel_id=1, source_target_pairs={{0,16},{4,20},{8,24},{12,28},{16,0},{20,4},{24,8},{28,12},{1,17},{... | collective-permute-start | bytes 3080 | tf_op jit(solution)/shard_map/ppermute | solution.py:557
  66.0 3.8 %collective-permute-start.16 = (f32[16,16]{1,0:T(8,128)S(1)}, f32[16,16]{1,0:T(8,128)S(1)}, u32[]{:S(2)}, u32[]{:S(2)}) collective-permute-start(f32[16,16]{1,0:T(8,128)S(1)} %get-tuple-element.158.refs_0_), channel_id=1, source_target_pairs={{0,8},{4,12},{8,0},{12,4},{16,24},{20,28},{24,16},{28,20},{1,9},{5... | collective-permute-start | bytes 3080 | tf_op jit(solution)/shard_map/ppermute | solution.py:557
  69.8 1.9 %collective-permute-start.19 = (f32[16,64]{1,0:T(8,128)S(1)}, f32[16,64]{1,0:T(8,128)S(1)}, u32[]{:S(2)}, u32[]{:S(2)}) collective-permute-start(f32[16,64]{1,0:T(8,128)S(1)} %shard_map.95.refs_1_), channel_id=1, source_target_pairs={{0,4},{4,0},{8,12},{12,8},{16,20},{20,16},{24,28},{28,24},{1,5},{5... | collective-permute-start | bytes 12296 | tf_op jit(solution)/shard_map/ppermute | solution.py:557
  71.8 8.1 %collective-permute-start.22 = (f32[16,256]{1,0:T(8,128)S(1)}, f32[16,256]{1,0:T(8,128)S(1)}, u32[]{:S(2)}, u32[]{:S(2)}) collective-permute-start(f32[16,256]{1,0:T(8,128)S(1)} %shard_map.97.refs_22_), channel_id=1, source_target_pairs={{0,3},{1,2},{2,1},{3,0},{4,7},{5,6},{6,5},{7,4},{8,11},{9,10},{10,... | collective-permute-start | bytes 49160 | tf_op jit(solution)/shard_map/ppermute | solution.py:557
  73.7 6.3 %collective-permute-start.21 = (f32[16,256]{1,0:T(8,128)S(1)}, f32[16,256]{1,0:T(8,128)S(1)}, u32[]{:S(2)}, u32[]{:S(2)}) collective-permute-start(f32[16,256]{1,0:T(8,128)S(1)} %shard_map.97.refs_22_), channel_id=1, source_target_pairs={{0,2},{1,3},{2,0},{3,1},{4,6},{5,7},{6,4},{7,5},{8,10},{9,11},{10,... | collective-permute-start | bytes 49160 | tf_op jit(solution)/shard_map/ppermute | solution.py:557
  75.7 4.3 %collective-permute-start.20 = (f32[16,256]{1,0:T(8,128)S(1)}, f32[16,256]{1,0:T(8,128)S(1)}, u32[]{:S(2)}, u32[]{:S(2)}) collective-permute-start(f32[16,256]{1,0:T(8,128)S(1)} %shard_map.97.refs_22_), channel_id=1, source_target_pairs={{0,1},{1,0},{2,3},{3,2},{4,5},{5,4},{6,7},{7,6},{8,9},{9,8},{10,11... | collective-permute-start | bytes 49160 | tf_op jit(solution)/shard_map/ppermute | solution.py:557
